TPU v7x, 128 devices: a whole 4x4x4 slice. The times are simulated.
128 devices in a mesh: dp: 8 (over y, core), fs: 16 (over z, x).
Axes of the slice: x: 4, y: 4, z: 4, core: 2. Of those that a mesh axis runs over, the one named last changes fastest.
Arguments:
- hidden_in: bfloat16 [2, 32768, 768], P(None, ('dp', 'fs')), may hold values from -24 to 24
- out_grad: bfloat16 [2, 32768, 768], P(None, ('dp', 'fs')), may hold values from -24 to 24
- segments: int32 [2, 32768], P(None, ('dp', 'fs')), may hold values from -1 to 4, as said below
- mask_pos: int32 [2, 128, 16, 2], P(None, ('dp', 'fs')), may hold values from -1 to 255, as said below
- mask_labels: int32 [2, 128, 16, 2], replicated, may hold values from -1 to 51199, as said below
- loss_scale: float32 [], replicated, may hold values from 8192 to 32768
- w_qkv: bfloat16 [768, 2304], P(('dp', 'fs')), may hold values from -0.21875 to 0.21875
- b_query: bfloat16 [768], P(('dp', 'fs')), may hold values from -1.75 to 1.75
- b_value: bfloat16 [768], P(('dp', 'fs')), may hold values from -1.75 to 1.75
- w_attn: bfloat16 [768, 768], P(('dp', 'fs')), may hold values from -1.75 to 1.75
- b_attn: bfloat16 [768], P(('dp', 'fs')), may hold values from -1.75 to 1.75
- attn_gain: bfloat16 [768], P(('dp', 'fs')), may hold values from 0.25 to 1.75
- attn_shift: bfloat16 [768], P(('dp', 'fs')), may hold values from -1.75 to 1.75
- w_expand: bfloat16 [768, 3072], P(('dp', 'fs')), may hold values from -0.21875 to 0.21875
- b_expand: bfloat16 [3072], P(('dp', 'fs')), may hold values from -1.75 to 1.75
- w_shrink: bfloat16 [3072, 768], P(('dp', 'fs')), may hold values from -0.109375 to 0.109375
- b_shrink: bfloat16 [768], P(('dp', 'fs')), may hold values from -1.75 to 1.75
- ffn_gain: bfloat16 [768], P(('dp', 'fs')), may hold values from 0.25 to 1.75
- ffn_shift: bfloat16 [768], P(('dp', 'fs')), may hold values from -1.75 to 1.75
- w_dense: bfloat16 [768, 768], P(('dp', 'fs')), may hold values from -0.21875 to 0.21875
- b_dense: bfloat16 [768], P(('dp', 'fs')), may hold values from -1.75 to 1.75
- dense_gain: bfloat16 [768], P(('dp', 'fs')), may hold values from 0.25 to 1.75
- dense_shift: bfloat16 [768], P(('dp', 'fs')), may hold values from -1.75 to 1.75
- w_vocab: bfloat16 [768, 51200], P(None, ('dp', 'fs')), may hold values from -0.21875 to 0.21875
- b_vocab: bfloat16 [51200], P(('dp', 'fs'))
Outputs:
- activations: bfloat16 [2, 32768, 768], P(None, ('dp', 'fs'))
- loss: float32 [], replicated
- hidden_grad: float32 [2, 32768, 768], P(None, ('dp', 'fs'))
- g_qkv: float32 [768, 2304], P(('dp', 'fs'))
- g_query: float32 [768], P(('dp', 'fs'))
- g_value: float32 [768], P(('dp', 'fs'))
- g_attn: float32 [768, 768], P(('dp', 'fs'))
- g_attn_bias: float32 [768], P(('dp', 'fs'))
- g_attn_gain: float32 [768], P(('dp', 'fs'))
- g_attn_shift: float32 [768], P(('dp', 'fs'))
- g_expand: float32 [768, 3072], P(('dp', 'fs'))
- g_expand_bias: float32 [3072], P(('dp', 'fs'))
- g_shrink: float32 [3072, 768], P(('dp', 'fs'))
- g_shrink_bias: float32 [768], P(('dp', 'fs'))
- g_ffn_gain: float32 [768], P(('dp', 'fs'))
- g_ffn_shift: float32 [768], P(('dp', 'fs'))
- g_dense: float32 [768, 768], P(('dp', 'fs'))
- g_dense_bias: float32 [768], P(('dp', 'fs'))
- g_dense_gain: float32 [768], P(('dp', 'fs'))
- g_dense_shift: float32 [768], P(('dp', 'fs'))
- g_vocab: float32 [768, 51200], P(None, ('dp', 'fs'))
- g_vocab_bias: float32 [51200], P(('dp', 'fs'))
Inputs may be any that keep to these rules, and one draw needn't show every extreme that they name: `segments`: in each micro-batch each device's block of 256 tokens holds sequences numbered 0, 1, ... in order, then -1 on padding at its end; each sequence has 32 to 256 tokens and the first at least half of 256; in every micro-batch some device's block is one sequence of 256 tokens, and some other device's block holds the most sequences. `mask_pos`: entry [m, d, f, s] is the place within device d's block of a masked token whose row goes to the device with d's dp index and fs index f, or -1 for an empty slot; the places of one device and micro-batch are distinct and never padding; in every micro-batch some device fills all its slots, and some device receives 2 rows from every device with its dp index. `mask_labels`: entry [m, o, j, s] is the label of the row in slot s that device o receives from the device with o's dp index and fs index j, and -1 exactly where that slot of mask_pos is empty.
All inputs are finite; a program needn't handle non-finite values.
Results may differ from a plain program's by a relative error of at most 0.015.
Values may be sent and summed in bfloat16 or wider, within the bound.
No kernel may reach another device: no remote copies, remote signals or barrier semaphores. Data moves between devices by JAX's collectives and lax.ppermute only.
A program may use at most 256 MiB of HBM per device.

v0:
```python
import jax
import jax.numpy as jnp
from jax import lax
from jax.sharding import PartitionSpec as P

HEAD_DIM = 64


EPS = 1e-05
HALF_ROOT = 0.7071067811865476
NORMAL_PEAK = 0.3989422804014327
MASKED = -1e30


def merged(array, axis, combine):
    everything = jax.tree.map(lambda part: lax.all_gather(part, axis), array)
    leading = jax.tree.map(lambda part: part[0], everything)

    def turn(k, so_far):
        return combine(so_far, jax.tree.map(lambda part: part[k], everything))

    return lax.fori_loop(1, lax.axis_size(axis), turn, leading)


def gelu_value(values):
    return 0.5 * values * (1.0 + lax.erf(values * HALF_ROOT))


def gelu_slope(values):
    return 0.5 * (1.0 + lax.erf(values * HALF_ROOT)) + values * NORMAL_PEAK * jnp.exp(
        -0.5 * values * values
    )


def layer_norm(values, gain, shift):
    center = values - jnp.mean(values, axis=-1, keepdims=True)
    inverse = lax.rsqrt(jnp.mean(center * center, axis=-1, keepdims=True) + EPS)
    normed = center * inverse
    return (normed * gain + shift, normed, inverse)


def norm_back(grad, normed, inverse, gain):
    scaled = grad * gain
    inner = (
        scaled
        - jnp.mean(scaled, axis=-1, keepdims=True)
        - normed * jnp.mean(scaled * normed, axis=-1, keepdims=True)
    )
    return inner * inverse


def column_sum(values):
    return jnp.sum(values, axis=0, dtype=jnp.float32)


def matmul(left, right):
    return jnp.dot(left, right, preferred_element_type=jnp.float32)


def matmul_tn(left, right):
    return lax.dot_general(
        left, right, (((0,), (0,)), ((), ())), preferred_element_type=jnp.float32
    )


def matmul_nt(left, right):
    return lax.dot_general(
        left, right, (((1,), (1,)), ((), ())), preferred_element_type=jnp.float32
    )


def join_stats(first, second):
    top = jnp.maximum(first[0], second[0])
    total = first[1] * jnp.exp(first[0] - top) + second[1] * jnp.exp(second[0] - top)
    return (top, total, first[2] + second[2])


def local_stats(spread_rows, vocab_w, vocab_b, row_labels, offset):
    logits = matmul(spread_rows, vocab_w) + vocab_b
    column = offset + jnp.arange(vocab_w.shape[1], dtype=jnp.int32)
    hit = row_labels[:, None] == column[None, :]
    top = jnp.max(logits, axis=1)
    total = jnp.sum(jnp.exp(logits - top[:, None]), axis=1)
    label_logit = jnp.sum(jnp.where(hit, logits, 0.0), axis=1)
    return (logits, hit, top, total, label_logit)


def vocab_backward(spread_rows, logits, hit, log_sum, row_weight, vocab_w):
    probs = jnp.exp(logits - log_sum[:, None])
    dlogits = (row_weight[:, None] * (probs - hit.astype(jnp.float32))).astype(jnp.bfloat16)
    part = matmul_nt(dlogits, vocab_w)
    grad_w = matmul_tn(spread_rows, dlogits)
    grad_b = column_sum(dlogits)
    return (part, grad_w, grad_b)


def fetch_layer(
    w_qkv,
    b_query,
    b_value,
    w_attn,
    b_attn,
    attn_gain,
    attn_shift,
    w_expand,
    b_expand,
    w_shrink,
    b_shrink,
    ffn_gain,
    ffn_shift,
    w_dense,
    b_dense,
    dense_gain,
    dense_shift,
):
    return (
        lax.all_gather(w_qkv, ("dp", "fs"), axis=0, tiled=True),
        lax.all_gather(b_query, ("dp", "fs"), axis=0, tiled=True),
        lax.all_gather(b_value, ("dp", "fs"), axis=0, tiled=True),
        lax.all_gather(w_attn, ("dp", "fs"), axis=0, tiled=True),
        lax.all_gather(b_attn, ("dp", "fs"), axis=0, tiled=True),
        lax.all_gather(attn_gain, ("dp", "fs"), axis=0, tiled=True),
        lax.all_gather(attn_shift, ("dp", "fs"), axis=0, tiled=True),
        lax.all_gather(w_expand, ("dp", "fs"), axis=0, tiled=True),
        lax.all_gather(b_expand, ("dp", "fs"), axis=0, tiled=True),
        lax.all_gather(w_shrink, ("dp", "fs"), axis=0, tiled=True),
        lax.all_gather(b_shrink, ("dp", "fs"), axis=0, tiled=True),
        lax.all_gather(ffn_gain, ("dp", "fs"), axis=0, tiled=True),
        lax.all_gather(ffn_shift, ("dp", "fs"), axis=0, tiled=True),
        lax.all_gather(w_dense, ("dp", "fs"), axis=0, tiled=True),
        lax.all_gather(b_dense, ("dp", "fs"), axis=0, tiled=True),
        lax.all_gather(dense_gain, ("dp", "fs"), axis=0, tiled=True),
        lax.all_gather(dense_shift, ("dp", "fs"), axis=0, tiled=True),
    )


def reduce_layer(grads):
    return (
        lax.psum_scatter(grads[0], ("dp", "fs"), scatter_dimension=0, tiled=True),
        lax.psum_scatter(grads[1], ("dp", "fs"), scatter_dimension=0, tiled=True),
        lax.psum_scatter(grads[2], ("dp", "fs"), scatter_dimension=0, tiled=True),
        lax.psum_scatter(grads[3], ("dp", "fs"), scatter_dimension=0, tiled=True),
        lax.psum_scatter(grads[4], ("dp", "fs"), scatter_dimension=0, tiled=True),
        lax.psum_scatter(grads[5], ("dp", "fs"), scatter_dimension=0, tiled=True),
        lax.psum_scatter(grads[6], ("dp", "fs"), scatter_dimension=0, tiled=True),
        lax.psum_scatter(grads[7], ("dp", "fs"), scatter_dimension=0, tiled=True),
        lax.psum_scatter(grads[8], ("dp", "fs"), scatter_dimension=0, tiled=True),
        lax.psum_scatter(grads[9], ("dp", "fs"), scatter_dimension=0, tiled=True),
        lax.psum_scatter(grads[10], ("dp", "fs"), scatter_dimension=0, tiled=True),
        lax.psum_scatter(grads[11], ("dp", "fs"), scatter_dimension=0, tiled=True),
        lax.psum_scatter(grads[12], ("dp", "fs"), scatter_dimension=0, tiled=True),
        lax.psum_scatter(grads[13], ("dp", "fs"), scatter_dimension=0, tiled=True),
        lax.psum_scatter(grads[14], ("dp", "fs"), scatter_dimension=0, tiled=True),
        lax.psum_scatter(grads[15], ("dp", "fs"), scatter_dimension=0, tiled=True),
        lax.psum_scatter(grads[16], ("dp", "fs"), scatter_dimension=0, tiled=True),
    )


def vocab_fetch(w_vocab, b_vocab):
    return (
        lax.all_gather(w_vocab, "fs", axis=1, tiled=True),
        lax.all_gather(b_vocab, "fs", axis=0, tiled=True),
    )


def vocab_reduce(grad_w, grad_b):
    return (
        lax.psum_scatter(grad_w, "fs", scatter_dimension=1, tiled=True),
        lax.psum_scatter(grad_b, "fs", scatter_dimension=0, tiled=True),
    )


def attention_scores(query, keys, allowed, factor):
    raw = jnp.einsum("qhd,khd->hqk", query, keys, preferred_element_type=jnp.float32)
    return jnp.where(allowed, raw * factor, MASKED)


def run_batch(x, seg, cotangent, positions, labels, norm, loss_scale, full, vocab_w, vocab_b):
    (
        w_qkv,
        b_query,
        b_value,
        w_attn,
        b_attn,
        attn_gain,
        attn_shift,
        w_expand,
        b_expand,
        w_shrink,
        b_shrink,
        ffn_gain,
        ffn_shift,
        w_dense,
        b_dense,
        dense_gain,
        dense_shift,
    ) = full
    tokens, width = x.shape
    heads = width // HEAD_DIM
    factor = HEAD_DIM ** (-0.5)
    united = matmul(x, w_qkv)
    query = (united[:, :width] + b_query).astype(jnp.bfloat16).reshape(tokens, heads, HEAD_DIM)
    keys = united[:, width : 2 * width].astype(jnp.bfloat16).reshape(tokens, heads, HEAD_DIM)
    values = (
        (united[:, 2 * width :] + b_value).astype(jnp.bfloat16).reshape(tokens, heads, HEAD_DIM)
    )
    allowed = (seg[:, None] == seg[None, :])[None]
    scores = attention_scores(query, keys, allowed, factor)
    peak = jnp.max(scores, axis=-1, keepdims=True)
    expo = jnp.exp(scores - peak)
    total = jnp.sum(expo, axis=-1, keepdims=True)
    weights = (expo / total).astype(jnp.bfloat16)
    log_total = peak + jnp.log(total)
    attended = (
        jnp.einsum("hqk,khd->qhd", weights, values, preferred_element_type=jnp.float32)
        .reshape(tokens, width)
        .astype(jnp.bfloat16)
    )
    branch = matmul(attended, w_attn) + b_attn
    first, normed1, inverse1 = layer_norm(x.astype(jnp.float32) + branch, attn_gain, attn_shift)
    first_low = first.astype(jnp.bfloat16)
    pre = matmul(first_low, w_expand) + b_expand
    act = gelu_value(pre).astype(jnp.bfloat16)
    second = first + matmul(act, w_shrink) + b_shrink
    settled, normed2, inverse2 = layer_norm(second, ffn_gain, ffn_shift)
    settled_low = settled.astype(jnp.bfloat16)
    place = jnp.arange(tokens, dtype=jnp.int32)
    select = (positions[:, None] == place[None, :]).astype(jnp.bfloat16)
    rows = positions.shape[0]
    peers = lax.axis_size("fs")
    picked = matmul(select, settled_low).astype(jnp.bfloat16).reshape(peers, rows // peers, width)
    arrived = lax.all_to_all(picked, "fs", split_axis=0, concat_axis=0, tiled=True).reshape(
        rows, width
    )
    dense_pre = matmul(arrived, w_dense) + b_dense
    head_val, normed3, inverse3 = layer_norm(gelu_value(dense_pre), dense_gain, dense_shift)
    head_out = head_val.astype(jnp.bfloat16)
    spread_rows = lax.all_gather(head_out, "dp", axis=0, tiled=True)
    grouped = labels.reshape(lax.axis_size("dp"), peers, rows)
    row_labels = lax.dynamic_index_in_dim(grouped, lax.axis_index("fs"), 1, False).reshape(-1)
    offset = lax.axis_index("dp") * vocab_w.shape[1]
    own_start = lax.axis_index("dp") * rows
    logits, hit, top, total_v, label_logit = local_stats(
        spread_rows, vocab_w, vocab_b, row_labels, offset
    )
    top, total_v, label_logit = merged((top, total_v, label_logit), "dp", join_stats)
    live = (row_labels >= 0).astype(jnp.float32)
    log_sum = top + jnp.log(total_v)
    part, grad_w, grad_b = vocab_backward(
        spread_rows, logits, hit, log_sum, loss_scale * norm * live, vocab_w
    )
    row_grad = lax.psum_scatter(part, "dp", scatter_dimension=0, tiled=True)
    own_loss = lax.dynamic_slice_in_dim((log_sum - label_logit) * live, own_start, rows)
    loss_term = jnp.sum(own_loss) * norm
    g_dense_gain = column_sum(row_grad * normed3)
    g_dense_shift = column_sum(row_grad)
    ddense = (norm_back(row_grad, normed3, inverse3, dense_gain) * gelu_slope(dense_pre)).astype(
        jnp.bfloat16
    )
    g_dense = matmul_tn(arrived, ddense)
    g_dense_bias = column_sum(ddense)
    dpicked = matmul_nt(ddense, w_dense).astype(jnp.bfloat16).reshape(peers, rows // peers, width)
    returned = lax.all_to_all(dpicked, "fs", split_axis=0, concat_axis=0, tiled=True).reshape(
        rows, width
    )
    dout = cotangent.astype(jnp.float32) + matmul_tn(select, returned)
    g_ffn_gain = column_sum(dout * normed2)
    g_ffn_shift = column_sum(dout)
    dsecond = norm_back(dout, normed2, inverse2, ffn_gain)
    dffn = dsecond.astype(jnp.bfloat16)
    g_shrink = matmul_tn(act, dffn)
    g_shrink_bias = column_sum(dffn)
    dpre = (matmul_nt(dffn, w_shrink) * gelu_slope(pre)).astype(jnp.bfloat16)
    g_expand = matmul_tn(first_low, dpre)
    g_expand_bias = column_sum(dpre)
    dfirst = dsecond + matmul_nt(dpre, w_expand)
    g_attn_gain = column_sum(dfirst * normed1)
    g_attn_shift = column_sum(dfirst)
    dresidual = norm_back(dfirst, normed1, inverse1, attn_gain)
    dbranch = dresidual.astype(jnp.bfloat16)
    g_attn = matmul_tn(attended, dbranch)
    g_attn_bias = column_sum(dbranch)
    dattended = matmul_nt(dbranch, w_attn).astype(jnp.bfloat16).reshape(tokens, heads, HEAD_DIM)
    probs = jnp.exp(attention_scores(query, keys, allowed, factor) - log_total)
    dprobs = jnp.einsum("qhd,khd->hqk", dattended, values, preferred_element_type=jnp.float32)
    inner = jnp.sum(probs * dprobs, axis=-1, keepdims=True)
    dscores = (probs * (dprobs - inner)).astype(jnp.bfloat16)
    dquery = (
        (jnp.einsum("hqk,khd->qhd", dscores, keys, preferred_element_type=jnp.float32) * factor)
        .astype(jnp.bfloat16)
        .reshape(tokens, width)
    )
    dkeys = (
        (jnp.einsum("hqk,qhd->khd", dscores, query, preferred_element_type=jnp.float32) * factor)
        .astype(jnp.bfloat16)
        .reshape(tokens, width)
    )
    dvalues = (
        jnp.einsum("hqk,qhd->khd", weights, dattended, preferred_element_type=jnp.float32)
        .astype(jnp.bfloat16)
        .reshape(tokens, width)
    )
    dfused = jnp.concatenate([dquery, dkeys, dvalues], axis=1)
    g_qkv = matmul_tn(x, dfused)
    g_query = column_sum(dquery)
    g_value = column_sum(dvalues)
    dinput = dresidual + matmul_nt(dfused, w_qkv)
    layer_grads = (
        g_qkv,
        g_query,
        g_value,
        g_attn,
        g_attn_bias,
        g_attn_gain,
        g_attn_shift,
        g_expand,
        g_expand_bias,
        g_shrink,
        g_shrink_bias,
        g_ffn_gain,
        g_ffn_shift,
        g_dense,
        g_dense_bias,
        g_dense_gain,
        g_dense_shift,
    )
    return (settled_low, dinput, layer_grads, (grad_w, grad_b), loss_term)


def add_trees(first, second):
    if first is None:
        return second
    return jax.tree.map(jnp.add, first, second)


def body(
    hidden_in,
    out_grad,
    segments,
    mask_pos,
    mask_labels,
    loss_scale,
    w_qkv,
    b_query,
    b_value,
    w_attn,
    b_attn,
    attn_gain,
    attn_shift,
    w_expand,
    b_expand,
    w_shrink,
    b_shrink,
    ffn_gain,
    ffn_shift,
    w_dense,
    b_dense,
    dense_gain,
    dense_shift,
    w_vocab,
    b_vocab,
):
    micro = hidden_in.shape[0]
    flat_labels = mask_labels.reshape(micro, -1)
    counts = jnp.sum((flat_labels >= 0).astype(jnp.float32), axis=1)
    norms = 1.0 / (counts * micro)
    outputs_seen = []
    input_grads = []
    loss_terms = []
    layer_parts = None
    vocab_parts = None
    for index in range(micro):
        full = fetch_layer(
            w_qkv,
            b_query,
            b_value,
            w_attn,
            b_attn,
            attn_gain,
            attn_shift,
            w_expand,
            b_expand,
            w_shrink,
            b_shrink,
            ffn_gain,
            ffn_shift,
            w_dense,
            b_dense,
            dense_gain,
            dense_shift,
        )
        vocab_w, vocab_b = vocab_fetch(w_vocab, b_vocab)
        settled, dinput, layer_grads, vocab_grads, loss_term = run_batch(
            hidden_in[index],
            segments[index],
            out_grad[index],
            mask_pos[index].reshape(-1),
            flat_labels[index],
            norms[index],
            loss_scale,
            full,
            vocab_w,
            vocab_b,
        )
        outputs_seen.append(settled)
        input_grads.append(dinput)
        loss_terms.append(loss_term)
        layer_parts = add_trees(layer_parts, tuple(reduce_layer(layer_grads)))
        vocab_parts = add_trees(vocab_parts, tuple(vocab_reduce(vocab_grads[0], vocab_grads[1])))
    loss = lax.psum(jnp.sum(jnp.stack(loss_terms)), ("dp", "fs"))
    return (
        jnp.stack(outputs_seen),
        loss,
        jnp.stack(input_grads),
        layer_parts[0],
        layer_parts[1],
        layer_parts[2],
        layer_parts[3],
        layer_parts[4],
        layer_parts[5],
        layer_parts[6],
        layer_parts[7],
        layer_parts[8],
        layer_parts[9],
        layer_parts[10],
        layer_parts[11],
        layer_parts[12],
        layer_parts[13],
        layer_parts[14],
        layer_parts[15],
        layer_parts[16],
        vocab_parts[0],
        vocab_parts[1],
    )


def solution(mesh):
    in_specs = (
        P(None, ("dp", "fs"), None),
        P(None, ("dp", "fs"), None),
        P(None, ("dp", "fs")),
        P(None, ("dp", "fs"), None, None),
        P(),
        P(),
        P(("dp", "fs"), None),
        P(("dp", "fs")),
        P(("dp", "fs")),
        P(("dp", "fs"), None),
        P(("dp", "fs")),
        P(("dp", "fs")),
        P(("dp", "fs")),
        P(("dp", "fs"), None),
        P(("dp", "fs")),
        P(("dp", "fs"), None),
        P(("dp", "fs")),
        P(("dp", "fs")),
        P(("dp", "fs")),
        P(("dp", "fs"), None),
        P(("dp", "fs")),
        P(("dp", "fs")),
        P(("dp", "fs")),
        P(None, ("dp", "fs")),
        P(("dp", "fs")),
    )
    out_specs = (
        P(None, ("dp", "fs"), None),
        P(),
        P(None, ("dp", "fs"), None),
        P(("dp", "fs"), None),
        P(("dp", "fs")),
        P(("dp", "fs")),
        P(("dp", "fs"), None),
        P(("dp", "fs")),
        P(("dp", "fs")),
        P(("dp", "fs")),
        P(("dp", "fs"), None),
        P(("dp", "fs")),
        P(("dp", "fs"), None),
        P(("dp", "fs")),
        P(("dp", "fs")),
        P(("dp", "fs")),
        P(("dp", "fs"), None),
        P(("dp", "fs")),
        P(("dp", "fs")),
        P(("dp", "fs")),
        P(None, ("dp", "fs")),
        P(("dp", "fs")),
    )
    return jax.shard_map(body, mesh=mesh, in_specs=in_specs, out_specs=out_specs, check_vma=False)
```

profile of v0, /device:TPU:0, one launch (start us, length us, event | category | flops | bytes accessed | tf_op | source)
XLA Modules:
  0.0 1741.7 jit_solution(9276349179400505381)
XLA Ops:
  21.2 69.5 %all-reduce.34 = (bf16[768]{0:T(1024)(128)(2,1)S(1)}, bf16[768]{0:T(1024)(128)(2,1)S(1)}, bf16[768]{0:T(1024)(128)(2,1)S(1)}, bf16[768]{0:T(1024)(128)(2,1)S(1)}...) all-reduce(bf16[768]{0:T(1024)(128)(2,1)S(1)} %dynamic-update-slice, ...), channel_id=1, replica_groups=mesh['dp'=8,'fs'=16] {'dp','fs'}, use_global_device_ids=true, to_apply=%add | all-reduce | flops 11520 | bytes 46080
  105.1 39.8 %all-gather.27.cloned.1.call-done = bf16[128,6,2304]{2,1,0:T(8,128)(2,1)} async-done(((bf16[1,6,2304]{2,1,0:T(8,128)(2,1)}), bf16[128,6,2304]{2,1,0:T(8,128)(2,1)}) %all-gather.27.cloned.1.call-update) | async-done | bytes 3538960 | tf_op jit(solution)/shard_map/all_gather | solution.py:117
  144.9 6.6 reshape.452
  180.0 33.7 %all-gather.31.cloned.1.call-done = bf16[128,6,3072]{2,1,0:T(8,128)(2,1)} async-done(((bf16[1,6,3072]{2,1,0:T(8,128)(2,1)}), bf16[128,6,3072]{2,1,0:T(8,128)(2,1)}) %all-gather.31.cloned.1.call-update) | async-done | bytes 4718608 | tf_op jit(solution)/shard_map/all_gather | solution.py:124
  213.7 7.9 reshape.456
  221.6 5.7 convolution_add_fusion.5
  227.3 53.8 %all-gather.23.cloned.1.call-done = bf16[3072,768]{1,0:T(8,128)(2,1)} async-done(((bf16[24,768]{1,0:T(8,128)(2,1)}), bf16[3072,768]{1,0:T(8,128)(2,1)}) %all-gather.23.cloned.1.call-update) | async-done | bytes 4718608 | tf_op jit(solution)/shard_map/all_gather | solution.py:126
  281.1 5.2 fusion.99
  296.8 4.5 all-to-all-start
  304.6 4.4 all-to-all-done
  309.0 4.1 all-to-all-start.1
  323.7 75.3 %all-reduce.12 = bf16[6400]{0:T(1024)(128)(2,1)} all-reduce(bf16[6400]{0:T(1024)(128)(2,1)} %dynamic-update-slice.12), channel_id=1, replica_groups=mesh['dp'=8,'fs'=16] {'fs'}, use_global_device_ids=true, to_apply=%add.12 | all-reduce | flops 6400 | bytes 25600
  418.7 14.1 all_gather.144
  432.7 14.1 all_gather.135
  446.8 5.8 fusion.100
  452.6 9.3 all-gather.10
  463.1 6.1 fusion.101
  469.2 3.7 fusion.7
  473.0 8.4 all-gather.14
  482.5 9.2 all-gather.15
  492.9 8.3 all-gather.11
  502.4 9.2 all-gather.12
  512.8 8.3 all-gather.13
  522.3 27.6 %while.38 = (s32[]{:T(128)}, f32[256]{0:T(256)}, f32[256]{0:T(256)}, f32[256]{0:T(256)}, f32[8,256]{1,0:T(8,128)}, /*index=5*/f32[8,256]{1,0:T(8,128)}, f32[8,256]{1,0:T(8,128)}, s32[]{:T(128)}, s32[]{:T(128)}, s32[]{:T(128)}) while((s32[]{:T(128)}, f32[256]{0:T(256)}, f32[256]{0:T(256)}, f32[256]{0:T(256)}, f32[8,256]{1,0:T(8,128)}, ...), condition=%wide.region_18.19_spmd, body=%wide.region_17.18_spmd.sunk | while | flops 1797 | bytes 15503 | solution.py:22
  549.9 27.7 %while.39 = (s32[]{:T(128)}, f32[256]{0:T(256)}, f32[256]{0:T(256)}, f32[256]{0:T(256)}, f32[8,256]{1,0:T(8,128)}, /*index=5*/f32[8,256]{1,0:T(8,128)}, f32[8,256]{1,0:T(8,128)}, s32[]{:T(128)}, s32[]{:T(128)}, s32[]{:T(128)}) while((s32[]{:T(128)}, f32[256]{0:T(256)}, f32[256]{0:T(256)}, f32[256]{0:T(256)}, f32[8,256]{1,0:T(8,128)}, ...), condition=%wide.region_27.28_spmd, body=%wide.region_26.27_spmd.sunk | while | flops 1797 | bytes 15503 | solution.py:22
  580.1 9.2 convert_reduce_fusion
  591.0 7.4 fusion.103
  598.5 8.5 fusion.102
  609.7 15.0 reduce-scatter.14.cloned.1.call-done
  627.3 30.2 %reduce-scatter.12.cloned.1.call-done = f32[32,768]{1,0:T(8,128)} async-done(((f32[256,768]{1,0:T(8,128)}), f32[32,768]{1,0:T(8,128)}) %reduce-scatter.12.cloned.1.call-update) | async-done | bytes 98320 | tf_op jit(solution)/shard_map/reduce_scatter | solution.py:252
  664.2 7.0 all-to-all-start.3
  678.9 5.9 all-to-all-start.2
  697.3 6.1 convert_reduce_fusion.2
  740.0 3.9 add_bitcast_fusion
  747.5 4.8 convolution_add_fusion.3
  753.3 11.9 fusion.105
  765.3 13.4 convolution_add_fusion
  786.3 5.2 convolution_add_fusion.4
  791.5 408.0 %fusion.82 = (f32[8,768]{1,0:T(8,128)}, f32[8,3072]{1,0:T(8,128)}, f32[8,768]{1,0:T(8,128)}) fusion(f32[768,768]{1,0:T(8,128)} %convolution_add_fusion.7, f32[768,3072]{1,0:T(8,128)} %convolution_add_fusion.4, f32[768,768]{1,0:T(8,128)S(1)} %copy-done.13), kind=kCustom, calls=%all-reduce-scatter.3 | all-reduce-scatter fusion | flops 4718593 | bytes 14303232
  1214.4 15.2 collective-permute-start.23
  1229.6 4.7 collective-permute-start.22
  1248.0 6.0 collective-permute-start.14
  1259.1 3.9 collective-permute-start.10
  1263.0 4.0 collective-permute-start.9
  1275.5 4.0 collective-permute-start.5
  1284.0 5.8 collective-permute-start.2
  1328.0 4.7 collective-permute-start.78
  1339.6 3.7 collective-permute-start.73
  1354.9 4.4 collective-permute-start.69
  1363.8 5.8 collective-permute-start.66
  1369.7 3.9 collective-permute-start.65
  1393.9 70.9 %all-reduce.29 = f32[6400]{0:T(1024)S(1)} all-reduce(f32[6400]{0:T(1024)S(1)} %add.637), channel_id=47, replica_groups=mesh['dp'=8,'fs'=16] {'fs'}, use_global_device_ids=true, to_apply=%region_107.108.clone | all-reduce | flops 6400 | bytes 51200
  1477.1 4.4 fusion.24
  1498.7 4.0 fusion.23
  1503.0 64.6 %all-reduce.33 = (f32[]{:T(128)}, f32[768]{0:T(1024)S(1)}, f32[768]{0:T(1024)S(1)}, f32[768]{0:T(1024)S(1)}, f32[768]{0:T(1024)S(1)}, /*index=5*/f32[768]{0:T(10...) all-reduce(f32[]{:T(128)S(6)} %reduce_sum.585, ...), channel_id=1, replica_groups=mesh['dp'=8,'fs'=16] {'dp','fs'}, use_global_device_ids=true, to_apply=%region_29.30 | all-reduce | flops 11521 | bytes 92168 | tf_op jit(solution)/shard_map/psum | solution.py:410
  1574.6 4.5 collective-permute-start.46
  1586.6 6.9 collective-permute-start.42
  1596.0 15.3 concatenate.8
  1611.4 26.5 %concatenate.10 = f32[262,768]{1,0:T(8,128)S(1)} concatenate(f32[6,768]{1,0:T(8,128)S(1)} %copy-done.110, f32[8,768]{1,0:T(8,128)} %copy-done.159, f32[8,768]{1,0:T(8,128)} %copy-done.160, f32[8,768]{1,0:T(8,128)} %copy-done.161, f32[8,768]{1,0:T(8,128)} %copy-done.162, f32[8,768]{1,0:T(8,128)} %collective-permute-done.90, f32[8,768]{1,0:T(8,128)} %collective-permute-done.89, ...), dimensions={0} | concatenate | bytes 1609728
  1637.8 3.7 collective-permute-start.41
  1644.3 3.8 collective-permute-start.39
  1648.1 5.4 collective-permute-start.38
  1662.9 5.8 collective-permute-start.34
  1676.5 53.7 %concatenate.9 = f32[262,3072]{1,0:T(8,128)} concatenate(f32[6,3072]{1,0:T(8,128)S(1)} %copy-done.92, f32[8,3072]{1,0:T(8,128)S(1)} %copy-done.90, f32[8,3072]{1,0:T(8,128)S(1)} %copy-done.94, f32[8,3072]{1,0:T(8,128)S(1)} %copy-done.96, f32[8,3072]{1,0:T(8,128)S(1)} %copy-done.98, f32[8,3072]{1,0:T(8,128)} %collective-permute-done.58, f32[8,3072]{1,0:T(8,128)} %collective-permute-done.57, ...), dimensions={0} | concatenate | bytes 6438912
  (899 shorter events, 438.8 us)
Async XLA Ops:
  7.2 94.7 %all-gather.29.cloned.1.call-start = ((), (), s32[]{:S(2)}) async-start(), calls=%async_computation.15 | async-start | bytes 1585152 | tf_op jit(solution)/shard_map/all_gather | solution.py:120
  7.9 137.0 %all-gather.27.cloned.1.call-start = ((), (), s32[]{:S(2)}) async-start(), calls=%async_computation.14 | async-start | bytes 4755456 | tf_op jit(solution)/shard_map/all_gather | solution.py:117
  8.7 205.0 %all-gather.31.cloned.1.call-start = ((), (), s32[]{:S(2)}) async-start(), calls=%async_computation.16 | async-start | bytes 6340608 | tf_op jit(solution)/shard_map/all_gather | solution.py:124
  9.4 271.7 %all-gather.23.cloned.1.call-start = ((), (), s32[]{:S(2)}) async-start(), calls=%async_computation.8 | async-start | bytes 4755456 | tf_op jit(solution)/shard_map/all_gather | solution.py:126
  10.0 396.2 %all-gather.33.cloned.1.call-start = ((), (), s32[]{:S(2)}) async-start(), calls=%async_computation.17 | async-start | bytes 1585152 | tf_op jit(solution)/shard_map/all_gather | solution.py:130
  10.6 436.2 %all-gather.25.cloned.1.call-start = ((), (), s32[]{:S(2)}) async-start(), calls=%async_computation.9 | async-start | bytes 10444800 | tf_op jit(solution)/shard_map/all_gather | solution.py:161
  309.0 101.9 %all-to-all-start.1 = ((bf16[16,2,768]{2,1,0:T(2,128)(2,1)}), bf16[16,2,768]{2,1,0:T(2,128)(2,1)}, u32[]{:S(2)}, u32[]{:S(2)}) async-start(bf16[16,2,768]{2,1,0:T(2,128)(2,1)} %reshape.388), calls=%async_computation.1 | async-start | bytes 98304 | tf_op jit(solution)/shard_map/all_to_all | solution.py:232
  313.1 311.6 %reduce-scatter.14.cloned.1.call-start = ((), (), s32[]{:S(2)}) async-start(), calls=%async_computation.11 | async-start | bytes 884736 | tf_op jit(solution)/shard_map/reduce_scatter | solution.py:252
  598.4 59.1 %reduce-scatter.12.cloned.1.call-start = ((), (), s32[]{:S(2)}) async-start(), calls=%async_computation.10 | async-start | bytes 884736 | tf_op jit(solution)/shard_map/reduce_scatter | solution.py:252
  664.2 14.6 all-to-all-start.3
  684.8 1047.1 %all-reduce.38.cloned.1.call-start = ((), (), s32[]{:S(2)}) async-start(), calls=%async_computation.18 | async-start | bytes 14155776
  743.9 990.9 %reduce-scatter.16.cloned.1.call-start = ((), (), s32[]{:S(2)}) async-start(), calls=%async_computation.12 | async-start | bytes 9510912 | tf_op jit(solution)/shard_map/reduce_scatter | solution.py:148
  752.4 982.5 %reduce-scatter.18.cloned.1.call-start = ((), (), s32[]{:S(2)}) async-start(), calls=%async_computation.13 | async-start | bytes 20889600 | tf_op jit(solution)/shard_map/reduce_scatter | solution.py:168
  1205.4 24.2 %collective-permute-start.27 = (f32[8,768]{1,0:T(8,128)}, f32[8,768]{1,0:T(8,128)S(1)}, u32[]{:S(2)}, u32[]{:S(2)}) collective-permute-start(f32[8,768]{1,0:T(8,128)} %get-tuple-element.536), channel_id=1, source_target_pairs={{0,28},{1,29},{2,30},{3,31},{4,32},{5,33},{6,34},{7,35},{8,36},{9,... | collective-permute-start | bytes 73736
  1210.3 24.0 %collective-permute-start.26 = (f32[8,768]{1,0:T(8,128)}, f32[8,768]{1,0:T(8,128)S(1)}, u32[]{:S(2)}, u32[]{:S(2)}) collective-permute-start(f32[8,768]{1,0:T(8,128)} %get-tuple-element.536), channel_id=1, source_target_pairs={{0,27},{1,28},{2,29},{3,30},{4,31},{5,32},{6,33},{7,34},{8,35},{9,... | collective-permute-start | bytes 73736
  1211.7 24.8 %collective-permute-start.25 = (f32[8,768]{1,0:T(8,128)}, f32[8,768]{1,0:T(8,128)S(1)}, u32[]{:S(2)}, u32[]{:S(2)}) collective-permute-start(f32[8,768]{1,0:T(8,128)} %get-tuple-element.536), channel_id=1, source_target_pairs={{0,26},{1,27},{2,28},{3,29},{4,30},{5,31},{6,32},{7,33},{8,34},{9,... | collective-permute-start | bytes 73736
  1213.1 24.8 %collective-permute-start.24 = (f32[8,768]{1,0:T(8,128)}, f32[8,768]{1,0:T(8,128)S(1)}, u32[]{:S(2)}, u32[]{:S(2)}) collective-permute-start(f32[8,768]{1,0:T(8,128)} %get-tuple-element.536), channel_id=1, source_target_pairs={{0,25},{1,26},{2,27},{3,28},{4,29},{5,30},{6,31},{7,32},{8,33},{9,... | collective-permute-start | bytes 73736
  1214.4 24.8 %collective-permute-start.23 = (f32[8,768]{1,0:T(8,128)}, f32[8,768]{1,0:T(8,128)S(1)}, u32[]{:S(2)}, u32[]{:S(2)}) collective-permute-start(f32[8,768]{1,0:T(8,128)} %get-tuple-element.536), channel_id=1, source_target_pairs={{0,24},{1,25},{2,26},{3,27},{4,28},{5,29},{6,30},{7,31},{8,32},{9,... | collective-permute-start | bytes 73736
  1239.2 14.8 collective-permute-start.18
  1241.5 13.8 collective-permute-start.17
  1243.7 13.6 collective-permute-start.16
  1248.0 15.0 collective-permute-start.14
  1255.3 13.8 collective-permute-start.12
  1257.3 14.7 collective-permute-start.11
  1259.1 16.4 collective-permute-start.10
  1263.0 16.5 collective-permute-start.9
  1267.0 13.8 collective-permute-start.8
  1269.1 14.8 collective-permute-start.7
  1272.0 17.7 %collective-permute-start.6 = (f32[8,768]{1,0:T(8,128)}, f32[8,768]{1,0:T(8,128)S(1)}, u32[]{:S(2)}, u32[]{:S(2)}) collective-permute-start(f32[8,768]{1,0:T(8,128)} %get-tuple-element.536), channel_id=1, source_target_pairs={{0,7},{1,8},{2,9},{3,10},{4,11},{5,12},{6,13},{7,14},{8,15},{9,16}... | collective-permute-start | bytes 73736
  1275.5 17.4 collective-permute-start.5
  1279.5 15.0 collective-permute-start.4
  1280.9 16.8 collective-permute-start.3
  1284.0 15.0 collective-permute-start.2
  1319.2 13.6 collective-permute-start.82
  1339.6 14.0 collective-permute-start.73
  1343.4 40.6 %collective-permute-start.62 = (f32[8,3072]{1,0:T(8,128)}, f32[8,3072]{1,0:T(8,128)S(1)}, u32[]{:S(2)}, u32[]{:S(2)}) collective-permute-start(f32[8,3072]{1,0:T(8,128)} %get-tuple-element.537), channel_id=1, source_target_pairs={{0,31},{1,32},{2,33},{3,34},{4,35},{5,36},{6,37},{7,38},{8,39},{9,... | collective-permute-start | bytes 294920
  1353.6 27.3 %collective-permute-start.63 = (f32[6,3072]{1,0:T(8,128)S(1)}, f32[6,3072]{1,0:T(8,128)S(1)}, u32[]{:S(2)}, u32[]{:S(2)}) collective-permute-start(f32[6,3072]{1,0:T(8,128)S(1)} %slice.125), channel_id=1, source_target_pairs={{0,32},{1,33},{2,34},{3,35},{4,36},{5,37},{6,38},{7,39},{8,40},{9,... | collective-permute-start | bytes 221192
  1376.4 93.3 %collective-permute-start.61 = (f32[8,3072]{1,0:T(8,128)}, f32[8,3072]{1,0:T(8,128)S(1)}, u32[]{:S(2)}, u32[]{:S(2)}) collective-permute-start(f32[8,3072]{1,0:T(8,128)} %get-tuple-element.537), channel_id=1, source_target_pairs={{0,30},{1,31},{2,32},{3,33},{4,34},{5,35},{6,36},{7,37},{8,38},{9,... | collective-permute-start | bytes 294920
  1378.2 92.9 %collective-permute-start.60 = (f32[8,3072]{1,0:T(8,128)}, f32[8,3072]{1,0:T(8,128)S(1)}, u32[]{:S(2)}, u32[]{:S(2)}) collective-permute-start(f32[8,3072]{1,0:T(8,128)} %get-tuple-element.537), channel_id=1, source_target_pairs={{0,29},{1,30},{2,31},{3,32},{4,33},{5,34},{6,35},{7,36},{8,37},{9,... | collective-permute-start | bytes 294920
  1379.6 92.9 %collective-permute-start.59 = (f32[8,3072]{1,0:T(8,128)}, f32[8,3072]{1,0:T(8,128)S(1)}, u32[]{:S(2)}, u32[]{:S(2)}) collective-permute-start(f32[8,3072]{1,0:T(8,128)} %get-tuple-element.537), channel_id=1, source_target_pairs={{0,28},{1,29},{2,30},{3,31},{4,32},{5,33},{6,34},{7,35},{8,36},{9,... | collective-permute-start | bytes 294920
  1380.9 92.9 %collective-permute-start.58 = (f32[8,3072]{1,0:T(8,128)}, f32[8,3072]{1,0:T(8,128)}, u32[]{:S(2)}, u32[]{:S(2)}) collective-permute-start(f32[8,3072]{1,0:T(8,128)} %get-tuple-element.537), channel_id=1, source_target_pairs={{0,27},{1,28},{2,29},{3,30},{4,31},{5,32},{6,33},{7,34},{8,35},{9,... | collective-permute-start | bytes 294920
  1384.0 91.2 %collective-permute-start.57 = (f32[8,3072]{1,0:T(8,128)}, f32[8,3072]{1,0:T(8,128)}, u32[]{:S(2)}, u32[]{:S(2)}) collective-permute-start(f32[8,3072]{1,0:T(8,128)} %get-tuple-element.537), channel_id=1, source_target_pairs={{0,26},{1,27},{2,28},{3,29},{4,30},{5,31},{6,32},{7,33},{8,34},{9,... | collective-permute-start | bytes 294920
  1469.7 17.5 %collective-permute-start.56 = (f32[8,3072]{1,0:T(8,128)}, f32[8,3072]{1,0:T(8,128)S(1)}, u32[]{:S(2)}, u32[]{:S(2)}) collective-permute-start(f32[8,3072]{1,0:T(8,128)} %get-tuple-element.537), channel_id=1, source_target_pairs={{0,25},{1,26},{2,27},{3,28},{4,29},{5,30},{6,31},{7,32},{8,33},{9,... | collective-permute-start | bytes 294920
  1471.2 18.1 %collective-permute-start.55 = (f32[8,3072]{1,0:T(8,128)}, f32[8,3072]{1,0:T(8,128)S(1)}, u32[]{:S(2)}, u32[]{:S(2)}) collective-permute-start(f32[8,3072]{1,0:T(8,128)} %get-tuple-element.537), channel_id=1, source_target_pairs={{0,24},{1,25},{2,26},{3,27},{4,28},{5,29},{6,30},{7,31},{8,32},{9,... | collective-permute-start | bytes 294920
  1472.5 20.4 %collective-permute-start.54 = (f32[8,3072]{1,0:T(8,128)}, f32[8,3072]{1,0:T(8,128)S(1)}, u32[]{:S(2)}, u32[]{:S(2)}) collective-permute-start(f32[8,3072]{1,0:T(8,128)} %get-tuple-element.537), channel_id=1, source_target_pairs={{0,23},{1,24},{2,25},{3,26},{4,27},{5,28},{6,29},{7,30},{8,31},{9,... | collective-permute-start | bytes 294920
  1473.8 21.1 %collective-permute-start.53 = (f32[8,3072]{1,0:T(8,128)}, f32[8,3072]{1,0:T(8,128)S(1)}, u32[]{:S(2)}, u32[]{:S(2)}) collective-permute-start(f32[8,3072]{1,0:T(8,128)} %get-tuple-element.537), channel_id=1, source_target_pairs={{0,22},{1,23},{2,24},{3,25},{4,26},{5,27},{6,28},{7,29},{8,30},{9,... | collective-permute-start | bytes 294920
  1475.1 21.7 %collective-permute-start.52 = (f32[8,3072]{1,0:T(8,128)}, f32[8,3072]{1,0:T(8,128)}, u32[]{:S(2)}, u32[]{:S(2)}) collective-permute-start(f32[8,3072]{1,0:T(8,128)} %get-tuple-element.537), channel_id=1, source_target_pairs={{0,21},{1,22},{2,23},{3,24},{4,25},{5,26},{6,27},{7,28},{8,29},{9,... | collective-permute-start | bytes 294920
  1487.2 87.3 %collective-permute-start.51 = (f32[8,3072]{1,0:T(8,128)S(1)}, f32[8,3072]{1,0:T(8,128)}, u32[]{:S(2)}, u32[]{:S(2)}) collective-permute-start(f32[8,3072]{1,0:T(8,128)S(1)} %copy-done.71), channel_id=1, source_target_pairs={{0,20},{1,21},{2,22},{3,23},{4,24},{5,25},{6,26},{7,27},{8,28},{9,... | collective-permute-start | bytes 294920
  1489.3 89.8 %collective-permute-start.50 = (f32[8,3072]{1,0:T(8,128)S(1)}, f32[8,3072]{1,0:T(8,128)}, u32[]{:S(2)}, u32[]{:S(2)}) collective-permute-start(f32[8,3072]{1,0:T(8,128)S(1)} %copy-done.71), channel_id=1, source_target_pairs={{0,19},{1,20},{2,21},{3,22},{4,23},{5,24},{6,25},{7,26},{8,27},{9,... | collective-permute-start | bytes 294920
  1493.0 88.4 %collective-permute-start.49 = (f32[8,3072]{1,0:T(8,128)S(1)}, f32[8,3072]{1,0:T(8,128)}, u32[]{:S(2)}, u32[]{:S(2)}) collective-permute-start(f32[8,3072]{1,0:T(8,128)S(1)} %copy-done.71), channel_id=1, source_target_pairs={{0,18},{1,19},{2,20},{3,21},{4,22},{5,23},{6,24},{7,25},{8,26},{9,... | collective-permute-start | bytes 294920
  1494.9 89.3 %collective-permute-start.48 = (f32[8,3072]{1,0:T(8,128)S(1)}, f32[8,3072]{1,0:T(8,128)}, u32[]{:S(2)}, u32[]{:S(2)}) collective-permute-start(f32[8,3072]{1,0:T(8,128)S(1)} %copy-done.71), channel_id=1, source_target_pairs={{0,17},{1,18},{2,19},{3,20},{4,21},{5,22},{6,23},{7,24},{8,25},{9,... | collective-permute-start | bytes 294920
  1496.8 89.8 %collective-permute-start.47 = (f32[8,3072]{1,0:T(8,128)S(1)}, f32[8,3072]{1,0:T(8,128)}, u32[]{:S(2)}, u32[]{:S(2)}) collective-permute-start(f32[8,3072]{1,0:T(8,128)S(1)} %copy-done.71), channel_id=1, source_target_pairs={{0,16},{1,17},{2,18},{3,19},{4,20},{5,21},{6,22},{7,23},{8,24},{9,... | collective-permute-start | bytes 294920
  1574.6 63.3 %collective-permute-start.46 = (f32[8,3072]{1,0:T(8,128)S(1)}, f32[8,3072]{1,0:T(8,128)S(1)}, u32[]{:S(2)}, u32[]{:S(2)}) collective-permute-start(f32[8,3072]{1,0:T(8,128)S(1)} %copy-done.71), channel_id=1, source_target_pairs={{0,15},{1,16},{2,17},{3,18},{4,19},{5,20},{6,21},{7,22},{8,23},{9,... | collective-permute-start | bytes 294920
  1579.1 62.5 %collective-permute-start.45 = (f32[8,3072]{1,0:T(8,128)S(1)}, f32[8,3072]{1,0:T(8,128)S(1)}, u32[]{:S(2)}, u32[]{:S(2)}) collective-permute-start(f32[8,3072]{1,0:T(8,128)S(1)} %copy-done.71), channel_id=1, source_target_pairs={{0,14},{1,15},{2,16},{3,17},{4,18},{5,19},{6,20},{7,21},{8,22},{9,... | collective-permute-start | bytes 294920
  1581.4 62.9 %collective-permute-start.44 = (f32[8,3072]{1,0:T(8,128)S(1)}, f32[8,3072]{1,0:T(8,128)S(1)}, u32[]{:S(2)}, u32[]{:S(2)}) collective-permute-start(f32[8,3072]{1,0:T(8,128)S(1)} %copy-done.71), channel_id=1, source_target_pairs={{0,13},{1,14},{2,15},{3,16},{4,17},{5,18},{6,19},{7,20},{8,21},{9,... | collective-permute-start | bytes 294920
  1584.2 63.9 %collective-permute-start.43 = (f32[8,3072]{1,0:T(8,128)S(1)}, f32[8,3072]{1,0:T(8,128)S(1)}, u32[]{:S(2)}, u32[]{:S(2)}) collective-permute-start(f32[8,3072]{1,0:T(8,128)S(1)} %copy-done.71), channel_id=1, source_target_pairs={{0,12},{1,13},{2,14},{3,15},{4,16},{5,17},{6,18},{7,19},{8,20},{9,... | collective-permute-start | bytes 294920
  1586.6 67.0 %collective-permute-start.42 = (f32[8,3072]{1,0:T(8,128)S(1)}, f32[8,3072]{1,0:T(8,128)S(1)}, u32[]{:S(2)}, u32[]{:S(2)}) collective-permute-start(f32[8,3072]{1,0:T(8,128)S(1)} %copy-done.71), channel_id=1, source_target_pairs={{0,11},{1,12},{2,13},{3,14},{4,15},{5,16},{6,17},{7,18},{8,19},{9,... | collective-permute-start | bytes 294920
  1637.8 20.0 %collective-permute-start.41 = (f32[8,3072]{1,0:T(8,128)S(1)}, f32[8,3072]{1,0:T(8,128)S(1)}, u32[]{:S(2)}, u32[]{:S(2)}) collective-permute-start(f32[8,3072]{1,0:T(8,128)S(1)} %copy-done.71), channel_id=1, source_target_pairs={{0,10},{1,11},{2,12},{3,13},{4,14},{5,15},{6,16},{7,17},{8,18},{9,... | collective-permute-start | bytes 294920
  1641.6 18.0 %collective-permute-start.40 = (f32[8,3072]{1,0:T(8,128)S(1)}, f32[8,3072]{1,0:T(8,128)S(1)}, u32[]{:S(2)}, u32[]{:S(2)}) collective-permute-start(f32[8,3072]{1,0:T(8,128)S(1)} %copy-done.71), channel_id=1, source_target_pairs={{0,9},{1,10},{2,11},{3,12},{4,13},{5,14},{6,15},{7,16},{8,17},{9,1... | collective-permute-start | bytes 294920
  1644.3 18.6 %collective-permute-start.39 = (f32[8,3072]{1,0:T(8,128)S(1)}, f32[8,3072]{1,0:T(8,128)S(1)}, u32[]{:S(2)}, u32[]{:S(2)}) collective-permute-start(f32[8,3072]{1,0:T(8,128)S(1)} %copy-done.71), channel_id=1, source_target_pairs={{0,8},{1,9},{2,10},{3,11},{4,12},{5,13},{6,14},{7,15},{8,16},{9,17... | collective-permute-start | bytes 294920
  1648.1 20.7 %collective-permute-start.38 = (f32[8,3072]{1,0:T(8,128)S(1)}, f32[8,3072]{1,0:T(8,128)S(1)}, u32[]{:S(2)}, u32[]{:S(2)}) collective-permute-start(f32[8,3072]{1,0:T(8,128)S(1)} %copy-done.71), channel_id=1, source_target_pairs={{0,7},{1,8},{2,9},{3,10},{4,11},{5,12},{6,13},{7,14},{8,15},{9,16}... | collective-permute-start | bytes 294920
  1653.5 18.5 %collective-permute-start.37 = (f32[8,3072]{1,0:T(8,128)S(1)}, f32[8,3072]{1,0:T(8,128)S(1)}, u32[]{:S(2)}, u32[]{:S(2)}) collective-permute-start(f32[8,3072]{1,0:T(8,128)S(1)} %copy-done.71), channel_id=1, source_target_pairs={{0,6},{1,7},{2,8},{3,9},{4,10},{5,11},{6,12},{7,13},{8,14},{9,15},... | collective-permute-start | bytes 294920
  1657.8 17.1 collective-permute-start.36
  1659.6 15.3 collective-permute-start.35
  (256 other events, 13264.4 us)
Sparse Core Ops, SparseCore 0:
  10.8 66.7 all-gather.28
  80.4 64.4 all-gather.26
  148.0 65.6 all-gather.30
  216.4 64.6 all-gather.22
  283.7 61.7 all-gather.32
  347.5 75.1 all-gather.24
  598.5 26.1 reduce-scatter.13
  627.2 30.2 reduce-scatter.11
  744.1 170.0 all-reduce.37
  920.3 224.3 reduce-scatter.15
  1149.2 136.7 reduce-scatter.17
where the time goes:
time: 1760 us; the launch traced here: 1740 us
  blocking collectives  769 us (44%)
  starting transfers between devices  276 us (16%)
  local copies, waits for them, and re-layouts  222 us (13%)
  waiting for transfers between devices  187 us (11%)
  matrix products  163 us (9%)
  other arithmetic  102 us (6%)
  between operations  23.6 us (1%)
    unnamed x4, blocking collectives  624 us
    unnamed x97, starting transfers between devices  254 us
    unnamed x479, local copies, waits for them, and re-layouts  165 us
    psum x1, blocking collectives, body(): loss = lax.psum(jnp.sum(jnp.stack(loss_terms)), ('dp', 'fs'))  64.6 us
    dot_general x14, matrix products, matmul_tn(): lax.dot_general(left, right, (((0,), (0,)), ((), ())), preferred_element_...  54.9 us
    all_gather x1, waiting for transfers between devices, fetch_layer(): lax.all_gather(w_shrink, ('dp', 'fs'), axis=0, tiled=True)  53.8 us
    all_gather x6, blocking collectives, merged(): everything = jax.tree.map(lambda part: lax.all_gather(part, axis), array)  52.8 us
    dot_general x12, matrix products, matmul_nt(): lax.dot_general(left, right, (((1,), (1,)), ((), ())), preferred_element_...  46.2 us
  transfers between devices with their start and end apart: 111, of which 10 were waited for; matrix products, arithmetic and copies ran while one was open for 42% of the time, Pallas kernels for 0%

commit v1 on v0

v1 whole, which is shorter than its diff:
```python
import functools

import jax
import jax.numpy as jnp
from jax import lax
from jax.experimental import pallas as pl
from jax.experimental.pallas import tpu as pltpu
from jax.sharding import Mesh
from jax.sharding import PartitionSpec as P

HEAD_DIM = 64
EPS = 1e-05
HALF_ROOT = 0.7071067811865476
NORMAL_PEAK = 0.3989422804014327
MASKED = -1e30

BF = jnp.bfloat16
F32 = jnp.float32
NY, NC, NZ, NX = 4, 2, 4, 4
SIZES = {"y": NY, "c": NC, "z": NZ, "x": NX}
EVERY = ("y", "c", "z", "x")


def fetch(array, axis, k):
    n = SIZES[axis]
    return lax.ppermute(array, axis, [((i + k) % n, i) for i in range(n)])


def give(array, axis, k):
    n = SIZES[axis]
    return lax.ppermute(array, axis, [(i, (i + k) % n) for i in range(n)])


def yz_pairs(a, b):
    return [
        (((y + a) % NY) * NZ + (z + b) % NZ, y * NZ + z) for y in range(NY) for z in range(NZ)
    ]


def fetch_yz(array, a, b):
    if a == 0 and b == 0:
        return array
    return lax.ppermute(array, ("y", "z"), yz_pairs(a, b))


def give_yz(array, a, b):
    if a == 0 and b == 0:
        return array
    return lax.ppermute(array, ("y", "z"), [(j, i) for i, j in yz_pairs(a, b)])


def in_order(pieces, index):
    n = len(pieces)
    twice = jnp.stack(pieces + pieces)
    return lax.dynamic_slice_in_dim(twice, (n - index) % n, n, 0)


def place_kernel(route, coords, *refs):
    first, second = route
    own, other, out, sems = refs[0:4], refs[4:8], refs[8], refs[9]
    at = {"y": coords[0], "c": coords[1], "z": coords[2]}
    copies = []
    for kb in range(4):
        for ka in range(4):
            place = {
                first: lax.rem(at[first] + ka, 4),
                second: lax.rem(at[second] + kb, 4),
            }
            for kc, source in enumerate((own, other)):
                core = lax.rem(at["c"] + kc, 2)
                copy = pltpu.make_async_copy(
                    source[kb].at[ka],
                    out.at[place["y"], core, place["z"]],
                    sems.at[kc, kb, ka],
                )
                copy.start()
                copies.append(copy)
    for copy in copies:
        copy.wait()


def place(own, other, route, coords):
    _, rows, width = own[0].shape
    anywhere = pl.BlockSpec(memory_space=pl.ANY)
    return pl.pallas_call(
        functools.partial(place_kernel, route),
        out_shape=jax.ShapeDtypeStruct((NY, NC, NZ, rows, width), own[0].dtype),
        in_specs=[pl.BlockSpec(memory_space=pltpu.SMEM)] + [anywhere] * 8,
        out_specs=anywhere,
        scratch_shapes=[pltpu.SemaphoreType.DMA((2, 4, 4))],
        cost_estimate=pl.CostEstimate(
            flops=0, bytes_accessed=2 * 32 * rows * width * 2, transcendentals=0
        ),
    )(coords, *own, *other)


def gather_pieces(block, route):
    first, second = route
    plane = jnp.stack([block] + [fetch(block, first, k) for k in (1, 2, 3)])
    own = [plane] + [fetch(plane, second, k) for k in (1, 2, 3)]
    other = [fetch(piece, "c", 1) for piece in own]
    return own, other


def gather_weight(shard, route, coords):
    pieces = [shard] + [fetch(shard, "x", k) for k in (1, 2, 3)]
    block = in_order(pieces, lax.axis_index("x")).reshape(NX * shard.shape[0], shard.shape[1])
    own, other = gather_pieces(block, route)
    return place(own, other, route, coords).reshape(-1, shard.shape[1])


def total(parts):
    out = parts[0].astype(F32)
    for part in parts[1:]:
        out = out + part.astype(F32)
    return out


def scatter_sum(grad, route):
    n = grad.shape[1]
    rows = grad.shape[0] // 128
    at = {axis: lax.axis_index(axis) for axis in EVERY}
    grad = grad.astype(BF).reshape(NY, NC, NZ, NX * rows, n)
    away = lax.dynamic_index_in_dim(grad, 1 - at["c"], 1, False)
    here = lax.dynamic_index_in_dim(grad, at["c"], 1, False)
    got = give(away, "c", 1)
    for axis in route:
        dim = 0 if (axis == "y" or here.ndim == 3) else 1

        def cut(k):
            index = (at[axis] + k) % 4
            mine = lax.dynamic_index_in_dim(here, index, dim, False)
            if got is None:
                return mine
            theirs = lax.dynamic_index_in_dim(got, index, dim, False)
            return (mine.astype(F32) + theirs.astype(F32)).astype(BF)

        parts = [cut(0)] + [give(cut(k), axis, k) for k in (1, 2, 3)]
        here, got = total(parts).astype(BF), None
    here = here.reshape(NX, rows, n)
    parts = [lax.dynamic_index_in_dim(here, at["x"], 0, False)]
    for k in (1, 2, 3):
        parts.append(
            give(lax.dynamic_index_in_dim(here, (at["x"] + k) % NX, 0, False), "x", k)
        )
    return total(parts)


def sum_everywhere(value):
    for axis in EVERY:
        n = SIZES[axis]
        pieces = [value] + [fetch(value, axis, k) for k in range(1, n)]
        value = jnp.sum(in_order(pieces, lax.axis_index(axis)), axis=0)
    return value


def gelu_value(values):
    return 0.5 * values * (1.0 + lax.erf(values * HALF_ROOT))


def gelu_slope(values):
    return 0.5 * (1.0 + lax.erf(values * HALF_ROOT)) + values * NORMAL_PEAK * jnp.exp(
        -0.5 * values * values
    )


def layer_norm(values, gain, shift):
    center = values - jnp.mean(values, axis=-1, keepdims=True)
    inverse = lax.rsqrt(jnp.mean(center * center, axis=-1, keepdims=True) + EPS)
    normed = center * inverse
    return (normed * gain + shift, normed, inverse)


def norm_back(grad, normed, inverse, gain):
    scaled = grad * gain
    inner = (
        scaled
        - jnp.mean(scaled, axis=-1, keepdims=True)
        - normed * jnp.mean(scaled * normed, axis=-1, keepdims=True)
    )
    return inner * inverse


def column_sum(values):
    return jnp.sum(values, axis=0, dtype=F32)


def matmul(left, right):
    return jnp.dot(left, right, preferred_element_type=F32)


def matmul_tn(left, right):
    return lax.dot_general(left, right, (((0,), (0,)), ((), ())), preferred_element_type=F32)


def matmul_nt(left, right):
    return lax.dot_general(left, right, (((1,), (1,)), ((), ())), preferred_element_type=F32)


def body(
    hidden_in,
    out_grad,
    segments,
    mask_pos,
    mask_labels,
    loss_scale,
    w_qkv,
    b_query,
    b_value,
    w_attn,
    b_attn,
    attn_gain,
    attn_shift,
    w_expand,
    b_expand,
    w_shrink,
    b_shrink,
    ffn_gain,
    ffn_shift,
    w_dense,
    b_dense,
    dense_gain,
    dense_shift,
    w_vocab,
    b_vocab,
):
    micro, block, width = hidden_in.shape
    tokens = micro * block
    heads = width // HEAD_DIM
    factor = HEAD_DIM ** (-0.5)
    at = {axis: lax.axis_index(axis) for axis in EVERY}
    coords = jnp.stack([at["y"], at["c"], at["z"]]).astype(jnp.int32)

    vectors = (
        b_query,
        b_value,
        b_attn,
        attn_gain,
        attn_shift,
        b_shrink,
        ffn_gain,
        ffn_shift,
        b_dense,
        dense_gain,
        dense_shift,
    )
    small = jnp.concatenate(
        [jnp.stack(vectors, axis=1), b_expand.reshape(w_qkv.shape[0], -1)], axis=1
    )
    small = jnp.pad(small, ((0, 0), (0, 128 - small.shape[1])))
    qkv_all = gather_weight(jnp.concatenate([w_qkv, small], axis=1), ("y", "z"), coords)
    attn_full = gather_weight(w_attn, ("z", "y"), coords)
    expand_full = gather_weight(w_expand, ("z", "y"), coords)
    shrink_full = gather_weight(w_shrink, ("y", "z"), coords)
    dense_full = gather_weight(w_dense, ("z", "y"), coords)
    qkv_full = qkv_all[:, : 3 * width]
    rows_of = qkv_all[:, 3 * width :].T.astype(F32)
    (
        b_query,
        b_value,
        b_attn,
        attn_gain,
        attn_shift,
        b_shrink,
        ffn_gain,
        ffn_shift,
        b_dense,
        dense_gain,
        dense_shift,
    ) = (rows_of[i] for i in range(len(vectors)))
    b_expand = qkv_all[:, 3 * width + 11 : 3 * width + 15].astype(F32).reshape(-1)

    own_w = w_vocab.T
    piece_w = [own_w] + [fetch(own_w, "x", k) for k in (1, 2, 3)]
    piece_b = [b_vocab] + [fetch(b_vocab, "x", k) for k in (1, 2, 3)]
    half_w = jnp.stack(piece_w)
    half_b = jnp.stack(piece_b)
    per = own_w.shape[0]
    vocab_w = jnp.concatenate([half_w, fetch(half_w, "c", 1)]).reshape(-1, width)
    vocab_b = jnp.concatenate([half_b, fetch(half_b, "c", 1)]).reshape(-1).astype(F32)
    start = jnp.stack(
        [
            (((at["y"] * NC + (at["c"] + kc) % NC) * NZ + at["z"]) * NX + (at["x"] + kx) % NX)
            * per
            for kc in range(NC)
            for kx in range(NX)
        ]
    )
    column = (start[:, None] + jnp.arange(per, dtype=jnp.int32)[None, :]).reshape(-1)

    flat_labels = mask_labels.reshape(micro, -1)
    counts = jnp.sum((flat_labels >= 0).astype(F32), axis=1)
    norms = 1.0 / (counts * micro)
    slots = mask_labels.shape[-1]
    peers = NZ * NX
    grid = mask_labels.reshape(micro, NY, NC, peers, NZ, NX, slots)
    grid = lax.dynamic_index_in_dim(grid, at["c"], 2, False)
    grid = lax.dynamic_index_in_dim(grid, at["x"], 4, False)
    grid = grid.transpose(1, 3, 0, 2, 4).reshape(NY, NZ, -1)
    grid = jnp.concatenate([grid, grid], axis=0)
    grid = lax.dynamic_slice_in_dim(grid, at["y"], NY, 0)
    grid = jnp.concatenate([grid, grid], axis=1)
    grid = lax.dynamic_slice_in_dim(grid, at["z"], NZ, 1)
    labels = grid.reshape(-1)
    rows = micro * peers * slots
    row_norm = jnp.broadcast_to(norms[None, :, None], (NY * NZ, micro, peers * slots)).reshape(-1)
    live = (labels >= 0).astype(F32)
    row_weight = live * row_norm
    positions = mask_pos.reshape(micro, -1)
    shifted = jnp.where(
        positions >= 0, positions + block * jnp.arange(micro, dtype=jnp.int32)[:, None], -1
    ).reshape(-1)
    select = (shifted[:, None] == jnp.arange(tokens, dtype=jnp.int32)[None, :]).astype(BF)

    x = hidden_in.reshape(tokens, width)
    united = matmul(x, qkv_full)

    def split(values):
        return values.astype(BF).reshape(micro, block, heads, HEAD_DIM)

    query = split(united[:, :width] + b_query)
    keys = split(united[:, width : 2 * width])
    values = split(united[:, 2 * width :] + b_value)
    allowed = (segments[:, :, None] == segments[:, None, :])[:, None]
    raw = jnp.einsum("mqhd,mkhd->mhqk", query, keys, preferred_element_type=F32)
    scores = jnp.where(allowed, raw * factor, MASKED)
    expo = jnp.exp(scores - jnp.max(scores, axis=-1, keepdims=True))
    probs = expo / jnp.sum(expo, axis=-1, keepdims=True)
    weights = probs.astype(BF)
    attended = (
        jnp.einsum("mhqk,mkhd->mqhd", weights, values, preferred_element_type=F32)
        .reshape(tokens, width)
        .astype(BF)
    )
    branch = matmul(attended, attn_full) + b_attn
    first, normed1, inverse1 = layer_norm(x.astype(F32) + branch, attn_gain, attn_shift)
    first_low = first.astype(BF)
    pre = matmul(first_low, expand_full) + b_expand
    act = gelu_value(pre).astype(BF)
    second = first + matmul(act, shrink_full) + b_shrink
    settled, normed2, inverse2 = layer_norm(second, ffn_gain, ffn_shift)
    settled_low = settled.astype(BF)

    picked = matmul(select, settled_low).astype(BF)
    dense_pre = matmul(picked, dense_full) + b_dense
    head_val, normed3, inverse3 = layer_norm(gelu_value(dense_pre), dense_gain, dense_shift)
    head_out = head_val.astype(BF)
    spread = jnp.concatenate([fetch_yz(head_out, a, b) for a in range(NY) for b in range(NZ)])
    logits = matmul_nt(spread, vocab_w) + vocab_b
    hit = labels[:, None] == column[None, :]
    top = jnp.max(logits, axis=1)
    expl = jnp.exp(logits - top[:, None])
    part_sum = jnp.sum(expl, axis=1)
    label_logit = jnp.sum(jnp.where(hit, logits, 0.0), axis=1)
    stats = jnp.stack([top, part_sum, label_logit])
    seen = [stats]
    for a in range(NY):
        for b in range(NZ):
            if (a, b) != (0, 0):
                there = fetch_yz(stats, a, b).reshape(3, NY, NZ, rows)
                there = jnp.roll(there, (a, b), axis=(1, 2))
                seen.append(there.reshape(3, -1))
    top_all = functools.reduce(jnp.maximum, [s[0] for s in seen])
    sum_all = sum(s[1] * jnp.exp(s[0] - top_all) for s in seen)
    label_all = sum(s[2] for s in seen)
    log_sum = top_all + jnp.log(sum_all)
    scale = loss_scale * row_weight
    dlogits = (
        (scale * jnp.exp(top - log_sum))[:, None] * expl
        - jnp.where(hit, scale[:, None], 0.0)
    ).astype(BF)
    part = matmul(dlogits, vocab_w).astype(BF).reshape(NY, NZ, rows, width)
    row_grad = total(
        [give_yz(part[a, b], a, b) for a in range(NY) for b in range(NZ)]
    )
    loss_own = jnp.sum((row_weight * (log_sum - label_all))[:rows])
    loss = sum_everywhere(jnp.broadcast_to(loss_own, (8, 128)))[0, 0]
    grad_w = matmul_tn(dlogits, spread).astype(BF).reshape(NC, NX, per, width)
    grad_b = column_sum(dlogits).reshape(NC, NX, per)
    grad_w = (grad_w[0].astype(F32) + give(grad_w[1], "c", 1).astype(F32)).astype(BF)
    grad_b = grad_b[0] + give(grad_b[1], "c", 1)
    g_vocab = total([grad_w[0]] + [give(grad_w[k], "x", k) for k in (1, 2, 3)]).T
    g_vocab_bias = total([grad_b[0]] + [give(grad_b[k], "x", k) for k in (1, 2, 3)])

    g_dense_gain = column_sum(row_grad * normed3)
    g_dense_shift = column_sum(row_grad)
    ddense = (norm_back(row_grad, normed3, inverse3, dense_gain) * gelu_slope(dense_pre)).astype(BF)
    g_dense = scatter_sum(matmul_tn(picked, ddense), ("z", "y"))
    g_dense_bias = column_sum(ddense)
    drows = matmul_nt(ddense, dense_full).astype(BF)

    dout = out_grad.reshape(tokens, width).astype(F32) + matmul_tn(select, drows)
    g_ffn_gain = column_sum(dout * normed2)
    g_ffn_shift = column_sum(dout)
    dsecond = norm_back(dout, normed2, inverse2, ffn_gain)
    dffn = dsecond.astype(BF)
    g_shrink = scatter_sum(matmul_tn(act, dffn), ("y", "z"))
    g_shrink_bias = column_sum(dffn)
    dpre = (matmul_nt(dffn, shrink_full) * gelu_slope(pre)).astype(BF)
    g_expand = scatter_sum(matmul_tn(first_low, dpre), ("z", "y"))
    g_expand_bias = column_sum(dpre)
    dfirst = dsecond + matmul_nt(dpre, expand_full)
    g_attn_gain = column_sum(dfirst * normed1)
    g_attn_shift = column_sum(dfirst)
    dresidual = norm_back(dfirst, normed1, inverse1, attn_gain)
    dbranch = dresidual.astype(BF)
    g_attn = scatter_sum(matmul_tn(attended, dbranch), ("z", "y"))
    g_attn_bias = column_sum(dbranch)
    dattended = matmul_nt(dbranch, attn_full).astype(BF).reshape(micro, block, heads, HEAD_DIM)
    dprobs = jnp.einsum("mqhd,mkhd->mhqk", dattended, values, preferred_element_type=F32)
    inner = jnp.sum(probs * dprobs, axis=-1, keepdims=True)
    dscores = (probs * (dprobs - inner)).astype(BF)

    def merge(array):
        return array.astype(BF).reshape(tokens, width)

    dquery = merge(
        jnp.einsum("mhqk,mkhd->mqhd", dscores, keys, preferred_element_type=F32) * factor
    )
    dkeys = merge(
        jnp.einsum("mhqk,mqhd->mkhd", dscores, query, preferred_element_type=F32) * factor
    )
    dvalues = merge(
        jnp.einsum("mhqk,mqhd->mkhd", weights, dattended, preferred_element_type=F32)
    )
    dfused = jnp.concatenate([dquery, dkeys, dvalues], axis=1)
    g_qkv = scatter_sum(matmul_tn(x, dfused), ("y", "z"))
    g_query = column_sum(dquery)
    g_value = column_sum(dvalues)
    dinput = dresidual + matmul_nt(dfused, qkv_full)

    sums = jnp.stack(
        [
            g_query,
            g_value,
            g_attn_bias,
            g_attn_gain,
            g_attn_shift,
            g_shrink_bias,
            g_ffn_gain,
            g_ffn_shift,
            g_dense_bias,
            g_dense_gain,
            g_dense_shift,
        ],
        axis=1,
    )
    sums = jnp.concatenate([sums, g_expand_bias.reshape(width, -1)], axis=1)
    sums = jnp.pad(sums, ((0, 0), (0, 128 - sums.shape[1])))
    sums = scatter_sum(sums, ("z", "y"))
    return (
        settled_low.reshape(hidden_in.shape),
        loss,
        dinput.reshape(hidden_in.shape),
        g_qkv,
        sums[:, 0],
        sums[:, 1],
        g_attn,
        sums[:, 2],
        sums[:, 3],
        sums[:, 4],
        g_expand,
        sums[:, 11:15].reshape(-1),
        g_shrink,
        sums[:, 5],
        sums[:, 6],
        sums[:, 7],
        g_dense,
        sums[:, 8],
        sums[:, 9],
        sums[:, 10],
        g_vocab,
        g_vocab_bias,
    )


def solution(mesh):
    split = Mesh(mesh.devices.reshape(NY, NC, NZ, NX), EVERY)
    whole, one = P(), P(EVERY)
    tokens3 = P(None, EVERY, None)
    matrix = P(EVERY, None)
    in_specs = (
        tokens3,
        tokens3,
        P(None, EVERY),
        P(None, EVERY, None, None),
        whole,
        whole,
        matrix,
        one,
        one,
        matrix,
        one,
        one,
        one,
        matrix,
        one,
        matrix,
        one,
        one,
        one,
        matrix,
        one,
        one,
        one,
        P(None, EVERY),
        one,
    )
    out_specs = (
        tokens3,
        whole,
        tokens3,
        matrix,
        one,
        one,
        matrix,
        one,
        one,
        one,
        matrix,
        one,
        matrix,
        one,
        one,
        one,
        matrix,
        one,
        one,
        one,
        P(None, EVERY),
        one,
    )
    return jax.shard_map(body, mesh=split, in_specs=in_specs, out_specs=out_specs, check_vma=False)
```

time: 1760 us -> 1310 us (0.74)
  blocking collectives: 769 us -> 0 us
  Pallas kernels: 0 us -> 481 us
  matrix products: 163 us -> 91 us
  starting transfers between devices: 276 us -> 253 us
  between operations: 23.6 us -> 4.22 us
  local copies, waits for them, and re-layouts: 222 us -> 203 us
  other arithmetic: 102 us -> 83.9 us
    unnamed x4 -> x0, blocking collectives: 624 us -> none
    pallas_call x0 -> x5, Pallas kernels: none -> 481 us  [place(): pl.pallas_call(functools.partial(place_kernel, route), out_shape=jax.Shap...]
    unnamed x97 -> x0, starting transfers between devices: 254 us -> none
    ppermute x0 -> x196, starting transfers between devices: none -> 253 us  [the longest x83 96.8 us: fetch(): return lax.ppermute(array, axis, [((i + k) % n, i) for i in range(n)])]
    ppermute x0 -> x196, waiting for transfers between devices: none -> 175 us  [the longest x83 80.8 us: fetch(): return lax.ppermute(array, axis, [((i + k) % n, i) for i in range(n)])]
    unnamed x479 -> x310, local copies, waits for them, and re-layouts: 165 us -> 28.2 us
    all_gather x6 -> x0, waiting for transfers between devices: 127 us -> none  [the longest x1 53.8 us: fetch_layer(): lax.all_gather(w_shrink, ('dp', 'fs'), axis=0, tiled=True)]
    all_gather x8 -> x0, blocking collectives: 80.9 us -> none  [the longest x6 52.8 us: merged(): everything = jax.tree.map(lambda part: lax.all_gather(part, axis), array)]
  transfers between devices with their start and end apart: 111 -> 196, of which waited for: 10 -> 61; matrix products, arithmetic and copies ran while one was open for 42% -> 18% of each run, Pallas kernels for 0% -> 37%
where the time goes in v1:
time: 1310 us; the launch traced here: 1290 us
  Pallas kernels  481 us (37%)
  starting transfers between devices  253 us (19%)
  local copies, waits for them, and re-layouts  203 us (15%)
  waiting for transfers between devices  175 us (13%)
  matrix products  91 us (7%)
  other arithmetic  83.9 us (6%)
    pallas_call x5, Pallas kernels, place(): pl.pallas_call(functools.partial(place_kernel, route), out_shape=jax.Shap...  481 us
    ppermute x83, starting transfers between devices, fetch(): return lax.ppermute(array, axis, [((i + k) % n, i) for i in range(n)])  96.8 us
    ppermute x83, waiting for transfers between devices, fetch(): return lax.ppermute(array, axis, [((i + k) % n, i) for i in range(n)])  80.8 us
    ppermute x68, waiting for transfers between devices, give(): return lax.ppermute(array, axis, [(i, (i + k) % n) for i in range(n)])  79.2 us
    ppermute x68, starting transfers between devices, give(): return lax.ppermute(array, axis, [(i, (i + k) % n) for i in range(n)])  71.7 us
    ppermute x30, starting transfers between devices, fetch_yz(): return lax.ppermute(array, ('y', 'z'), yz_pairs(a, b))  58.6 us
    dot_general x7, matrix products, matmul(): return jnp.dot(left, right, preferred_element_type=F32)  29.1 us
    unnamed x310, local copies, waits for them, and re-layouts  28.2 us
  transfers between devices with their start and end apart: 196, of which 61 were waited for; matrix products, arithmetic and copies ran while one was open for 18% of the time, Pallas kernels for 37%

profile of v1, /device:TPU:0, one launch (start us, length us, event | category | flops | bytes accessed | tf_op | source)
XLA Modules:
  0.0 1290.5 jit_solution(3571364979907649977)
XLA Ops:
  10.7 2.9 collective-permute-start
  36.0 4.4 collective-permute-done.14
  40.4 4.9 collective-permute-done.15
  49.3 4.9 collective-permute-done.53
  54.3 5.0 collective-permute-done.54
  67.8 3.7 collective-permute-start.17
  79.0 3.0 collective-permute-start.4
  101.6 3.2 collective-permute-start.80
  114.5 5.0 collective-permute-start.81
  126.1 37.8 %shard_map.409 = bf16[4,2,4,24,768]{4,3,2,1,0:T(8,128)(2,1)} custom-call(s32[3]{0:T(128)} %pad_add_fusion.coords, bf16[4,24,768]{2,1,0:T(8,128)(2,1)} %copy-done.35, bf16[4,24,768]{2,1,0:T(8,128)(2,1)} %copy-done.48, bf16[4,24,768]{2,1,0:T(8,128)(2,1)} %copy-done.49, bf16[4,24,768]{2,1,0:T(8,128)(2,1)} %collective-permute-done.21.refs_3_, ...), custom_call_target="tpu_custom_call" | custom-call | bytes 2359296 | tf_op jit(solution)/shard_map/pallas_call | solution.py:85
  163.9 37.8 %shard_map.412 = bf16[4,2,4,24,768]{4,3,2,1,0:T(8,128)(2,1)} custom-call(s32[3]{0:T(128)} %pad_add_fusion.coords, bf16[4,24,768]{2,1,0:T(8,128)(2,1)} %copy-done.36, bf16[4,24,768]{2,1,0:T(8,128)(2,1)} %collective-permute-done.58.refs_1_, bf16[4,24,768]{2,1,0:T(8,128)(2,1)} %collective-permute-done.59.refs_2_, ...), custom_call_target="tpu_custom_call" | custom-call | bytes 2359296 | tf_op jit(solution)/shard_map/pallas_call | solution.py:85
  208.5 10.4 collective-permute-start.33
  220.1 3.5 collective-permute-start.45
  223.6 115.2 %shard_map.408 = bf16[4,2,4,24,2432]{4,3,2,1,0:T(8,128)(2,1)} custom-call(s32[3]{0:T(128)} %pad_add_fusion.coords, bf16[4,24,2432]{2,1,0:T(8,128)(2,1)} %copy-done.18, bf16[4,24,2432]{2,1,0:T(8,128)(2,1)} %collective-permute-done.6.refs_1_, bf16[4,24,2432]{2,1,0:T(8,128)(2,1)} %collective-permute-done.7.refs_2_, ...), custom_call_target="tpu_custom_call" | custom-call | bytes 7471104 | tf_op jit(solution)/shard_map/pallas_call | solution.py:85
  340.6 4.1 convolution_bitcast_fusion
  359.0 15.5 %collective-permute-done.46.refs_2_ = bf16[4,96,768]{2,1,0:T(8,128)(2,1)S(1)} collective-permute-done((bf16[4,96,768]{2,1,0:T(8,128)(2,1)}, bf16[4,96,768]{2,1,0:T(8,128)(2,1)S(1)}, u32[]{:S(2)}, u32[]{:S(2)}) %collective-permute-start.46) | collective-permute-done | bytes 589856 | tf_op jit(solution)/shard_map/ppermute | solution.py:26
  374.5 11.6 collective-permute-done.47.refs_3_
  388.9 145.0 %shard_map.410 = bf16[4,2,4,24,3072]{4,3,2,1,0:T(8,128)(2,1)} custom-call(s32[3]{0:T(128)} %pad_add_fusion.coords, bf16[4,24,3072]{2,1,0:T(8,128)(2,1)} %pad_maximum_fusion.1.refs_0_, bf16[4,24,3072]{2,1,0:T(8,128)(2,1)} %collective-permute-done.32.refs_1_, bf16[4,24,3072]{2,1,0:T(8,128)(2,1)} %collective-permute-done.33.refs_2_, ...), custom_call_target="tpu_custom_call" | custom-call | bytes 9437184 | tf_op jit(solution)/shard_map/pallas_call | solution.py:85
  534.0 8.1 multiply_convert_fusion.1
  542.1 145.0 %shard_map.411 = bf16[4,2,4,96,768]{4,3,2,1,0:T(8,128)(2,1)} custom-call(s32[3]{0:T(128)} %pad_add_fusion.coords, bf16[4,96,768]{2,1,0:T(8,128)(2,1)} %pad_maximum_fusion.2.refs_0_, bf16[4,96,768]{2,1,0:T(8,128)(2,1)} %collective-permute-done.45.refs_1_, bf16[4,96,768]{2,1,0:T(8,128)(2,1)} %copy-done.30, bf16[4,96,768]{2,1,0:T(8,128)(2,1)} %copy-done.31, ...), custom_call_target="tpu_custom_call" | custom-call | bytes 9437184 | tf_op jit(solution)/shard_map/pallas_call | solution.py:85
  687.2 6.5 fusion.223
  703.3 3.0 collective-permute-start.69
  711.4 4.2 collective-permute-start.73
  721.3 5.5 collective-permute-start.77
  730.3 5.9 collective-permute-done.78
  736.3 3.8 constant_dynamic-update-slice_fusion.56
  740.1 8.1 add_reduce_fusion
  748.2 4.5 fusion.4
  753.5 3.1 collective-permute-start.101
  778.7 4.1 collective-permute-start.95
  820.1 3.0 collective-permute-start.88
  921.5 3.2 collective-permute-start.103
  925.5 8.4 convert_reduce_fusion
  933.9 8.0 convolution_convert_fusion.4
  941.9 6.1 convolution_convert_fusion
  967.2 3.7 collective-permute-start.195
  979.3 3.3 collective-permute-start.107
  985.6 3.4 collective-permute-done.108
  989.8 4.3 collective-permute-done.109
  994.4 3.4 collective-permute-done.110
  998.3 4.6 collective-permute-done.111
  1003.4 4.3 collective-permute-done.112
  1023.8 3.2 collective-permute-start.115
  1038.2 4.1 multiply_reduce_fusion.1
  1045.7 8.8 fusion.226
  1054.5 3.6 multiply_reduce_fusion.2
  1063.6 4.5 multiply_reduce_fusion
  1068.1 4.3 multiply_convert_fusion
  1074.3 4.0 fusion.225
  1083.2 3.2 fusion.24
  1086.5 3.9 convolution_convert_fusion.3
  1091.8 4.9 convolution_convert_fusion.2
  1096.7 4.4 convolution_convert_fusion.1
  1114.8 3.3 copy_bitcast_fusion
  1130.3 3.2 dynamic-slice_bitcast_fusion
  1166.4 4.7 collective-permute-done.182
  1174.0 5.7 collective-permute-done.131
  1179.7 3.9 collective-permute-done.129
  1188.9 3.3 collective-permute-done.134
  1226.4 16.5 %collective-permute-done.161 = bf16[4,24,3072]{2,1,0:T(8,128)(2,1)S(1)} collective-permute-done((bf16[4,24,3072]{2,1,0:T(8,128)(2,1)S(1)}, bf16[4,24,3072]{2,1,0:T(8,128)(2,1)S(1)}, u32[]{:S(2)}, u32[]{:S(2)}) %collective-permute-start.161) | collective-permute-done | bytes 589856 | tf_op jit(solution)/shard_map/ppermute | solution.py:31
  1248.1 6.3 collective-permute-done.171
  1254.6 5.4 collective-permute-done.170
  1260.0 3.4 collective-permute-start.164
  1263.4 4.3 collective-permute-done.169
  (984 shorter events, 502.0 us)
Async XLA Ops:
  10.7 48.8 %collective-permute-start = (bf16[6,2432]{1,0:T(8,128)(2,1)S(1)}, bf16[6,2432]{1,0:T(8,128)(2,1)S(1)}, u32[]{:S(2)}, u32[]{:S(2)}) collective-permute-start(bf16[6,2432]{1,0:T(8,128)(2,1)S(1)} %fusion.122), channel_id=1, source_target_pairs={{1,0},{2,1},{3,2},{0,3},{5,4},{6,5},{7,6},{4,7},{9,8},{10,9},{11,1... | collective-permute-start | bytes 87560 | tf_op jit(solution)/shard_map/ppermute | solution.py:26
  13.6 47.5 %collective-permute-start.1 = (bf16[6,2432]{1,0:T(8,128)(2,1)S(1)}, bf16[6,2432]{1,0:T(8,128)(2,1)S(1)}, u32[]{:S(2)}, u32[]{:S(2)}) collective-permute-start(bf16[6,2432]{1,0:T(8,128)(2,1)S(1)} %fusion.122), channel_id=1, source_target_pairs={{2,0},{3,1},{0,2},{1,3},{6,4},{7,5},{4,6},{5,7},{10,8},{11,9},{8,1... | collective-permute-start | bytes 87560 | tf_op jit(solution)/shard_map/ppermute | solution.py:26
  17.3 14.1 %collective-permute-start.86 = (bf16[400]{0:T(512)(128)(2,1)}, bf16[400]{0:T(512)(128)(2,1)S(1)}, u32[]{:S(2)}, u32[]{:S(2)}) collective-permute-start(bf16[400]{0:T(512)(128)(2,1)} %param.49), channel_id=1, source_target_pairs={{3,0},{0,1},{1,2},{2,3},{7,4},{4,5},{5,6},{6,7},{11,8},{8,9},{9,10... | collective-permute-start | bytes 2408 | tf_op jit(solution)/shard_map/ppermute | solution.py:26
  28.1 34.8 %collective-permute-start.2 = (bf16[6,2432]{1,0:T(8,128)(2,1)S(1)}, bf16[6,2432]{1,0:T(8,128)(2,1)S(1)}, u32[]{:S(2)}, u32[]{:S(2)}) collective-permute-start(bf16[6,2432]{1,0:T(8,128)(2,1)S(1)} %fusion.122), channel_id=1, source_target_pairs={{3,0},{0,1},{1,2},{2,3},{7,4},{4,5},{5,6},{6,7},{11,8},{8,9},{9,10... | collective-permute-start | bytes 87560 | tf_op jit(solution)/shard_map/ppermute | solution.py:26
  28.6 36.9 %collective-permute-start.26 = (bf16[6,3072]{1,0:T(8,128)(2,1)S(1)}, bf16[6,3072]{1,0:T(8,128)(2,1)S(1)}, u32[]{:S(2)}, u32[]{:S(2)}) collective-permute-start(bf16[6,3072]{1,0:T(8,128)(2,1)S(1)} %copy-done.39), channel_id=1, source_target_pairs={{1,0},{2,1},{3,2},{0,3},{5,4},{6,5},{7,6},{4,7},{9,8},{10,9},{11,1... | collective-permute-start | bytes 110600 | tf_op jit(solution)/shard_map/ppermute | solution.py:26
  101.6 19.5 %collective-permute-start.80 = (bf16[400,768]{1,0:T(8,128)(2,1)S(1)}, bf16[400,768]{1,0:T(8,128)(2,1)S(1)}, u32[]{:S(2)}, u32[]{:S(2)}) collective-permute-start(bf16[400,768]{1,0:T(8,128)(2,1)S(1)} %bitcast.671), channel_id=1, source_target_pairs={{1,0},{2,1},{3,2},{0,3},{5,4},{6,5},{7,6},{4,7},{9,8},{10,9},{11,1... | collective-permute-start | bytes 1843208 | tf_op jit(solution)/shard_map/ppermute | solution.py:26
  114.5 90.8 %collective-permute-start.81 = (bf16[400,768]{1,0:T(8,128)(2,1)S(1)}, bf16[400,768]{1,0:T(8,128)(2,1)S(1)}, u32[]{:S(2)}, u32[]{:S(2)}) collective-permute-start(bf16[400,768]{1,0:T(8,128)(2,1)S(1)} %bitcast.672), channel_id=1, source_target_pairs={{2,0},{3,1},{0,2},{1,3},{6,4},{7,5},{4,6},{5,7},{10,8},{11,9},{8,1... | collective-permute-start | bytes 1843208 | tf_op jit(solution)/shard_map/ppermute | solution.py:26
  119.5 86.1 %collective-permute-start.82 = (bf16[400,768]{1,0:T(8,128)(2,1)S(1)}, bf16[400,768]{1,0:T(8,128)(2,1)S(1)}, u32[]{:S(2)}, u32[]{:S(2)}) collective-permute-start(bf16[400,768]{1,0:T(8,128)(2,1)S(1)} %bitcast.673), channel_id=1, source_target_pairs={{3,0},{0,1},{1,2},{2,3},{7,4},{4,5},{5,6},{6,7},{11,8},{8,9},{9,10... | collective-permute-start | bytes 1843208 | tf_op jit(solution)/shard_map/ppermute | solution.py:26
  119.6 83.1 %collective-permute-start.6 = (bf16[4,24,2432]{2,1,0:T(8,128)(2,1)S(1)}, bf16[4,24,2432]{2,1,0:T(8,128)(2,1)}, u32[]{:S(2)}, u32[]{:S(2)}) collective-permute-start(bf16[4,24,2432]{2,1,0:T(8,128)(2,1)S(1)} %pad_maximum_fusion.3.refs_0_), channel_id=1, source_target_pairs={{4,0},{8,4},{12,8},{0,12},{5,1},{9,5},{13,9},{1,13},{6,2},{10,6},{... | collective-permute-start | bytes 1400840 | tf_op jit(solution)/shard_map/ppermute | solution.py:26
  119.7 83.0 %collective-permute-start.7 = (bf16[4,24,2432]{2,1,0:T(8,128)(2,1)S(1)}, bf16[4,24,2432]{2,1,0:T(8,128)(2,1)}, u32[]{:S(2)}, u32[]{:S(2)}) collective-permute-start(bf16[4,24,2432]{2,1,0:T(8,128)(2,1)S(1)} %pad_maximum_fusion.3.refs_0_), channel_id=1, source_target_pairs={{8,0},{12,4},{0,8},{4,12},{9,1},{13,5},{1,9},{5,13},{10,2},{14,6},... | collective-permute-start | bytes 1400840 | tf_op jit(solution)/shard_map/ppermute | solution.py:26
  121.1 84.0 %collective-permute-start.8 = (bf16[4,24,2432]{2,1,0:T(8,128)(2,1)S(1)}, bf16[4,24,2432]{2,1,0:T(8,128)(2,1)}, u32[]{:S(2)}, u32[]{:S(2)}) collective-permute-start(bf16[4,24,2432]{2,1,0:T(8,128)(2,1)S(1)} %pad_maximum_fusion.3.refs_0_), channel_id=1, source_target_pairs={{12,0},{0,4},{4,8},{8,12},{13,1},{1,5},{5,9},{9,13},{14,2},{2,6},{... | collective-permute-start | bytes 1400840 | tf_op jit(solution)/shard_map/ppermute | solution.py:26
  202.7 153.8 %collective-permute-start.32 = (bf16[4,24,3072]{2,1,0:T(8,128)(2,1)}, bf16[4,24,3072]{2,1,0:T(8,128)(2,1)}, u32[]{:S(2)}, u32[]{:S(2)}) collective-permute-start(bf16[4,24,3072]{2,1,0:T(8,128)(2,1)} %pad_maximum_fusion.1.refs_0_), channel_id=1, source_target_pairs={{32,0},{64,32},{96,64},{0,96},{33,1},{65,33},{97,65},{1,97},{34,2}... | collective-permute-start | bytes 1769480 | tf_op jit(solution)/shard_map/ppermute | solution.py:26
  205.3 14.7 %collective-permute-start.11 = (bf16[4,24,2432]{2,1,0:T(8,128)(2,1)}, bf16[4,24,2432]{2,1,0:T(8,128)(2,1)}, u32[]{:S(2)}, u32[]{:S(2)}) collective-permute-start(bf16[4,24,2432]{2,1,0:T(8,128)(2,1)} %collective-permute-done.7.refs_2_), channel_id=1, source_target_pairs={{16,0},{0,16},{17,1},{1,17},{18,2},{2,18},{19,3},{3,19},{20,4},{4,... | collective-permute-start | bytes 1400840 | tf_op jit(solution)/shard_map/ppermute | solution.py:26
  205.7 14.4 %collective-permute-start.12 = (bf16[4,24,2432]{2,1,0:T(8,128)(2,1)}, bf16[4,24,2432]{2,1,0:T(8,128)(2,1)}, u32[]{:S(2)}, u32[]{:S(2)}) collective-permute-start(bf16[4,24,2432]{2,1,0:T(8,128)(2,1)} %collective-permute-done.8.refs_3_), channel_id=1, source_target_pairs={{16,0},{0,16},{17,1},{1,17},{18,2},{2,18},{19,3},{3,19},{20,4},{4,... | collective-permute-start | bytes 1400840 | tf_op jit(solution)/shard_map/ppermute | solution.py:26
  208.5 148.1 %collective-permute-start.33 = (bf16[4,24,3072]{2,1,0:T(8,128)(2,1)}, bf16[4,24,3072]{2,1,0:T(8,128)(2,1)}, u32[]{:S(2)}, u32[]{:S(2)}) collective-permute-start(bf16[4,24,3072]{2,1,0:T(8,128)(2,1)} %pad_maximum_fusion.1.refs_0_), channel_id=1, source_target_pairs={{64,0},{96,32},{0,64},{32,96},{65,1},{97,33},{1,65},{33,97},{66,2}... | collective-permute-start | bytes 1769480 | tf_op jit(solution)/shard_map/ppermute | solution.py:26
  219.0 138.5 %collective-permute-start.34 = (bf16[4,24,3072]{2,1,0:T(8,128)(2,1)}, bf16[4,24,3072]{2,1,0:T(8,128)(2,1)}, u32[]{:S(2)}, u32[]{:S(2)}) collective-permute-start(bf16[4,24,3072]{2,1,0:T(8,128)(2,1)} %pad_maximum_fusion.1.refs_0_), channel_id=1, source_target_pairs={{96,0},{0,32},{32,64},{64,96},{97,1},{1,33},{33,65},{65,97},{98,2}... | collective-permute-start | bytes 1769480 | tf_op jit(solution)/shard_map/ppermute | solution.py:26
  220.1 137.4 %collective-permute-start.35 = (bf16[4,24,3072]{2,1,0:T(8,128)(2,1)}, bf16[4,24,3072]{2,1,0:T(8,128)(2,1)}, u32[]{:S(2)}, u32[]{:S(2)}) collective-permute-start(bf16[4,24,3072]{2,1,0:T(8,128)(2,1)} %pad_maximum_fusion.1.refs_0_), channel_id=1, source_target_pairs={{16,0},{0,16},{17,1},{1,17},{18,2},{2,18},{19,3},{3,19},{20,4},{4,... | collective-permute-start | bytes 1769480 | tf_op jit(solution)/shard_map/ppermute | solution.py:26
  220.1 137.9 %collective-permute-start.45 = (bf16[4,96,768]{2,1,0:T(8,128)(2,1)}, bf16[4,96,768]{2,1,0:T(8,128)(2,1)}, u32[]{:S(2)}, u32[]{:S(2)}) collective-permute-start(bf16[4,96,768]{2,1,0:T(8,128)(2,1)} %pad_maximum_fusion.2.refs_0_), channel_id=1, source_target_pairs={{4,0},{8,4},{12,8},{0,12},{5,1},{9,5},{13,9},{1,13},{6,2},{10,6},{... | collective-permute-start | bytes 1769480 | tf_op jit(solution)/shard_map/ppermute | solution.py:26
  356.5 18.0 %collective-permute-start.46 = (bf16[4,96,768]{2,1,0:T(8,128)(2,1)}, bf16[4,96,768]{2,1,0:T(8,128)(2,1)S(1)}, u32[]{:S(2)}, u32[]{:S(2)}) collective-permute-start(bf16[4,96,768]{2,1,0:T(8,128)(2,1)} %pad_maximum_fusion.2.refs_0_), channel_id=1, source_target_pairs={{8,0},{12,4},{0,8},{4,12},{9,1},{13,5},{1,9},{5,13},{10,2},{14,6},... | collective-permute-start | bytes 1769480 | tf_op jit(solution)/shard_map/ppermute | solution.py:26
  356.6 29.6 %collective-permute-start.47 = (bf16[4,96,768]{2,1,0:T(8,128)(2,1)}, bf16[4,96,768]{2,1,0:T(8,128)(2,1)S(1)}, u32[]{:S(2)}, u32[]{:S(2)}) collective-permute-start(bf16[4,96,768]{2,1,0:T(8,128)(2,1)} %pad_maximum_fusion.2.refs_0_), channel_id=1, source_target_pairs={{12,0},{0,4},{4,8},{8,12},{13,1},{1,5},{5,9},{9,13},{14,2},{2,6},{... | collective-permute-start | bytes 1769480 | tf_op jit(solution)/shard_map/ppermute | solution.py:26
  357.5 28.7 %collective-permute-start.36 = (bf16[4,24,3072]{2,1,0:T(8,128)(2,1)}, bf16[4,24,3072]{2,1,0:T(8,128)(2,1)S(1)}, u32[]{:S(2)}, u32[]{:S(2)}) collective-permute-start(bf16[4,24,3072]{2,1,0:T(8,128)(2,1)} %collective-permute-done.32.refs_1_), channel_id=1, source_target_pairs={{16,0},{0,16},{17,1},{1,17},{18,2},{2,18},{19,3},{3,19},{20,4},{4,... | collective-permute-start | bytes 1769480 | tf_op jit(solution)/shard_map/ppermute | solution.py:26
  357.5 29.2 %collective-permute-start.37 = (bf16[4,24,3072]{2,1,0:T(8,128)(2,1)}, bf16[4,24,3072]{2,1,0:T(8,128)(2,1)S(1)}, u32[]{:S(2)}, u32[]{:S(2)}) collective-permute-start(bf16[4,24,3072]{2,1,0:T(8,128)(2,1)} %collective-permute-done.33.refs_2_), channel_id=1, source_target_pairs={{16,0},{0,16},{17,1},{1,17},{18,2},{2,18},{19,3},{3,19},{20,4},{4,... | collective-permute-start | bytes 1769480 | tf_op jit(solution)/shard_map/ppermute | solution.py:26
  358.0 29.1 %collective-permute-start.38 = (bf16[4,24,3072]{2,1,0:T(8,128)(2,1)}, bf16[4,24,3072]{2,1,0:T(8,128)(2,1)S(1)}, u32[]{:S(2)}, u32[]{:S(2)}) collective-permute-start(bf16[4,24,3072]{2,1,0:T(8,128)(2,1)} %collective-permute-done.34.refs_3_), channel_id=1, source_target_pairs={{16,0},{0,16},{17,1},{1,17},{18,2},{2,18},{19,3},{3,19},{20,4},{4,... | collective-permute-start | bytes 1769480 | tf_op jit(solution)/shard_map/ppermute | solution.py:26
  374.5 167.6 %collective-permute-start.48 = (bf16[4,96,768]{2,1,0:T(8,128)(2,1)}, bf16[4,96,768]{2,1,0:T(8,128)(2,1)}, u32[]{:S(2)}, u32[]{:S(2)}) collective-permute-start(bf16[4,96,768]{2,1,0:T(8,128)(2,1)} %pad_maximum_fusion.2.refs_0_), channel_id=1, source_target_pairs={{16,0},{0,16},{17,1},{1,17},{18,2},{2,18},{19,3},{3,19},{20,4},{4,... | collective-permute-start | bytes 1769480 | tf_op jit(solution)/shard_map/ppermute | solution.py:26
  386.2 350.1 %collective-permute-start.83 = (bf16[4,400,768]{2,1,0:T(8,128)(2,1)}, bf16[4,400,768]{2,1,0:T(8,128)(2,1)}, u32[]{:S(2)}, u32[]{:S(2)}) collective-permute-start(bf16[4,400,768]{2,1,0:T(8,128)(2,1)} %pad_maximum_fusion), channel_id=1, source_target_pairs={{16,0},{0,16},{17,1},{1,17},{18,2},{2,18},{19,3},{3,19},{20,4},{4,... | collective-permute-start | bytes 7372808 | tf_op jit(solution)/shard_map/ppermute | solution.py:26
  386.2 155.9 %collective-permute-start.49 = (bf16[4,96,768]{2,1,0:T(8,128)(2,1)}, bf16[4,96,768]{2,1,0:T(8,128)(2,1)}, u32[]{:S(2)}, u32[]{:S(2)}) collective-permute-start(bf16[4,96,768]{2,1,0:T(8,128)(2,1)} %collective-permute-done.45.refs_1_), channel_id=1, source_target_pairs={{16,0},{0,16},{17,1},{1,17},{18,2},{2,18},{19,3},{3,19},{20,4},{4,... | collective-permute-start | bytes 1769480 | tf_op jit(solution)/shard_map/ppermute | solution.py:26
  386.7 155.4 %collective-permute-start.50 = (bf16[4,96,768]{2,1,0:T(8,128)(2,1)S(1)}, bf16[4,96,768]{2,1,0:T(8,128)(2,1)}, u32[]{:S(2)}, u32[]{:S(2)}) collective-permute-start(bf16[4,96,768]{2,1,0:T(8,128)(2,1)S(1)} %collective-permute-done.46.refs_2_), channel_id=1, source_target_pairs={{16,0},{0,16},{17,1},{1,17},{18,2},{2,18},{19,3},{3,19},{20,4},{4,... | collective-permute-start | bytes 1769480 | tf_op jit(solution)/shard_map/ppermute | solution.py:26
  388.3 153.8 %collective-permute-start.51 = (bf16[4,96,768]{2,1,0:T(8,128)(2,1)S(1)}, bf16[4,96,768]{2,1,0:T(8,128)(2,1)}, u32[]{:S(2)}, u32[]{:S(2)}) collective-permute-start(bf16[4,96,768]{2,1,0:T(8,128)(2,1)S(1)} %collective-permute-done.47.refs_3_), channel_id=1, source_target_pairs={{16,0},{0,16},{17,1},{1,17},{18,2},{2,18},{19,3},{3,19},{20,4},{4,... | collective-permute-start | bytes 1769480 | tf_op jit(solution)/shard_map/ppermute | solution.py:26
  753.5 19.6 %collective-permute-start.101 = (f32[3,1024]{1,0:T(4,128)}, f32[3,1024]{1,0:T(4,128)}, u32[]{:S(2)}, u32[]{:S(2)}) collective-permute-start(f32[3,1024]{1,0:T(4,128)} %pad_maximum_fusion.18), channel_id=1, source_target_pairs={{104,0},{108,4},{96,8},{100,12},{8,32},{12,36},{0,40},{4,44},{40,6... | collective-permute-start | bytes 36872 | tf_op jit(solution)/shard_map/ppermute | solution.py:43
  756.5 22.1 %collective-permute-start.100 = (f32[3,1024]{1,0:T(4,128)}, f32[3,1024]{1,0:T(4,128)}, u32[]{:S(2)}, u32[]{:S(2)}) collective-permute-start(f32[3,1024]{1,0:T(4,128)} %pad_maximum_fusion.18), channel_id=1, source_target_pairs={{100,0},{104,4},{108,8},{96,12},{4,32},{8,36},{12,40},{0,44},{36,6... | collective-permute-start | bytes 36872 | tf_op jit(solution)/shard_map/ppermute | solution.py:43
  762.5 69.0 %collective-permute-start.99 = (f32[3,1024]{1,0:T(4,128)}, f32[3,1024]{1,0:T(4,128)}, u32[]{:S(2)}, u32[]{:S(2)}) collective-permute-start(f32[3,1024]{1,0:T(4,128)} %pad_maximum_fusion.18), channel_id=1, source_target_pairs={{96,0},{100,4},{104,8},{108,12},{0,32},{4,36},{8,40},{12,44},{32,6... | collective-permute-start | bytes 36872 | tf_op jit(solution)/shard_map/ppermute | solution.py:43
  764.2 26.2 %collective-permute-start.98 = (f32[3,1024]{1,0:T(4,128)}, f32[3,1024]{1,0:T(4,128)}, u32[]{:S(2)}, u32[]{:S(2)}) collective-permute-start(f32[3,1024]{1,0:T(4,128)} %pad_maximum_fusion.18), channel_id=1, source_target_pairs={{76,0},{64,4},{68,8},{72,12},{108,32},{96,36},{100,40},{104,44},{1... | collective-permute-start | bytes 36872 | tf_op jit(solution)/shard_map/ppermute | solution.py:43
  766.2 27.1 %collective-permute-start.97 = (f32[3,1024]{1,0:T(4,128)}, f32[3,1024]{1,0:T(4,128)}, u32[]{:S(2)}, u32[]{:S(2)}) collective-permute-start(f32[3,1024]{1,0:T(4,128)} %pad_maximum_fusion.18), channel_id=1, source_target_pairs={{72,0},{76,4},{64,8},{68,12},{104,32},{108,36},{96,40},{100,44},{8... | collective-permute-start | bytes 36872 | tf_op jit(solution)/shard_map/ppermute | solution.py:43
  773.1 25.5 %collective-permute-start.96 = (f32[3,1024]{1,0:T(4,128)}, f32[3,1024]{1,0:T(4,128)}, u32[]{:S(2)}, u32[]{:S(2)}) collective-permute-start(f32[3,1024]{1,0:T(4,128)} %pad_maximum_fusion.18), channel_id=1, source_target_pairs={{68,0},{72,4},{76,8},{64,12},{100,32},{104,36},{108,40},{96,44},{4... | collective-permute-start | bytes 36872 | tf_op jit(solution)/shard_map/ppermute | solution.py:43
  778.7 41.4 %collective-permute-start.95 = (f32[3,1024]{1,0:T(4,128)}, f32[3,1024]{1,0:T(4,128)}, u32[]{:S(2)}, u32[]{:S(2)}) collective-permute-start(f32[3,1024]{1,0:T(4,128)} %pad_maximum_fusion.18), channel_id=1, source_target_pairs={{64,0},{68,4},{72,8},{76,12},{96,32},{100,36},{104,40},{108,44},{0... | collective-permute-start | bytes 36872 | tf_op jit(solution)/shard_map/ppermute | solution.py:43
  793.3 16.3 %collective-permute-start.93 = (f32[3,1024]{1,0:T(4,128)}, f32[3,1024]{1,0:T(4,128)}, u32[]{:S(2)}, u32[]{:S(2)}) collective-permute-start(f32[3,1024]{1,0:T(4,128)} %pad_maximum_fusion.18), channel_id=1, source_target_pairs={{40,0},{44,4},{32,8},{36,12},{72,32},{76,36},{64,40},{68,44},{104,... | collective-permute-start | bytes 36872 | tf_op jit(solution)/shard_map/ppermute | solution.py:43
  798.5 15.1 %collective-permute-start.92 = (f32[3,1024]{1,0:T(4,128)}, f32[3,1024]{1,0:T(4,128)}, u32[]{:S(2)}, u32[]{:S(2)}) collective-permute-start(f32[3,1024]{1,0:T(4,128)} %pad_maximum_fusion.18), channel_id=1, source_target_pairs={{36,0},{40,4},{44,8},{32,12},{68,32},{72,36},{76,40},{64,44},{100,... | collective-permute-start | bytes 36872 | tf_op jit(solution)/shard_map/ppermute | solution.py:43
  803.6 31.9 %collective-permute-start.91 = (f32[3,1024]{1,0:T(4,128)}, f32[3,1024]{1,0:T(4,128)}, u32[]{:S(2)}, u32[]{:S(2)}) collective-permute-start(f32[3,1024]{1,0:T(4,128)} %pad_maximum_fusion.18), channel_id=1, source_target_pairs={{32,0},{36,4},{40,8},{44,12},{64,32},{68,36},{72,40},{76,44},{96,6... | collective-permute-start | bytes 36872 | tf_op jit(solution)/shard_map/ppermute | solution.py:43
  809.6 30.0 %collective-permute-start.90 = (f32[3,1024]{1,0:T(4,128)}, f32[3,1024]{1,0:T(4,128)}, u32[]{:S(2)}, u32[]{:S(2)}) collective-permute-start(f32[3,1024]{1,0:T(4,128)} %pad_maximum_fusion.18), channel_id=1, source_target_pairs={{12,0},{0,4},{4,8},{8,12},{44,32},{32,36},{36,40},{40,44},{76,64},... | collective-permute-start | bytes 36872 | tf_op jit(solution)/shard_map/ppermute | solution.py:43
  813.6 30.1 %collective-permute-start.89 = (f32[3,1024]{1,0:T(4,128)}, f32[3,1024]{1,0:T(4,128)}, u32[]{:S(2)}, u32[]{:S(2)}) collective-permute-start(f32[3,1024]{1,0:T(4,128)} %pad_maximum_fusion.18), channel_id=1, source_target_pairs={{8,0},{12,4},{0,8},{4,12},{40,32},{44,36},{32,40},{36,44},{72,64},... | collective-permute-start | bytes 36872 | tf_op jit(solution)/shard_map/ppermute | solution.py:43
  820.1 69.9 %collective-permute-start.88 = (f32[3,1024]{1,0:T(4,128)}, f32[3,1024]{1,0:T(4,128)}, u32[]{:S(2)}, u32[]{:S(2)}) collective-permute-start(f32[3,1024]{1,0:T(4,128)} %pad_maximum_fusion.18), channel_id=1, source_target_pairs={{4,0},{8,4},{12,8},{0,12},{36,32},{40,36},{44,40},{32,44},{68,64},... | collective-permute-start | bytes 36872 | tf_op jit(solution)/shard_map/ppermute | solution.py:43
  921.5 37.1 %collective-permute-start.103 = (f32[8,128]{1,0:T(8,128)}, f32[8,128]{1,0:T(8,128)}, u32[]{:S(2)}, u32[]{:S(2)}) collective-permute-start(f32[8,128]{1,0:T(8,128)} %broadcast_in_dim.35), channel_id=1, source_target_pairs={{32,0},{64,32},{96,64},{0,96},{33,1},{65,33},{97,65},{1,97},{34,2}... | collective-permute-start | bytes 12296 | tf_op jit(solution)/shard_map/ppermute | solution.py:26
  924.6 35.5 %collective-permute-start.104 = (f32[8,128]{1,0:T(8,128)}, f32[8,128]{1,0:T(8,128)}, u32[]{:S(2)}, u32[]{:S(2)}) collective-permute-start(f32[8,128]{1,0:T(8,128)} %broadcast_in_dim.35), channel_id=1, source_target_pairs={{64,0},{96,32},{0,64},{32,96},{65,1},{97,33},{1,65},{33,97},{66,2}... | collective-permute-start | bytes 12296 | tf_op jit(solution)/shard_map/ppermute | solution.py:26
  924.6 36.8 %collective-permute-start.105 = (f32[8,128]{1,0:T(8,128)}, f32[8,128]{1,0:T(8,128)}, u32[]{:S(2)}, u32[]{:S(2)}) collective-permute-start(f32[8,128]{1,0:T(8,128)} %broadcast_in_dim.35), channel_id=1, source_target_pairs={{96,0},{0,32},{32,64},{64,96},{97,1},{1,33},{33,65},{65,97},{98,2}... | collective-permute-start | bytes 12296 | tf_op jit(solution)/shard_map/ppermute | solution.py:26
  949.1 61.3 %collective-permute-start.127 = (bf16[64,768]{1,0:T(8,128)(2,1)}, bf16[64,768]{1,0:T(8,128)(2,1)}, u32[]{:S(2)}, u32[]{:S(2)}) collective-permute-start(bf16[64,768]{1,0:T(8,128)(2,1)} %get-tuple-element.97), channel_id=1, source_target_pairs={{0,108},{4,96},{8,100},{12,104},{32,12},{36,0},{40,4},{44,8},{64,4... | collective-permute-start | bytes 294920 | tf_op jit(solution)/shard_map/ppermute | solution.py:49
  951.0 60.7 %collective-permute-start.126 = (bf16[64,768]{1,0:T(8,128)(2,1)}, bf16[64,768]{1,0:T(8,128)(2,1)}, u32[]{:S(2)}, u32[]{:S(2)}) collective-permute-start(bf16[64,768]{1,0:T(8,128)(2,1)} %get-tuple-element.98), channel_id=1, source_target_pairs={{0,104},{4,108},{8,96},{12,100},{32,8},{36,12},{40,0},{44,4},{64,4... | collective-permute-start | bytes 294920 | tf_op jit(solution)/shard_map/ppermute | solution.py:49
  973.9 39.6 %collective-permute-start.125 = (bf16[64,768]{1,0:T(8,128)(2,1)}, bf16[64,768]{1,0:T(8,128)(2,1)S(1)}, u32[]{:S(2)}, u32[]{:S(2)}) collective-permute-start(bf16[64,768]{1,0:T(8,128)(2,1)} %get-tuple-element.99), channel_id=1, source_target_pairs={{0,100},{4,104},{8,108},{12,96},{32,4},{36,8},{40,12},{44,0},{64,3... | collective-permute-start | bytes 294920 | tf_op jit(solution)/shard_map/ppermute | solution.py:49
  976.1 39.8 %collective-permute-start.124 = (bf16[64,768]{1,0:T(8,128)(2,1)}, bf16[64,768]{1,0:T(8,128)(2,1)S(1)}, u32[]{:S(2)}, u32[]{:S(2)}) collective-permute-start(bf16[64,768]{1,0:T(8,128)(2,1)} %get-tuple-element.100), channel_id=1, source_target_pairs={{0,96},{4,100},{8,104},{12,108},{32,0},{36,4},{40,8},{44,12},{64,3... | collective-permute-start | bytes 294920 | tf_op jit(solution)/shard_map/ppermute | solution.py:49
  1110.5 24.0 %collective-permute-start.148 = (bf16[4,4,24,768]{3,2,0,1:T(8,128)(2,1)S(1)}, bf16[4,4,24,768]{3,2,0,1:T(8,128)(2,1)}, u32[]{:S(2)}, u32[]{:S(2)}) collective-permute-start(bf16[4,4,24,768]{3,2,0,1:T(8,128)(2,1)S(1)} %copy_bitcast_fusion.2), channel_id=1, source_target_pairs={{0,16},{16,0},{1,17},{17,1},{2,18},{18,2},{3,19},{19,3},{4,20},{20... | collective-permute-start | bytes 1769480 | tf_op jit(solution)/shard_map/ppermute | solution.py:31
  1122.2 34.9 %collective-permute-start.128 = (bf16[4,4,24,2304]{3,2,1,0:T(8,128)(2,1)}, bf16[4,4,24,2304]{3,2,1,0:T(8,128)(2,1)}, u32[]{:S(2)}, u32[]{:S(2)}) collective-permute-start(bf16[4,4,24,2304]{3,2,1,0:T(8,128)(2,1)} %dynamic-slice_bitcast_fusion.1), channel_id=1, source_target_pairs={{0,16},{16,0},{1,17},{17,1},{2,18},{18,2},{3,19},{19,3},{4,20},{20... | collective-permute-start | bytes 5308424 | tf_op jit(solution)/shard_map/ppermute | solution.py:31
  1161.3 18.4 %collective-permute-start.131 = (bf16[4,24,2304]{2,1,0:T(8,128)(2,1)}, bf16[4,24,2304]{2,1,0:T(8,128)(2,1)}, u32[]{:S(2)}, u32[]{:S(2)}) collective-permute-start(bf16[4,24,2304]{2,1,0:T(8,128)(2,1)} %get-tuple-element.81), channel_id=1, source_target_pairs={{0,96},{32,0},{64,32},{96,64},{1,97},{33,1},{65,33},{97,65},{2,98}... | collective-permute-start | bytes 1327112 | tf_op jit(solution)/shard_map/ppermute | solution.py:31
  1163.1 16.6 %collective-permute-start.130 = (bf16[4,24,2304]{2,1,0:T(8,128)(2,1)S(1)}, bf16[4,24,2304]{2,1,0:T(8,128)(2,1)}, u32[]{:S(2)}, u32[]{:S(2)}) collective-permute-start(bf16[4,24,2304]{2,1,0:T(8,128)(2,1)S(1)} %get-tuple-element.82), channel_id=1, source_target_pairs={{0,64},{32,96},{64,0},{96,32},{1,65},{33,97},{65,1},{97,33},{2,66}... | collective-permute-start | bytes 1327112 | tf_op jit(solution)/shard_map/ppermute | solution.py:31
  1165.4 18.2 %collective-permute-start.129 = (bf16[4,24,2304]{2,1,0:T(8,128)(2,1)S(1)}, bf16[4,24,2304]{2,1,0:T(8,128)(2,1)}, u32[]{:S(2)}, u32[]{:S(2)}) collective-permute-start(bf16[4,24,2304]{2,1,0:T(8,128)(2,1)S(1)} %get-tuple-element.80), channel_id=1, source_target_pairs={{0,32},{32,64},{64,96},{96,0},{1,33},{33,65},{65,97},{97,1},{2,34}... | collective-permute-start | bytes 1327112 | tf_op jit(solution)/shard_map/ppermute | solution.py:31
  1166.4 57.1 %collective-permute-start.188 = (bf16[4,400,768]{2,1,0:T(8,128)(2,1)}, bf16[4,400,768]{2,1,0:T(8,128)(2,1)S(1)}, u32[]{:S(2)}, u32[]{:S(2)}) collective-permute-start(bf16[4,400,768]{2,1,0:T(8,128)(2,1)} %bitcast.670), channel_id=1, source_target_pairs={{0,16},{16,0},{1,17},{17,1},{2,18},{18,2},{3,19},{19,3},{4,20},{20... | collective-permute-start | bytes 7372808 | tf_op jit(solution)/shard_map/ppermute | solution.py:31
  1171.1 46.5 %collective-permute-start.158 = (bf16[4,4,24,3072]{3,2,0,1:T(8,128)(2,1)}, bf16[4,4,24,3072]{3,2,0,1:T(8,128)(2,1)}, u32[]{:S(2)}, u32[]{:S(2)}) collective-permute-start(bf16[4,4,24,3072]{3,2,0,1:T(8,128)(2,1)} %copy_bitcast_fusion), channel_id=1, source_target_pairs={{0,16},{16,0},{1,17},{17,1},{2,18},{18,2},{3,19},{19,3},{4,20},{20... | collective-permute-start | bytes 7077896 | tf_op jit(solution)/shard_map/ppermute | solution.py:31
  1198.3 26.9 %collective-permute-start.168 = (bf16[4,4,96,768]{3,2,1,0:T(8,128)(2,1)}, bf16[4,4,96,768]{3,2,1,0:T(8,128)(2,1)S(1)}, u32[]{:S(2)}, u32[]{:S(2)}) collective-permute-start(bf16[4,4,96,768]{3,2,1,0:T(8,128)(2,1)} %dynamic-slice_bitcast_fusion), channel_id=1, source_target_pairs={{0,16},{16,0},{1,17},{17,1},{2,18},{18,2},{3,19},{19,3},{4,20},{20... | collective-permute-start | bytes 7077896 | tf_op jit(solution)/shard_map/ppermute | solution.py:31
  1220.5 22.5 %collective-permute-start.161 = (bf16[4,24,3072]{2,1,0:T(8,128)(2,1)S(1)}, bf16[4,24,3072]{2,1,0:T(8,128)(2,1)S(1)}, u32[]{:S(2)}, u32[]{:S(2)}) collective-permute-start(bf16[4,24,3072]{2,1,0:T(8,128)(2,1)S(1)} %get-tuple-element.78), channel_id=1, source_target_pairs={{0,12},{4,0},{8,4},{12,8},{1,13},{5,1},{9,5},{13,9},{2,14},{6,2},{... | collective-permute-start | bytes 1769480 | tf_op jit(solution)/shard_map/ppermute | solution.py:31
  1222.2 20.8 %collective-permute-start.160 = (bf16[4,24,3072]{2,1,0:T(8,128)(2,1)S(1)}, bf16[4,24,3072]{2,1,0:T(8,128)(2,1)S(1)}, u32[]{:S(2)}, u32[]{:S(2)}) collective-permute-start(bf16[4,24,3072]{2,1,0:T(8,128)(2,1)S(1)} %get-tuple-element.79), channel_id=1, source_target_pairs={{0,8},{4,12},{8,0},{12,4},{1,9},{5,13},{9,1},{13,5},{2,10},{6,14},... | collective-permute-start | bytes 1769480 | tf_op jit(solution)/shard_map/ppermute | solution.py:31
  1222.6 23.9 %collective-permute-start.159 = (bf16[4,24,3072]{2,1,0:T(8,128)(2,1)S(1)}, bf16[4,24,3072]{2,1,0:T(8,128)(2,1)S(1)}, u32[]{:S(2)}, u32[]{:S(2)}) collective-permute-start(bf16[4,24,3072]{2,1,0:T(8,128)(2,1)S(1)} %get-tuple-element.77), channel_id=1, source_target_pairs={{0,4},{4,8},{8,12},{12,0},{1,5},{5,9},{9,13},{13,1},{2,6},{6,10},{... | collective-permute-start | bytes 1769480 | tf_op jit(solution)/shard_map/ppermute | solution.py:31
  1224.4 44.4 %collective-permute-start.191 = (bf16[400,768]{1,0:T(8,128)(2,1)S(1)}, bf16[400,768]{1,0:T(8,128)(2,1)S(1)}, u32[]{:S(2)}, u32[]{:S(2)}) collective-permute-start(bf16[400,768]{1,0:T(8,128)(2,1)S(1)} %get-tuple-element.88), channel_id=1, source_target_pairs={{0,3},{1,0},{2,1},{3,2},{4,7},{5,4},{6,5},{7,6},{8,11},{9,8},{10,9... | collective-permute-start | bytes 1843208 | tf_op jit(solution)/shard_map/ppermute | solution.py:31
  1225.2 43.8 %collective-permute-start.190 = (bf16[400,768]{1,0:T(8,128)(2,1)S(1)}, bf16[400,768]{1,0:T(8,128)(2,1)S(1)}, u32[]{:S(2)}, u32[]{:S(2)}) collective-permute-start(bf16[400,768]{1,0:T(8,128)(2,1)S(1)} %get-tuple-element.89), channel_id=1, source_target_pairs={{0,2},{1,3},{2,0},{3,1},{4,6},{5,7},{6,4},{7,5},{8,10},{9,11},{10,... | collective-permute-start | bytes 1843208 | tf_op jit(solution)/shard_map/ppermute | solution.py:31
  1243.0 17.1 %collective-permute-start.170 = (bf16[4,96,768]{2,1,0:T(8,128)(2,1)S(1)}, bf16[4,96,768]{2,1,0:T(8,128)(2,1)S(1)}, u32[]{:S(2)}, u32[]{:S(2)}) collective-permute-start(bf16[4,96,768]{2,1,0:T(8,128)(2,1)S(1)} %get-tuple-element.76), channel_id=1, source_target_pairs={{0,64},{32,96},{64,0},{96,32},{1,65},{33,97},{65,1},{97,33},{2,66}... | collective-permute-start | bytes 1769480 | tf_op jit(solution)/shard_map/ppermute | solution.py:31
  1246.4 21.3 %collective-permute-start.169 = (bf16[4,96,768]{2,1,0:T(8,128)(2,1)S(1)}, bf16[4,96,768]{2,1,0:T(8,128)(2,1)S(1)}, u32[]{:S(2)}, u32[]{:S(2)}) collective-permute-start(bf16[4,96,768]{2,1,0:T(8,128)(2,1)S(1)} %get-tuple-element.74), channel_id=1, source_target_pairs={{0,32},{32,64},{64,96},{96,0},{1,33},{33,65},{65,97},{97,1},{2,34}... | collective-permute-start | bytes 1769480 | tf_op jit(solution)/shard_map/ppermute | solution.py:31
  1254.4 16.7 %collective-permute-start.189 = (bf16[400,768]{1,0:T(8,128)(2,1)S(1)}, bf16[400,768]{1,0:T(8,128)(2,1)S(1)}, u32[]{:S(2)}, u32[]{:S(2)}) collective-permute-start(bf16[400,768]{1,0:T(8,128)(2,1)S(1)} %get-tuple-element.87), channel_id=1, source_target_pairs={{0,1},{1,2},{2,3},{3,0},{4,5},{5,6},{6,7},{7,4},{8,9},{9,10},{10,1... | collective-permute-start | bytes 1843208 | tf_op jit(solution)/shard_map/ppermute | solution.py:31
  (247 other events, 3009.8 us)

commit v2 on v1

--- a/solution.py
+++ b/solution.py
@@ -1,10 +1,6 @@
-import functools
-
 import jax
 import jax.numpy as jnp
 from jax import lax
-from jax.experimental import pallas as pl
-from jax.experimental.pallas import tpu as pltpu
 from jax.sharding import Mesh
 from jax.sharding import PartitionSpec as P
 
@@ -31,82 +27,44 @@
     return lax.ppermute(array, axis, [(i, (i + k) % n) for i in range(n)])
 
 
-def yz_pairs(a, b):
-    return [
-        (((y + a) % NY) * NZ + (z + b) % NZ, y * NZ + z) for y in range(NY) for z in range(NZ)
-    ]
-
-
-def fetch_yz(array, a, b):
-    if a == 0 and b == 0:
-        return array
-    return lax.ppermute(array, ("y", "z"), yz_pairs(a, b))
-
-
-def give_yz(array, a, b):
-    if a == 0 and b == 0:
-        return array
-    return lax.ppermute(array, ("y", "z"), [(j, i) for i, j in yz_pairs(a, b)])
-
-
 def in_order(pieces, index):
     n = len(pieces)
     twice = jnp.stack(pieces + pieces)
     return lax.dynamic_slice_in_dim(twice, (n - index) % n, n, 0)
 
 
-def place_kernel(route, coords, *refs):
-    first, second = route
-    own, other, out, sems = refs[0:4], refs[4:8], refs[8], refs[9]
-    at = {"y": coords[0], "c": coords[1], "z": coords[2]}
-    copies = []
-    for kb in range(4):
-        for ka in range(4):
-            place = {
-                first: lax.rem(at[first] + ka, 4),
-                second: lax.rem(at[second] + kb, 4),
-            }
-            for kc, source in enumerate((own, other)):
-                core = lax.rem(at["c"] + kc, 2)
-                copy = pltpu.make_async_copy(
-                    source[kb].at[ka],
-                    out.at[place["y"], core, place["z"]],
-                    sems.at[kc, kb, ka],
-                )
-                copy.start()
-                copies.append(copy)
-    for copy in copies:
-        copy.wait()
-
-
-def place(own, other, route, coords):
-    _, rows, width = own[0].shape
-    anywhere = pl.BlockSpec(memory_space=pl.ANY)
-    return pl.pallas_call(
-        functools.partial(place_kernel, route),
-        out_shape=jax.ShapeDtypeStruct((NY, NC, NZ, rows, width), own[0].dtype),
-        in_specs=[pl.BlockSpec(memory_space=pltpu.SMEM)] + [anywhere] * 8,
-        out_specs=anywhere,
-        scratch_shapes=[pltpu.SemaphoreType.DMA((2, 4, 4))],
-        cost_estimate=pl.CostEstimate(
-            flops=0, bytes_accessed=2 * 32 * rows * width * 2, transcendentals=0
-        ),
-    )(coords, *own, *other)
-
-
-def gather_pieces(block, route):
-    first, second = route
-    plane = jnp.stack([block] + [fetch(block, first, k) for k in (1, 2, 3)])
-    own = [plane] + [fetch(plane, second, k) for k in (1, 2, 3)]
-    other = [fetch(piece, "c", 1) for piece in own]
-    return own, other
-
-
-def gather_weight(shard, route, coords):
+def gather_x(shard):
     pieces = [shard] + [fetch(shard, "x", k) for k in (1, 2, 3)]
-    block = in_order(pieces, lax.axis_index("x")).reshape(NX * shard.shape[0], shard.shape[1])
-    own, other = gather_pieces(block, route)
-    return place(own, other, route, coords).reshape(-1, shard.shape[1])
+    return in_order(pieces, lax.axis_index("x"))
+
+
+def swap(array, axes):
+    return lax.all_to_all(array, axes, 0, 0, tiled=True)
+
+
+def scatter_sum(grads):
+    n = grads[0].shape[1]
+    rows = [grad.shape[0] // 128 for grad in grads]
+    core = lax.axis_index("c")
+
+    def half(c):
+        cut = [
+            lax.dynamic_index_in_dim(
+                grad.astype(BF).reshape(NY, NC, NZ, NX * r, n), c, 1, False
+            ).reshape(NY * NZ, NX * r, n)
+            for grad, r in zip(grads, rows)
+        ]
+        return cut[0] if len(cut) == 1 else jnp.concatenate(cut, axis=1)
+
+    got = give(half(1 - core), "c", 1)
+    mine = (half(core).astype(F32) + got.astype(F32)).astype(BF)
+    mine = jnp.sum(swap(mine, ("y", "z")).astype(F32), axis=0).astype(BF)
+    parts, start = [], 0
+    for r in rows:
+        parts.append(mine[start : start + NX * r].reshape(NX, r, n))
+        start += NX * r
+    mine = parts[0] if len(parts) == 1 else jnp.concatenate(parts, axis=1)
+    return jnp.sum(swap(mine, "x").astype(F32), axis=0)
 
 
 def total(parts):
@@ -116,42 +74,11 @@
     return out
 
 
-def scatter_sum(grad, route):
-    n = grad.shape[1]
-    rows = grad.shape[0] // 128
-    at = {axis: lax.axis_index(axis) for axis in EVERY}
-    grad = grad.astype(BF).reshape(NY, NC, NZ, NX * rows, n)
-    away = lax.dynamic_index_in_dim(grad, 1 - at["c"], 1, False)
-    here = lax.dynamic_index_in_dim(grad, at["c"], 1, False)
-    got = give(away, "c", 1)
-    for axis in route:
-        dim = 0 if (axis == "y" or here.ndim == 3) else 1
-
-        def cut(k):
-            index = (at[axis] + k) % 4
-            mine = lax.dynamic_index_in_dim(here, index, dim, False)
-            if got is None:
-                return mine
-            theirs = lax.dynamic_index_in_dim(got, index, dim, False)
-            return (mine.astype(F32) + theirs.astype(F32)).astype(BF)
-
-        parts = [cut(0)] + [give(cut(k), axis, k) for k in (1, 2, 3)]
-        here, got = total(parts).astype(BF), None
-    here = here.reshape(NX, rows, n)
-    parts = [lax.dynamic_index_in_dim(here, at["x"], 0, False)]
-    for k in (1, 2, 3):
-        parts.append(
-            give(lax.dynamic_index_in_dim(here, (at["x"] + k) % NX, 0, False), "x", k)
-        )
-    return total(parts)
-
-
-def sum_everywhere(value):
-    for axis in EVERY:
-        n = SIZES[axis]
-        pieces = [value] + [fetch(value, axis, k) for k in range(1, n)]
-        value = jnp.sum(in_order(pieces, lax.axis_index(axis)), axis=0)
-    return value
+def three(value):
+    high = lax.reduce_precision(value, 8, 7)
+    rest = value - high
+    middle = lax.reduce_precision(rest, 8, 7)
+    return [high, middle, lax.reduce_precision(rest - middle, 8, 7)]
 
 
 def gelu_value(values):
@@ -229,8 +156,6 @@
     heads = width // HEAD_DIM
     factor = HEAD_DIM ** (-0.5)
     at = {axis: lax.axis_index(axis) for axis in EVERY}
-    coords = jnp.stack([at["y"], at["c"], at["z"]]).astype(jnp.int32)
-
     vectors = (
         b_query,
         b_value,
@@ -248,13 +173,27 @@
         [jnp.stack(vectors, axis=1), b_expand.reshape(w_qkv.shape[0], -1)], axis=1
     )
     small = jnp.pad(small, ((0, 0), (0, 128 - small.shape[1])))
-    qkv_all = gather_weight(jnp.concatenate([w_qkv, small], axis=1), ("y", "z"), coords)
-    attn_full = gather_weight(w_attn, ("z", "y"), coords)
-    expand_full = gather_weight(w_expand, ("z", "y"), coords)
-    shrink_full = gather_weight(w_shrink, ("y", "z"), coords)
-    dense_full = gather_weight(w_dense, ("z", "y"), coords)
-    qkv_full = qkv_all[:, : 3 * width]
-    rows_of = qkv_all[:, 3 * width :].T.astype(F32)
+    fused = jnp.concatenate([w_qkv, small, w_attn, w_expand, w_dense], axis=1)
+    fused = gather_x(fused).reshape(-1, fused.shape[1])
+    tall = gather_x(w_shrink)
+    tall = tall.transpose(1, 0, 2).reshape(fused.shape[0], -1)
+    layer = lax.all_gather(
+        jnp.concatenate([fused, tall], axis=1), ("y", "c", "z"), axis=0, tiled=True
+    )
+    ends = [3 * width, 128, width, w_expand.shape[1], width]
+    ends = [sum(ends[: i + 1]) for i in range(len(ends))]
+    qkv_full = layer[:, : ends[0]]
+    vec_full = layer[:, ends[0] : ends[1]]
+    attn_full = layer[:, ends[1] : ends[2]]
+    expand_full = layer[:, ends[2] : ends[3]]
+    dense_full = layer[:, ends[3] : ends[4]]
+    shrink_full = (
+        layer[:, ends[4] :]
+        .reshape(NY * NC * NZ, -1, NX, width)
+        .transpose(0, 2, 1, 3)
+        .reshape(-1, width)
+    )
+    rows_of = vec_full.T.astype(F32)
     (
         b_query,
         b_value,
@@ -268,7 +207,7 @@
         dense_gain,
         dense_shift,
     ) = (rows_of[i] for i in range(len(vectors)))
-    b_expand = qkv_all[:, 3 * width + 11 : 3 * width + 15].astype(F32).reshape(-1)
+    b_expand = vec_full[:, 11:15].astype(F32).reshape(-1)
 
     own_w = w_vocab.T
     piece_w = [own_w] + [fetch(own_w, "x", k) for k in (1, 2, 3)]
@@ -296,16 +235,21 @@
     grid = mask_labels.reshape(micro, NY, NC, peers, NZ, NX, slots)
     grid = lax.dynamic_index_in_dim(grid, at["c"], 2, False)
     grid = lax.dynamic_index_in_dim(grid, at["x"], 4, False)
-    grid = grid.transpose(1, 3, 0, 2, 4).reshape(NY, NZ, -1)
-    grid = jnp.concatenate([grid, grid], axis=0)
-    grid = lax.dynamic_slice_in_dim(grid, at["y"], NY, 0)
-    grid = jnp.concatenate([grid, grid], axis=1)
-    grid = lax.dynamic_slice_in_dim(grid, at["z"], NZ, 1)
-    labels = grid.reshape(-1)
+    labels = grid.transpose(1, 3, 0, 2, 4).reshape(-1)
     rows = micro * peers * slots
     row_norm = jnp.broadcast_to(norms[None, :, None], (NY * NZ, micro, peers * slots)).reshape(-1)
     live = (labels >= 0).astype(F32)
     row_weight = live * row_norm
+    hit = labels[:, None] == column[None, :]
+    scale = loss_scale * row_weight
+    own_first = (at["y"] * NZ + at["z"]) * rows
+    own_weight = lax.dynamic_slice_in_dim(row_weight, own_first, rows)
+    label_w = matmul(hit.astype(BF), vocab_w)
+    label_b = jnp.sum(jnp.where(hit, vocab_b, 0.0), axis=1, keepdims=True)
+    label_w = jnp.concatenate([label_w, jnp.pad(label_b, ((0, 0), (0, 127)))], axis=1)
+    label_w = swap(label_w.astype(BF).reshape(NY * NZ, rows, -1), ("y", "z"))
+    label_w = jnp.sum(label_w.astype(F32), axis=0)
+    label_w, label_b = label_w[:, :width], label_w[:, width]
     positions = mask_pos.reshape(micro, -1)
     shifted = jnp.where(
         positions >= 0, positions + block * jnp.arange(micro, dtype=jnp.int32)[:, None], -1
@@ -345,36 +289,37 @@
     dense_pre = matmul(picked, dense_full) + b_dense
     head_val, normed3, inverse3 = layer_norm(gelu_value(dense_pre), dense_gain, dense_shift)
     head_out = head_val.astype(BF)
-    spread = jnp.concatenate([fetch_yz(head_out, a, b) for a in range(NY) for b in range(NZ)])
+    spread = lax.all_gather(head_out, ("y", "z"), axis=0, tiled=True)
     logits = matmul_nt(spread, vocab_w) + vocab_b
-    hit = labels[:, None] == column[None, :]
     top = jnp.max(logits, axis=1)
     expl = jnp.exp(logits - top[:, None])
     part_sum = jnp.sum(expl, axis=1)
-    label_logit = jnp.sum(jnp.where(hit, logits, 0.0), axis=1)
-    stats = jnp.stack([top, part_sum, label_logit])
-    seen = [stats]
-    for a in range(NY):
-        for b in range(NZ):
-            if (a, b) != (0, 0):
-                there = fetch_yz(stats, a, b).reshape(3, NY, NZ, rows)
-                there = jnp.roll(there, (a, b), axis=(1, 2))
-                seen.append(there.reshape(3, -1))
-    top_all = functools.reduce(jnp.maximum, [s[0] for s in seen])
-    sum_all = sum(s[1] * jnp.exp(s[0] - top_all) for s in seen)
-    label_all = sum(s[2] for s in seen)
+    part = matmul(jnp.where(hit, 0.0, expl).astype(BF), vocab_w)
+    stats = jnp.stack(three(top) + three(part_sum), axis=1)
+    stats = jnp.pad(stats, ((0, 0), (0, 128 - stats.shape[1])))
+    part = jnp.concatenate([part, stats], axis=1).astype(BF).reshape(NY * NZ, rows, -1)
+    part = swap(part, ("y", "z")).astype(F32)
+    stats = part[:, :, width : width + 6]
+    tops = stats[:, :, 0] + stats[:, :, 1] + stats[:, :, 2]
+    sums = stats[:, :, 3] + stats[:, :, 4] + stats[:, :, 5]
+    top_all = jnp.max(tops, axis=0)
+    share = jnp.exp(tops - top_all)
+    sum_all = jnp.sum(sums * share, axis=0)
     log_sum = top_all + jnp.log(sum_all)
-    scale = loss_scale * row_weight
+    label_logit = jnp.sum(head_out.astype(F32) * label_w, axis=1) + label_b
+    mixed = jnp.sum((share / sum_all)[:, :, None] * part[:, :, :width], axis=0)
+    row_grad = (loss_scale * own_weight)[:, None] * (
+        mixed + (jnp.exp(label_logit - log_sum) - 1.0)[:, None] * label_w
+    )
+    loss_own = jnp.sum(own_weight * (log_sum - label_logit))
+    told = jnp.concatenate([log_sum, loss_own[None], jnp.zeros(128 - rows - 1, F32)])
+    told = lax.all_gather(told, ("y", "z"))
+    log_sums = told[:, :rows].reshape(-1)
+    loss = jnp.sum(lax.all_gather(jnp.sum(told[:, rows]), ("c", "x")))
     dlogits = (
-        (scale * jnp.exp(top - log_sum))[:, None] * expl
+        (scale * jnp.exp(top - log_sums))[:, None] * expl
         - jnp.where(hit, scale[:, None], 0.0)
     ).astype(BF)
-    part = matmul(dlogits, vocab_w).astype(BF).reshape(NY, NZ, rows, width)
-    row_grad = total(
-        [give_yz(part[a, b], a, b) for a in range(NY) for b in range(NZ)]
-    )
-    loss_own = jnp.sum((row_weight * (log_sum - label_all))[:rows])
-    loss = sum_everywhere(jnp.broadcast_to(loss_own, (8, 128)))[0, 0]
     grad_w = matmul_tn(dlogits, spread).astype(BF).reshape(NC, NX, per, width)
     grad_b = column_sum(dlogits).reshape(NC, NX, per)
     grad_w = (grad_w[0].astype(F32) + give(grad_w[1], "c", 1).astype(F32)).astype(BF)
@@ -385,7 +330,7 @@
     g_dense_gain = column_sum(row_grad * normed3)
     g_dense_shift = column_sum(row_grad)
     ddense = (norm_back(row_grad, normed3, inverse3, dense_gain) * gelu_slope(dense_pre)).astype(BF)
-    g_dense = scatter_sum(matmul_tn(picked, ddense), ("z", "y"))
+    g_dense = matmul_tn(picked, ddense)
     g_dense_bias = column_sum(ddense)
     drows = matmul_nt(ddense, dense_full).astype(BF)
 
@@ -394,17 +339,19 @@
     g_ffn_shift = column_sum(dout)
     dsecond = norm_back(dout, normed2, inverse2, ffn_gain)
     dffn = dsecond.astype(BF)
-    g_shrink = scatter_sum(matmul_tn(act, dffn), ("y", "z"))
+    g_shrink = matmul_tn(act, dffn)
+    g_both = scatter_sum([g_shrink, g_dense])
+    g_shrink, g_dense = g_both[: w_shrink.shape[0]], g_both[w_shrink.shape[0] :]
     g_shrink_bias = column_sum(dffn)
     dpre = (matmul_nt(dffn, shrink_full) * gelu_slope(pre)).astype(BF)
-    g_expand = scatter_sum(matmul_tn(first_low, dpre), ("z", "y"))
+    g_expand = scatter_sum([matmul_tn(first_low, dpre)])
     g_expand_bias = column_sum(dpre)
     dfirst = dsecond + matmul_nt(dpre, expand_full)
     g_attn_gain = column_sum(dfirst * normed1)
     g_attn_shift = column_sum(dfirst)
     dresidual = norm_back(dfirst, normed1, inverse1, attn_gain)
     dbranch = dresidual.astype(BF)
-    g_attn = scatter_sum(matmul_tn(attended, dbranch), ("z", "y"))
+    g_attn = matmul_tn(attended, dbranch)
     g_attn_bias = column_sum(dbranch)
     dattended = matmul_nt(dbranch, attn_full).astype(BF).reshape(micro, block, heads, HEAD_DIM)
     dprobs = jnp.einsum("mqhd,mkhd->mhqk", dattended, values, preferred_element_type=F32)
@@ -424,7 +371,7 @@
         jnp.einsum("mhqk,mqhd->mkhd", weights, dattended, preferred_element_type=F32)
     )
     dfused = jnp.concatenate([dquery, dkeys, dvalues], axis=1)
-    g_qkv = scatter_sum(matmul_tn(x, dfused), ("y", "z"))
+    g_qkv = matmul_tn(x, dfused)
     g_query = column_sum(dquery)
     g_value = column_sum(dvalues)
     dinput = dresidual + matmul_nt(dfused, qkv_full)
@@ -447,7 +394,8 @@
     )
     sums = jnp.concatenate([sums, g_expand_bias.reshape(width, -1)], axis=1)
     sums = jnp.pad(sums, ((0, 0), (0, 128 - sums.shape[1])))
-    sums = scatter_sum(sums, ("z", "y"))
+    last = scatter_sum([jnp.concatenate([g_qkv.astype(BF), g_attn.astype(BF), sums.astype(BF)], axis=1)])
+    g_qkv, g_attn, sums = last[:, : 3 * width], last[:, 3 * width : 4 * width], last[:, 4 * width :]
     return (
         settled_low.reshape(hidden_in.shape),
         loss,

time: 1310 us -> 609 us (0.46)
  Pallas kernels: 481 us -> 0 us
  starting transfers between devices: 253 us -> 64.8 us
  local copies, waits for them, and re-layouts: 203 us -> 115 us
  blocking collectives: 0 us -> 50 us
  matrix products: 91 us -> 108 us
    pallas_call x5 -> x0, Pallas kernels: 481 us -> none  [place(): pl.pallas_call(functools.partial(place_kernel, route), out_shape=jax.Shap...]
    all_to_all x0 -> x8, waiting for transfers between devices: none -> 84.8 us  [swap(): return lax.all_to_all(array, axes, 0, 0, tiled=True)]
    ppermute x45 -> x0, starting transfers between devices: 84.6 us -> none  [the longest x30 58.6 us: fetch_yz(): return lax.ppermute(array, ('y', 'z'), yz_pairs(a, b))]
    ppermute x68 -> x11, waiting for transfers between devices: 79.2 us -> 0.03 us  [give(): return lax.ppermute(array, axis, [(i, (i + k) % n) for i in range(n)])]
    ppermute x83 -> x14, starting transfers between devices: 96.8 us -> 18 us  [fetch(): return lax.ppermute(array, axis, [((i + k) % n, i) for i in range(n)])]
    squeeze x64 -> x0, local copies, waits for them, and re-layouts: 74.1 us -> none  [the longest x15 20.4 us: body(): label_all = sum((s[2] for s in seen))]
    ppermute x68 -> x11, starting transfers between devices: 71.7 us -> 10 us  [give(): return lax.ppermute(array, axis, [(i, (i + k) % n) for i in range(n)])]
    all_gather x0 -> x2, waiting for transfers between devices: none -> 50.2 us  [the longest x1 40 us: body(): lax.all_gather(jnp.concatenate([fused, tall], axis=1), ('y', 'c', 'z'), a...]
  transfers between devices with their start and end apart: 196 -> 35, of which waited for: 61 -> 15; matrix products, arithmetic and copies ran while one was open for 18% -> 31% of each run, Pallas kernels for 37% -> 0%
where the time goes in v2:
time: 609 us; the launch traced here: 598 us
  waiting for transfers between devices  166 us (27%)
  local copies, waits for them, and re-layouts  115 us (19%)
  matrix products  108 us (18%)
  other arithmetic  77.7 us (13%)
  starting transfers between devices  64.8 us (11%)
  blocking collectives  50 us (8%)
  between operations  16.7 us (3%)
    all_to_all x8, waiting for transfers between devices, swap(): return lax.all_to_all(array, axes, 0, 0, tiled=True)  84.8 us
    all_gather x1, waiting for transfers between devices, body(): lax.all_gather(jnp.concatenate([fused, tall], axis=1), ('y', 'c', 'z'), a...  40 us
    dot_general x8, matrix products, matmul(): return jnp.dot(left, right, preferred_element_type=F32)  37.4 us
    all_to_all x8, starting transfers between devices, swap(): return lax.all_to_all(array, axes, 0, 0, tiled=True)  36.7 us
    ppermute x14, waiting for transfers between devices, fetch(): return lax.ppermute(array, axis, [((i + k) % n, i) for i in range(n)])  31.2 us
    unnamed x1, blocking collectives  30.2 us
    dot_general x5, matrix products, matmul_nt(): lax.dot_general(left, right, (((1,), (1,)), ((), ())), preferred_element_...  28.6 us
    unnamed x274, local copies, waits for them, and re-layouts  27.8 us
  transfers between devices with their start and end apart: 35, of which 15 were waited for; matrix products, arithmetic and copies ran while one was open for 31% of the time, Pallas kernels for 0%

profile of v2, /device:TPU:0, one launch (start us, length us, event | category | flops | bytes accessed | tf_op | source)
XLA Modules:
  0.0 597.8 jit_solution(2441184492894895188)
XLA Ops:
  19.5 2.8 collective-permute-start
  24.0 2.4 collective-permute-start.3
  32.0 2.5 collective-permute-done.5
  40.1 22.6 %collective-permute-done.6 = bf16[400,768]{1,0:T(8,128)(2,1)S(1)} collective-permute-done((bf16[400,768]{1,0:T(8,128)(2,1)S(1)}, bf16[400,768]{1,0:T(8,128)(2,1)S(1)}, u32[]{:S(2)}, u32[]{:S(2)}) %collective-permute-start.6) | collective-permute-done | bytes 614432 | tf_op jit(solution)/shard_map/ppermute | solution.py:22
  62.8 3.4 collective-permute-done.8
  67.9 40.0 %all-gather.5.cloned.1.call-done = bf16[768,10112]{1,0:T(8,128)(2,1)} async-done(((bf16[24,10112]{1,0:T(8,128)(2,1)}), bf16[768,10112]{1,0:T(8,128)(2,1)}) %all-gather.5.cloned.1.call-update) | async-done | bytes 15532048 | tf_op jit(solution)/shard_map/all_gather | solution.py:180
  111.2 4.3 convolution_bitcast_fusion
  123.3 2.4 fusion.118
  127.5 4.8 slice.303
  132.3 9.7 %reshape.473 = bf16[32,24,4,768]{3,2,1,0:T(4,128)(2,1)} reshape(bf16[768,3072]{1,0:T(8,128)(2,1)} %slice.303) | data formatting | bytes 9437184 | tf_op jit(solution)/shard_map/reshape | solution.py:192
  142.0 3.2 copy.256
  145.3 8.3 %multiply_convert_fusion.1 = (bf16[512,3072]{1,0:T(8,128)(2,1)S(1)}, f32[512,3072]{1,0:T(8,128)}) fusion(f32[3072]{0:T(1024)S(1)} %reshape.502, bf16[768,10112]{1,0:T(8,128)(2,1)} %all-gather.5.cloned.1.call-done, f32[512,768]{1,0:T(8,128)S(1)} %get-tuple-element.110, f32[768]{0:T(1024)S(1)} %get-tuple-element.40, f32[768]{0:T(1024)S(1)} %get-tuple-element.41, ...), kind=kOutput, calls=%fused_computation.27 | convolution fusion | flops 2427322368 | bytes 15751168 | tf_op jit(solution)/shard_map/dot_general | solution.py:116
  153.6 2.8 fusion.119
  158.7 2.5 fusion.113
  162.7 2.8 collective-permute-start.10
  185.0 3.3 constant_dynamic-update-slice_fusion.13
  188.3 7.9 %fusion.33 = bf16[16,64,768]{2,1,0:T(8,128)(2,1)S(1)} fusion(bf16[3200,768,1]{1,0,2:T(8,128)(2,1)} %bitcast.266, s32[3200]{0:T(1024)S(1)} %copy-done.44, s32[16,64]{1,0:T(8,128)S(1)} %copy.262), kind=kOutput, calls=%fused_computation.63 | convolution fusion | flops 5037228032 | bytes 6504960 | tf_op jit(solution)/shard_map/dot_general | solution.py:116
  196.2 10.2 %all-gather.7.cloned.1.call-done = bf16[1024,768]{1,0:T(8,128)(2,1)} async-done(((bf16[64,768]{1,0:T(8,128)(2,1)}), bf16[1024,768]{1,0:T(8,128)(2,1)}) %all-gather.7.cloned.1.call-update) | async-done | bytes 1572880 | tf_op jit(solution)/shard_map/all_gather | solution.py:292
  206.3 8.5 %add_reduce_fusion = (f32[1024]{0:T(1024)S(1)}, f32[1024,3200]{1,0:T(8,128)S(1)}) fusion(f32[3200]{0:T(1024)S(1)} %reshape.503, bf16[1024,768]{1,0:T(8,128)(2,1)} %all-gather.7.cloned.1.call-done, bf16[3200,768]{1,0:T(8,128)(2,1)} %bitcast.267), kind=kOutput, calls=%fused_computation.12 | convolution fusion | flops 5039717376 | bytes 19612160 | tf_op jit(solution)/shard_map/dot_general | solution.py:124
  214.8 6.9 %fusion.2 = (bf16[1024]{0:T(1024)(128)(2,1)S(1)}, f32[1024]{0:T(1024)S(1)}, bf16[1024,3200]{1,0:T(8,128)(2,1)}) fusion(f32[3200]{0:T(1024)S(1)} %reshape.503, s32[3200]{0:T(1024)S(1)} %copy-done.44, s32[1024]{0:T(1024)S(1)} %copy-done.52, f32[1024]{0:T(1024)S(1)} %get-tuple-element.116, f32[1024,3200]{1,0:T(8,128)S(1)} %get-tuple-element.117), kind=kLoop, calls=%fused_computation.5 | loop fusion | flops 26212352 | bytes 19700736 | tf_op jit(solution)/shard_map/reduce_sum | solution.py:248
  223.4 5.1 all-to-all-start.1
  230.5 9.1 %convolution_convert_fusion.4 = bf16[16,64,768]{2,1,0:T(8,128)(2,1)S(1)} fusion(bf16[16,64,3200]{2,1,0:T(8,128)(2,1)} %bitcast.229, bf16[3200,768,1]{1,0,2:T(8,128)(2,1)} %bitcast.268), kind=kOutput, calls=%fused_computation.64 | convolution fusion | flops 5033951232 | bytes 13041664 | tf_op jit(solution)/shard_map/dot_general | solution.py:116
  241.1 13.3 %all-to-all-done.1 = bf16[16,64,896]{2,1,0:T(8,128)(2,1)S(1)} async-done(((bf16[16,64,896]{2,1,0:T(8,128)(2,1)}), bf16[16,64,896]{2,1,0:T(8,128)(2,1)S(1)}, u32[]{:S(2)}, u32[]{:S(2)}) %all-to-all-start.1) | async-done | bytes 1835040 | tf_op jit(solution)/shard_map/all_to_all | solution.py:42
  254.4 4.4 all-to-all-start
  262.4 19.5 %all-to-all-done = bf16[16,64,896]{2,1,0:T(8,128)(2,1)} async-done(((bf16[16,64,896]{2,1,0:T(8,128)(2,1)}), bf16[16,64,896]{2,1,0:T(8,128)(2,1)}, u32[]{:S(2)}, u32[]{:S(2)}) %all-to-all-start) | async-done | bytes 1835040 | tf_op jit(solution)/shard_map/all_to_all | solution.py:42
  292.2 4.3 multiply_reduce_fusion.1
  296.5 2.7 convert_reduce_fusion.6
  299.2 4.4 convolution_convert_fusion.1
  303.7 5.3 fusion.124
  309.1 5.0 convolution_convert_fusion.2
  314.1 6.1 %multiply_reduce_fusion.2 = (bf16[768]{0:T(1024)(128)(2,1)}, f32[512]{0:T(512)S(1)}, f32[512]{0:T(512)S(1)}, bf16[768]{0:T(1024)(128)(2,1)}, f32[512,768]{1,0:T(8,128)S(1)}) fusion(f32[512,768]{1,0:T(8,128)S(1)} %copy-done.13, f32[512]{0:T(512)S(1)} %copy-done.82, f32[512]{0:T(512)S(1)} %copy-done.67, f32[768]{0:T(1024)S(1)} %copy-done.73, ...), kind=kOutput, calls=%fused_computation.72 | convolution fusion | flops 2419848704 | bytes 12597248 | tf_op jit(solution)/shard_map/dot_general | solution.py:124
  321.3 3.5 convolution_convert_fusion.7
  327.3 5.7 fusion.123
  333.0 6.8 %multiply_reduce_fusion = (f32[2,12,256]{2,1,0:T(8,128)S(1)}, f32[2,12,256,256]{2,3,1,0:T(8,128)}) fusion(f32[2,12,256,256]{2,3,1,0:T(8,128)} %copy-done.14, f32[2,12,256]{2,1,0:T(8,128)S(1)} %copy-done.63, bf16[2,256,12,64]{1,0,3,2:T(2,128)(2,1)S(1)} %copy-done.35, bf16[2,256,12,64]{1,0,3,2:T(2,128)(2,1)S(1)} %copy-done.37), kind=kOutput, calls=%fused_computation.26 | convolution fusion | flops 206039040 | bytes 14204928 | tf_op jit(solution)/shard_map/mqhd,mkhd->mhqk/dot_general | solution.py:357
  339.9 4.3 multiply_convert_fusion
  348.2 19.8 %all-gather.1 = f32[16,1,128]{2,1,0:T(1,128)} all-gather(f32[1,1,128]{2,1,0:T(1,128)S(1)} %maximum_bitcast_fusion), channel_id=2, replica_groups=mesh['y'=4,'c'=2,'z'=4,'x'=4] {'y','z'}, dimensions={0}, use_global_device_ids=true | all-gather | bytes 8704 | tf_op jit(solution)/shard_map/all_gather | solution.py:316
  370.2 4.3 constant_dynamic-slice_fusion.3
  376.3 2.5 constant_dynamic-slice_fusion.5
  393.4 2.8 fusion.16
  396.2 7.5 %copy.278 = bf16[768,3200]{1,0:T(8,128)(2,1)} copy(bf16[768,3200]{0,1:T(8,128)(2,1)} %fusion.16) | data formatting | bytes 9830400 | tf_op jit(solution)/shard_map/concatenate | solution.py:397
  403.7 4.4 constant_dynamic-slice_fusion.7
  408.2 3.9 fusion.20
  412.1 5.8 all-to-all-start.4
  418.0 8.3 %convert_reduce_fusion = (f32[3200]{0:T(1024)S(1)}, bf16[1024,3200]{1,0:T(8,128)(2,1)S(1)}) fusion(f32[1024]{0:T(1024)S(1)} %copy-done.74, s32[3200]{0:T(1024)S(1)} %copy-done.44, s32[1024]{0:T(1024)S(1)} %copy-done.53, f32[1024]{0:T(1024)S(1)} %copy-done.55, f32[1024,3200]{1,0:T(8,128)} %copy-done, f32[3200]{0:T(1024)S(1)} %copy-done.46, ...), kind=kLoop, calls=%fused_computation.8 | loop fusion | flops 29488000 | bytes 19715584 | tf_op jit(solution)/shard_map/reduce_sum | solution.py:112
  426.3 7.3 %convolution_convert_fusion = bf16[3200,768]{1,0:T(8,128)(2,1)} fusion(bf16[1024,3200]{1,0:T(8,128)(2,1)S(1)} %get-tuple-element.61, bf16[1024,768]{1,0:T(8,128)(2,1)S(1)} %copy-done.105), kind=kOutput, calls=%fused_computation.17 | convolution fusion | flops 5035622400 | bytes 13041664 | tf_op jit(solution)/shard_map/dot_general | solution.py:120
  433.6 17.9 %all-to-all-done.4 = bf16[16,24,3072]{2,1,0:T(8,128)(2,1)} async-done(((bf16[16,24,3072]{2,1,0:T(8,128)(2,1)}), bf16[16,24,3072]{2,1,0:T(8,128)(2,1)}, u32[]{:S(2)}, u32[]{:S(2)}) %all-to-all-start.4) | async-done | bytes 2359328 | tf_op jit(solution)/shard_map/all_to_all | solution.py:42
  454.4 4.2 all-to-all-start.5
  458.6 3.8 fusion.18
  462.4 2.5 all-to-all-done.5
  464.9 6.0 %all-to-all-start.2 = ((bf16[16,24,3200]{2,1,0:T(8,128)(2,1)}), bf16[16,24,3200]{2,1,0:T(8,128)(2,1)S(1)}, u32[]{:S(2)}, u32[]{:S(2)}) async-start(bf16[16,24,3200]{2,1,0:T(8,128)(2,1)} %fusion.18), calls=%async_computation.2 | async-start | bytes 4915200 | tf_op jit(solution)/shard_map/all_to_all | solution.py:42
  471.0 5.1 fusion.114
  476.1 4.2 add_convert_fusion
  480.3 22.5 %all-to-all-done.2 = bf16[16,24,3200]{2,1,0:T(8,128)(2,1)S(1)} async-done(((bf16[16,24,3200]{2,1,0:T(8,128)(2,1)}), bf16[16,24,3200]{2,1,0:T(8,128)(2,1)S(1)}, u32[]{:S(2)}, u32[]{:S(2)}) %all-to-all-start.2) | async-done | bytes 2457632 | tf_op jit(solution)/shard_map/all_to_all | solution.py:42
  504.2 4.3 all-to-all-start.6
  512.2 2.5 collective-permute-start.23
  516.1 3.2 fusion.17
  523.8 2.8 collective-permute-start.20
  526.6 5.2 fusion.42
  531.8 30.2 %all-reduce.4 = f32[8]{0:T(128)S(1)} all-reduce(f32[8]{0:T(128)S(1)} %dynamic-update-slice), channel_id=1, replica_groups=mesh['y'=4,'c'=2,'z'=4,'x'=4] {'c','x'}, use_global_device_ids=true, to_apply=%add.4 | all-reduce | flops 8 | bytes 64
  563.3 2.9 fusion.65
  569.7 3.4 all-to-all-start.3
  574.2 5.5 all-to-all-done.3
  579.7 3.4 all-to-all-start.7
  585.9 3.5 all-to-all-done.7
  (484 shorter events, 130.6 us)
Async XLA Ops:
  7.2 100.7 %all-gather.5.cloned.1.call-start = ((), (), s32[]{:S(2)}) async-start(), calls=%async_computation.8 | async-start | bytes 16017408 | tf_op jit(solution)/shard_map/all_gather | solution.py:180
  17.9 18.7 %copy-start.23 = (bf16[768,400]{0,1:T(8,128)(2,1)S(1)}, bf16[768,400]{0,1:T(8,128)(2,1)}, u32[]{:S(2)}) copy-start(bf16[768,400]{0,1:T(8,128)(2,1)} %param.48) | copy-start | bytes 1843204
  17.9 21.7 %copy-start.97 = (s32[2,1,16,2]{2,3,1,0:T(2,128)S(1)}, s32[2,1,16,2]{2,3,1,0:T(2,128)}, u32[]{:S(2)}) copy-start(s32[2,1,16,2]{2,3,1,0:T(2,128)} %param.28) | copy-start | bytes 772
  17.9 22.1 %copy-start.88 = (s32[2,256]{1,0:T(2,128)S(1)}, s32[2,256]{1,0:T(2,128)}, u32[]{:S(2)}) copy-start(s32[2,256]{1,0:T(2,128)} %param.27) | copy-start | bytes 6148
  19.5 15.9 %collective-permute-start = (bf16[6,7040]{1,0:T(8,128)(2,1)S(1)}, bf16[6,7040]{1,0:T(8,128)(2,1)S(1)}, u32[]{:S(2)}, u32[]{:S(2)}) collective-permute-start(bf16[6,7040]{1,0:T(8,128)(2,1)S(1)} %constant_dynamic-update-slice_fusion), channel_id=1, source_target_pairs={{1,0},{2,1},{3,2},{0,3},{5,4},{6,5},{7,6},{4,7},{9,8},{10,9},{11,1... | collective-permute-start | bytes 253448 | tf_op jit(solution)/shard_map/ppermute | solution.py:22
  22.3 13.1 %collective-permute-start.1 = (bf16[6,7040]{1,0:T(8,128)(2,1)S(1)}, bf16[6,7040]{1,0:T(8,128)(2,1)S(1)}, u32[]{:S(2)}, u32[]{:S(2)}) collective-permute-start(bf16[6,7040]{1,0:T(8,128)(2,1)S(1)} %constant_dynamic-update-slice_fusion), channel_id=1, source_target_pairs={{2,0},{3,1},{0,2},{1,3},{6,4},{7,5},{4,6},{5,7},{10,8},{11,9},{8,1... | collective-permute-start | bytes 253448 | tf_op jit(solution)/shard_map/ppermute | solution.py:22
  23.1 12.3 %collective-permute-start.2 = (bf16[6,7040]{1,0:T(8,128)(2,1)S(1)}, bf16[6,7040]{1,0:T(8,128)(2,1)S(1)}, u32[]{:S(2)}, u32[]{:S(2)}) collective-permute-start(bf16[6,7040]{1,0:T(8,128)(2,1)S(1)} %constant_dynamic-update-slice_fusion), channel_id=1, source_target_pairs={{3,0},{0,1},{1,2},{2,3},{7,4},{4,5},{5,6},{6,7},{11,8},{8,9},{9,10... | collective-permute-start | bytes 253448 | tf_op jit(solution)/shard_map/ppermute | solution.py:22
  24.0 4.7 collective-permute-start.3
  26.3 5.7 collective-permute-start.4
  28.7 5.8 collective-permute-start.5
  36.5 169.8 %all-gather.7.cloned.1.call-start = ((), (), s32[]{:S(2)}) async-start(), calls=%async_computation.9 | async-start | bytes 1671168 | tf_op jit(solution)/shard_map/all_gather | solution.py:292
  36.6 26.2 %collective-permute-start.6 = (bf16[400,768]{1,0:T(8,128)(2,1)S(1)}, bf16[400,768]{1,0:T(8,128)(2,1)S(1)}, u32[]{:S(2)}, u32[]{:S(2)}) collective-permute-start(bf16[400,768]{1,0:T(8,128)(2,1)S(1)} %bitcast.251), channel_id=1, source_target_pairs={{1,0},{2,1},{3,2},{0,3},{5,4},{6,5},{7,6},{4,7},{9,8},{10,9},{11,1... | collective-permute-start | bytes 1843208 | tf_op jit(solution)/shard_map/ppermute | solution.py:22
  38.7 24.1 %collective-permute-start.7 = (bf16[400,768]{1,0:T(8,128)(2,1)S(1)}, bf16[400,768]{1,0:T(8,128)(2,1)S(1)}, u32[]{:S(2)}, u32[]{:S(2)}) collective-permute-start(bf16[400,768]{1,0:T(8,128)(2,1)S(1)} %bitcast.252), channel_id=1, source_target_pairs={{2,0},{3,1},{0,2},{1,3},{6,4},{7,5},{4,6},{5,7},{10,8},{11,9},{8,1... | collective-permute-start | bytes 1843208 | tf_op jit(solution)/shard_map/ppermute | solution.py:22
  38.8 27.3 %collective-permute-start.8 = (bf16[400,768]{1,0:T(8,128)(2,1)S(1)}, bf16[400,768]{1,0:T(8,128)(2,1)S(1)}, u32[]{:S(2)}, u32[]{:S(2)}) collective-permute-start(bf16[400,768]{1,0:T(8,128)(2,1)S(1)} %bitcast.253), channel_id=1, source_target_pairs={{3,0},{0,1},{1,2},{2,3},{7,4},{4,5},{5,6},{6,7},{11,8},{8,9},{9,10... | collective-permute-start | bytes 1843208 | tf_op jit(solution)/shard_map/ppermute | solution.py:22
  40.0 117.2 %copy-start.103 = (s32[64]{0:T(128)}, s32[64]{0:T(128)S(1)}, u32[]{:S(2)}) copy-start(s32[64]{0:T(128)S(1)} %compare_select_fusion.4) | copy-start | bytes 772
  62.7 48.4 %copy-start.25 = (bf16[400,768]{1,0:T(8,128)(2,1)}, bf16[400,768]{1,0:T(8,128)(2,1)S(1)}, u32[]{:S(2)}) copy-start(bf16[400,768]{1,0:T(8,128)(2,1)S(1)} %collective-permute-done.6) | copy-start | bytes 1843204
  62.8 48.4 %copy-start.27 = (bf16[400,768]{1,0:T(8,128)(2,1)}, bf16[400,768]{1,0:T(8,128)(2,1)S(1)}, u32[]{:S(2)}) copy-start(bf16[400,768]{1,0:T(8,128)(2,1)S(1)} %collective-permute-done.7) | copy-start | bytes 1843204
  66.1 45.0 %copy-start.29 = (bf16[400,768]{1,0:T(8,128)(2,1)}, bf16[400,768]{1,0:T(8,128)(2,1)S(1)}, u32[]{:S(2)}) copy-start(bf16[400,768]{1,0:T(8,128)(2,1)S(1)} %collective-permute-done.8) | copy-start | bytes 1843204
  67.9 117.1 %collective-permute-start.9 = (bf16[4,400,768]{2,1,0:T(8,128)(2,1)}, bf16[4,400,768]{2,1,0:T(8,128)(2,1)}, u32[]{:S(2)}, u32[]{:S(2)}) collective-permute-start(bf16[4,400,768]{2,1,0:T(8,128)(2,1)} %pad_maximum_fusion.1), channel_id=1, source_target_pairs={{16,0},{0,16},{17,1},{1,17},{18,2},{2,18},{19,3},{3,19},{20,4},{4,... | collective-permute-start | bytes 7372808 | tf_op jit(solution)/shard_map/ppermute | solution.py:22
  111.1 42.5 %copy-start.72 = (f32[768]{0:T(1024)}, f32[768]{0:T(1024)S(1)}, u32[]{:S(2)}) copy-start(f32[768]{0:T(1024)S(1)} %get-tuple-element.41) | copy-start | bytes 9220
  111.1 42.5 %copy-start.94 = (f32[768]{0:T(1024)}, f32[768]{0:T(1024)S(1)}, u32[]{:S(2)}) copy-start(f32[768]{0:T(1024)S(1)} %get-tuple-element.40) | copy-start | bytes 9220
  111.1 45.7 %copy-start.56 = (f32[768]{0:T(1024)}, f32[768]{0:T(1024)S(1)}, u32[]{:S(2)}) copy-start(f32[768]{0:T(1024)S(1)} %get-tuple-element.38) | copy-start | bytes 9220
  111.2 50.2 %copy-start.49 = (f32[768]{0:T(1024)}, f32[768]{0:T(1024)S(1)}, u32[]{:S(2)}) copy-start(f32[768]{0:T(1024)S(1)} %get-tuple-element.34) | copy-start | bytes 9220
  111.2 50.2 %copy-start.58 = (f32[768]{0:T(1024)}, f32[768]{0:T(1024)S(1)}, u32[]{:S(2)}) copy-start(f32[768]{0:T(1024)S(1)} %get-tuple-element.35) | copy-start | bytes 9220
  125.7 27.9 %copy-start.12 = (f32[512,768]{1,0:T(8,128)}, f32[512,768]{1,0:T(8,128)S(1)}, u32[]{:S(2)}) copy-start(f32[512,768]{1,0:T(8,128)S(1)} %get-tuple-element.110) | copy-start | bytes 4718596
  125.7 27.9 %copy-start.66 = (f32[512]{0:T(512)}, f32[512]{0:T(512)S(1)}, u32[]{:S(2)}) copy-start(f32[512]{0:T(512)S(1)} %broadcast_multiply_fusion.6) | copy-start | bytes 6148
  126.0 27.6 %copy-start.81 = (f32[512]{0:T(512)}, f32[512]{0:T(512)S(1)}, u32[]{:S(2)}) copy-start(f32[512]{0:T(512)S(1)} %add_rsqrt_fusion.1) | copy-start | bytes 6148
  127.5 17.8 %copy-start.79 = (f32[3072]{0:T(1024)}, f32[3072]{0:T(1024)S(1)}, u32[]{:S(2)}) copy-start(f32[3072]{0:T(1024)S(1)} %reshape.502) | copy-start | bytes 36868
  157.2 25.2 %copy-start.26 = (bf16[400,768]{1,0:T(8,128)(2,1)S(1)}, bf16[400,768]{1,0:T(8,128)(2,1)}, u32[]{:S(2)}) copy-start(bf16[400,768]{1,0:T(8,128)(2,1)} %copy-done.25) | copy-start | bytes 1843204
  158.7 24.6 %copy-start.28 = (bf16[400,768]{1,0:T(8,128)(2,1)S(1)}, bf16[400,768]{1,0:T(8,128)(2,1)}, u32[]{:S(2)}) copy-start(bf16[400,768]{1,0:T(8,128)(2,1)} %copy-done.27) | copy-start | bytes 1843204
  162.7 7.2 %collective-permute-start.10 = (bf16[400]{0:T(512)(128)(2,1)S(1)}, bf16[400]{0:T(512)(128)(2,1)S(1)}, u32[]{:S(2)}, u32[]{:S(2)}) collective-permute-start(bf16[400]{0:T(512)(128)(2,1)S(1)} %copy-done.102), channel_id=1, source_target_pairs={{1,0},{2,1},{3,2},{0,3},{5,4},{6,5},{7,6},{4,7},{9,8},{10,9},{11,1... | collective-permute-start | bytes 2408 | tf_op jit(solution)/shard_map/ppermute | solution.py:22
  165.4 5.1 collective-permute-start.11
  166.3 4.8 collective-permute-start.12
  168.1 16.0 %copy-start.30 = (bf16[400,768]{1,0:T(8,128)(2,1)S(1)}, bf16[400,768]{1,0:T(8,128)(2,1)}, u32[]{:S(2)}) copy-start(bf16[400,768]{1,0:T(8,128)(2,1)} %copy-done.29) | copy-start | bytes 1843204
  171.7 9.9 %collective-permute-start.13 = (bf16[4,400]{1,0:T(4,128)(2,1)}, bf16[4,400]{1,0:T(4,128)(2,1)}, u32[]{:S(2)}, u32[]{:S(2)}) collective-permute-start(bf16[4,400]{1,0:T(4,128)(2,1)} %pad_maximum_fusion.6), channel_id=1, source_target_pairs={{16,0},{0,16},{17,1},{1,17},{18,2},{2,18},{19,3},{3,19},{20,4},{4,... | collective-permute-start | bytes 9608 | tf_op jit(solution)/shard_map/ppermute | solution.py:22
  182.3 32.5 %copy-start.45 = (f32[3200]{0:T(1024)}, f32[3200]{0:T(1024)S(1)}, u32[]{:S(2)}) copy-start(f32[3200]{0:T(1024)S(1)} %reshape.503) | copy-start | bytes 38404
  223.4 30.9 %all-to-all-start.1 = ((bf16[16,64,896]{2,1,0:T(8,128)(2,1)}), bf16[16,64,896]{2,1,0:T(8,128)(2,1)S(1)}, u32[]{:S(2)}, u32[]{:S(2)}) async-start(bf16[16,64,896]{2,1,0:T(8,128)(2,1)} %pad_maximum_fusion.3), calls=%async_computation.1 | async-start | bytes 3670016 | tf_op jit(solution)/shard_map/all_to_all | solution.py:42
  239.6 19.8 %copy-start.48 = (s32[2,128,16,2]{1,3,2,0:T(2,128)S(1)}, s32[2,128,16,2]{1,3,2,0:T(2,128)}, u32[]{:S(2)}) copy-start(s32[2,128,16,2]{1,3,2,0:T(2,128)} %param.29) | copy-start | bytes 98308
  241.1 20.2 %copy-start.50 = (f32[768]{0:T(1024)S(1)}, f32[768]{0:T(1024)}, u32[]{:S(2)}) copy-start(f32[768]{0:T(1024)} %copy-done.49) | copy-start | bytes 9220
  241.1 20.2 %copy-start.59 = (f32[768]{0:T(1024)S(1)}, f32[768]{0:T(1024)}, u32[]{:S(2)}) copy-start(f32[768]{0:T(1024)} %copy-done.58) | copy-start | bytes 9220
  241.1 20.2 %copy-start.78 = (f32[64]{0:T(128)S(1)}, f32[64]{0:T(128)}, u32[]{:S(2)}) copy-start(f32[64]{0:T(128)} %copy-done.77) | copy-start | bytes 772
  241.1 20.2 %copy-start.90 = (f32[64]{0:T(128)S(1)}, f32[64]{0:T(128)}, u32[]{:S(2)}) copy-start(f32[64]{0:T(128)} %copy-done.89) | copy-start | bytes 772
  254.4 27.6 %all-to-all-start = ((bf16[16,64,896]{2,1,0:T(8,128)(2,1)}), bf16[16,64,896]{2,1,0:T(8,128)(2,1)}, u32[]{:S(2)}, u32[]{:S(2)}) async-start(bf16[16,64,896]{2,1,0:T(8,128)(2,1)} %pad_maximum_fusion.2), calls=%async_computation | async-start | bytes 3670016 | tf_op jit(solution)/shard_map/all_to_all | solution.py:42
  260.3 29.1 %copy-start.64 = (f32[1024]{0:T(1024)}, f32[1024]{0:T(1024)S(1)}, u32[]{:S(2)}) copy-start(f32[1024]{0:T(1024)S(1)} %get-tuple-element.63) | copy-start | bytes 12292
  321.3 68.4 %copy-start.10 = (f32[512,768]{1,0:T(8,128)}, f32[512,768]{1,0:T(8,128)S(1)}, u32[]{:S(2)}) copy-start(f32[512,768]{1,0:T(8,128)S(1)} %get-tuple-element.69) | copy-start | bytes 4718596
  376.3 99.8 %collective-permute-start.16 = (bf16[16,120,768]{2,1,0:T(8,128)(2,1)}, bf16[16,120,768]{2,1,0:T(8,128)(2,1)}, u32[]{:S(2)}, u32[]{:S(2)}) collective-permute-start(bf16[16,120,768]{2,1,0:T(8,128)(2,1)} %pad_maximum_fusion), channel_id=1, source_target_pairs={{0,16},{16,0},{1,17},{17,1},{2,18},{18,2},{3,19},{19,3},{4,20},{20... | collective-permute-start | bytes 8847368 | tf_op jit(solution)/shard_map/ppermute | solution.py:27
  378.8 29.4 %collective-permute-start.15 = (bf16[16,24,3072]{2,1,0:T(8,128)(2,1)}, bf16[16,24,3072]{2,1,0:T(8,128)(2,1)}, u32[]{:S(2)}, u32[]{:S(2)}) collective-permute-start(bf16[16,24,3072]{2,1,0:T(8,128)(2,1)} %bitcast.73), channel_id=1, source_target_pairs={{0,16},{16,0},{1,17},{17,1},{2,18},{18,2},{3,19},{19,3},{4,20},{20... | collective-permute-start | bytes 7077896 | tf_op jit(solution)/shard_map/ppermute | solution.py:27
  408.1 50.5 %collective-permute-start.14 = (bf16[16,24,3200]{2,1,0:T(8,128)(2,1)}, bf16[16,24,3200]{2,1,0:T(8,128)(2,1)}, u32[]{:S(2)}, u32[]{:S(2)}) collective-permute-start(bf16[16,24,3200]{2,1,0:T(8,128)(2,1)} %bitcast.70), channel_id=1, source_target_pairs={{0,16},{16,0},{1,17},{17,1},{2,18},{18,2},{3,19},{19,3},{4,20},{20... | collective-permute-start | bytes 7372808 | tf_op jit(solution)/shard_map/ppermute | solution.py:27
  412.1 39.4 %all-to-all-start.4 = ((bf16[16,24,3072]{2,1,0:T(8,128)(2,1)}), bf16[16,24,3072]{2,1,0:T(8,128)(2,1)}, u32[]{:S(2)}, u32[]{:S(2)}) async-start(bf16[16,24,3072]{2,1,0:T(8,128)(2,1)} %fusion.20), calls=%async_computation.4 | async-start | bytes 4718592 | tf_op jit(solution)/shard_map/all_to_all | solution.py:42
  454.4 10.6 %all-to-all-start.5 = ((bf16[4,6,3072]{2,1,0:T(8,128)(2,1)}), bf16[4,6,3072]{2,1,0:T(8,128)(2,1)S(1)}, u32[]{:S(2)}, u32[]{:S(2)}) async-start(bf16[4,6,3072]{2,1,0:T(8,128)(2,1)} %reshape.491), calls=%async_computation.5 | async-start | bytes 393216 | tf_op jit(solution)/shard_map/all_to_all | solution.py:42
  464.9 37.9 %all-to-all-start.2 = ((bf16[16,24,3200]{2,1,0:T(8,128)(2,1)}), bf16[16,24,3200]{2,1,0:T(8,128)(2,1)S(1)}, u32[]{:S(2)}, u32[]{:S(2)}) async-start(bf16[16,24,3200]{2,1,0:T(8,128)(2,1)} %fusion.18), calls=%async_computation.2 | async-start | bytes 4915200 | tf_op jit(solution)/shard_map/all_to_all | solution.py:42
  476.1 40.0 %collective-permute-start.17 = (bf16[4,400,768]{2,1,0:T(8,128)(2,1)}, bf16[4,400,768]{2,1,0:T(8,128)(2,1)}, u32[]{:S(2)}, u32[]{:S(2)}) collective-permute-start(bf16[4,400,768]{2,1,0:T(8,128)(2,1)} %bitcast.82), channel_id=1, source_target_pairs={{0,16},{16,0},{1,17},{17,1},{2,18},{18,2},{3,19},{19,3},{4,20},{20... | collective-permute-start | bytes 7372808 | tf_op jit(solution)/shard_map/ppermute | solution.py:27
  480.3 28.3 %copy-start.108 = (u32[128]{0:T(128)S(1)}, u32[128]{0:T(128)}, u32[]{:S(2)}) copy-start(u32[128]{0:T(128)} %constant.258) | copy-start | bytes 1540
  480.3 29.1 %copy-start.51 = (f32[16,1,128]{2,1,0:T(1,128)S(1)}, f32[16,1,128]{2,1,0:T(1,128)}, u32[]{:S(2)}) copy-start(f32[16,1,128]{2,1,0:T(1,128)} %all-gather.1) | copy-start | bytes 24580
  504.2 65.4 %all-to-all-start.6 = ((bf16[16,120,768]{2,1,0:T(8,128)(2,1)}), bf16[16,120,768]{2,1,0:T(8,128)(2,1)S(1)}, u32[]{:S(2)}, u32[]{:S(2)}) async-start(bf16[16,120,768]{2,1,0:T(8,128)(2,1)} %add_convert_fusion), calls=%async_computation.6 | async-start | bytes 5898240 | tf_op jit(solution)/shard_map/all_to_all | solution.py:42
  509.4 2.2 collective-permute-start.21
  511.6 12.2 %collective-permute-start.22 = (f32[400]{0:T(512)S(1)}, f32[400]{0:T(512)S(1)}, u32[]{:S(2)}, u32[]{:S(2)}) collective-permute-start(f32[400]{0:T(512)S(1)} %bitcast.276), channel_id=1, source_target_pairs={{0,1},{1,2},{2,3},{3,0},{4,5},{5,6},{6,7},{7,4},{8,9},{9,10},{10,1... | collective-permute-start | bytes 4808 | tf_op jit(solution)/shard_map/ppermute | solution.py:27
  512.2 50.4 %collective-permute-start.23 = (f32[400]{0:T(512)S(1)}, f32[400]{0:T(512)S(1)}, u32[]{:S(2)}, u32[]{:S(2)}) collective-permute-start(f32[400]{0:T(512)S(1)} %bitcast.275), channel_id=1, source_target_pairs={{0,2},{1,3},{2,0},{3,1},{4,6},{5,7},{6,4},{7,5},{8,10},{9,11},{10,... | collective-permute-start | bytes 4808 | tf_op jit(solution)/shard_map/ppermute | solution.py:27
  514.7 48.0 %collective-permute-start.24 = (f32[400]{0:T(512)S(1)}, f32[400]{0:T(512)S(1)}, u32[]{:S(2)}, u32[]{:S(2)}) collective-permute-start(f32[400]{0:T(512)S(1)} %bitcast.274), channel_id=1, source_target_pairs={{0,3},{1,0},{2,1},{3,2},{4,7},{5,4},{6,5},{7,6},{8,11},{9,8},{10,9... | collective-permute-start | bytes 4808 | tf_op jit(solution)/shard_map/ppermute | solution.py:27
  522.1 41.2 %collective-permute-start.18 = (bf16[400,768]{1,0:T(8,128)(2,1)}, bf16[400,768]{1,0:T(8,128)(2,1)}, u32[]{:S(2)}, u32[]{:S(2)}) collective-permute-start(bf16[400,768]{1,0:T(8,128)(2,1)} %get-tuple-element.88), channel_id=1, source_target_pairs={{0,1},{1,2},{2,3},{3,0},{4,5},{5,6},{6,7},{7,4},{8,9},{9,10},{10,1... | collective-permute-start | bytes 1843208 | tf_op jit(solution)/shard_map/ppermute | solution.py:27
  522.7 40.6 %collective-permute-start.19 = (bf16[400,768]{1,0:T(8,128)(2,1)}, bf16[400,768]{1,0:T(8,128)(2,1)}, u32[]{:S(2)}, u32[]{:S(2)}) collective-permute-start(bf16[400,768]{1,0:T(8,128)(2,1)} %get-tuple-element.90), channel_id=1, source_target_pairs={{0,2},{1,3},{2,0},{3,1},{4,6},{5,7},{6,4},{7,5},{8,10},{9,11},{10,... | collective-permute-start | bytes 1843208 | tf_op jit(solution)/shard_map/ppermute | solution.py:27
  523.8 39.5 %collective-permute-start.20 = (bf16[400,768]{1,0:T(8,128)(2,1)}, bf16[400,768]{1,0:T(8,128)(2,1)}, u32[]{:S(2)}, u32[]{:S(2)}) collective-permute-start(bf16[400,768]{1,0:T(8,128)(2,1)} %get-tuple-element.89), channel_id=1, source_target_pairs={{0,3},{1,0},{2,1},{3,2},{4,7},{5,4},{6,5},{7,6},{8,11},{9,8},{10,9... | collective-permute-start | bytes 1843208 | tf_op jit(solution)/shard_map/ppermute | solution.py:27
  569.7 10.1 %all-to-all-start.3 = ((bf16[4,6,3200]{2,1,0:T(8,128)(2,1)}), bf16[4,6,3200]{2,1,0:T(8,128)(2,1)S(1)}, u32[]{:S(2)}, u32[]{:S(2)}) async-start(bf16[4,6,3200]{2,1,0:T(8,128)(2,1)} %reshape.488), calls=%async_computation.3 | async-start | bytes 409600 | tf_op jit(solution)/shard_map/all_to_all | solution.py:42
  579.7 9.7 %all-to-all-start.7 = ((bf16[4,30,768]{2,1,0:T(8,128)(2,1)}), bf16[4,30,768]{2,1,0:T(8,128)(2,1)S(1)}, u32[]{:S(2)}, u32[]{:S(2)}) async-start(bf16[4,30,768]{2,1,0:T(8,128)(2,1)} %pad_maximum_fusion.5), calls=%async_computation.7 | async-start | bytes 393216 | tf_op jit(solution)/shard_map/all_to_all | solution.py:42
  (90 other events, 396.2 us)
Sparse Core Ops, SparseCore 0:
  36.6 71.2 all-gather.4
  162.8 43.4 all-gather.6

commit v3 on v2

--- a/solution.py
+++ b/solution.py
@@ -42,29 +42,39 @@
     return lax.all_to_all(array, axes, 0, 0, tiled=True)
 
 
-def scatter_sum(grads):
-    n = grads[0].shape[1]
-    rows = [grad.shape[0] // 128 for grad in grads]
+def blocks(grad):
+    return grad.astype(BF).reshape(NY, NC, NZ, -1, grad.shape[1])
+
+
+def half(grads, core, axis):
+    cut = [lax.dynamic_index_in_dim(grad, core, 1, False) for grad in grads]
+    cut = [part.reshape((NY * NZ,) + part.shape[2:]) for part in cut]
+    return cut[0] if len(cut) == 1 else jnp.concatenate(cut, axis=axis)
+
+
+def sum_cores(grads, axis):
     core = lax.axis_index("c")
-
-    def half(c):
-        cut = [
-            lax.dynamic_index_in_dim(
-                grad.astype(BF).reshape(NY, NC, NZ, NX * r, n), c, 1, False
-            ).reshape(NY * NZ, NX * r, n)
-            for grad, r in zip(grads, rows)
-        ]
-        return cut[0] if len(cut) == 1 else jnp.concatenate(cut, axis=1)
-
-    got = give(half(1 - core), "c", 1)
-    mine = (half(core).astype(F32) + got.astype(F32)).astype(BF)
-    mine = jnp.sum(swap(mine, ("y", "z")).astype(F32), axis=0).astype(BF)
-    parts, start = [], 0
-    for r in rows:
-        parts.append(mine[start : start + NX * r].reshape(NX, r, n))
-        start += NX * r
-    mine = parts[0] if len(parts) == 1 else jnp.concatenate(parts, axis=1)
+    return half(grads, core, axis), give(half(grads, 1 - core, axis), "c", 1)
+
+
+def add_cores(pair):
+    return (pair[0].astype(F32) + pair[1].astype(F32)).astype(BF)
+
+
+def sum_yz(mine):
+    return jnp.sum(swap(mine, ("y", "z")).astype(F32), axis=0).astype(BF)
+
+
+def sum_x(mine):
     return jnp.sum(swap(mine, "x").astype(F32), axis=0)
+
+
+def split_three(value):
+    return jnp.pad(jnp.stack(three(value)), (0, 765)).astype(BF)
+
+
+def after(*arrays):
+    return lax.optimization_barrier(arrays)
 
 
 def total(parts):
@@ -169,9 +179,8 @@
         dense_gain,
         dense_shift,
     )
-    small = jnp.concatenate(
-        [jnp.stack(vectors, axis=1), b_expand.reshape(w_qkv.shape[0], -1)], axis=1
-    )
+    small = after(jnp.stack(vectors))[0].T
+    small = jnp.concatenate([small, b_expand.reshape(w_qkv.shape[0], -1)], axis=1)
     small = jnp.pad(small, ((0, 0), (0, 128 - small.shape[1])))
     fused = jnp.concatenate([w_qkv, small, w_attn, w_expand, w_dense], axis=1)
     fused = gather_x(fused).reshape(-1, fused.shape[1])
@@ -180,6 +189,7 @@
     layer = lax.all_gather(
         jnp.concatenate([fused, tall], axis=1), ("y", "c", "z"), axis=0, tiled=True
     )
+    layer, w_vocab = after(layer, w_vocab)
     ends = [3 * width, 128, width, w_expand.shape[1], width]
     ends = [sum(ends[: i + 1]) for i in range(len(ends))]
     qkv_full = layer[:, : ends[0]]
@@ -187,12 +197,15 @@
     attn_full = layer[:, ends[1] : ends[2]]
     expand_full = layer[:, ends[2] : ends[3]]
     dense_full = layer[:, ends[3] : ends[4]]
-    shrink_full = (
-        layer[:, ends[4] :]
-        .reshape(NY * NC * NZ, -1, NX, width)
-        .transpose(0, 2, 1, 3)
-        .reshape(-1, width)
-    )
+    shrink_full = jnp.stack(
+        [
+            layer[:, ends[4] + k * width : ends[4] + (k + 1) * width].reshape(
+                NY * NC * NZ, -1, width
+            )
+            for k in range(NX)
+        ],
+        axis=1,
+    ).reshape(-1, width)
     rows_of = vec_full.T.astype(F32)
     (
         b_query,
@@ -244,12 +257,6 @@
     scale = loss_scale * row_weight
     own_first = (at["y"] * NZ + at["z"]) * rows
     own_weight = lax.dynamic_slice_in_dim(row_weight, own_first, rows)
-    label_w = matmul(hit.astype(BF), vocab_w)
-    label_b = jnp.sum(jnp.where(hit, vocab_b, 0.0), axis=1, keepdims=True)
-    label_w = jnp.concatenate([label_w, jnp.pad(label_b, ((0, 0), (0, 127)))], axis=1)
-    label_w = swap(label_w.astype(BF).reshape(NY * NZ, rows, -1), ("y", "z"))
-    label_w = jnp.sum(label_w.astype(F32), axis=0)
-    label_w, label_b = label_w[:, :width], label_w[:, width]
     positions = mask_pos.reshape(micro, -1)
     shifted = jnp.where(
         positions >= 0, positions + block * jnp.arange(micro, dtype=jnp.int32)[:, None], -1
@@ -289,33 +296,46 @@
     dense_pre = matmul(picked, dense_full) + b_dense
     head_val, normed3, inverse3 = layer_norm(gelu_value(dense_pre), dense_gain, dense_shift)
     head_out = head_val.astype(BF)
-    spread = lax.all_gather(head_out, ("y", "z"), axis=0, tiled=True)
+    head_out, vocab_w = after(head_out, vocab_w)
+    spread = swap(
+        jnp.broadcast_to(head_out, (NY * NZ,) + head_out.shape), ("y", "z")
+    ).reshape(-1, width)
+    label_w = matmul(hit.astype(BF), vocab_w)
+    label_b = jnp.sum(jnp.where(hit, vocab_b, 0.0), axis=1, keepdims=True)
+    label_w = jnp.concatenate([label_w, jnp.pad(label_b, ((0, 0), (0, 127)))], axis=1)
+    spread, label_w = after(spread, label_w.astype(BF).reshape(NY * NZ, rows, -1))
+    label_w = swap(label_w, ("y", "z"))
+    label_w = jnp.sum(label_w.astype(F32), axis=0)
+    label_w, label_b = label_w[:, :width], label_w[:, width]
     logits = matmul_nt(spread, vocab_w) + vocab_b
     top = jnp.max(logits, axis=1)
     expl = jnp.exp(logits - top[:, None])
     part_sum = jnp.sum(expl, axis=1)
-    part = matmul(jnp.where(hit, 0.0, expl).astype(BF), vocab_w)
-    stats = jnp.stack(three(top) + three(part_sum), axis=1)
-    stats = jnp.pad(stats, ((0, 0), (0, 128 - stats.shape[1])))
-    part = jnp.concatenate([part, stats], axis=1).astype(BF).reshape(NY * NZ, rows, -1)
-    part = swap(part, ("y", "z")).astype(F32)
-    stats = part[:, :, width : width + 6]
-    tops = stats[:, :, 0] + stats[:, :, 1] + stats[:, :, 2]
-    sums = stats[:, :, 3] + stats[:, :, 4] + stats[:, :, 5]
+    other = jnp.where(hit, 0.0, expl).astype(BF)
+    other, label_w, label_b = after(other, label_w, label_b)
+    part = matmul(other, vocab_w).astype(BF).reshape(NY * NZ, rows, width)
+    stats = jnp.stack(three(top) + three(part_sum)).astype(BF)
+    stats = jnp.concatenate([stats[:, :width], stats[:, width:].reshape(2, width)])
+    stats = jnp.broadcast_to(stats, (NY * NZ,) + stats.shape)
+    part = swap(jnp.concatenate([part, stats], axis=1), ("y", "z"))
+    stats = part[:, rows:]
+    stats = jnp.concatenate(
+        [stats[:, :6], stats[:, 6:].reshape(NY * NZ, 6, NY * NZ * rows - width)], axis=2
+    ).astype(F32)
+    tops = stats[:, 0] + stats[:, 1] + stats[:, 2]
+    sums = stats[:, 3] + stats[:, 4] + stats[:, 5]
     top_all = jnp.max(tops, axis=0)
-    share = jnp.exp(tops - top_all)
-    sum_all = jnp.sum(sums * share, axis=0)
-    log_sum = top_all + jnp.log(sum_all)
+    shares = jnp.exp(tops - top_all)
+    sum_all = jnp.sum(sums * shares, axis=0)
+    log_sums = top_all + jnp.log(sum_all)
+    log_sum = lax.dynamic_slice_in_dim(log_sums, own_first, rows)
+    share = lax.dynamic_slice_in_dim(shares / sum_all, own_first, rows, 1)
     label_logit = jnp.sum(head_out.astype(F32) * label_w, axis=1) + label_b
-    mixed = jnp.sum((share / sum_all)[:, :, None] * part[:, :, :width], axis=0)
+    mixed = jnp.sum(share[:, :, None] * part[:, :rows].astype(F32), axis=0)
     row_grad = (loss_scale * own_weight)[:, None] * (
         mixed + (jnp.exp(label_logit - log_sum) - 1.0)[:, None] * label_w
     )
     loss_own = jnp.sum(own_weight * (log_sum - label_logit))
-    told = jnp.concatenate([log_sum, loss_own[None], jnp.zeros(128 - rows - 1, F32)])
-    told = lax.all_gather(told, ("y", "z"))
-    log_sums = told[:, :rows].reshape(-1)
-    loss = jnp.sum(lax.all_gather(jnp.sum(told[:, rows]), ("c", "x")))
     dlogits = (
         (scale * jnp.exp(top - log_sums))[:, None] * expl
         - jnp.where(hit, scale[:, None], 0.0)
@@ -340,17 +360,26 @@
     dsecond = norm_back(dout, normed2, inverse2, ffn_gain)
     dffn = dsecond.astype(BF)
     g_shrink = matmul_tn(act, dffn)
-    g_both = scatter_sum([g_shrink, g_dense])
-    g_shrink, g_dense = g_both[: w_shrink.shape[0]], g_both[w_shrink.shape[0] :]
+    loss_row = jnp.where(
+        (jnp.arange(NC) == at["c"])[None, :, None, None, None], split_three(loss_own), 0.0
+    ).astype(BF)
+    loss_row = jnp.broadcast_to(loss_row, (NY, NC, NZ, 8, width))
+    tall_pair = sum_cores([blocks(g_shrink), blocks(g_dense), loss_row], 1)
     g_shrink_bias = column_sum(dffn)
     dpre = (matmul_nt(dffn, shrink_full) * gelu_slope(pre)).astype(BF)
-    g_expand = scatter_sum([matmul_tn(first_low, dpre)])
+    g_expand = matmul_tn(first_low, dpre)
+    wide_pair = sum_cores([blocks(g_expand)], 2)
     g_expand_bias = column_sum(dpre)
     dfirst = dsecond + matmul_nt(dpre, expand_full)
     g_attn_gain = column_sum(dfirst * normed1)
     g_attn_shift = column_sum(dfirst)
     dresidual = norm_back(dfirst, normed1, inverse1, attn_gain)
     dbranch = dresidual.astype(BF)
+    dbranch, got = after(dbranch, tall_pair[1])
+    tall_sum = add_cores((tall_pair[0], got))
+    tall_all = swap(tall_sum, ("y", "z")).astype(F32)
+    tall_sum = jnp.sum(tall_all[:, :120], axis=0).astype(BF)
+    loss_row = split_three(jnp.sum(tall_all[:, 120, :3]))
     g_attn = matmul_tn(attended, dbranch)
     g_attn_bias = column_sum(dbranch)
     dattended = matmul_nt(dbranch, attn_full).astype(BF).reshape(micro, block, heads, HEAD_DIM)
@@ -394,8 +423,28 @@
     )
     sums = jnp.concatenate([sums, g_expand_bias.reshape(width, -1)], axis=1)
     sums = jnp.pad(sums, ((0, 0), (0, 128 - sums.shape[1])))
-    last = scatter_sum([jnp.concatenate([g_qkv.astype(BF), g_attn.astype(BF), sums.astype(BF)], axis=1)])
-    g_qkv, g_attn, sums = last[:, : 3 * width], last[:, 3 * width : 4 * width], last[:, 4 * width :]
+    wide = sum_yz(add_cores(wide_pair))
+    tall = sum_x(
+        jnp.concatenate(
+            [tall_sum[:96].reshape(NX, -1, width), jnp.broadcast_to(loss_row, (NX, 8, width))],
+            axis=1,
+        )
+    )
+    last_pair = sum_cores([blocks(g_qkv), blocks(g_attn), blocks(sums)], 2)
+    last_pair, wide, tall = after(last_pair, wide, tall)
+    last = sum_yz(add_cores(last_pair))
+    last = jnp.concatenate([last, tall_sum[96:120], wide], axis=1)
+    last = sum_x(last.reshape(NX, -1, last.shape[1]))
+    ends = [3 * width, width, 128, width, w_expand.shape[1]]
+    ends = [sum(ends[: i + 1]) for i in range(len(ends))]
+    g_qkv = last[:, : ends[0]]
+    g_attn = last[:, ends[0] : ends[1]]
+    sums = last[:, ends[1] : ends[2]]
+    g_dense = last[:, ends[2] : ends[3]]
+    g_expand = last[:, ends[3] :]
+    g_shrink = tall[:24]
+    loss = jnp.full((8, 128), jnp.sum(tall[24, :3]))
+    loss = (loss + give(loss, "c", 1))[0, 0]
     return (
         settled_low.reshape(hidden_in.shape),
         loss,

time: 609 us -> 550 us (0.903); the launches traced: 598 us -> 547 us
  blocking collectives: 50 us -> 0 us
  local copies, waits for them, and re-layouts: 115 us -> 88.6 us
  other arithmetic: 77.7 us -> 95.9 us
  starting transfers between devices: 64.8 us -> 81.9 us
  waiting for transfers between devices: 166 us -> 151 us
  between operations: 16.7 us -> 27.5 us
    unnamed x1 -> x0, blocking collectives: 30.2 us -> none
    ppermute x14, waiting for transfers between devices: 31.2 us -> 3.88 us  [fetch(): return lax.ppermute(array, axis, [((i + k) % n, i) for i in range(n)])]
    ppermute x11 -> x12, waiting for transfers between devices: 0.03 us -> 21.2 us  [give(): return lax.ppermute(array, axis, [(i, (i + k) % n) for i in range(n)])]
    all_gather x1, waiting for transfers between devices: 40 us -> 60.4 us  [body(): lax.all_gather(jnp.concatenate([fused, tall], axis=1), ('y', 'c', 'z'), a...]
    all_gather x1 -> x0, blocking collectives: 19.8 us -> none  [body(): told = lax.all_gather(told, ('y', 'z'))]
    all_to_all x8, waiting for transfers between devices: 84.8 us -> 65.7 us  [swap(): return lax.all_to_all(array, axes, 0, 0, tiled=True)]
    ppermute x14, starting transfers between devices: 18 us -> 31.5 us  [fetch(): return lax.ppermute(array, axis, [((i + k) % n, i) for i in range(n)])]
    reshape x6 -> x4, local copies, waits for them, and re-layouts: 15.8 us -> 2.58 us  [the longest x1 1.46 us: body(): stats[:, 6:].reshape(NY * NZ, 6, NY * NZ * rows - width)]
  transfers between devices with their start and end apart: 35 -> 35, of which waited for: 15 -> 15; matrix products, arithmetic and copies ran while one was open for 31% -> 36% of each run, Pallas kernels for 0% -> 0%
where the time goes in v3:
time: 550 us; the launch traced here: 547 us
  waiting for transfers between devices  151 us (27%)
  matrix products  102 us (19%)
  other arithmetic  95.9 us (17%)
  local copies, waits for them, and re-layouts  88.6 us (16%)
  starting transfers between devices  81.9 us (15%)
  between operations  27.5 us (5%)
    all_to_all x8, waiting for transfers between devices, swap(): return lax.all_to_all(array, axes, 0, 0, tiled=True)  65.7 us
    all_gather x1, waiting for transfers between devices, body(): lax.all_gather(jnp.concatenate([fused, tall], axis=1), ('y', 'c', 'z'), a...  60.4 us
    all_to_all x8, starting transfers between devices, swap(): return lax.all_to_all(array, axes, 0, 0, tiled=True)  41 us
    dot_general x8, matrix products, matmul(): return jnp.dot(left, right, preferred_element_type=F32)  37.2 us
    ppermute x14, starting transfers between devices, fetch(): return lax.ppermute(array, axis, [((i + k) % n, i) for i in range(n)])  31.5 us
    dot_general x5, matrix products, matmul_nt(): lax.dot_general(left, right, (((1,), (1,)), ((), ())), preferred_element_...  28.7 us
    unnamed x227, local copies, waits for them, and re-layouts  24 us
    dot_general x7, matrix products, matmul_tn(): lax.dot_general(left, right, (((0,), (0,)), ((), ())), preferred_element_...  22 us
  transfers between devices with their start and end apart: 35, of which 15 were waited for; matrix products, arithmetic and copies ran while one was open for 36% of the time, Pallas kernels for 0%

profile of v3, /device:TPU:0, one launch (start us, length us, event | category | flops | bytes accessed | tf_op | source)
XLA Modules:
  0.0 546.8 jit_solution(2927117956531332285)
XLA Ops:
  7.2 2.9 collective-permute-start.3
  10.2 2.3 collective-permute-start.4
  27.4 3.3 collective-permute-start.10
  39.6 60.4 %all-gather.2.cloned.1.call-done = bf16[768,10112]{1,0:T(8,128)(2,1)} async-done(((bf16[24,10112]{1,0:T(8,128)(2,1)}), bf16[768,10112]{1,0:T(8,128)(2,1)}) %all-gather.2.cloned.1.call-update) | async-done | bytes 15532048 | tf_op jit(solution)/shard_map/all_gather | solution.py:189
  102.0 3.1 collective-permute-start.7
  106.2 12.5 %collective-permute-start.8 = (bf16[400,768]{1,0:T(8,128)(2,1)}, bf16[400,768]{1,0:T(8,128)(2,1)}, u32[]{:S(2)}, u32[]{:S(2)}) collective-permute-start(bf16[400,768]{1,0:T(8,128)(2,1)} %bitcast.46), channel_id=1, source_target_pairs={{3,0},{0,1},{1,2},{2,3},{7,4},{4,5},{5,6},{6,7},{11,8},{8,9},{9,10... | collective-permute-start | bytes 1843208 | tf_op jit(solution)/shard_map/ppermute | solution.py:22
  118.7 4.2 fusion.117
  123.7 2.8 slice_reduce_fusion.2
  126.6 4.1 convolution_bitcast_fusion
  130.7 2.1 copy-done.14
  133.1 3.3 fusion.31
  136.4 2.2 reshape.513
  146.4 2.4 fusion.123
  150.0 8.2 %multiply_convert_fusion.1 = (bf16[512,3072]{1,0:T(8,128)(2,1)S(1)}, f32[512,3072]{1,0:T(8,128)}) fusion(f32[3072]{0:T(1024)S(1)} %copy-done.69, bf16[768,10112]{1,0:T(8,128)(2,1)} %all-gather.2.cloned.1.call-done, f32[512,768]{1,0:T(8,128)S(1)} %get-tuple-element.152, f32[768]{0:T(1024)S(1)} %copy-done.77, f32[768]{0:T(1024)S(1)} %copy-done.64, ...), kind=kOutput, calls=%fused_computation.26 | convolution fusion | flops 2427322368 | bytes 15751168 | tf_op jit(solution)/shard_map/dot_general | solution.py:126
  158.3 2.8 fusion.124
  164.2 2.4 fusion.116
  171.8 2.1 copy-done.45
  175.2 5.1 all-to-all-start
  180.4 7.9 %fusion.28 = bf16[1024,768]{1,0:T(8,128)(2,1)S(1)} fusion(bf16[3200,768]{1,0:T(8,128)(2,1)} %bitcast.266, s32[3200]{0:T(1024)S(1)} %add.479, s32[1024]{0:T(1024)S(1)} %copy-done.43), kind=kOutput, calls=%fused_computation.61 | convolution fusion | flops 5037228032 | bytes 6504960 | tf_op jit(solution)/shard_map/dot_general | solution.py:126
  189.8 15.8 %all-to-all-done = bf16[16,64,768]{2,1,0:T(8,128)(2,1)S(1)} async-done(((bf16[16,64,768]{2,1,0:T(8,128)(2,1)}), bf16[16,64,768]{2,1,0:T(8,128)(2,1)S(1)}, u32[]{:S(2)}, u32[]{:S(2)}) %all-to-all-start) | async-done | bytes 1572896 | tf_op jit(solution)/shard_map/all_to_all | solution.py:42
  206.8 3.7 all-to-all-start.1
  210.5 8.4 %add_reduce_fusion = (f32[1024]{0:T(1024)S(1)}, f32[1024,3200]{1,0:T(8,128)S(1)}) fusion(f32[3200]{0:T(1024)S(1)} %copy-done.37, bf16[1024,768]{1,0:T(8,128)(2,1)} %bitcast.254, bf16[3200,768]{1,0:T(8,128)(2,1)} %bitcast.267), kind=kOutput, calls=%fused_computation.12 | convolution fusion | flops 5039717376 | bytes 19612160 | tf_op jit(solution)/shard_map/dot_general | solution.py:134
  219.0 6.7 %fusion.4 = (bf16[1024,3200]{1,0:T(8,128)(2,1)}, f32[1024]{0:T(1024)S(1)}) fusion(f32[1024,3200]{1,0:T(8,128)S(1)} %get-tuple-element.159, f32[1024]{0:T(1024)S(1)} %get-tuple-element.158, f32[3200]{0:T(1024)S(1)} %copy-done.37, s32[3200]{0:T(1024)S(1)} %add.479, s32[1024]{0:T(1024)S(1)} %copy-done.43), kind=kLoop, calls=%fused_computation.7 | loop fusion | flops 19659776 | bytes 19698688 | tf_op jit(solution)/shard_map/convert_element_type | solution.py:314
  225.8 10.6 %all-to-all-done.1 = bf16[16,64,896]{2,1,0:T(8,128)(2,1)S(1)} async-done(((bf16[16,64,896]{2,1,0:T(8,128)(2,1)}), bf16[16,64,896]{2,1,0:T(8,128)(2,1)S(1)}, u32[]{:S(2)}, u32[]{:S(2)}) %all-to-all-start.1) | async-done | bytes 1835040 | tf_op jit(solution)/shard_map/all_to_all | solution.py:42
  237.9 9.0 %convolution_convert_fusion.4 = bf16[1024,768]{1,0:T(8,128)(2,1)S(1)} fusion(bf16[1024,3200]{1,0:T(8,128)(2,1)} %get-tuple-element.43, bf16[3200,768]{1,0:T(8,128)(2,1)} %bitcast.268), kind=kOutput, calls=%fused_computation.62 | convolution fusion | flops 5033951232 | bytes 13041664 | tf_op jit(solution)/shard_map/dot_general | solution.py:126
  248.3 4.0 all-to-all-start.2
  258.1 17.4 %all-to-all-done.2 = bf16[16,72,768]{2,1,0:T(8,128)(2,1)S(1)} async-done(((bf16[16,72,768]{2,1,0:T(8,128)(2,1)}), bf16[16,72,768]{2,1,0:T(8,128)(2,1)S(1)}, u32[]{:S(2)}, u32[]{:S(2)}) %all-to-all-start.2) | async-done | bytes 1769504 | tf_op jit(solution)/shard_map/all_to_all | solution.py:42
  296.8 3.7 multiply_reduce_fusion.2
  300.6 2.1 convert_reduce_fusion.4
  302.9 3.0 convolution_convert_fusion.3
  306.3 4.7 fusion.129
  312.9 3.4 convolution_convert_fusion.1
  320.7 6.5 %multiply_reduce_fusion.3 = (bf16[768]{0:T(1024)(128)(2,1)S(1)}, f32[512]{0:T(512)S(1)}, f32[512]{0:T(512)S(1)}, bf16[768]{0:T(1024)(128)(2,1)S(1)}, f32[512,768]{1,0:T(8,128)}) fusion(f32[512,768]{1,0:T(8,128)S(1)} %copy-done.8, f32[512]{0:T(512)S(1)} %copy-done.72, f32[512]{0:T(512)S(1)} %copy-done.63, f32[768]{0:T(1024)S(1)} %copy-done.65, ...), kind=kOutput, calls=%fused_computation.70 | convolution fusion | flops 2419848704 | bytes 12597248 | tf_op jit(solution)/shard_map/dot_general | solution.py:134
  333.7 3.5 fusion.114
  337.3 11.7 %convert_reduce_fusion = (f32[3200]{0:T(1024)}, bf16[1024,3200]{1,0:T(8,128)(2,1)}) fusion(f32[1024]{0:T(1024)S(1)} %broadcast_multiply_fusion, s32[3200]{0:T(1024)S(1)} %add.479, s32[1024]{0:T(1024)S(1)} %copy-done.44, f32[1024]{0:T(1024)S(1)} %copy-done.49, f32[1024,3200]{1,0:T(8,128)} %copy-done, f32[3200]{0:T(1024)S(1)} %copy-done.38, f32[1024]{0:T(1024)S(1)} %copy-done.68), kind=kLoop, calls=%fused_computation.10 | loop fusion | flops 29488000 | bytes 19715584 | tf_op jit(solution)/shard_map/reduce_sum | solution.py:122
  349.0 4.0 fusion.17
  353.1 3.1 convolution_convert_fusion.7
  358.7 5.1 fusion.128
  363.9 4.4 multiply_reduce_fusion
  368.3 3.4 add_convert_fusion
  371.7 4.1 all-to-all-start.4
  380.9 6.1 %multiply_convert_fusion = bf16[2,12,256,256]{2,3,1,0:T(8,128)(2,1)S(1)} fusion(f32[2,12,256,256]{2,3,1,0:T(8,128)} %get-tuple-element.163, f32[2,12,256]{2,1,0:T(8,128)S(1)} %copy-done.57, f32[2,12,256,256]{2,3,1,0:T(8,128)} %copy-done.9, f32[2,12,256]{2,1,0:T(8,128)S(1)} %copy-done.56), kind=kLoop, calls=%fused_computation.24 | loop fusion | flops 6291456 | bytes 15777792 | tf_op jit(solution)/shard_map/convert_element_type | solution.py:388
  392.6 3.4 concatenate.73
  402.2 2.0 convolution_convert_fusion.2
  407.4 11.1 %all-to-all-done.4 = bf16[16,128,768]{2,1,0:T(8,128)(2,1)S(1)} async-done(((bf16[16,128,768]{2,1,0:T(8,128)(2,1)}), bf16[16,128,768]{2,1,0:T(8,128)(2,1)S(1)}, u32[]{:S(2)}, u32[]{:S(2)}) %all-to-all-start.4) | async-done | bytes 3145760 | tf_op jit(solution)/shard_map/all_to_all | solution.py:42
  418.5 11.1 %all-to-all-start.3 = ((bf16[16,24,3072]{2,1,0:T(8,128)(2,1)}), bf16[16,24,3072]{2,1,0:T(8,128)(2,1)}, u32[]{:S(2)}, u32[]{:S(2)}) async-start(bf16[16,24,3072]{2,1,0:T(8,128)(2,1)} %fusion.17), calls=%async_computation.3 | async-start | bytes 4718592 | tf_op jit(solution)/shard_map/all_to_all | solution.py:42
  429.6 8.7 %convolution_convert_fusion = bf16[3200,768]{1,0:T(8,128)(2,1)S(1)} fusion(bf16[1024,3200]{1,0:T(8,128)(2,1)} %get-tuple-element.89, bf16[1024,768]{1,0:T(8,128)(2,1)} %bitcast.255), kind=kOutput, calls=%fused_computation.15 | convolution fusion | flops 5035622400 | bytes 13041664 | tf_op jit(solution)/shard_map/dot_general | solution.py:130
  438.3 2.6 fusion.118
  441.6 2.6 copy-done.1
  450.2 3.1 slice_reduce_fusion
  454.7 7.2 %all-to-all-done.3 = bf16[16,24,3072]{2,1,0:T(8,128)(2,1)} async-done(((bf16[16,24,3072]{2,1,0:T(8,128)(2,1)}), bf16[16,24,3072]{2,1,0:T(8,128)(2,1)}, u32[]{:S(2)}, u32[]{:S(2)}) %all-to-all-start.3) | async-done | bytes 2359328 | tf_op jit(solution)/shard_map/all_to_all | solution.py:42
  461.9 3.6 all-to-all-start.5
  467.2 2.8 reduce_sum.421
  471.9 3.7 add_convert_fusion.1
  475.5 4.4 all-to-all-start.6
  480.0 3.0 fusion.15
  485.0 2.7 collective-permute-start.21
  491.5 17.7 %collective-permute-done.25 = f32[400]{0:T(512)S(1)} collective-permute-done((f32[400]{0:T(512)S(1)}, f32[400]{0:T(512)S(1)}, u32[]{:S(2)}, u32[]{:S(2)}) %collective-permute-start.25) | collective-permute-done | bytes 1632 | tf_op jit(solution)/shard_map/ppermute | solution.py:27
  509.2 2.8 collective-permute-start.24
  512.0 2.5 collective-permute-done.24
  515.1 2.6 fusion.60
  519.1 2.0 reduce_sum.426
  522.1 4.8 all-to-all-start.7
  526.9 5.9 %fusion.37 = f32[512,768]{1,0:T(8,128)} fusion(f32[512,768]{1,0:T(8,128)S(1)} %copy-done.25, bf16[512,2304]{0,1:T(8,128)(2,1)} %copy-done.39, bf16[768,10112]{1,0:T(8,128)(2,1)} %all-gather.2.cloned.1.call-done), kind=kOutput, calls=%fused_computation.91 | convolution fusion | flops 1812332544 | bytes 9043968 | tf_op jit(solution)/shard_map/dot_general | solution.py:134
  (441 shorter events, 130.3 us)
Async XLA Ops:
  7.2 92.8 %all-gather.2.cloned.1.call-start = ((), (), s32[]{:S(2)}) async-start(), calls=%async_computation.8 | async-start | bytes 16017408 | tf_op jit(solution)/shard_map/all_gather | solution.py:189
  7.2 14.1 %collective-permute-start.3 = (bf16[24,768]{1,0:T(8,128)(2,1)}, bf16[24,768]{1,0:T(8,128)(2,1)S(1)}, u32[]{:S(2)}, u32[]{:S(2)}) collective-permute-start(bf16[24,768]{1,0:T(8,128)(2,1)} %param.40), channel_id=1, source_target_pairs={{1,0},{2,1},{3,2},{0,3},{5,4},{6,5},{7,6},{4,7},{9,8},{10,9},{11,1... | collective-permute-start | bytes 110600 | tf_op jit(solution)/shard_map/ppermute | solution.py:22
  10.1 13.2 %collective-permute-start.5 = (bf16[24,768]{1,0:T(8,128)(2,1)}, bf16[24,768]{1,0:T(8,128)(2,1)S(1)}, u32[]{:S(2)}, u32[]{:S(2)}) collective-permute-start(bf16[24,768]{1,0:T(8,128)(2,1)} %param.40), channel_id=1, source_target_pairs={{3,0},{0,1},{1,2},{2,3},{7,4},{4,5},{5,6},{6,7},{11,8},{8,9},{9,10... | collective-permute-start | bytes 110600 | tf_op jit(solution)/shard_map/ppermute | solution.py:22
  10.2 13.1 %collective-permute-start.4 = (bf16[24,768]{1,0:T(8,128)(2,1)}, bf16[24,768]{1,0:T(8,128)(2,1)S(1)}, u32[]{:S(2)}, u32[]{:S(2)}) collective-permute-start(bf16[24,768]{1,0:T(8,128)(2,1)} %param.40), channel_id=1, source_target_pairs={{2,0},{3,1},{0,2},{1,3},{6,4},{7,5},{4,6},{5,7},{10,8},{11,9},{8,1... | collective-permute-start | bytes 110600 | tf_op jit(solution)/shard_map/ppermute | solution.py:22
  16.4 11.0 %copy-start.83 = (bf16[400]{0:T(512)(128)(2,1)S(1)}, bf16[400]{0:T(512)(128)(2,1)}, u32[]{:S(2)}) copy-start(bf16[400]{0:T(512)(128)(2,1)} %param.49) | copy-start | bytes 2404
  17.9 14.4 %copy-start.82 = (s32[2,1,16,2]{2,3,1,0:T(2,128)S(1)}, s32[2,1,16,2]{2,3,1,0:T(2,128)}, u32[]{:S(2)}) copy-start(s32[2,1,16,2]{2,3,1,0:T(2,128)} %param.28) | copy-start | bytes 772
  17.9 8.3 %collective-permute-start.2 = (bf16[6,7040]{1,0:T(8,128)(2,1)S(1)}, bf16[6,7040]{1,0:T(8,128)(2,1)S(1)}, u32[]{:S(2)}, u32[]{:S(2)}) collective-permute-start(bf16[6,7040]{1,0:T(8,128)(2,1)S(1)} %constant_dynamic-update-slice_fusion), channel_id=1, source_target_pairs={{3,0},{0,1},{1,2},{2,3},{7,4},{4,5},{5,6},{6,7},{11,8},{8,9},{9,10... | collective-permute-start | bytes 253448 | tf_op jit(solution)/shard_map/ppermute | solution.py:22
  19.7 6.5 %collective-permute-start.1 = (bf16[6,7040]{1,0:T(8,128)(2,1)S(1)}, bf16[6,7040]{1,0:T(8,128)(2,1)S(1)}, u32[]{:S(2)}, u32[]{:S(2)}) collective-permute-start(bf16[6,7040]{1,0:T(8,128)(2,1)S(1)} %constant_dynamic-update-slice_fusion), channel_id=1, source_target_pairs={{2,0},{3,1},{0,2},{1,3},{6,4},{7,5},{4,6},{5,7},{10,8},{11,9},{8,1... | collective-permute-start | bytes 253448 | tf_op jit(solution)/shard_map/ppermute | solution.py:22
  20.5 12.2 %copy-start.74 = (s32[2,256]{1,0:T(2,128)S(1)}, s32[2,256]{1,0:T(2,128)}, u32[]{:S(2)}) copy-start(s32[2,256]{1,0:T(2,128)} %param.27) | copy-start | bytes 6148
  21.3 12.7 %copy-start.40 = (s32[2,128,16,2]{1,3,2,0:T(2,128)S(1)}, s32[2,128,16,2]{1,3,2,0:T(2,128)}, u32[]{:S(2)}) copy-start(s32[2,128,16,2]{1,3,2,0:T(2,128)} %param.29) | copy-start | bytes 98308
  21.3 4.8 collective-permute-start
  27.4 7.1 %collective-permute-start.10 = (bf16[400]{0:T(512)(128)(2,1)S(1)}, bf16[400]{0:T(512)(128)(2,1)S(1)}, u32[]{:S(2)}, u32[]{:S(2)}) collective-permute-start(bf16[400]{0:T(512)(128)(2,1)S(1)} %copy-done.83), channel_id=1, source_target_pairs={{1,0},{2,1},{3,2},{0,3},{5,4},{6,5},{7,6},{4,7},{9,8},{10,9},{11,1... | collective-permute-start | bytes 2408 | tf_op jit(solution)/shard_map/ppermute | solution.py:22
  30.7 4.8 collective-permute-start.12
  30.7 5.1 collective-permute-start.11
  35.8 1.2 collective-permute-start.13
  36.4 63.5 %copy-start.42 = (s32[1024]{0:T(1024)}, s32[1024]{0:T(1024)S(1)}, u32[]{:S(2)}) copy-start(s32[1024]{0:T(1024)S(1)} %reshape.519) | copy-start | bytes 12292
  37.1 62.8 %copy-start.36 = (f32[3200]{0:T(1024)}, f32[3200]{0:T(1024)S(1)}, u32[]{:S(2)}) copy-start(f32[3200]{0:T(1024)S(1)} %reshape.554) | copy-start | bytes 38404
  102.0 59.4 %collective-permute-start.7 = (bf16[400,768]{1,0:T(8,128)(2,1)}, bf16[400,768]{1,0:T(8,128)(2,1)}, u32[]{:S(2)}, u32[]{:S(2)}) collective-permute-start(bf16[400,768]{1,0:T(8,128)(2,1)} %bitcast.46), channel_id=1, source_target_pairs={{2,0},{3,1},{0,2},{1,3},{6,4},{7,5},{4,6},{5,7},{10,8},{11,9},{8,1... | collective-permute-start | bytes 1843208 | tf_op jit(solution)/shard_map/ppermute | solution.py:22
  105.0 56.4 %collective-permute-start.6 = (bf16[400,768]{1,0:T(8,128)(2,1)}, bf16[400,768]{1,0:T(8,128)(2,1)}, u32[]{:S(2)}, u32[]{:S(2)}) collective-permute-start(bf16[400,768]{1,0:T(8,128)(2,1)} %bitcast.46), channel_id=1, source_target_pairs={{1,0},{2,1},{3,2},{0,3},{5,4},{6,5},{7,6},{4,7},{9,8},{10,9},{11,1... | collective-permute-start | bytes 1843208 | tf_op jit(solution)/shard_map/ppermute | solution.py:22
  106.2 55.2 %collective-permute-start.8 = (bf16[400,768]{1,0:T(8,128)(2,1)}, bf16[400,768]{1,0:T(8,128)(2,1)}, u32[]{:S(2)}, u32[]{:S(2)}) collective-permute-start(bf16[400,768]{1,0:T(8,128)(2,1)} %bitcast.46), channel_id=1, source_target_pairs={{3,0},{0,1},{1,2},{2,3},{7,4},{4,5},{5,6},{6,7},{11,8},{8,9},{9,10... | collective-permute-start | bytes 1843208 | tf_op jit(solution)/shard_map/ppermute | solution.py:22
  133.1 6.7 %copy-start.5 = (bf16[2,256,12,64]{1,0,3,2:T(2,128)(2,1)}, bf16[2,256,12,64]{1,0,3,2:T(2,128)(2,1)S(1)}, u32[]{:S(2)}) copy-start(bf16[2,256,12,64]{1,0,3,2:T(2,128)(2,1)S(1)} %reshape.514) | copy-start | bytes 2359300
  148.8 9.4 %copy-start.7 = (f32[512,768]{1,0:T(8,128)}, f32[512,768]{1,0:T(8,128)S(1)}, u32[]{:S(2)}) copy-start(f32[512,768]{1,0:T(8,128)S(1)} %get-tuple-element.152) | copy-start | bytes 4718596
  148.8 9.4 %copy-start.62 = (f32[512]{0:T(512)}, f32[512]{0:T(512)S(1)}, u32[]{:S(2)}) copy-start(f32[512]{0:T(512)S(1)} %broadcast_multiply_fusion.6) | copy-start | bytes 6148
  149.2 9.1 %copy-start.71 = (f32[512]{0:T(512)}, f32[512]{0:T(512)S(1)}, u32[]{:S(2)}) copy-start(f32[512]{0:T(512)S(1)} %add_rsqrt_fusion.1) | copy-start | bytes 6148
  149.9 8.4 %copy-start.13 = (bf16[32,4,24,768]{3,2,1,0:T(8,128)(2,1)}, bf16[32,4,24,768]{3,2,1,0:T(8,128)(2,1)S(1)}, u32[]{:S(2)}) copy-start(bf16[32,4,24,768]{3,2,1,0:T(8,128)(2,1)S(1)} %pad_maximum_fusion) | copy-start | bytes 14155780
  150.0 8.3 %copy-start.80 = (f32[768]{0:T(1024)S(1)}, f32[768]{0:T(1024)}, u32[]{:S(2)}) copy-start(f32[768]{0:T(1024)} %get-tuple-element.67) | copy-start | bytes 9220
  163.4 8.1 %collective-permute-start.9 = (bf16[4,400,768]{2,1,0:T(8,128)(2,1)S(1)}, bf16[4,400,768]{2,1,0:T(8,128)(2,1)S(1)}, u32[]{:S(2)}, u32[]{:S(2)}) collective-permute-start(bf16[4,400,768]{2,1,0:T(8,128)(2,1)S(1)} %pad_maximum_fusion.2), channel_id=1, source_target_pairs={{16,0},{0,16},{17,1},{1,17},{18,2},{2,18},{19,3},{3,19},{20,4},{4,... | collective-permute-start | bytes 7372808 | tf_op jit(solution)/shard_map/ppermute | solution.py:22
  163.9 6.5 %copy-start.19 = (bf16[512,768]{1,0:T(8,128)(2,1)}, bf16[512,768]{1,0:T(8,128)(2,1)S(1)}, u32[]{:S(2)}) copy-start(bf16[512,768]{1,0:T(8,128)(2,1)S(1)} %add_convert_fusion.2) | copy-start | bytes 2359300
  164.2 7.4 %copy-start.34 = (bf16[64,768]{1,0:T(8,128)(2,1)}, bf16[64,768]{1,0:T(8,128)(2,1)S(1)}, u32[]{:S(2)}) copy-start(bf16[64,768]{1,0:T(8,128)(2,1)S(1)} %convolution_convert_fusion.9) | copy-start | bytes 294916
  167.0 6.9 %copy-start.27 = (bf16[64,768]{1,0:T(8,128)(2,1)}, bf16[64,768]{1,0:T(8,128)(2,1)S(1)}, u32[]{:S(2)}) copy-start(bf16[64,768]{1,0:T(8,128)(2,1)S(1)} %add_convert_fusion.3) | copy-start | bytes 294916
  175.2 30.4 %all-to-all-start = ((bf16[16,64,768]{2,1,0:T(8,128)(2,1)}), bf16[16,64,768]{2,1,0:T(8,128)(2,1)S(1)}, u32[]{:S(2)}, u32[]{:S(2)}) async-start(bf16[16,64,768]{2,1,0:T(8,128)(2,1)} %broadcast_in_dim.74), calls=%async_computation | async-start | bytes 3145728 | tf_op jit(solution)/shard_map/all_to_all | solution.py:42
  180.4 7.9 %copy-start.26 = (bf16[1024,128]{1,0:T(8,128)(2,1)S(1)}, bf16[1024,128]{1,0:T(8,128)(2,1)}, u32[]{:S(2)}) copy-start(bf16[1024,128]{1,0:T(8,128)(2,1)} %pad.24.clone) | copy-start | bytes 786436
  188.3 22.1 %copy-start.37 = (f32[3200]{0:T(1024)S(1)}, f32[3200]{0:T(1024)}, u32[]{:S(2)}) copy-start(f32[3200]{0:T(1024)} %copy-done.36) | copy-start | bytes 38404
  206.8 29.6 %all-to-all-start.1 = ((bf16[16,64,896]{2,1,0:T(8,128)(2,1)}), bf16[16,64,896]{2,1,0:T(8,128)(2,1)S(1)}, u32[]{:S(2)}, u32[]{:S(2)}) async-start(bf16[16,64,896]{2,1,0:T(8,128)(2,1)} %pad_maximum_fusion.5), calls=%async_computation.1 | async-start | bytes 3670016 | tf_op jit(solution)/shard_map/all_to_all | solution.py:42
  218.9 6.7 %copy-start = (f32[1024,3200]{1,0:T(8,128)}, f32[1024,3200]{1,0:T(8,128)S(1)}, u32[]{:S(2)}) copy-start(f32[1024,3200]{1,0:T(8,128)S(1)} %get-tuple-element.159) | copy-start | bytes 39321604
  218.9 6.7 %copy-start.48 = (f32[1024]{0:T(1024)}, f32[1024]{0:T(1024)S(1)}, u32[]{:S(2)}) copy-start(f32[1024]{0:T(1024)S(1)} %get-tuple-element.158) | copy-start | bytes 12292
  248.3 43.3 %copy-start.21 = (f32[64,768]{1,0:T(8,128)S(1)}, f32[64,768]{1,0:T(8,128)}, u32[]{:S(2)}) copy-start(f32[64,768]{1,0:T(8,128)} %copy-done.20) | copy-start | bytes 589828
  248.3 27.2 %all-to-all-start.2 = ((bf16[16,72,768]{2,1,0:T(8,128)(2,1)}), bf16[16,72,768]{2,1,0:T(8,128)(2,1)S(1)}, u32[]{:S(2)}, u32[]{:S(2)}) async-start(bf16[16,72,768]{2,1,0:T(8,128)(2,1)} %pad_maximum_fusion.6), calls=%async_computation.2 | async-start | bytes 3538944 | tf_op jit(solution)/shard_map/all_to_all | solution.py:42
  318.0 31.0 %collective-permute-start.16 = (bf16[16,24,3072]{2,1,0:T(8,128)(2,1)}, bf16[16,24,3072]{2,1,0:T(8,128)(2,1)}, u32[]{:S(2)}, u32[]{:S(2)}) collective-permute-start(bf16[16,24,3072]{2,1,0:T(8,128)(2,1)} %bitcast.83), channel_id=1, source_target_pairs={{0,16},{16,0},{1,17},{17,1},{2,18},{18,2},{3,19},{19,3},{4,20},{20... | collective-permute-start | bytes 7077896 | tf_op jit(solution)/shard_map/ppermute | solution.py:27
  320.0 13.7 %copy-start.59 = (f32[1024]{0:T(1024)S(1)}, f32[1024]{0:T(1024)}, u32[]{:S(2)}) copy-start(f32[1024]{0:T(1024)} %copy-done.58) | copy-start | bytes 12292
  320.0 32.9 %collective-permute-start.14 = (bf16[16,128,768]{2,1,0:T(8,128)(2,1)}, bf16[16,128,768]{2,1,0:T(8,128)(2,1)}, u32[]{:S(2)}, u32[]{:S(2)}) collective-permute-start(bf16[16,128,768]{2,1,0:T(8,128)(2,1)} %pad_maximum_fusion.1), channel_id=1, source_target_pairs={{0,16},{16,0},{1,17},{17,1},{2,18},{18,2},{3,19},{19,3},{4,20},{20... | collective-permute-start | bytes 9437192 | tf_op jit(solution)/shard_map/ppermute | solution.py:27
  330.3 6.9 %copy-start.38 = (f32[3200]{0:T(1024)S(1)}, f32[3200]{0:T(1024)}, u32[]{:S(2)}) copy-start(f32[3200]{0:T(1024)} %copy-done.36) | copy-start | bytes 38404
  330.3 6.9 %copy-start.44 = (s32[1024]{0:T(1024)S(1)}, s32[1024]{0:T(1024)}, u32[]{:S(2)}) copy-start(s32[1024]{0:T(1024)} %copy-done.42) | copy-start | bytes 12292
  330.3 6.9 %copy-start.49 = (f32[1024]{0:T(1024)S(1)}, f32[1024]{0:T(1024)}, u32[]{:S(2)}) copy-start(f32[1024]{0:T(1024)} %copy-done.48) | copy-start | bytes 12292
  330.3 6.9 %copy-start.68 = (f32[1024]{0:T(1024)S(1)}, f32[1024]{0:T(1024)}, u32[]{:S(2)}) copy-start(f32[1024]{0:T(1024)} %get-tuple-element.90) | copy-start | bytes 12292
  337.2 15.9 %copy-start.15 = (bf16[512,768]{1,0:T(8,128)(2,1)}, bf16[512,768]{1,0:T(8,128)(2,1)S(1)}, u32[]{:S(2)}) copy-start(bf16[512,768]{1,0:T(8,128)(2,1)S(1)} %get-tuple-element.46) | copy-start | bytes 2359300
  353.1 10.7 %slice-start = ((s8[6291456]{0:T(1024)(128)(4,1)}), s8[2097152]{0:T(1024)(128)(4,1)S(1)}, s32[]{:S(2)}) async-start(s8[6291456]{0:T(1024)(128)(4,1)} %bitcast.226), calls=%async_computation.9 | async-start | bytes 4194304
  371.7 46.8 %all-to-all-start.4 = ((bf16[16,128,768]{2,1,0:T(8,128)(2,1)}), bf16[16,128,768]{2,1,0:T(8,128)(2,1)S(1)}, u32[]{:S(2)}, u32[]{:S(2)}) async-start(bf16[16,128,768]{2,1,0:T(8,128)(2,1)} %add_convert_fusion), calls=%async_computation.4 | async-start | bytes 6291456 | tf_op jit(solution)/shard_map/all_to_all | solution.py:42
  407.3 64.5 %collective-permute-start.15 = (bf16[16,24,3200]{2,1,0:T(8,128)(2,1)}, bf16[16,24,3200]{2,1,0:T(8,128)(2,1)}, u32[]{:S(2)}, u32[]{:S(2)}) collective-permute-start(bf16[16,24,3200]{2,1,0:T(8,128)(2,1)} %pad_maximum_fusion.4), channel_id=1, source_target_pairs={{0,16},{16,0},{1,17},{17,1},{2,18},{18,2},{3,19},{19,3},{4,20},{20... | collective-permute-start | bytes 7372808 | tf_op jit(solution)/shard_map/ppermute | solution.py:27
  418.5 43.4 %all-to-all-start.3 = ((bf16[16,24,3072]{2,1,0:T(8,128)(2,1)}), bf16[16,24,3072]{2,1,0:T(8,128)(2,1)}, u32[]{:S(2)}, u32[]{:S(2)}) async-start(bf16[16,24,3072]{2,1,0:T(8,128)(2,1)} %fusion.17), calls=%async_computation.3 | async-start | bytes 4718592 | tf_op jit(solution)/shard_map/all_to_all | solution.py:42
  440.9 39.1 %collective-permute-start.18 = (bf16[4,400,768]{2,1,0:T(8,128)(2,1)}, bf16[4,400,768]{2,1,0:T(8,128)(2,1)}, u32[]{:S(2)}, u32[]{:S(2)}) collective-permute-start(bf16[4,400,768]{2,1,0:T(8,128)(2,1)} %bitcast.93), channel_id=1, source_target_pairs={{0,16},{16,0},{1,17},{17,1},{2,18},{18,2},{3,19},{19,3},{4,20},{20... | collective-permute-start | bytes 7372808 | tf_op jit(solution)/shard_map/ppermute | solution.py:27
  450.2 15.3 %copy-start.23 = (bf16[4,1,4,24,768]{4,3,2,1,0:T(8,128)(2,1)S(1)}, bf16[4,1,4,24,768]{4,3,2,1,0:T(8,128)(2,1)}, u32[]{:S(2)}) copy-start(bf16[4,1,4,24,768]{4,3,2,1,0:T(8,128)(2,1)} %get-tuple-element.126) | copy-start | bytes 1769476
  461.9 9.9 %all-to-all-start.5 = ((bf16[4,32,768]{2,1,0:T(8,128)(2,1)}), bf16[4,32,768]{2,1,0:T(8,128)(2,1)S(1)}, u32[]{:S(2)}, u32[]{:S(2)}) async-start(bf16[4,32,768]{2,1,0:T(8,128)(2,1)} %pad_maximum_fusion.9), calls=%async_computation.5 | async-start | bytes 393216 | tf_op jit(solution)/shard_map/all_to_all | solution.py:42
  475.5 43.5 %all-to-all-start.6 = ((bf16[16,24,3200]{2,1,0:T(8,128)(2,1)}), bf16[16,24,3200]{2,1,0:T(8,128)(2,1)}, u32[]{:S(2)}, u32[]{:S(2)}) async-start(bf16[16,24,3200]{2,1,0:T(8,128)(2,1)} %add_convert_fusion.1), calls=%async_computation.6 | async-start | bytes 4915200 | tf_op jit(solution)/shard_map/all_to_all | solution.py:42
  484.4 30.7 %collective-permute-start.19 = (bf16[400,768]{1,0:T(8,128)(2,1)}, bf16[400,768]{1,0:T(8,128)(2,1)S(1)}, u32[]{:S(2)}, u32[]{:S(2)}) collective-permute-start(bf16[400,768]{1,0:T(8,128)(2,1)} %get-tuple-element.120), channel_id=1, source_target_pairs={{0,1},{1,2},{2,3},{3,0},{4,5},{5,6},{6,7},{7,4},{8,9},{9,10},{10,1... | collective-permute-start | bytes 1843208 | tf_op jit(solution)/shard_map/ppermute | solution.py:27
  485.0 30.1 %collective-permute-start.21 = (bf16[400,768]{1,0:T(8,128)(2,1)}, bf16[400,768]{1,0:T(8,128)(2,1)}, u32[]{:S(2)}, u32[]{:S(2)}) collective-permute-start(bf16[400,768]{1,0:T(8,128)(2,1)} %get-tuple-element.121), channel_id=1, source_target_pairs={{0,3},{1,0},{2,1},{3,2},{4,7},{5,4},{6,5},{7,6},{8,11},{9,8},{10,9... | collective-permute-start | bytes 1843208 | tf_op jit(solution)/shard_map/ppermute | solution.py:27
  487.6 27.4 %collective-permute-start.20 = (bf16[400,768]{1,0:T(8,128)(2,1)}, bf16[400,768]{1,0:T(8,128)(2,1)}, u32[]{:S(2)}, u32[]{:S(2)}) collective-permute-start(bf16[400,768]{1,0:T(8,128)(2,1)} %get-tuple-element.122), channel_id=1, source_target_pairs={{0,2},{1,3},{2,0},{3,1},{4,6},{5,7},{6,4},{7,5},{8,10},{9,11},{10,... | collective-permute-start | bytes 1843208 | tf_op jit(solution)/shard_map/ppermute | solution.py:27
  488.2 1.2 collective-permute-start.22
  489.4 19.8 %collective-permute-start.25 = (f32[400]{0:T(512)S(1)}, f32[400]{0:T(512)S(1)}, u32[]{:S(2)}, u32[]{:S(2)}) collective-permute-start(f32[400]{0:T(512)S(1)} %bitcast.275), channel_id=1, source_target_pairs={{0,3},{1,0},{2,1},{3,2},{4,7},{5,4},{6,5},{7,6},{8,11},{9,8},{10,9... | collective-permute-start | bytes 4808 | tf_op jit(solution)/shard_map/ppermute | solution.py:27
  491.1 20.9 %collective-permute-start.23 = (f32[400]{0:T(512)S(1)}, f32[400]{0:T(512)S(1)}, u32[]{:S(2)}, u32[]{:S(2)}) collective-permute-start(f32[400]{0:T(512)S(1)} %bitcast.274), channel_id=1, source_target_pairs={{0,1},{1,2},{2,3},{3,0},{4,5},{5,6},{6,7},{7,4},{8,9},{9,10},{10,1... | collective-permute-start | bytes 4808 | tf_op jit(solution)/shard_map/ppermute | solution.py:27
  509.2 5.3 collective-permute-start.24
  517.7 9.2 %copy-start.25 = (f32[512,768]{1,0:T(8,128)S(1)}, f32[512,768]{1,0:T(8,128)}, u32[]{:S(2)}) copy-start(f32[512,768]{1,0:T(8,128)} %get-tuple-element.98) | copy-start | bytes 4718596
  519.0 14.5 %collective-permute-start.17 = (f32[8,128]{1,0:T(8,128)S(1)}, f32[8,128]{1,0:T(8,128)S(1)}, u32[]{:S(2)}, u32[]{:S(2)}) collective-permute-start(f32[8,128]{1,0:T(8,128)S(1)} %broadcast_in_dim.128), channel_id=1, source_target_pairs={{0,16},{16,0},{1,17},{17,1},{2,18},{18,2},{3,19},{19,3},{4,20},{20... | collective-permute-start | bytes 12296 | tf_op jit(solution)/shard_map/ppermute | solution.py:27
  522.1 14.1 %all-to-all-start.7 = ((bf16[4,6,7040]{2,1,0:T(8,128)(2,1)}), bf16[4,6,7040]{2,1,0:T(8,128)(2,1)S(1)}, u32[]{:S(2)}, u32[]{:S(2)}) async-start(bf16[4,6,7040]{2,1,0:T(8,128)(2,1)} %reshape.550), calls=%async_computation.7 | async-start | bytes 901120 | tf_op jit(solution)/shard_map/all_to_all | solution.py:42
  (69 other events, 218.4 us)
Sparse Core Ops, SparseCore 0:
  27.5 72.4 all-gather.1

commit v4 on v3

--- a/solution.py
+++ b/solution.py
@@ -1,6 +1,8 @@
 import jax
 import jax.numpy as jnp
 from jax import lax
+from jax.experimental import pallas as pl
+from jax.experimental.pallas import tpu as pltpu
 from jax.sharding import Mesh
 from jax.sharding import PartitionSpec as P
 
@@ -132,6 +134,177 @@
 
 def matmul_nt(left, right):
     return lax.dot_general(left, right, (((1,), (1,)), ((), ())), preferred_element_type=F32)
+
+
+def dot_nn(left, right):
+    return lax.dot_general(left, right, (((1,), (0,)), ((), ())), preferred_element_type=F32)
+
+
+def dot_nt(left, right):
+    return lax.dot_general(left, right, (((1,), (1,)), ((), ())), preferred_element_type=F32)
+
+
+def dot_tn(left, right):
+    return lax.dot_general(left, right, (((0,), (0,)), ((), ())), preferred_element_type=F32)
+
+
+def attention_forward_kernel(
+    x_ref,
+    row_ref,
+    col_ref,
+    wq_ref,
+    wk_ref,
+    wv_ref,
+    wa_ref,
+    vec_ref,
+    qkv_ref,
+    probs_ref,
+    attended_ref,
+    first_ref,
+    low_ref,
+    normed_ref,
+    inverse_ref,
+):
+    tokens, width = x_ref.shape
+    pair = 2 * HEAD_DIM
+    factor = HEAD_DIM ** (-0.5)
+    x = x_ref[...]
+    qkv_ref[:, :width] = (dot_nn(x, wq_ref[...]) + vec_ref[0:1]).astype(BF)
+    qkv_ref[:, width : 2 * width] = dot_nn(x, wk_ref[...]).astype(BF)
+    qkv_ref[:, 2 * width :] = (dot_nn(x, wv_ref[...]) + vec_ref[1:2]).astype(BF)
+    allowed = row_ref[...] == col_ref[...]
+    lower = lax.broadcasted_iota(jnp.int32, (tokens, pair), 1) < HEAD_DIM
+    for h in range(width // pair):
+        lanes = slice(h * pair, (h + 1) * pair)
+        query = qkv_ref[:, lanes]
+        keys = qkv_ref[:, width + h * pair : width + (h + 1) * pair]
+        values = qkv_ref[:, 2 * width + h * pair : 2 * width + (h + 1) * pair]
+        zero = jnp.zeros_like(query)
+        outs = []
+        for side in range(2):
+            mine = jnp.where(lower, query, zero) if side == 0 else jnp.where(lower, zero, query)
+            scores = jnp.where(allowed, dot_nt(mine, keys) * factor, MASKED)
+            expo = jnp.exp(scores - jnp.max(scores, axis=1, keepdims=True))
+            probs = (expo / jnp.sum(expo, axis=1, keepdims=True)).astype(BF)
+            probs_ref[2 * h + side] = probs
+            outs.append(dot_nn(probs, values))
+        attended_ref[:, lanes] = jnp.where(lower, outs[0], outs[1]).astype(BF)
+    branch = dot_nn(attended_ref[...], wa_ref[...]) + vec_ref[2:3]
+    first, normed, inverse = layer_norm(x.astype(F32) + branch, vec_ref[3:4], vec_ref[4:5])
+    first_ref[...] = first
+    low_ref[...] = first.astype(BF)
+    normed_ref[...] = normed
+    inverse_ref[...] = inverse
+
+
+def weight_spec(width, block):
+    return pl.BlockSpec((width, width), lambda m: (0, block))
+
+
+def attention_forward(x, segments, layer, first_block, vec):
+    micro, block = segments.shape
+    tokens, width = x.shape
+    heads = width // HEAD_DIM
+    here = lambda n: pl.BlockSpec((block, n), lambda m: (m, 0))
+    return pl.pallas_call(
+        attention_forward_kernel,
+        grid=(micro,),
+        in_specs=[
+            here(width),
+            pl.BlockSpec((None, 1, block), lambda m: (m, 0, 0)),
+            pl.BlockSpec((None, block, 1), lambda m: (m, 0, 0)),
+            weight_spec(width, first_block),
+            weight_spec(width, first_block + 1),
+            weight_spec(width, first_block + 2),
+            weight_spec(width, first_block + 3),
+            pl.BlockSpec(vec.shape, lambda m: (0, 0)),
+        ],
+        out_specs=[
+            here(3 * width),
+            pl.BlockSpec((None, heads, block, block), lambda m: (m, 0, 0, 0)),
+            here(width),
+            here(width),
+            here(width),
+            here(width),
+            here(1),
+        ],
+        out_shape=[
+            jax.ShapeDtypeStruct((tokens, 3 * width), BF),
+            jax.ShapeDtypeStruct((micro, heads, block, block), BF),
+            jax.ShapeDtypeStruct((tokens, width), BF),
+            jax.ShapeDtypeStruct((tokens, width), F32),
+            jax.ShapeDtypeStruct((tokens, width), BF),
+            jax.ShapeDtypeStruct((tokens, width), F32),
+            jax.ShapeDtypeStruct((tokens, 1), F32),
+        ],
+        compiler_params=pltpu.CompilerParams(vmem_limit_bytes=48 * 1024 * 1024),
+        cost_estimate=pl.CostEstimate(
+            flops=4_000_000_000, bytes_accessed=16_000_000, transcendentals=2_000_000
+        ),
+    )(x, segments[:, None, :], segments[:, :, None], layer, layer, layer, layer, vec)
+
+
+def attention_backward_kernel(dbranch_ref, qkv_ref, probs_ref, wa_ref, out_ref, sum_ref):
+    tokens, width = dbranch_ref.shape
+    pair = 2 * HEAD_DIM
+    factor = HEAD_DIM ** (-0.5)
+    dattended = dot_nt(dbranch_ref[...], wa_ref[...]).astype(BF)
+    lower = lax.broadcasted_iota(jnp.int32, (tokens, pair), 1) < HEAD_DIM
+    for h in range(width // pair):
+        lanes = slice(h * pair, (h + 1) * pair)
+        query = qkv_ref[:, lanes]
+        keys = qkv_ref[:, width + h * pair : width + (h + 1) * pair]
+        values = qkv_ref[:, 2 * width + h * pair : 2 * width + (h + 1) * pair]
+        grad = dattended[:, lanes]
+        zero = jnp.zeros_like(grad)
+        parts = []
+        for side in range(2):
+            mine = jnp.where(lower, grad, zero) if side == 0 else jnp.where(lower, zero, grad)
+            low = probs_ref[2 * h + side]
+            probs = low.astype(F32)
+            dprobs = dot_nt(mine, values)
+            inner = jnp.sum(probs * dprobs, axis=1, keepdims=True)
+            dscores = (probs * (dprobs - inner)).astype(BF)
+            parts.append(
+                (dot_nn(dscores, keys) * factor, dot_tn(dscores, query) * factor, dot_tn(low, grad))
+            )
+        for i in range(3):
+            start = i * width + h * pair
+            out_ref[:, start : start + pair] = jnp.where(lower, parts[0][i], parts[1][i]).astype(BF)
+    seen = jnp.sum(out_ref[...].astype(F32), axis=0, keepdims=True)
+
+    @pl.when(pl.program_id(0) == 0)
+    def _():
+        sum_ref[...] = seen
+
+    @pl.when(pl.program_id(0) > 0)
+    def _():
+        sum_ref[...] += seen
+
+
+def attention_backward(dbranch, qkv, probs, layer, attn_block):
+    micro, heads, block, _ = probs.shape
+    tokens, width = dbranch.shape
+    here = lambda n: pl.BlockSpec((block, n), lambda m: (m, 0))
+    return pl.pallas_call(
+        attention_backward_kernel,
+        grid=(micro,),
+        in_specs=[
+            here(width),
+            here(3 * width),
+            pl.BlockSpec((None, heads, block, block), lambda m: (m, 0, 0, 0)),
+            weight_spec(width, attn_block),
+        ],
+        out_specs=[here(3 * width), pl.BlockSpec((1, 3 * width), lambda m: (0, 0))],
+        out_shape=[
+            jax.ShapeDtypeStruct((tokens, 3 * width), BF),
+            jax.ShapeDtypeStruct((1, 3 * width), F32),
+        ],
+        compiler_params=pltpu.CompilerParams(vmem_limit_bytes=48 * 1024 * 1024),
+        cost_estimate=pl.CostEstimate(
+            flops=3_000_000_000, bytes_accessed=10_000_000, transcendentals=0
+        ),
+    )(dbranch, qkv, probs, layer)
 
 
 def body(
@@ -182,46 +355,13 @@
     small = after(jnp.stack(vectors))[0].T
     small = jnp.concatenate([small, b_expand.reshape(w_qkv.shape[0], -1)], axis=1)
     small = jnp.pad(small, ((0, 0), (0, 128 - small.shape[1])))
-    fused = jnp.concatenate([w_qkv, small, w_attn, w_expand, w_dense], axis=1)
+    fused = jnp.concatenate([w_expand, w_qkv, w_attn, w_dense, small], axis=1)
     fused = gather_x(fused).reshape(-1, fused.shape[1])
     tall = gather_x(w_shrink)
     tall = tall.transpose(1, 0, 2).reshape(fused.shape[0], -1)
     layer = lax.all_gather(
-        jnp.concatenate([fused, tall], axis=1), ("y", "c", "z"), axis=0, tiled=True
-    )
-    layer, w_vocab = after(layer, w_vocab)
-    ends = [3 * width, 128, width, w_expand.shape[1], width]
-    ends = [sum(ends[: i + 1]) for i in range(len(ends))]
-    qkv_full = layer[:, : ends[0]]
-    vec_full = layer[:, ends[0] : ends[1]]
-    attn_full = layer[:, ends[1] : ends[2]]
-    expand_full = layer[:, ends[2] : ends[3]]
-    dense_full = layer[:, ends[3] : ends[4]]
-    shrink_full = jnp.stack(
-        [
-            layer[:, ends[4] + k * width : ends[4] + (k + 1) * width].reshape(
-                NY * NC * NZ, -1, width
-            )
-            for k in range(NX)
-        ],
-        axis=1,
-    ).reshape(-1, width)
-    rows_of = vec_full.T.astype(F32)
-    (
-        b_query,
-        b_value,
-        b_attn,
-        attn_gain,
-        attn_shift,
-        b_shrink,
-        ffn_gain,
-        ffn_shift,
-        b_dense,
-        dense_gain,
-        dense_shift,
-    ) = (rows_of[i] for i in range(len(vectors)))
-    b_expand = vec_full[:, 11:15].astype(F32).reshape(-1)
-
+        jnp.concatenate([tall, fused], axis=1), ("y", "c", "z"), axis=0, tiled=True
+    )
     own_w = w_vocab.T
     piece_w = [own_w] + [fetch(own_w, "x", k) for k in (1, 2, 3)]
     piece_b = [b_vocab] + [fetch(b_vocab, "x", k) for k in (1, 2, 3)]
@@ -257,35 +397,55 @@
     scale = loss_scale * row_weight
     own_first = (at["y"] * NZ + at["z"]) * rows
     own_weight = lax.dynamic_slice_in_dim(row_weight, own_first, rows)
+    label_w = matmul(hit.astype(BF), vocab_w)
+    label_b = jnp.sum(jnp.where(hit, vocab_b, 0.0), axis=1, keepdims=True)
+    label_w = jnp.concatenate([label_w, jnp.pad(label_b, ((0, 0), (0, 127)))], axis=1)
+    label_w = swap(label_w.astype(BF).reshape(NY * NZ, rows, -1), ("y", "z"))
+    label_w = jnp.sum(label_w.astype(F32), axis=0)
+    label_w, label_b = label_w[:, :width], label_w[:, width]
     positions = mask_pos.reshape(micro, -1)
     shifted = jnp.where(
         positions >= 0, positions + block * jnp.arange(micro, dtype=jnp.int32)[:, None], -1
     ).reshape(-1)
     select = (shifted[:, None] == jnp.arange(tokens, dtype=jnp.int32)[None, :]).astype(BF)
 
+    layer, label_w, label_b, vocab_w, select = after(layer, label_w, label_b, vocab_w, select)
+    ends = [NX * width, w_expand.shape[1], 3 * width, width, width, 128]
+    ends = [sum(ends[: i + 1]) for i in range(len(ends))]
+    expand_full = layer[:, ends[0] : ends[1]]
+    qkv_full = layer[:, ends[1] : ends[2]]
+    attn_block = ends[2] // width
+    dense_full = layer[:, ends[3] : ends[4]]
+    vec_full = layer[:, ends[4] :]
+    shrink_full = jnp.stack(
+        [
+            layer[:, k * width : (k + 1) * width].reshape(
+                NY * NC * NZ, -1, width
+            )
+            for k in range(NX)
+        ],
+        axis=1,
+    ).reshape(-1, width)
+    rows_of = vec_full[:, :16].T.astype(F32)
+    (
+        b_query,
+        b_value,
+        b_attn,
+        attn_gain,
+        attn_shift,
+        b_shrink,
+        ffn_gain,
+        ffn_shift,
+        b_dense,
+        dense_gain,
+        dense_shift,
+    ) = (rows_of[i] for i in range(len(vectors)))
+    b_expand = vec_full[:, 11:15].astype(F32).reshape(-1)
+
     x = hidden_in.reshape(tokens, width)
-    united = matmul(x, qkv_full)
-
-    def split(values):
-        return values.astype(BF).reshape(micro, block, heads, HEAD_DIM)
-
-    query = split(united[:, :width] + b_query)
-    keys = split(united[:, width : 2 * width])
-    values = split(united[:, 2 * width :] + b_value)
-    allowed = (segments[:, :, None] == segments[:, None, :])[:, None]
-    raw = jnp.einsum("mqhd,mkhd->mhqk", query, keys, preferred_element_type=F32)
-    scores = jnp.where(allowed, raw * factor, MASKED)
-    expo = jnp.exp(scores - jnp.max(scores, axis=-1, keepdims=True))
-    probs = expo / jnp.sum(expo, axis=-1, keepdims=True)
-    weights = probs.astype(BF)
-    attended = (
-        jnp.einsum("mhqk,mkhd->mqhd", weights, values, preferred_element_type=F32)
-        .reshape(tokens, width)
-        .astype(BF)
-    )
-    branch = matmul(attended, attn_full) + b_attn
-    first, normed1, inverse1 = layer_norm(x.astype(F32) + branch, attn_gain, attn_shift)
-    first_low = first.astype(BF)
+    qkv, probs, attended, first, first_low, normed1, inverse1 = attention_forward(
+        x, segments, layer, attn_block - 3, rows_of
+    )
     pre = matmul(first_low, expand_full) + b_expand
     act = gelu_value(pre).astype(BF)
     second = first + matmul(act, shrink_full) + b_shrink
@@ -296,23 +456,14 @@
     dense_pre = matmul(picked, dense_full) + b_dense
     head_val, normed3, inverse3 = layer_norm(gelu_value(dense_pre), dense_gain, dense_shift)
     head_out = head_val.astype(BF)
-    head_out, vocab_w = after(head_out, vocab_w)
     spread = swap(
         jnp.broadcast_to(head_out, (NY * NZ,) + head_out.shape), ("y", "z")
     ).reshape(-1, width)
-    label_w = matmul(hit.astype(BF), vocab_w)
-    label_b = jnp.sum(jnp.where(hit, vocab_b, 0.0), axis=1, keepdims=True)
-    label_w = jnp.concatenate([label_w, jnp.pad(label_b, ((0, 0), (0, 127)))], axis=1)
-    spread, label_w = after(spread, label_w.astype(BF).reshape(NY * NZ, rows, -1))
-    label_w = swap(label_w, ("y", "z"))
-    label_w = jnp.sum(label_w.astype(F32), axis=0)
-    label_w, label_b = label_w[:, :width], label_w[:, width]
     logits = matmul_nt(spread, vocab_w) + vocab_b
     top = jnp.max(logits, axis=1)
     expl = jnp.exp(logits - top[:, None])
     part_sum = jnp.sum(expl, axis=1)
     other = jnp.where(hit, 0.0, expl).astype(BF)
-    other, label_w, label_b = after(other, label_w, label_b)
     part = matmul(other, vocab_w).astype(BF).reshape(NY * NZ, rows, width)
     stats = jnp.stack(three(top) + three(part_sum)).astype(BF)
     stats = jnp.concatenate([stats[:, :width], stats[:, width:].reshape(2, width)])
@@ -336,17 +487,6 @@
         mixed + (jnp.exp(label_logit - log_sum) - 1.0)[:, None] * label_w
     )
     loss_own = jnp.sum(own_weight * (log_sum - label_logit))
-    dlogits = (
-        (scale * jnp.exp(top - log_sums))[:, None] * expl
-        - jnp.where(hit, scale[:, None], 0.0)
-    ).astype(BF)
-    grad_w = matmul_tn(dlogits, spread).astype(BF).reshape(NC, NX, per, width)
-    grad_b = column_sum(dlogits).reshape(NC, NX, per)
-    grad_w = (grad_w[0].astype(F32) + give(grad_w[1], "c", 1).astype(F32)).astype(BF)
-    grad_b = grad_b[0] + give(grad_b[1], "c", 1)
-    g_vocab = total([grad_w[0]] + [give(grad_w[k], "x", k) for k in (1, 2, 3)]).T
-    g_vocab_bias = total([grad_b[0]] + [give(grad_b[k], "x", k) for k in (1, 2, 3)])
-
     g_dense_gain = column_sum(row_grad * normed3)
     g_dense_shift = column_sum(row_grad)
     ddense = (norm_back(row_grad, normed3, inverse3, dense_gain) * gelu_slope(dense_pre)).astype(BF)
@@ -370,40 +510,36 @@
     g_expand = matmul_tn(first_low, dpre)
     wide_pair = sum_cores([blocks(g_expand)], 2)
     g_expand_bias = column_sum(dpre)
+    dpre, tall_mine = after(dpre, add_cores(tall_pair))
     dfirst = dsecond + matmul_nt(dpre, expand_full)
     g_attn_gain = column_sum(dfirst * normed1)
     g_attn_shift = column_sum(dfirst)
     dresidual = norm_back(dfirst, normed1, inverse1, attn_gain)
     dbranch = dresidual.astype(BF)
-    dbranch, got = after(dbranch, tall_pair[1])
-    tall_sum = add_cores((tall_pair[0], got))
-    tall_all = swap(tall_sum, ("y", "z")).astype(F32)
+    tall_all = swap(tall_mine, ("y", "z")).astype(F32)
     tall_sum = jnp.sum(tall_all[:, :120], axis=0).astype(BF)
     loss_row = split_three(jnp.sum(tall_all[:, 120, :3]))
     g_attn = matmul_tn(attended, dbranch)
     g_attn_bias = column_sum(dbranch)
-    dattended = matmul_nt(dbranch, attn_full).astype(BF).reshape(micro, block, heads, HEAD_DIM)
-    dprobs = jnp.einsum("mqhd,mkhd->mhqk", dattended, values, preferred_element_type=F32)
-    inner = jnp.sum(probs * dprobs, axis=-1, keepdims=True)
-    dscores = (probs * (dprobs - inner)).astype(BF)
-
-    def merge(array):
-        return array.astype(BF).reshape(tokens, width)
-
-    dquery = merge(
-        jnp.einsum("mhqk,mkhd->mqhd", dscores, keys, preferred_element_type=F32) * factor
-    )
-    dkeys = merge(
-        jnp.einsum("mhqk,mqhd->mkhd", dscores, query, preferred_element_type=F32) * factor
-    )
-    dvalues = merge(
-        jnp.einsum("mhqk,mqhd->mkhd", weights, dattended, preferred_element_type=F32)
-    )
-    dfused = jnp.concatenate([dquery, dkeys, dvalues], axis=1)
+    dfused, fused_sum = attention_backward(dbranch, qkv, probs, layer, attn_block)
+    dfused, got = after(dfused, wide_pair[1])
+    wide_mine = add_cores((wide_pair[0], got))
     g_qkv = matmul_tn(x, dfused)
-    g_query = column_sum(dquery)
-    g_value = column_sum(dvalues)
+    g_query, g_value = fused_sum[0, :width], fused_sum[0, 2 * width :]
     dinput = dresidual + matmul_nt(dfused, qkv_full)
+
+    late_sums, dfused = after(log_sums, dfused)
+    dlogits = (
+        (scale * jnp.exp(top - late_sums))[:, None] * expl
+        - jnp.where(hit, scale[:, None], 0.0)
+    ).astype(BF)
+    grad_w = matmul_tn(dlogits, spread).astype(BF).reshape(NC, NX, per, width)
+    grad_b = column_sum(dlogits).reshape(NC, NX, 1, per)
+    grad_b = jnp.pad(grad_b, ((0, 0), (0, 0), (0, 7), (0, width - per))).astype(BF)
+    grad_w = jnp.concatenate([grad_w, grad_b], axis=2)
+    grad_w = (grad_w[0].astype(F32) + give(grad_w[1], "c", 1).astype(F32)).astype(BF)
+    grad_w = total([grad_w[0]] + [give(grad_w[k], "x", k) for k in (1, 2, 3)])
+    g_vocab, g_vocab_bias = grad_w[:per].T, grad_w[per, :per]
 
     sums = jnp.stack(
         [
@@ -418,12 +554,11 @@
             g_dense_bias,
             g_dense_gain,
             g_dense_shift,
-        ],
-        axis=1,
-    )
-    sums = jnp.concatenate([sums, g_expand_bias.reshape(width, -1)], axis=1)
+        ]
+    )
+    sums = jnp.concatenate([after(sums)[0].T, g_expand_bias.reshape(width, -1)], axis=1)
     sums = jnp.pad(sums, ((0, 0), (0, 128 - sums.shape[1])))
-    wide = sum_yz(add_cores(wide_pair))
+    wide = sum_yz(wide_mine)
     tall = sum_x(
         jnp.concatenate(
             [tall_sum[:96].reshape(NX, -1, width), jnp.broadcast_to(loss_row, (NX, 8, width))],

time: 550 us -> 480 us (0.87)
  waiting for transfers between devices: 151 us -> 113 us
  local copies, waits for them, and re-layouts: 88.6 us -> 54 us
  blocking collectives: 0 us -> 26.1 us
  Pallas kernels: 0 us -> 23.1 us
  other arithmetic: 95.9 us -> 75.5 us
  matrix products: 102 us -> 84.7 us
  starting transfers between devices: 81.9 us -> 69.7 us
    all_gather x1, waiting for transfers between devices: 60.4 us -> 0.02 us  [body(): lax.all_gather(jnp.concatenate([tall, fused], axis=1), ('y', 'c', 'z'), a...]
    all_to_all x0 -> x1, blocking collectives: none -> 26.1 us  [swap(): return lax.all_to_all(array, axes, 0, 0, tiled=True)]
    ppermute x14, waiting for transfers between devices: 3.88 us -> 29.7 us  [fetch(): return lax.ppermute(array, axis, [((i + k) % n, i) for i in range(n)])]
    pallas_call x0 -> x2, Pallas kernels: none -> 23.1 us  [the longest x1 12.1 us: attention_backward(): pl.pallas_call(attention_backward_kernel, grid=(micro,), in_specs=[here(w...]
    convert_element_type x7 -> x3, other arithmetic: 21.3 us -> 4.32 us  [the longest x1 3.29 us: body(): tall_all = swap(tall_mine, ('y', 'z')).astype(F32)]
    dot_general x6 -> x0, matrix products: 13.7 us -> none  [the longest x1 5.08 us: body(): jnp.einsum('mhqk,mqhd->mkhd', weights, dattended, preferred_element_type=...]
    ppermute x14, starting transfers between devices: 31.5 us -> 19.2 us  [fetch(): return lax.ppermute(array, axis, [((i + k) % n, i) for i in range(n)])]
    dot_general x8 -> x6, matrix products: 37.2 us -> 28.1 us  [matmul(): return jnp.dot(left, right, preferred_element_type=F32)]
  transfers between devices with their start and end apart: 35 -> 30, of which waited for: 15 -> 15; matrix products, arithmetic and copies ran while one was open for 36% -> 26% of each run, Pallas kernels for 0% -> 3%
where the time goes in v4:
time: 480 us; the launch traced here: 473 us
  waiting for transfers between devices  113 us (24%)
  matrix products  84.7 us (18%)
  other arithmetic  75.5 us (16%)
  starting transfers between devices  69.7 us (15%)
  local copies, waits for them, and re-layouts  54 us (11%)
  between operations  27.1 us (6%)
  blocking collectives  26.1 us (5%)
  Pallas kernels  23.1 us (5%)
    all_to_all x7, waiting for transfers between devices, swap(): return lax.all_to_all(array, axes, 0, 0, tiled=True)  66.6 us
    all_to_all x7, starting transfers between devices, swap(): return lax.all_to_all(array, axes, 0, 0, tiled=True)  45.2 us
    ppermute x14, waiting for transfers between devices, fetch(): return lax.ppermute(array, axis, [((i + k) % n, i) for i in range(n)])  29.7 us
    dot_general x4, matrix products, matmul_nt(): lax.dot_general(left, right, (((1,), (1,)), ((), ())), preferred_element_...  29.2 us
    dot_general x6, matrix products, matmul(): return jnp.dot(left, right, preferred_element_type=F32)  28.1 us
    dot_general x7, matrix products, matmul_tn(): lax.dot_general(left, right, (((0,), (0,)), ((), ())), preferred_element_...  27.4 us
    all_to_all x1, blocking collectives, swap(): return lax.all_to_all(array, axes, 0, 0, tiled=True)  26.1 us
    unnamed x117, local copies, waits for them, and re-layouts  20.9 us
  transfers between devices with their start and end apart: 30, of which 15 were waited for; matrix products, arithmetic and copies ran while one was open for 26% of the time, Pallas kernels for 3%

profile of v4, /device:TPU:0, one launch (start us, length us, event | category | flops | bytes accessed | tf_op | source)
XLA Modules:
  0.0 473.4 jit_solution(8175268578026152189)
XLA Ops:
  7.2 2.9 collective-permute-start
  10.2 2.3 collective-permute-start.1
  18.0 1.8 collective-permute-start.5
  21.4 2.0 collective-permute-start.3
  24.2 2.0 collective-permute-done.3
  27.5 2.7 collective-permute-start.7
  30.2 1.9 collective-permute-start.6
  32.2 13.7 %collective-permute-done.7 = bf16[400,768]{1,0:T(8,128)(2,1)S(1)} collective-permute-done((bf16[400,768]{1,0:T(8,128)(2,1)S(1)}, bf16[400,768]{1,0:T(8,128)(2,1)S(1)}, u32[]{:S(2)}, u32[]{:S(2)}) %collective-permute-start.7) | collective-permute-done | bytes 614432 | tf_op jit(solution)/shard_map/ppermute | solution.py:24
  45.9 11.7 %collective-permute-done.6 = bf16[400,768]{1,0:T(8,128)(2,1)S(1)} collective-permute-done((bf16[400,768]{1,0:T(8,128)(2,1)S(1)}, bf16[400,768]{1,0:T(8,128)(2,1)S(1)}, u32[]{:S(2)}, u32[]{:S(2)}) %collective-permute-start.6) | collective-permute-done | bytes 614432 | tf_op jit(solution)/shard_map/ppermute | solution.py:24
  57.6 1.8 pad_maximum_fusion.2
  59.4 2.5 collective-permute-start.10
  70.6 2.0 constant_dynamic-update-slice_fusion.16
  76.0 7.9 %fusion.34 = bf16[16,64,768]{2,1,0:T(8,128)(2,1)S(1)} fusion(bf16[3200,768,1]{1,0,2:T(8,128)(2,1)} %bitcast.237, s32[3200]{0:T(1024)S(1)} %add.385, s32[16,64]{1,0:T(8,128)S(1)} %copy.61), kind=kOutput, calls=%fused_computation.60 | convolution fusion | flops 5037228032 | bytes 6504960 | tf_op jit(solution)/shard_map/dot_general | solution.py:128
  85.4 8.4 %all-to-all-start = ((bf16[16,64,896]{2,1,0:T(8,128)(2,1)}), bf16[16,64,896]{2,1,0:T(8,128)(2,1)S(1)}, u32[]{:S(2)}, u32[]{:S(2)}) async-start(bf16[16,64,896]{2,1,0:T(8,128)(2,1)} %pad_maximum_fusion.5), calls=%async_computation | async-start | bytes 3670016 | tf_op jit(solution)/shard_map/all_to_all | solution.py:44
  94.4 27.5 %all-to-all-done = bf16[16,64,896]{2,1,0:T(8,128)(2,1)S(1)} async-done(((bf16[16,64,896]{2,1,0:T(8,128)(2,1)}), bf16[16,64,896]{2,1,0:T(8,128)(2,1)S(1)}, u32[]{:S(2)}, u32[]{:S(2)}) %all-to-all-start) | async-done | bytes 1835040 | tf_op jit(solution)/shard_map/all_to_all | solution.py:44
  126.0 4.7 fusion.86
  130.9 11.0 %shard_map.408 = (bf16[512,2304]{1,0:T(8,128)(2,1)}, bf16[2,12,256,256]{3,2,1,0:T(8,128)(2,1)}, bf16[512,768]{1,0:T(8,128)(2,1)S(1)}, f32[512,768]{1,0:T(8,128)S...) custom-call(bf16[512,768]{1,0:T(8,128)(2,1)S(1)} %bitcast.193, ...), custom_call_target="tpu_custom_call" | custom-call | flops 4000000000 | bytes 16000000 | tf_op jit(solution)/shard_map/pallas_call | solution.py:209
  142.0 7.0 %multiply_convert_fusion = (bf16[512,3072]{1,0:T(8,128)(2,1)S(1)}, f32[512,3072]{1,0:T(8,128)}) fusion(f32[3072]{0:T(1024)S(1)} %reshape.477, bf16[512,768]{1,0:T(8,128)(2,1)S(1)} %get-tuple-element.47, bf16[768,10112]{1,0:T(8,128)(2,1)} %all-gather.2.cloned.1.call-done.wq_ref.wk_ref.wv_ref.wa_ref), kind=kOutput, calls=%fused_computation.30 | convolution fusion | flops 2425356288 | bytes 14954496 | tf_op jit(solution)/shard_map/dot_general | solution.py:128
  150.6 2.7 fusion.89
  154.2 2.4 fusion.85
  157.2 26.1 %all_to_all.40 = bf16[16,64,768]{2,1,0:T(8,128)(2,1)S(1)} all-to-all(bf16[16,64,768]{2,1,0:T(8,128)(2,1)S(1)} %broadcast_in_dim.106), channel_id=1, replica_groups=mesh['y'=4,'c'=2,'z'=4,'x'=4] {'y','z'}, dimensions={0} | all-to-all | bytes 3145728 | tf_op jit(solution)/shard_map/all_to_all | solution.py:44
  183.3 8.6 %add_reduce_fusion = (f32[1024]{0:T(1024)S(1)}, f32[1024,3200]{1,0:T(8,128)S(1)}) fusion(f32[3200]{0:T(1024)S(1)} %reshape.476, bf16[1024,768]{1,0:T(8,128)(2,1)S(1)} %bitcast.225, bf16[3200,768]{1,0:T(8,128)(2,1)} %bitcast.238), kind=kOutput, calls=%fused_computation.10 | convolution fusion | flops 5039717376 | bytes 19612160 | tf_op jit(solution)/shard_map/dot_general | solution.py:136
  192.0 4.7 copy-done.8
  196.7 7.8 %fusion.31 = bf16[1024,768]{1,0:T(8,128)(2,1)} fusion(bf16[3200,768]{1,0:T(8,128)(2,1)S(1)} %bitcast.241, f32[1024,3200]{1,0:T(8,128)S(1)} %get-tuple-element.158, f32[1024]{0:T(1024)S(1)} %get-tuple-element.157, f32[3200]{0:T(1024)S(1)} %reshape.476, s32[3200]{0:T(1024)S(1)} %add.385, s32[1024]{0:T(1024)S(1)} %eq.74), kind=kOutput, calls=%fused_computation.59 | convolution fusion | flops 5050335232 | bytes 19629056 | tf_op jit(solution)/shard_map/dot_general | solution.py:128
  204.5 7.1 %fusion.7 = f32[1024]{0:T(1024)S(1)} fusion(f32[1024,3200]{1,0:T(8,128)} %copy-done.8, f32[1024]{0:T(1024)S(1)} %get-tuple-element.157, f32[3200]{0:T(1024)S(1)} %reshape.476), kind=kLoop, calls=%fused_computation.14 | loop fusion | flops 9829376 | bytes 13128192 | tf_op jit(solution)/shard_map/reduce_sum | solution.py:465
  211.7 2.7 pad_maximum_fusion.6
  214.5 4.8 %all-to-all-start.2 = ((bf16[16,72,768]{2,1,0:T(8,128)(2,1)}), bf16[16,72,768]{2,1,0:T(8,128)(2,1)}, u32[]{:S(2)}, u32[]{:S(2)}) async-start(bf16[16,72,768]{2,1,0:T(8,128)(2,1)} %pad_maximum_fusion.6), calls=%async_computation.2 | async-start | bytes 3538944 | tf_op jit(solution)/shard_map/all_to_all | solution.py:44
  220.3 22.6 %all-to-all-done.2 = bf16[16,72,768]{2,1,0:T(8,128)(2,1)} async-done(((bf16[16,72,768]{2,1,0:T(8,128)(2,1)}), bf16[16,72,768]{2,1,0:T(8,128)(2,1)}, u32[]{:S(2)}, u32[]{:S(2)}) %all-to-all-start.2) | async-done | bytes 1769504 | tf_op jit(solution)/shard_map/all_to_all | solution.py:44
  256.9 4.2 multiply_reduce_fusion.1
  261.1 2.5 convert_reduce_fusion.1
  263.9 2.9 convolution_convert_fusion.3
  268.6 1.9 pad_maximum_fusion.1
  270.7 8.9 %fusion.92 = (bf16[3072]{0:T(1024)(128)(2,1)S(1)}, bf16[512,3072]{1,0:T(8,128)(2,1)}) fusion(f32[512,3072]{1,0:T(8,128)} %get-tuple-element.153, f32[3072]{0:T(1024)S(1)} %reshape.477, bf16[3072,768]{1,0:T(8,128)(2,1)} %bitcast.207, f32[512,768]{1,0:T(8,128)} %copy-done.27), kind=kOutput, calls=%fused_computation.265 | convolution fusion | flops 2435183616 | bytes 15747072 | tf_op jit(solution)/shard_map/dot_general | solution.py:136
  280.2 4.8 %convolution_convert_fusion.2 = bf16[768,3072]{1,0:T(8,128)(2,1)S(1)} fusion(bf16[512,768]{1,0:T(8,128)(2,1)S(1)} %copy-done.7, bf16[512,3072]{1,0:T(8,128)(2,1)} %get-tuple-element.52), kind=kOutput, calls=%fused_computation.34 | convolution fusion | flops 2418278400 | bytes 8650752 | tf_op jit(solution)/shard_map/dot_general | solution.py:132
  285.0 2.6 constant_dynamic-slice_fusion
  288.3 3.8 add_convert_fusion
  292.4 6.4 %multiply_reduce_fusion.2 = (bf16[768]{0:T(1024)(128)(2,1)S(1)}, f32[512]{0:T(512)S(1)}, f32[512]{0:T(512)S(1)}, bf16[768]{0:T(1024)(128)(2,1)S(1)}, f32[512,768]{1,0:T(8,128)}) fusion(f32[512,768]{1,0:T(8,128)S(1)} %get-tuple-element.53, f32[768]{0:T(1024)S(1)} %get-tuple-element.78, f32[512,768]{1,0:T(8,128)S(1)} %copy-done.28, ...), kind=kOutput, calls=%fused_computation.64 | convolution fusion | flops 2419062272 | bytes 12593152 | tf_op jit(solution)/shard_map/dot_general | solution.py:136
  298.7 4.5 all-to-all-start.4
  303.3 2.0 convert_reduce_fusion.2
  305.4 12.1 %shard_map.409 = (bf16[512,2304]{1,0:T(8,128)(2,1)S(1)}, f32[1,2304]{1,0:T(1,128)S(1)}) custom-call(bf16[512,768]{1,0:T(8,128)(2,1)S(1)} %get-tuple-element.109.dbranch_ref, bf16[512,2304]{1,0:T(8,128)(2,1)S(1)} %copy-done, bf16[2,12,256,256]{3,2,1,0:T(8,128)(2,1)} %get-tuple-element.56.probs_ref, ...), custom_call_target="tpu_custom_call" | custom-call | flops 3000000000 | bytes 10000000 | tf_op jit(solution)/shard_map/pallas_call | solution.py:289
  319.2 2.1 convolution_convert_fusion.4
  321.3 2.0 convolution_convert_fusion.1
  327.4 4.2 fusion.24
  331.6 7.3 %fusion.80 = (bf16[3200]{0:T(1024)(128)(2,1)S(1)}, bf16[1024,3200]{1,0:T(8,128)(2,1)}) fusion(f32[1024]{0:T(1024)S(1)} %get-tuple-element.102, s32[3200]{0:T(1024)S(1)} %add.385, s32[1024]{0:T(1024)S(1)} %eq.74, f32[1024]{0:T(1024)S(1)} %get-tuple-element.157, f32[1024,3200]{1,0:T(8,128)S(1)} %bitcast.196, f32[3200]{0:T(1024)S(1)} %reshape.476, ...), kind=kLoop, calls=%fused_computation.259 | loop fusion | flops 26211200 | bytes 19709184 | tf_op jit(solution)/shard_map/reduce_sum | solution.py:124
  339.0 7.9 %all-to-all-done.4 = bf16[16,128,768]{2,1,0:T(8,128)(2,1)} async-done(((bf16[16,128,768]{2,1,0:T(8,128)(2,1)}), bf16[16,128,768]{2,1,0:T(8,128)(2,1)}, u32[]{:S(2)}, u32[]{:S(2)}) %all-to-all-start.4) | async-done | bytes 3145760 | tf_op jit(solution)/shard_map/all_to_all | solution.py:44
  346.9 10.4 %all-to-all-start.3 = ((bf16[16,24,3072]{2,1,0:T(8,128)(2,1)}), bf16[16,24,3072]{2,1,0:T(8,128)(2,1)}, u32[]{:S(2)}, u32[]{:S(2)}) async-start(bf16[16,24,3072]{2,1,0:T(8,128)(2,1)} %fusion.24), calls=%async_computation.3 | async-start | bytes 4718592 | tf_op jit(solution)/shard_map/all_to_all | solution.py:44
  357.3 10.9 %convolution_convert_fusion = bf16[3200,768]{1,0:T(8,128)(2,1)} fusion(bf16[1024,3200]{1,0:T(8,128)(2,1)} %get-tuple-element.101, bf16[1024,768]{1,0:T(8,128)(2,1)} %bitcast.226), kind=kOutput, calls=%fused_computation.15 | convolution fusion | flops 5035622400 | bytes 13041664 | tf_op jit(solution)/shard_map/dot_general | solution.py:132
  368.3 2.7 fusion.22
  372.8 3.3 convert_element_type.248
  376.1 2.6 copy-done.9
  384.7 3.0 slice_reduce_fusion
  390.4 6.9 %all-to-all-start.5 = ((bf16[4,32,768]{2,1,0:T(8,128)(2,1)}), bf16[4,32,768]{2,1,0:T(8,128)(2,1)S(1)}, u32[]{:S(2)}, u32[]{:S(2)}) async-start(bf16[4,32,768]{2,1,0:T(8,128)(2,1)} %pad_maximum_fusion.9), calls=%async_computation.5 | async-start | bytes 393216 | tf_op jit(solution)/shard_map/all_to_all | solution.py:44
  397.3 2.7 pad_maximum_fusion.3
  400.1 2.1 reduce_sum.361
  403.7 4.4 add_convert_fusion.1
  408.1 6.6 %all-to-all-start.6 = ((bf16[16,24,3200]{2,1,0:T(8,128)(2,1)}), bf16[16,24,3200]{2,1,0:T(8,128)(2,1)}, u32[]{:S(2)}, u32[]{:S(2)}) async-start(bf16[16,24,3200]{2,1,0:T(8,128)(2,1)} %add_convert_fusion.1), calls=%async_computation.6 | async-start | bytes 4915200 | tf_op jit(solution)/shard_map/all_to_all | solution.py:44
  414.8 3.2 fusion.23
  418.8 2.7 collective-permute-start.21
  423.6 5.3 %fusion.37 = f32[512,768]{1,0:T(8,128)} fusion(bf16[512,2304]{1,0:T(8,128)(2,1)S(1)} %copy-done.4, bf16[768,10112]{1,0:T(8,128)(2,1)} %all-gather.2.cloned.1.call-done.wq_ref.wk_ref.wv_ref.wa_ref, f32[512]{0:T(512)S(1)} %reduce.18, f32[512,768]{1,0:T(8,128)S(1)} %get-tuple-element.53, f32[512]{0:T(512)S(1)} %broadcast_multiply_fusion.1, ...), kind=kOutput, calls=%fused_computation.76 | convolution fusion | flops 1814298624 | bytes 10626048 | tf_op jit(solution)/shard_map/dot_general | solution.py:136
  430.7 4.1 collective-permute-done.19
  434.8 11.4 %collective-permute-done.21 = bf16[408,768]{1,0:T(8,128)(2,1)S(1)} collective-permute-done((bf16[408,768]{1,0:T(8,128)(2,1)S(1)}, bf16[408,768]{1,0:T(8,128)(2,1)S(1)}, u32[]{:S(2)}, u32[]{:S(2)}) %collective-permute-start.21) | collective-permute-done | bytes 626720 | tf_op jit(solution)/shard_map/ppermute | solution.py:29
  448.7 2.0 reduce_sum.366
  451.6 3.5 all-to-all-start.7
  456.2 6.5 %all-to-all-done.7 = bf16[4,6,7040]{2,1,0:T(8,128)(2,1)S(1)} async-done(((bf16[4,6,7040]{2,1,0:T(8,128)(2,1)}), bf16[4,6,7040]{2,1,0:T(8,128)(2,1)S(1)}, u32[]{:S(2)}, u32[]{:S(2)}) %all-to-all-start.7) | async-done | bytes 337952 | tf_op jit(solution)/shard_map/all_to_all | solution.py:44
  (303 shorter events, 68.7 us)
Async XLA Ops:
  7.2 115.1 %all-gather.2.cloned.1.call-start = ((), (), s32[]{:S(2)}) async-start(), calls=%async_computation.8 | async-start | bytes 16017408 | tf_op jit(solution)/shard_map/all_gather | solution.py:362
  7.2 14.1 %collective-permute-start = (bf16[24,768]{1,0:T(8,128)(2,1)}, bf16[24,768]{1,0:T(8,128)(2,1)S(1)}, u32[]{:S(2)}, u32[]{:S(2)}) collective-permute-start(bf16[24,768]{1,0:T(8,128)(2,1)} %param.40), channel_id=1, source_target_pairs={{1,0},{2,1},{3,2},{0,3},{5,4},{6,5},{7,6},{4,7},{9,8},{10,9},{11,1... | collective-permute-start | bytes 110600 | tf_op jit(solution)/shard_map/ppermute | solution.py:24
  10.1 13.2 %collective-permute-start.2 = (bf16[24,768]{1,0:T(8,128)(2,1)}, bf16[24,768]{1,0:T(8,128)(2,1)S(1)}, u32[]{:S(2)}, u32[]{:S(2)}) collective-permute-start(bf16[24,768]{1,0:T(8,128)(2,1)} %param.40), channel_id=1, source_target_pairs={{3,0},{0,1},{1,2},{2,3},{7,4},{4,5},{5,6},{6,7},{11,8},{8,9},{9,10... | collective-permute-start | bytes 110600 | tf_op jit(solution)/shard_map/ppermute | solution.py:24
  10.2 13.2 %collective-permute-start.1 = (bf16[24,768]{1,0:T(8,128)(2,1)}, bf16[24,768]{1,0:T(8,128)(2,1)S(1)}, u32[]{:S(2)}, u32[]{:S(2)}) collective-permute-start(bf16[24,768]{1,0:T(8,128)(2,1)} %param.40), channel_id=1, source_target_pairs={{2,0},{3,1},{0,2},{1,3},{6,4},{7,5},{4,6},{5,7},{10,8},{11,9},{8,1... | collective-permute-start | bytes 110600 | tf_op jit(solution)/shard_map/ppermute | solution.py:24
  15.7 11.7 %copy-start.20 = (bf16[768,400]{0,1:T(8,128)(2,1)S(1)}, bf16[768,400]{0,1:T(8,128)(2,1)}, u32[]{:S(2)}) copy-start(bf16[768,400]{0,1:T(8,128)(2,1)} %param.48) | copy-start | bytes 1843204
  18.0 8.3 %collective-permute-start.5 = (bf16[6,7040]{1,0:T(8,128)(2,1)S(1)}, bf16[6,7040]{1,0:T(8,128)(2,1)S(1)}, u32[]{:S(2)}, u32[]{:S(2)}) collective-permute-start(bf16[6,7040]{1,0:T(8,128)(2,1)S(1)} %constant_dynamic-update-slice_fusion.8), channel_id=1, source_target_pairs={{3,0},{0,1},{1,2},{2,3},{7,4},{4,5},{5,6},{6,7},{11,8},{8,9},{9,10... | collective-permute-start | bytes 253448 | tf_op jit(solution)/shard_map/ppermute | solution.py:24
  19.8 6.5 %collective-permute-start.4 = (bf16[6,7040]{1,0:T(8,128)(2,1)S(1)}, bf16[6,7040]{1,0:T(8,128)(2,1)S(1)}, u32[]{:S(2)}, u32[]{:S(2)}) collective-permute-start(bf16[6,7040]{1,0:T(8,128)(2,1)S(1)} %constant_dynamic-update-slice_fusion.8), channel_id=1, source_target_pairs={{2,0},{3,1},{0,2},{1,3},{6,4},{7,5},{4,6},{5,7},{10,8},{11,9},{8,1... | collective-permute-start | bytes 253448 | tf_op jit(solution)/shard_map/ppermute | solution.py:24
  21.4 4.9 %collective-permute-start.3 = (bf16[6,7040]{1,0:T(8,128)(2,1)S(1)}, bf16[6,7040]{1,0:T(8,128)(2,1)S(1)}, u32[]{:S(2)}, u32[]{:S(2)}) collective-permute-start(bf16[6,7040]{1,0:T(8,128)(2,1)S(1)} %constant_dynamic-update-slice_fusion.8), channel_id=1, source_target_pairs={{1,0},{2,1},{3,2},{0,3},{5,4},{6,5},{7,6},{4,7},{9,8},{10,9},{11,1... | collective-permute-start | bytes 253448 | tf_op jit(solution)/shard_map/ppermute | solution.py:24
  26.6 32.9 %copy-start.35 = (bf16[400]{0:T(512)(128)(2,1)S(1)}, bf16[400]{0:T(512)(128)(2,1)}, u32[]{:S(2)}) copy-start(bf16[400]{0:T(512)(128)(2,1)} %param.49) | copy-start | bytes 2404
  27.5 18.4 %collective-permute-start.7 = (bf16[400,768]{1,0:T(8,128)(2,1)S(1)}, bf16[400,768]{1,0:T(8,128)(2,1)S(1)}, u32[]{:S(2)}, u32[]{:S(2)}) collective-permute-start(bf16[400,768]{1,0:T(8,128)(2,1)S(1)} %bitcast.213), channel_id=1, source_target_pairs={{2,0},{3,1},{0,2},{1,3},{6,4},{7,5},{4,6},{5,7},{10,8},{11,9},{8,1... | collective-permute-start | bytes 1843208 | tf_op jit(solution)/shard_map/ppermute | solution.py:24
  30.2 27.4 %collective-permute-start.6 = (bf16[400,768]{1,0:T(8,128)(2,1)S(1)}, bf16[400,768]{1,0:T(8,128)(2,1)S(1)}, u32[]{:S(2)}, u32[]{:S(2)}) collective-permute-start(bf16[400,768]{1,0:T(8,128)(2,1)S(1)} %bitcast.214), channel_id=1, source_target_pairs={{1,0},{2,1},{3,2},{0,3},{5,4},{6,5},{7,6},{4,7},{9,8},{10,9},{11,1... | collective-permute-start | bytes 1843208 | tf_op jit(solution)/shard_map/ppermute | solution.py:24
  32.0 25.5 %collective-permute-start.8 = (bf16[400,768]{1,0:T(8,128)(2,1)S(1)}, bf16[400,768]{1,0:T(8,128)(2,1)S(1)}, u32[]{:S(2)}, u32[]{:S(2)}) collective-permute-start(bf16[400,768]{1,0:T(8,128)(2,1)S(1)} %bitcast.215), channel_id=1, source_target_pairs={{3,0},{0,1},{1,2},{2,3},{7,4},{4,5},{5,6},{6,7},{11,8},{8,9},{9,10... | collective-permute-start | bytes 1843208 | tf_op jit(solution)/shard_map/ppermute | solution.py:24
  45.9 11.7 %copy-start.21 = (bf16[400,768]{1,0:T(8,128)(2,1)}, bf16[400,768]{1,0:T(8,128)(2,1)S(1)}, u32[]{:S(2)}) copy-start(bf16[400,768]{1,0:T(8,128)(2,1)S(1)} %collective-permute-done.7) | copy-start | bytes 1843204
  57.6 6.9 %copy-start.32 = (s32[2,128,16,2]{1,3,2,0:T(2,128)S(1)}, s32[2,128,16,2]{1,3,2,0:T(2,128)}, u32[]{:S(2)}) copy-start(s32[2,128,16,2]{1,3,2,0:T(2,128)} %param.29) | copy-start | bytes 98308
  59.4 15.0 %collective-permute-start.9 = (bf16[4,400,768]{2,1,0:T(8,128)(2,1)}, bf16[4,400,768]{2,1,0:T(8,128)(2,1)S(1)}, u32[]{:S(2)}, u32[]{:S(2)}) collective-permute-start(bf16[4,400,768]{2,1,0:T(8,128)(2,1)} %pad_maximum_fusion.2), channel_id=1, source_target_pairs={{16,0},{0,16},{17,1},{1,17},{18,2},{2,18},{19,3},{3,19},{20,4},{4,... | collective-permute-start | bytes 7372808 | tf_op jit(solution)/shard_map/ppermute | solution.py:24
  59.4 5.5 %collective-permute-start.10 = (bf16[400]{0:T(512)(128)(2,1)S(1)}, bf16[400]{0:T(512)(128)(2,1)S(1)}, u32[]{:S(2)}, u32[]{:S(2)}) collective-permute-start(bf16[400]{0:T(512)(128)(2,1)S(1)} %copy-done.35), channel_id=1, source_target_pairs={{1,0},{2,1},{3,2},{0,3},{5,4},{6,5},{7,6},{4,7},{9,8},{10,9},{11,1... | collective-permute-start | bytes 2408 | tf_op jit(solution)/shard_map/ppermute | solution.py:24
  61.9 4.8 %collective-permute-start.12 = (bf16[400]{0:T(512)(128)(2,1)S(1)}, bf16[400]{0:T(512)(128)(2,1)S(1)}, u32[]{:S(2)}, u32[]{:S(2)}) collective-permute-start(bf16[400]{0:T(512)(128)(2,1)S(1)} %copy-done.35), channel_id=1, source_target_pairs={{3,0},{0,1},{1,2},{2,3},{7,4},{4,5},{5,6},{6,7},{11,8},{8,9},{9,10... | collective-permute-start | bytes 2408 | tf_op jit(solution)/shard_map/ppermute | solution.py:24
  61.9 5.1 %collective-permute-start.11 = (bf16[400]{0:T(512)(128)(2,1)S(1)}, bf16[400]{0:T(512)(128)(2,1)S(1)}, u32[]{:S(2)}, u32[]{:S(2)}) collective-permute-start(bf16[400]{0:T(512)(128)(2,1)S(1)} %copy-done.35), channel_id=1, source_target_pairs={{2,0},{3,1},{0,2},{1,3},{6,4},{7,5},{4,6},{5,7},{10,8},{11,9},{8,1... | collective-permute-start | bytes 2408 | tf_op jit(solution)/shard_map/ppermute | solution.py:24
  64.4 8.2 %copy-start.22 = (bf16[400,768]{1,0:T(8,128)(2,1)S(1)}, bf16[400,768]{1,0:T(8,128)(2,1)}, u32[]{:S(2)}) copy-start(bf16[400,768]{1,0:T(8,128)(2,1)} %copy-done.21) | copy-start | bytes 1843204
  67.0 1.8 collective-permute-start.13
  68.9 4.6 copy-start.24
  83.9 10.1 %copy-start.33 = (s32[2,256]{1,0:T(2,128)S(1)}, s32[2,256]{1,0:T(2,128)}, u32[]{:S(2)}) copy-start(s32[2,256]{1,0:T(2,128)} %param.27) | copy-start | bytes 6148
  83.9 10.1 %copy-start.34 = (s32[2,1,16,2]{2,3,1,0:T(2,128)S(1)}, s32[2,1,16,2]{2,3,1,0:T(2,128)}, u32[]{:S(2)}) copy-start(s32[2,1,16,2]{2,3,1,0:T(2,128)} %param.28) | copy-start | bytes 772
  85.4 36.5 %all-to-all-start = ((bf16[16,64,896]{2,1,0:T(8,128)(2,1)}), bf16[16,64,896]{2,1,0:T(8,128)(2,1)S(1)}, u32[]{:S(2)}, u32[]{:S(2)}) async-start(bf16[16,64,896]{2,1,0:T(8,128)(2,1)} %pad_maximum_fusion.5), calls=%async_computation | async-start | bytes 3670016 | tf_op jit(solution)/shard_map/all_to_all | solution.py:44
  126.0 4.9 %copy-start.1 = (bf16[2,256,768]{2,1,0:T(8,128)(2,1)S(1)}, bf16[2,256,768]{2,1,0:T(8,128)(2,1)}, u32[]{:S(2)}) copy-start(bf16[2,256,768]{2,1,0:T(8,128)(2,1)} %param.25) | copy-start | bytes 2359300
  141.9 7.0 %copy-start.5 = (bf16[512,768]{1,0:T(8,128)(2,1)}, bf16[512,768]{1,0:T(8,128)(2,1)S(1)}, u32[]{:S(2)}) copy-start(bf16[512,768]{1,0:T(8,128)(2,1)S(1)} %get-tuple-element.59) | copy-start | bytes 2359300
  141.9 7.0 %copy-start.6 = (bf16[512,768]{1,0:T(8,128)(2,1)}, bf16[512,768]{1,0:T(8,128)(2,1)S(1)}, u32[]{:S(2)}) copy-start(bf16[512,768]{1,0:T(8,128)(2,1)S(1)} %get-tuple-element.47) | copy-start | bytes 2359300
  141.9 7.0 %copy-start.14 = (bf16[768,768]{1,0:T(8,128)(2,1)S(1)}, bf16[768,768]{1,0:T(8,128)(2,1)}, u32[]{:S(2)}) copy-start(bf16[768,768]{1,0:T(8,128)(2,1)} %get-tuple-element.117) | copy-start | bytes 3538948
  141.9 7.0 %copy-start.15 = (bf16[768,768]{1,0:T(8,128)(2,1)S(1)}, bf16[768,768]{1,0:T(8,128)(2,1)}, u32[]{:S(2)}) copy-start(bf16[768,768]{1,0:T(8,128)(2,1)} %get-tuple-element.118) | copy-start | bytes 3538948
  142.0 7.0 %copy-start.16 = (bf16[768,768]{1,0:T(8,128)(2,1)S(1)}, bf16[768,768]{1,0:T(8,128)(2,1)}, u32[]{:S(2)}) copy-start(bf16[768,768]{1,0:T(8,128)(2,1)} %get-tuple-element.119) | copy-start | bytes 3538948
  142.0 7.0 %copy-start.17 = (bf16[768,768]{1,0:T(8,128)(2,1)S(1)}, bf16[768,768]{1,0:T(8,128)(2,1)}, u32[]{:S(2)}) copy-start(bf16[768,768]{1,0:T(8,128)(2,1)} %get-tuple-element.120) | copy-start | bytes 3538948
  149.7 3.6 copy-start.18
  153.3 3.3 copy-start.11
  154.0 29.4 %copy-start.19 = (bf16[512,768]{1,0:T(8,128)(2,1)}, bf16[512,768]{1,0:T(8,128)(2,1)S(1)}, u32[]{:S(2)}) copy-start(bf16[512,768]{1,0:T(8,128)(2,1)S(1)} %add_convert_fusion.2) | copy-start | bytes 2359300
  157.2 39.4 %slice-start.5 = ((s8[4915200]{0:T(1024)(128)(4,1)}), s8[4194304]{0:T(1024)(128)(4,1)S(1)}, s32[]{:S(2)}) async-start(s8[4915200]{0:T(1024)(128)(4,1)} %bitcast.239), calls=%async_computation.14 | async-start | bytes 8388608
  183.3 8.6 %copy-start.29 = (bf16[16,64,768]{2,1,0:T(8,128)(2,1)}, bf16[16,64,768]{2,1,0:T(8,128)(2,1)S(1)}, u32[]{:S(2)}) copy-start(bf16[16,64,768]{2,1,0:T(8,128)(2,1)S(1)} %all_to_all.40) | copy-start | bytes 4718596
  183.3 13.3 %slice-start.6 = ((s8[4915200]{0:T(1024)(128)(4,1)}), s8[720896]{0:T(1024)(128)(4,1)S(1)}, s32[]{:S(2)}) async-start(s8[4915200]{0:T(1024)(128)(4,1)} %bitcast.239), calls=%async_computation.15 | async-start | bytes 1441792
  192.0 4.7 copy-start.8
  214.5 28.3 %all-to-all-start.2 = ((bf16[16,72,768]{2,1,0:T(8,128)(2,1)}), bf16[16,72,768]{2,1,0:T(8,128)(2,1)}, u32[]{:S(2)}, u32[]{:S(2)}) async-start(bf16[16,72,768]{2,1,0:T(8,128)(2,1)} %pad_maximum_fusion.6), calls=%async_computation.2 | async-start | bytes 3538944 | tf_op jit(solution)/shard_map/all_to_all | solution.py:44
  270.5 17.8 %collective-permute-start.14 = (bf16[16,128,768]{2,1,0:T(8,128)(2,1)}, bf16[16,128,768]{2,1,0:T(8,128)(2,1)}, u32[]{:S(2)}, u32[]{:S(2)}) collective-permute-start(bf16[16,128,768]{2,1,0:T(8,128)(2,1)} %pad_maximum_fusion.1), channel_id=1, source_target_pairs={{0,16},{16,0},{1,17},{17,1},{2,18},{18,2},{3,19},{19,3},{4,20},{20... | collective-permute-start | bytes 9437192 | tf_op jit(solution)/shard_map/ppermute | solution.py:29
  270.7 9.5 %copy-start.7 = (bf16[512,768]{1,0:T(8,128)(2,1)S(1)}, bf16[512,768]{1,0:T(8,128)(2,1)}, u32[]{:S(2)}) copy-start(bf16[512,768]{1,0:T(8,128)(2,1)} %copy-done.6) | copy-start | bytes 2359300
  285.0 3.3 copy-start.13
  287.6 33.7 %collective-permute-start.15 = (bf16[16,24,3072]{2,1,0:T(8,128)(2,1)}, bf16[16,24,3072]{2,1,0:T(8,128)(2,1)}, u32[]{:S(2)}, u32[]{:S(2)}) collective-permute-start(bf16[16,24,3072]{2,1,0:T(8,128)(2,1)} %bitcast.70), channel_id=1, source_target_pairs={{0,16},{16,0},{1,17},{17,1},{2,18},{18,2},{3,19},{19,3},{4,20},{20... | collective-permute-start | bytes 7077896 | tf_op jit(solution)/shard_map/ppermute | solution.py:29
  288.3 3.8 copy-start.28
  288.3 4.1 copy-start.36
  298.7 48.1 %all-to-all-start.4 = ((bf16[16,128,768]{2,1,0:T(8,128)(2,1)}), bf16[16,128,768]{2,1,0:T(8,128)(2,1)}, u32[]{:S(2)}, u32[]{:S(2)}) async-start(bf16[16,128,768]{2,1,0:T(8,128)(2,1)} %add_convert_fusion), calls=%async_computation.4 | async-start | bytes 6291456 | tf_op jit(solution)/shard_map/all_to_all | solution.py:44
  321.3 10.3 %slice-start = ((s8[13107200]{0:T(1024)(128)(4,1)}), s8[4194304]{0:T(1024)(128)(4,1)S(1)}, s32[]{:S(2)}) async-start(s8[13107200]{0:T(1024)(128)(4,1)} %bitcast.195), calls=%async_computation.9 | async-start | bytes 8388608
  321.3 10.3 %slice-start.1 = ((s8[13107200]{0:T(1024)(128)(4,1)}), s8[524288]{0:T(1024)(128)(4,1)S(1)}, s32[]{:S(2)}) async-start(s8[13107200]{0:T(1024)(128)(4,1)} %bitcast.195), calls=%async_computation.10 | async-start | bytes 1048576
  323.4 8.2 %slice-start.2 = ((s8[13107200]{0:T(1024)(128)(4,1)}), s8[4194304]{0:T(1024)(128)(4,1)S(1)}, s32[]{:S(2)}) async-start(s8[13107200]{0:T(1024)(128)(4,1)} %bitcast.195), calls=%async_computation.11 | async-start | bytes 8388608
  325.2 6.4 %slice-start.3 = ((s8[13107200]{0:T(1024)(128)(4,1)}), s8[4194304]{0:T(1024)(128)(4,1)S(1)}, s32[]{:S(2)}) async-start(s8[13107200]{0:T(1024)(128)(4,1)} %bitcast.195), calls=%async_computation.12 | async-start | bytes 8388608
  326.9 76.8 %collective-permute-start.16 = (bf16[16,24,3200]{2,1,0:T(8,128)(2,1)}, bf16[16,24,3200]{2,1,0:T(8,128)(2,1)}, u32[]{:S(2)}, u32[]{:S(2)}) collective-permute-start(bf16[16,24,3200]{2,1,0:T(8,128)(2,1)} %pad_maximum_fusion.4), channel_id=1, source_target_pairs={{0,16},{16,0},{1,17},{17,1},{2,18},{18,2},{3,19},{19,3},{4,20},{20... | collective-permute-start | bytes 7372808 | tf_op jit(solution)/shard_map/ppermute | solution.py:29
  346.9 43.6 %all-to-all-start.3 = ((bf16[16,24,3072]{2,1,0:T(8,128)(2,1)}), bf16[16,24,3072]{2,1,0:T(8,128)(2,1)}, u32[]{:S(2)}, u32[]{:S(2)}) async-start(bf16[16,24,3072]{2,1,0:T(8,128)(2,1)} %fusion.24), calls=%async_computation.3 | async-start | bytes 4718592 | tf_op jit(solution)/shard_map/all_to_all | solution.py:44
  371.0 5.1 %copy-start.10 = (bf16[2,4,408,768]{3,2,1,0:T(8,128)(2,1)}, bf16[2,4,408,768]{3,2,1,0:T(8,128)(2,1)S(1)}, u32[]{:S(2)}) copy-start(bf16[2,4,408,768]{3,2,1,0:T(8,128)(2,1)S(1)} %fusion.22) | copy-start | bytes 15040516
  372.8 42.0 %collective-permute-start.18 = (bf16[4,408,768]{2,1,0:T(8,128)(2,1)}, bf16[4,408,768]{2,1,0:T(8,128)(2,1)}, u32[]{:S(2)}, u32[]{:S(2)}) collective-permute-start(bf16[4,408,768]{2,1,0:T(8,128)(2,1)} %slice_bitcast_fusion), channel_id=1, source_target_pairs={{0,16},{16,0},{1,17},{17,1},{2,18},{18,2},{3,19},{19,3},{4,20},{20... | collective-permute-start | bytes 7520264 | tf_op jit(solution)/shard_map/ppermute | solution.py:29
  390.4 13.2 %all-to-all-start.5 = ((bf16[4,32,768]{2,1,0:T(8,128)(2,1)}), bf16[4,32,768]{2,1,0:T(8,128)(2,1)S(1)}, u32[]{:S(2)}, u32[]{:S(2)}) async-start(bf16[4,32,768]{2,1,0:T(8,128)(2,1)} %pad_maximum_fusion.9), calls=%async_computation.5 | async-start | bytes 393216 | tf_op jit(solution)/shard_map/all_to_all | solution.py:44
  408.1 40.5 %all-to-all-start.6 = ((bf16[16,24,3200]{2,1,0:T(8,128)(2,1)}), bf16[16,24,3200]{2,1,0:T(8,128)(2,1)}, u32[]{:S(2)}, u32[]{:S(2)}) async-start(bf16[16,24,3200]{2,1,0:T(8,128)(2,1)} %add_convert_fusion.1), calls=%async_computation.6 | async-start | bytes 4915200 | tf_op jit(solution)/shard_map/all_to_all | solution.py:44
  414.8 8.8 %copy-start.30 = (f32[512,768]{1,0:T(8,128)S(1)}, f32[512,768]{1,0:T(8,128)}, u32[]{:S(2)}) copy-start(f32[512,768]{1,0:T(8,128)} %get-tuple-element.162) | copy-start | bytes 4718596
  418.0 5.6 %copy-start.4 = (bf16[512,2304]{1,0:T(8,128)(2,1)S(1)}, bf16[512,2304]{1,0:T(8,128)(2,1)}, u32[]{:S(2)}) copy-start(bf16[512,2304]{1,0:T(8,128)(2,1)} %copy-done.2) | copy-start | bytes 7077892
  418.1 16.7 %collective-permute-start.19 = (bf16[408,768]{1,0:T(8,128)(2,1)S(1)}, bf16[408,768]{1,0:T(8,128)(2,1)S(1)}, u32[]{:S(2)}, u32[]{:S(2)}) collective-permute-start(bf16[408,768]{1,0:T(8,128)(2,1)S(1)} %get-tuple-element.127), channel_id=1, source_target_pairs={{0,1},{1,2},{2,3},{3,0},{4,5},{5,6},{6,7},{7,4},{8,9},{9,10},{10,1... | collective-permute-start | bytes 1880072 | tf_op jit(solution)/shard_map/ppermute | solution.py:29
  418.8 27.5 %collective-permute-start.21 = (bf16[408,768]{1,0:T(8,128)(2,1)S(1)}, bf16[408,768]{1,0:T(8,128)(2,1)S(1)}, u32[]{:S(2)}, u32[]{:S(2)}) collective-permute-start(bf16[408,768]{1,0:T(8,128)(2,1)S(1)} %get-tuple-element.128), channel_id=1, source_target_pairs={{0,3},{1,0},{2,1},{3,2},{4,7},{5,4},{6,5},{7,6},{8,11},{9,8},{10,9... | collective-permute-start | bytes 1880072 | tf_op jit(solution)/shard_map/ppermute | solution.py:29
  421.5 26.3 %collective-permute-start.20 = (bf16[408,768]{1,0:T(8,128)(2,1)S(1)}, bf16[408,768]{1,0:T(8,128)(2,1)S(1)}, u32[]{:S(2)}, u32[]{:S(2)}) collective-permute-start(bf16[408,768]{1,0:T(8,128)(2,1)S(1)} %get-tuple-element.129), channel_id=1, source_target_pairs={{0,2},{1,3},{2,0},{3,1},{4,6},{5,7},{6,4},{7,5},{8,10},{9,11},{10,... | collective-permute-start | bytes 1880072 | tf_op jit(solution)/shard_map/ppermute | solution.py:29
  423.5 6.0 %collective-permute-start.17 = (f32[8,128]{1,0:T(8,128)S(1)}, f32[8,128]{1,0:T(8,128)S(1)}, u32[]{:S(2)}, u32[]{:S(2)}) collective-permute-start(f32[8,128]{1,0:T(8,128)S(1)} %broadcast_in_dim.114), channel_id=1, source_target_pairs={{0,16},{16,0},{1,17},{17,1},{2,18},{18,2},{3,19},{19,3},{4,20},{20... | collective-permute-start | bytes 12296 | tf_op jit(solution)/shard_map/ppermute | solution.py:29
  430.7 20.0 %slice-start.4 = ((bf16[120,768]{1,0:T(8,128)(2,1)}), bf16[24,768]{1,0:T(8,128)(2,1)S(1)}, s32[]{:S(2)}) async-start(bf16[120,768]{1,0:T(8,128)(2,1)} %copy-done.31), calls=%async_computation.13 | async-start | bytes 73728 | tf_op jit(solution)/shard_map/slice | solution.py:571
  451.6 11.1 %all-to-all-start.7 = ((bf16[4,6,7040]{2,1,0:T(8,128)(2,1)}), bf16[4,6,7040]{2,1,0:T(8,128)(2,1)S(1)}, u32[]{:S(2)}, u32[]{:S(2)}) async-start(bf16[4,6,7040]{2,1,0:T(8,128)(2,1)} %reshape.472), calls=%async_computation.7 | async-start | bytes 901120 | tf_op jit(solution)/shard_map/all_to_all | solution.py:44
  (12 other events, 26.7 us)
Sparse Core Ops, SparseCore 0:
  27.6 72.4 all-gather.1

commit v5 on v4

--- a/solution.py
+++ b/solution.py
@@ -400,16 +400,15 @@
     label_w = matmul(hit.astype(BF), vocab_w)
     label_b = jnp.sum(jnp.where(hit, vocab_b, 0.0), axis=1, keepdims=True)
     label_w = jnp.concatenate([label_w, jnp.pad(label_b, ((0, 0), (0, 127)))], axis=1)
-    label_w = swap(label_w.astype(BF).reshape(NY * NZ, rows, -1), ("y", "z"))
-    label_w = jnp.sum(label_w.astype(F32), axis=0)
-    label_w, label_b = label_w[:, :width], label_w[:, width]
+    label_w = label_w.astype(BF).reshape(NY * NZ, rows, -1)
     positions = mask_pos.reshape(micro, -1)
     shifted = jnp.where(
         positions >= 0, positions + block * jnp.arange(micro, dtype=jnp.int32)[:, None], -1
     ).reshape(-1)
     select = (shifted[:, None] == jnp.arange(tokens, dtype=jnp.int32)[None, :]).astype(BF)
 
-    layer, label_w, label_b, vocab_w, select = after(layer, label_w, label_b, vocab_w, select)
+    layer, label_w, vocab_w, select = after(layer, label_w, vocab_w, select)
+    label_w = swap(label_w, ("y", "z"))
     ends = [NX * width, w_expand.shape[1], 3 * width, width, width, 128]
     ends = [sum(ends[: i + 1]) for i in range(len(ends))]
     expand_full = layer[:, ends[0] : ends[1]]
@@ -452,6 +451,9 @@
     settled, normed2, inverse2 = layer_norm(second, ffn_gain, ffn_shift)
     settled_low = settled.astype(BF)
 
+    select, label_w = after(select, label_w)
+    label_w = jnp.sum(label_w.astype(F32), axis=0)
+    label_w, label_b = label_w[:, :width], label_w[:, width]
     picked = matmul(select, settled_low).astype(BF)
     dense_pre = matmul(picked, dense_full) + b_dense
     head_val, normed3, inverse3 = layer_norm(gelu_value(dense_pre), dense_gain, dense_shift)
@@ -507,22 +509,20 @@
     tall_pair = sum_cores([blocks(g_shrink), blocks(g_dense), loss_row], 1)
     g_shrink_bias = column_sum(dffn)
     dpre = (matmul_nt(dffn, shrink_full) * gelu_slope(pre)).astype(BF)
+    dpre, tall_mine = after(dpre, add_cores(tall_pair))
     g_expand = matmul_tn(first_low, dpre)
     wide_pair = sum_cores([blocks(g_expand)], 2)
     g_expand_bias = column_sum(dpre)
-    dpre, tall_mine = after(dpre, add_cores(tall_pair))
     dfirst = dsecond + matmul_nt(dpre, expand_full)
     g_attn_gain = column_sum(dfirst * normed1)
     g_attn_shift = column_sum(dfirst)
     dresidual = norm_back(dfirst, normed1, inverse1, attn_gain)
     dbranch = dresidual.astype(BF)
-    tall_all = swap(tall_mine, ("y", "z")).astype(F32)
-    tall_sum = jnp.sum(tall_all[:, :120], axis=0).astype(BF)
-    loss_row = split_three(jnp.sum(tall_all[:, 120, :3]))
+    tall_all = swap(tall_mine, ("y", "z"))
     g_attn = matmul_tn(attended, dbranch)
     g_attn_bias = column_sum(dbranch)
     dfused, fused_sum = attention_backward(dbranch, qkv, probs, layer, attn_block)
-    dfused, got = after(dfused, wide_pair[1])
+    dfused, got, tall_all = after(dfused, wide_pair[1], tall_all)
     wide_mine = add_cores((wide_pair[0], got))
     g_qkv = matmul_tn(x, dfused)
     g_query, g_value = fused_sum[0, :width], fused_sum[0, 2 * width :]
@@ -559,27 +559,32 @@
     sums = jnp.concatenate([after(sums)[0].T, g_expand_bias.reshape(width, -1)], axis=1)
     sums = jnp.pad(sums, ((0, 0), (0, 128 - sums.shape[1])))
     wide = sum_yz(wide_mine)
-    tall = sum_x(
-        jnp.concatenate(
-            [tall_sum[:96].reshape(NX, -1, width), jnp.broadcast_to(loss_row, (NX, 8, width))],
-            axis=1,
-        )
-    )
     last_pair = sum_cores([blocks(g_qkv), blocks(g_attn), blocks(sums)], 2)
-    last_pair, wide, tall = after(last_pair, wide, tall)
+    last_pair, wide, tall_all = after(last_pair, wide, tall_all)
+    tall = jnp.sum(tall_all[:, :120].astype(F32), axis=0).astype(BF)
+    loss_row = split_three(jnp.sum(tall_all[:, 120, :3].astype(F32)))[:128]
+    tall_low = tall[:96].reshape(NX, 4, 6, width).transpose(0, 2, 1, 3).reshape(NX, 6, 4 * width)
+    early = jnp.concatenate(
+        [
+            wide.reshape(NX, 6, -1),
+            tall_low,
+            tall[96:].reshape(NX, 6, width),
+            jnp.broadcast_to(loss_row, (NX, 6, 128)),
+        ],
+        axis=2,
+    )
     last = sum_yz(add_cores(last_pair))
-    last = jnp.concatenate([last, tall_sum[96:120], wide], axis=1)
-    last = sum_x(last.reshape(NX, -1, last.shape[1]))
-    ends = [3 * width, width, 128, width, w_expand.shape[1]]
+    last = sum_x(jnp.concatenate([early, last.reshape(NX, 6, -1)], axis=2))
+    ends = [w_expand.shape[1], 4 * width, width, 128, 3 * width, width, 128]
     ends = [sum(ends[: i + 1]) for i in range(len(ends))]
-    g_qkv = last[:, : ends[0]]
-    g_attn = last[:, ends[0] : ends[1]]
-    sums = last[:, ends[1] : ends[2]]
-    g_dense = last[:, ends[2] : ends[3]]
-    g_expand = last[:, ends[3] :]
-    g_shrink = tall[:24]
-    loss = jnp.full((8, 128), jnp.sum(tall[24, :3]))
+    g_expand = last[:, : ends[0]]
+    g_shrink = last[:, ends[0] : ends[1]].reshape(6, 4, width).transpose(1, 0, 2).reshape(24, width)
+    g_dense = last[:, ends[1] : ends[2]]
+    loss = jnp.full((8, 128), jnp.sum(last[0, ends[2] : ends[2] + 3]))
     loss = (loss + give(loss, "c", 1))[0, 0]
+    g_qkv = last[:, ends[3] : ends[4]]
+    g_attn = last[:, ends[4] : ends[5]]
+    sums = last[:, ends[5] :]
     return (
         settled_low.reshape(hidden_in.shape),
         loss,

time: 480 us -> 490 us (1.021)
  local copies, waits for them, and re-layouts: 54 us -> 62.6 us
  starting transfers between devices: 69.7 us -> 61.4 us
  other arithmetic: 75.5 us -> 83.1 us
    all_gather x1, waiting for transfers between devices: 0.02 us -> 18.7 us  [body(): lax.all_gather(jnp.concatenate([tall, fused], axis=1), ('y', 'c', 'z'), a...]
    all_to_all x7 -> x6, waiting for transfers between devices: 66.6 us -> 51.6 us  [swap(): return lax.all_to_all(array, axes, 0, 0, tiled=True)]
    all_to_all x7 -> x6, starting transfers between devices: 45.2 us -> 34.3 us  [swap(): return lax.all_to_all(array, axes, 0, 0, tiled=True)]
    reduce_sum x5 -> x6, other arithmetic: 13.2 us -> 21.6 us  [column_sum(): return jnp.sum(values, axis=0, dtype=F32)]
    ppermute x14, waiting for transfers between devices: 29.7 us -> 22.5 us  [fetch(): return lax.ppermute(array, axis, [((i + k) % n, i) for i in range(n)])]
    unnamed x117 -> x177, local copies, waits for them, and re-layouts: 20.9 us -> 22.8 us
  transfers between devices with their start and end apart: 30 -> 29, of which waited for: 15 -> 13; matrix products, arithmetic and copies ran while one was open for 26% -> 26% of each run, Pallas kernels for 3% -> 5%
where the time goes in v5:
time: 490 us; the launch traced here: 482 us
  waiting for transfers between devices  109 us (22%)
  matrix products  87.5 us (18%)
  other arithmetic  83.1 us (17%)
  local copies, waits for them, and re-layouts  62.6 us (13%)
  starting transfers between devices  61.4 us (13%)
  between operations  27.5 us (6%)
  blocking collectives  27.1 us (6%)
  Pallas kernels  23.3 us (5%)
    all_to_all x6, waiting for transfers between devices, swap(): return lax.all_to_all(array, axes, 0, 0, tiled=True)  51.6 us
    all_to_all x6, starting transfers between devices, swap(): return lax.all_to_all(array, axes, 0, 0, tiled=True)  34.3 us
    dot_general x4, matrix products, matmul_nt(): lax.dot_general(left, right, (((1,), (1,)), ((), ())), preferred_element_...  31.6 us
    dot_general x6, matrix products, matmul(): return jnp.dot(left, right, preferred_element_type=F32)  30 us
    all_to_all x1, blocking collectives, swap(): return lax.all_to_all(array, axes, 0, 0, tiled=True)  27.1 us
    dot_general x7, matrix products, matmul_tn(): lax.dot_general(left, right, (((0,), (0,)), ((), ())), preferred_element_...  25.9 us
    unnamed x177, local copies, waits for them, and re-layouts  22.8 us
    ppermute x14, waiting for transfers between devices, fetch(): return lax.ppermute(array, axis, [((i + k) % n, i) for i in range(n)])  22.5 us
  transfers between devices with their start and end apart: 29, of which 13 were waited for; matrix products, arithmetic and copies ran while one was open for 26% of the time, Pallas kernels for 5%

profile of v5, /device:TPU:0, one launch (start us, length us, event | category | flops | bytes accessed | tf_op | source)
XLA Modules:
  0.0 481.6 jit_solution(10517411110938578043)
XLA Ops:
  7.2 2.9 collective-permute-start
  10.2 2.3 collective-permute-start.1
  21.4 2.0 collective-permute-start.3
  24.2 2.0 collective-permute-done.3
  27.4 2.7 collective-permute-start.7
  30.1 1.9 collective-permute-start.6
  32.2 3.1 collective-permute-start.10
  35.2 10.6 %collective-permute-done.7 = bf16[400,768]{1,0:T(8,128)(2,1)S(1)} collective-permute-done((bf16[400,768]{1,0:T(8,128)(2,1)S(1)}, bf16[400,768]{1,0:T(8,128)(2,1)S(1)}, u32[]{:S(2)}, u32[]{:S(2)}) %collective-permute-start.7) | collective-permute-done | bytes 614432 | tf_op jit(solution)/shard_map/ppermute | solution.py:24
  45.8 2.6 collective-permute-start.11
  48.5 9.1 %collective-permute-done.6 = bf16[400,768]{1,0:T(8,128)(2,1)S(1)} collective-permute-done((bf16[400,768]{1,0:T(8,128)(2,1)S(1)}, bf16[400,768]{1,0:T(8,128)(2,1)S(1)}, u32[]{:S(2)}, u32[]{:S(2)}) %collective-permute-start.6) | collective-permute-done | bytes 614432 | tf_op jit(solution)/shard_map/ppermute | solution.py:24
  68.5 3.3 constant_dynamic-update-slice_fusion.13
  71.7 8.1 %fusion.34 = bf16[16,64,768]{2,1,0:T(8,128)(2,1)S(1)} fusion(bf16[3200,768,1]{1,0,2:T(8,128)(2,1)} %bitcast.243, s32[3200]{0:T(1024)S(1)} %add.385, s32[16,64]{1,0:T(8,128)S(1)} %copy.62), kind=kOutput, calls=%fused_computation.60 | convolution fusion | flops 5037228032 | bytes 6504960 | tf_op jit(solution)/shard_map/dot_general | solution.py:128
  81.3 18.7 %all-gather.2.cloned.1.call-done.wq_ref.wk_ref.wv_ref.wa_ref = bf16[768,10112]{1,0:T(8,128)(2,1)} async-done(((bf16[24,10112]{1,0:T(8,128)(2,1)}), bf16[768,10112]{1,0:T(8,128)(2,1)}) %all-gather.2.cloned.1.call-update) | async-done | bytes 15532048 | tf_op jit(solution)/shard_map/all_gather | solution.py:362
  103.9 4.7 fusion.86
  108.5 5.6 %all-to-all-start = ((bf16[16,64,896]{2,1,0:T(8,128)(2,1)}), bf16[16,64,896]{2,1,0:T(8,128)(2,1)}, u32[]{:S(2)}, u32[]{:S(2)}) async-start(bf16[16,64,896]{2,1,0:T(8,128)(2,1)} %pad_maximum_fusion.5), calls=%async_computation | async-start | bytes 3670016 | tf_op jit(solution)/shard_map/all_to_all | solution.py:44
  114.4 11.1 %shard_map.408 = (bf16[512,2304]{1,0:T(8,128)(2,1)}, bf16[2,12,256,256]{3,2,1,0:T(8,128)(2,1)}, bf16[512,768]{1,0:T(8,128)(2,1)S(1)}, f32[512,768]{1,0:T(8,128)S...) custom-call(bf16[512,768]{1,0:T(8,128)(2,1)S(1)} %bitcast.198, ...), custom_call_target="tpu_custom_call" | custom-call | flops 4000000000 | bytes 16000000 | tf_op jit(solution)/shard_map/pallas_call | solution.py:209
  125.5 7.5 %multiply_convert_fusion = (bf16[512,3072]{1,0:T(8,128)(2,1)S(1)}, f32[512,3072]{1,0:T(8,128)}) fusion(f32[3072]{0:T(1024)S(1)} %reshape.498, bf16[512,768]{1,0:T(8,128)(2,1)S(1)} %get-tuple-element.49, bf16[768,10112]{1,0:T(8,128)(2,1)} %all-gather.2.cloned.1.call-done.wq_ref.wk_ref.wv_ref.wa_ref), kind=kOutput, calls=%fused_computation.30 | convolution fusion | flops 2425356288 | bytes 14954496 | tf_op jit(solution)/shard_map/dot_general | solution.py:128
  134.6 2.7 fusion.90
  138.9 3.3 all-to-all-done
  145.5 2.4 fusion.85
  149.1 27.1 %all_to_all.35 = bf16[16,64,768]{2,1,0:T(8,128)(2,1)S(1)} all-to-all(bf16[16,64,768]{2,1,0:T(8,128)(2,1)S(1)} %broadcast_in_dim.106), channel_id=1, replica_groups=mesh['y'=4,'c'=2,'z'=4,'x'=4] {'y','z'}, dimensions={0} | all-to-all | bytes 3145728 | tf_op jit(solution)/shard_map/all_to_all | solution.py:44
  176.2 8.6 %add_reduce_fusion = (f32[1024]{0:T(1024)S(1)}, f32[1024,3200]{1,0:T(8,128)S(1)}) fusion(f32[3200]{0:T(1024)S(1)} %reshape.497, bf16[1024,768]{1,0:T(8,128)(2,1)S(1)} %bitcast.230, bf16[3200,768]{1,0:T(8,128)(2,1)} %bitcast.244), kind=kOutput, calls=%fused_computation.10 | convolution fusion | flops 5039717376 | bytes 19612160 | tf_op jit(solution)/shard_map/dot_general | solution.py:136
  184.8 4.8 copy-done.9
  189.6 7.8 %fusion.31 = bf16[1024,768]{1,0:T(8,128)(2,1)} fusion(bf16[3200,768]{1,0:T(8,128)(2,1)S(1)} %bitcast.247, f32[1024,3200]{1,0:T(8,128)S(1)} %get-tuple-element.164, f32[1024]{0:T(1024)S(1)} %get-tuple-element.163, f32[3200]{0:T(1024)S(1)} %reshape.497, s32[3200]{0:T(1024)S(1)} %add.385, s32[1024]{0:T(1024)S(1)} %eq.74), kind=kOutput, calls=%fused_computation.59 | convolution fusion | flops 5050335232 | bytes 19629056 | tf_op jit(solution)/shard_map/dot_general | solution.py:128
  197.4 7.0 %fusion.7 = f32[1024]{0:T(1024)S(1)} fusion(f32[1024,3200]{1,0:T(8,128)} %copy-done.9, f32[1024]{0:T(1024)S(1)} %get-tuple-element.163, f32[3200]{0:T(1024)S(1)} %reshape.497), kind=kLoop, calls=%fused_computation.14 | loop fusion | flops 9829376 | bytes 13128192 | tf_op jit(solution)/shard_map/reduce_sum | solution.py:467
  204.5 2.7 pad_maximum_fusion.6
  207.3 4.6 all-to-all-start.2
  215.3 21.4 %all-to-all-done.2 = bf16[16,72,768]{2,1,0:T(8,128)(2,1)} async-done(((bf16[16,72,768]{2,1,0:T(8,128)(2,1)}), bf16[16,72,768]{2,1,0:T(8,128)(2,1)}, u32[]{:S(2)}, u32[]{:S(2)}) %all-to-all-start.2) | async-done | bytes 1769504 | tf_op jit(solution)/shard_map/all_to_all | solution.py:44
  241.7 1.9 multiply_reduce_fusion.13
  257.8 3.9 multiply_reduce_fusion.1
  261.7 2.1 convert_reduce_fusion.1
  264.0 2.9 convolution_convert_fusion.3
  268.7 1.9 pad_maximum_fusion.1
  270.9 10.7 %fusion.21 = bf16[512,3072]{1,0:T(8,128)(2,1)} fusion(f32[512,3072]{1,0:T(8,128)} %get-tuple-element.159, bf16[3072,768]{1,0:T(8,128)(2,1)} %bitcast.212, f32[3072]{0:T(1024)S(1)} %copy-done.51, f32[512,768]{1,0:T(8,128)S(1)} %copy-done.27), kind=kOutput, calls=%fused_computation.28 | convolution fusion | flops 2433613824 | bytes 15740928 | tf_op jit(solution)/shard_map/dot_general | solution.py:136
  281.7 3.6 add_convert_fusion
  285.3 4.6 all-to-all-start.3
  289.9 4.8 convolution_convert_fusion.2
  294.8 2.7 constant_dynamic-slice_fusion
  298.8 6.4 %multiply_reduce_fusion.2 = (bf16[768]{0:T(1024)(128)(2,1)S(1)}, f32[512]{0:T(512)S(1)}, f32[512]{0:T(512)S(1)}, bf16[768]{0:T(1024)(128)(2,1)S(1)}, f32[512,768]{1,0:T(8,128)}) fusion(f32[512,768]{1,0:T(8,128)S(1)} %get-tuple-element.56, f32[768]{0:T(1024)S(1)} %copy-done.47, f32[512,768]{1,0:T(8,128)S(1)} %copy-done.28, ...), kind=kOutput, calls=%fused_computation.64 | convolution fusion | flops 2419062272 | bytes 12593152 | tf_op jit(solution)/shard_map/dot_general | solution.py:136
  305.2 2.7 reduce.7
  308.5 2.3 convert_reduce_fusion.2
  310.8 12.3 %shard_map.409 = (bf16[512,2304]{1,0:T(8,128)(2,1)S(1)}, f32[1,2304]{1,0:T(1,128)S(1)}) custom-call(bf16[512,768]{1,0:T(8,128)(2,1)S(1)} %get-tuple-element.113.dbranch_ref, bf16[512,2304]{1,0:T(8,128)(2,1)S(1)} %copy-done, bf16[2,12,256,256]{3,2,1,0:T(8,128)(2,1)} %get-tuple-element.59.probs_ref, ...), custom_call_target="tpu_custom_call" | custom-call | flops 3000000000 | bytes 10000000 | tf_op jit(solution)/shard_map/pallas_call | solution.py:289
  325.6 1.9 convolution_convert_fusion.4
  328.7 5.3 %all-to-all-done.3 = bf16[16,128,768]{2,1,0:T(8,128)(2,1)} async-done(((bf16[16,128,768]{2,1,0:T(8,128)(2,1)}), bf16[16,128,768]{2,1,0:T(8,128)(2,1)}, u32[]{:S(2)}, u32[]{:S(2)}) %all-to-all-start.3) | async-done | bytes 3145760 | tf_op jit(solution)/shard_map/all_to_all | solution.py:44
  334.0 5.5 %convolution_convert_fusion.1 = bf16[2304,768]{0,1:T(8,128)(2,1)} fusion(bf16[512,2304]{1,0:T(8,128)(2,1)} %copy-done.5, bf16[512,768]{1,0:T(8,128)(2,1)S(1)} %bitcast.199), kind=kOutput, calls=%fused_computation.32 | convolution fusion | flops 1813708800 | bytes 6684672 | tf_op jit(solution)/shard_map/dot_general | solution.py:132
  339.6 11.0 %fusion.80 = (bf16[3200]{0:T(1024)(128)(2,1)S(1)}, bf16[1024,3200]{1,0:T(8,128)(2,1)}) fusion(f32[1024]{0:T(1024)S(1)} %copy-done.49, s32[3200]{0:T(1024)S(1)} %add.385, s32[1024]{0:T(1024)S(1)} %eq.74, f32[1024]{0:T(1024)S(1)} %get-tuple-element.163, f32[1024,3200]{1,0:T(8,128)} %copy-done.9, f32[3200]{0:T(1024)S(1)} %reshape.497, ...), kind=kLoop, calls=%fused_computation.261 | loop fusion | flops 26211200 | bytes 19709184 | tf_op jit(solution)/shard_map/reduce_sum | solution.py:124
  350.7 3.9 fusion.24
  354.6 10.6 %all-to-all-start.4 = ((bf16[16,24,3072]{2,1,0:T(8,128)(2,1)}), bf16[16,24,3072]{2,1,0:T(8,128)(2,1)}, u32[]{:S(2)}, u32[]{:S(2)}) async-start(bf16[16,24,3072]{2,1,0:T(8,128)(2,1)} %fusion.24), calls=%async_computation.4 | async-start | bytes 4718592 | tf_op jit(solution)/shard_map/all_to_all | solution.py:44
  366.2 3.3 pad_maximum_fusion.4
  369.5 6.3 %convolution_convert_fusion = bf16[3200,768]{1,0:T(8,128)(2,1)S(1)} fusion(bf16[1024,3200]{1,0:T(8,128)(2,1)S(1)} %bitcast.205, bf16[1024,768]{1,0:T(8,128)(2,1)S(1)} %bitcast.231), kind=kOutput, calls=%fused_computation.15 | convolution fusion | flops 5035622400 | bytes 13041664 | tf_op jit(solution)/shard_map/dot_general | solution.py:132
  376.2 2.2 copy-done.10
  380.8 17.9 %all-to-all-done.4 = bf16[16,24,3072]{2,1,0:T(8,128)(2,1)} async-done(((bf16[16,24,3072]{2,1,0:T(8,128)(2,1)}), bf16[16,24,3072]{2,1,0:T(8,128)(2,1)}, u32[]{:S(2)}, u32[]{:S(2)}) %all-to-all-start.4) | async-done | bytes 2359328 | tf_op jit(solution)/shard_map/all_to_all | solution.py:44
  398.7 2.1 reduce_sum.355
  400.8 3.8 add_convert_fusion.1
  404.6 4.7 all-to-all-start.5
  409.3 5.9 %fusion.37 = f32[512,768]{1,0:T(8,128)} fusion(bf16[512,2304]{1,0:T(8,128)(2,1)} %copy-done.5, bf16[768,10112]{1,0:T(8,128)(2,1)} %all-gather.2.cloned.1.call-done.wq_ref.wk_ref.wv_ref.wa_ref, f32[512]{0:T(512)S(1)} %copy-done.53, f32[512,768]{1,0:T(8,128)S(1)} %copy-done.2, f32[512]{0:T(512)S(1)} %copy-done.56, f32[512]{0:T(512)S(1)} %copy-done.58, ...), kind=kOutput, calls=%fused_computation.76 | convolution fusion | flops 1814298624 | bytes 10626048 | tf_op jit(solution)/shard_map/dot_general | solution.py:136
  421.5 2.2 slice_reduce_fusion
  427.2 3.1 fusion.23
  433.0 1.8 collective-permute-start.21
  437.2 3.7 all-to-all-done.5
  440.9 2.0 reduce_sum.358
  443.6 4.2 all-to-all-start.6
  447.9 9.8 %collective-permute-done.19 = bf16[408,768]{1,0:T(8,128)(2,1)} collective-permute-done((bf16[408,768]{1,0:T(8,128)(2,1)}, bf16[408,768]{1,0:T(8,128)(2,1)}, u32[]{:S(2)}, u32[]{:S(2)}) %collective-permute-start.19) | collective-permute-done | bytes 626720 | tf_op jit(solution)/shard_map/ppermute | solution.py:29
  457.7 4.7 collective-permute-done.21
  (360 shorter events, 85.0 us)
Async XLA Ops:
  7.2 92.8 %all-gather.2.cloned.1.call-start = ((), (), s32[]{:S(2)}) async-start(), calls=%async_computation.7 | async-start | bytes 16017408 | tf_op jit(solution)/shard_map/all_gather | solution.py:362
  7.2 14.1 %collective-permute-start = (bf16[24,768]{1,0:T(8,128)(2,1)}, bf16[24,768]{1,0:T(8,128)(2,1)S(1)}, u32[]{:S(2)}, u32[]{:S(2)}) collective-permute-start(bf16[24,768]{1,0:T(8,128)(2,1)} %param.40), channel_id=1, source_target_pairs={{1,0},{2,1},{3,2},{0,3},{5,4},{6,5},{7,6},{4,7},{9,8},{10,9},{11,1... | collective-permute-start | bytes 110600 | tf_op jit(solution)/shard_map/ppermute | solution.py:24
  10.1 13.2 %collective-permute-start.2 = (bf16[24,768]{1,0:T(8,128)(2,1)}, bf16[24,768]{1,0:T(8,128)(2,1)S(1)}, u32[]{:S(2)}, u32[]{:S(2)}) collective-permute-start(bf16[24,768]{1,0:T(8,128)(2,1)} %param.40), channel_id=1, source_target_pairs={{3,0},{0,1},{1,2},{2,3},{7,4},{4,5},{5,6},{6,7},{11,8},{8,9},{9,10... | collective-permute-start | bytes 110600 | tf_op jit(solution)/shard_map/ppermute | solution.py:24
  10.2 13.2 %collective-permute-start.1 = (bf16[24,768]{1,0:T(8,128)(2,1)}, bf16[24,768]{1,0:T(8,128)(2,1)S(1)}, u32[]{:S(2)}, u32[]{:S(2)}) collective-permute-start(bf16[24,768]{1,0:T(8,128)(2,1)} %param.40), channel_id=1, source_target_pairs={{2,0},{3,1},{0,2},{1,3},{6,4},{7,5},{4,6},{5,7},{10,8},{11,9},{8,1... | collective-permute-start | bytes 110600 | tf_op jit(solution)/shard_map/ppermute | solution.py:24
  15.7 11.7 %copy-start.21 = (bf16[768,400]{0,1:T(8,128)(2,1)S(1)}, bf16[768,400]{0,1:T(8,128)(2,1)}, u32[]{:S(2)}) copy-start(bf16[768,400]{0,1:T(8,128)(2,1)} %param.48) | copy-start | bytes 1843204
  15.7 16.5 %copy-start.65 = (bf16[400]{0:T(512)(128)(2,1)S(1)}, bf16[400]{0:T(512)(128)(2,1)}, u32[]{:S(2)}) copy-start(bf16[400]{0:T(512)(128)(2,1)} %param.49) | copy-start | bytes 2404
  18.0 8.3 %collective-permute-start.5 = (bf16[6,7040]{1,0:T(8,128)(2,1)S(1)}, bf16[6,7040]{1,0:T(8,128)(2,1)S(1)}, u32[]{:S(2)}, u32[]{:S(2)}) collective-permute-start(bf16[6,7040]{1,0:T(8,128)(2,1)S(1)} %constant_dynamic-update-slice_fusion.8), channel_id=1, source_target_pairs={{3,0},{0,1},{1,2},{2,3},{7,4},{4,5},{5,6},{6,7},{11,8},{8,9},{9,10... | collective-permute-start | bytes 253448 | tf_op jit(solution)/shard_map/ppermute | solution.py:24
  19.8 6.5 %collective-permute-start.4 = (bf16[6,7040]{1,0:T(8,128)(2,1)S(1)}, bf16[6,7040]{1,0:T(8,128)(2,1)S(1)}, u32[]{:S(2)}, u32[]{:S(2)}) collective-permute-start(bf16[6,7040]{1,0:T(8,128)(2,1)S(1)} %constant_dynamic-update-slice_fusion.8), channel_id=1, source_target_pairs={{2,0},{3,1},{0,2},{1,3},{6,4},{7,5},{4,6},{5,7},{10,8},{11,9},{8,1... | collective-permute-start | bytes 253448 | tf_op jit(solution)/shard_map/ppermute | solution.py:24
  21.4 4.9 %collective-permute-start.3 = (bf16[6,7040]{1,0:T(8,128)(2,1)S(1)}, bf16[6,7040]{1,0:T(8,128)(2,1)S(1)}, u32[]{:S(2)}, u32[]{:S(2)}) collective-permute-start(bf16[6,7040]{1,0:T(8,128)(2,1)S(1)} %constant_dynamic-update-slice_fusion.8), channel_id=1, source_target_pairs={{1,0},{2,1},{3,2},{0,3},{5,4},{6,5},{7,6},{4,7},{9,8},{10,9},{11,1... | collective-permute-start | bytes 253448 | tf_op jit(solution)/shard_map/ppermute | solution.py:24
  26.6 32.9 %copy-start.64 = (s32[2,1,16,2]{2,3,1,0:T(2,128)S(1)}, s32[2,1,16,2]{2,3,1,0:T(2,128)}, u32[]{:S(2)}) copy-start(s32[2,1,16,2]{2,3,1,0:T(2,128)} %param.28) | copy-start | bytes 772
  27.4 18.4 %collective-permute-start.7 = (bf16[400,768]{1,0:T(8,128)(2,1)S(1)}, bf16[400,768]{1,0:T(8,128)(2,1)S(1)}, u32[]{:S(2)}, u32[]{:S(2)}) collective-permute-start(bf16[400,768]{1,0:T(8,128)(2,1)S(1)} %bitcast.218), channel_id=1, source_target_pairs={{2,0},{3,1},{0,2},{1,3},{6,4},{7,5},{4,6},{5,7},{10,8},{11,9},{8,1... | collective-permute-start | bytes 1843208 | tf_op jit(solution)/shard_map/ppermute | solution.py:24
  30.1 27.4 %collective-permute-start.6 = (bf16[400,768]{1,0:T(8,128)(2,1)S(1)}, bf16[400,768]{1,0:T(8,128)(2,1)S(1)}, u32[]{:S(2)}, u32[]{:S(2)}) collective-permute-start(bf16[400,768]{1,0:T(8,128)(2,1)S(1)} %bitcast.219), channel_id=1, source_target_pairs={{1,0},{2,1},{3,2},{0,3},{5,4},{6,5},{7,6},{4,7},{9,8},{10,9},{11,1... | collective-permute-start | bytes 1843208 | tf_op jit(solution)/shard_map/ppermute | solution.py:24
  32.0 25.6 %collective-permute-start.8 = (bf16[400,768]{1,0:T(8,128)(2,1)S(1)}, bf16[400,768]{1,0:T(8,128)(2,1)S(1)}, u32[]{:S(2)}, u32[]{:S(2)}) collective-permute-start(bf16[400,768]{1,0:T(8,128)(2,1)S(1)} %bitcast.220), channel_id=1, source_target_pairs={{3,0},{0,1},{1,2},{2,3},{7,4},{4,5},{5,6},{6,7},{11,8},{8,9},{9,10... | collective-permute-start | bytes 1843208 | tf_op jit(solution)/shard_map/ppermute | solution.py:24
  32.2 29.0 %collective-permute-start.10 = (bf16[400]{0:T(512)(128)(2,1)S(1)}, bf16[400]{0:T(512)(128)(2,1)S(1)}, u32[]{:S(2)}, u32[]{:S(2)}) collective-permute-start(bf16[400]{0:T(512)(128)(2,1)S(1)} %copy-done.65), channel_id=1, source_target_pairs={{1,0},{2,1},{3,2},{0,3},{5,4},{6,5},{7,6},{4,7},{9,8},{10,9},{11,1... | collective-permute-start | bytes 2408 | tf_op jit(solution)/shard_map/ppermute | solution.py:24
  35.2 26.0 %collective-permute-start.12 = (bf16[400]{0:T(512)(128)(2,1)S(1)}, bf16[400]{0:T(512)(128)(2,1)S(1)}, u32[]{:S(2)}, u32[]{:S(2)}) collective-permute-start(bf16[400]{0:T(512)(128)(2,1)S(1)} %copy-done.65), channel_id=1, source_target_pairs={{3,0},{0,1},{1,2},{2,3},{7,4},{4,5},{5,6},{6,7},{11,8},{8,9},{9,10... | collective-permute-start | bytes 2408 | tf_op jit(solution)/shard_map/ppermute | solution.py:24
  45.8 15.4 %collective-permute-start.11 = (bf16[400]{0:T(512)(128)(2,1)S(1)}, bf16[400]{0:T(512)(128)(2,1)S(1)}, u32[]{:S(2)}, u32[]{:S(2)}) collective-permute-start(bf16[400]{0:T(512)(128)(2,1)S(1)} %copy-done.65), channel_id=1, source_target_pairs={{2,0},{3,1},{0,2},{1,3},{6,4},{7,5},{4,6},{5,7},{10,8},{11,9},{8,1... | collective-permute-start | bytes 2408 | tf_op jit(solution)/shard_map/ppermute | solution.py:24
  59.3 9.2 %collective-permute-start.9 = (bf16[4,400,768]{2,1,0:T(8,128)(2,1)}, bf16[4,400,768]{2,1,0:T(8,128)(2,1)}, u32[]{:S(2)}, u32[]{:S(2)}) collective-permute-start(bf16[4,400,768]{2,1,0:T(8,128)(2,1)} %pad_maximum_fusion.2), channel_id=1, source_target_pairs={{16,0},{0,16},{17,1},{1,17},{18,2},{2,18},{19,3},{3,19},{20,4},{4,... | collective-permute-start | bytes 7372808 | tf_op jit(solution)/shard_map/ppermute | solution.py:24
  59.8 84.1 %copy-start.37 = (bf16[64,512]{1,0:T(8,128)(2,1)}, bf16[64,512]{1,0:T(8,128)(2,1)S(1)}, u32[]{:S(2)}) copy-start(bf16[64,512]{1,0:T(8,128)(2,1)S(1)} %fusion.53) | copy-start | bytes 196612
  61.3 2.7 collective-permute-start.13
  108.5 5.8 %copy-start.3 = (bf16[2,256,768]{2,1,0:T(8,128)(2,1)S(1)}, bf16[2,256,768]{2,1,0:T(8,128)(2,1)}, u32[]{:S(2)}) copy-start(bf16[2,256,768]{2,1,0:T(8,128)(2,1)} %param.25) | copy-start | bytes 2359300
  108.5 33.6 %all-to-all-start = ((bf16[16,64,896]{2,1,0:T(8,128)(2,1)}), bf16[16,64,896]{2,1,0:T(8,128)(2,1)}, u32[]{:S(2)}, u32[]{:S(2)}) async-start(bf16[16,64,896]{2,1,0:T(8,128)(2,1)} %pad_maximum_fusion.5), calls=%async_computation | async-start | bytes 3670016 | tf_op jit(solution)/shard_map/all_to_all | solution.py:44
  114.4 11.1 %copy-start.50 = (f32[3072]{0:T(1024)}, f32[3072]{0:T(1024)S(1)}, u32[]{:S(2)}) copy-start(f32[3072]{0:T(1024)S(1)} %reshape.498) | copy-start | bytes 36868
  125.4 7.6 %copy-start.6 = (bf16[512,768]{1,0:T(8,128)(2,1)}, bf16[512,768]{1,0:T(8,128)(2,1)S(1)}, u32[]{:S(2)}) copy-start(bf16[512,768]{1,0:T(8,128)(2,1)S(1)} %get-tuple-element.63) | copy-start | bytes 2359300
  125.4 7.6 %copy-start.7 = (bf16[512,768]{1,0:T(8,128)(2,1)}, bf16[512,768]{1,0:T(8,128)(2,1)S(1)}, u32[]{:S(2)}) copy-start(bf16[512,768]{1,0:T(8,128)(2,1)S(1)} %get-tuple-element.49) | copy-start | bytes 2359300
  125.4 172.6 %copy-start.1 = (f32[512,768]{1,0:T(8,128)}, f32[512,768]{1,0:T(8,128)S(1)}, u32[]{:S(2)}) copy-start(f32[512,768]{1,0:T(8,128)S(1)} %get-tuple-element.56) | copy-start | bytes 4718596
  125.5 7.5 %copy-start.13 = (bf16[768,768]{1,0:T(8,128)(2,1)S(1)}, bf16[768,768]{1,0:T(8,128)(2,1)}, u32[]{:S(2)}) copy-start(bf16[768,768]{1,0:T(8,128)(2,1)} %get-tuple-element.121) | copy-start | bytes 3538948
  125.5 7.5 %copy-start.14 = (bf16[768,768]{1,0:T(8,128)(2,1)S(1)}, bf16[768,768]{1,0:T(8,128)(2,1)}, u32[]{:S(2)}) copy-start(bf16[768,768]{1,0:T(8,128)(2,1)} %get-tuple-element.122) | copy-start | bytes 3538948
  125.5 7.5 %copy-start.15 = (bf16[768,768]{1,0:T(8,128)(2,1)S(1)}, bf16[768,768]{1,0:T(8,128)(2,1)}, u32[]{:S(2)}) copy-start(bf16[768,768]{1,0:T(8,128)(2,1)} %get-tuple-element.123) | copy-start | bytes 3538948
  125.5 7.5 %copy-start.16 = (bf16[768,768]{1,0:T(8,128)(2,1)S(1)}, bf16[768,768]{1,0:T(8,128)(2,1)}, u32[]{:S(2)}) copy-start(bf16[768,768]{1,0:T(8,128)(2,1)} %get-tuple-element.124) | copy-start | bytes 3538948
  137.3 8.1 %copy-start.40 = (f32[512]{0:T(512)}, f32[512]{0:T(512)S(1)}, u32[]{:S(2)}) copy-start(f32[512]{0:T(512)S(1)} %broadcast_multiply_fusion.5) | copy-start | bytes 6148
  137.7 10.3 %copy-start.45 = (f32[512]{0:T(512)}, f32[512]{0:T(512)S(1)}, u32[]{:S(2)}) copy-start(f32[512]{0:T(512)S(1)} %add_rsqrt_fusion) | copy-start | bytes 6148
  147.9 28.2 %copy-start.62 = (f32[64]{0:T(128)}, f32[64]{0:T(128)S(1)}, u32[]{:S(2)}) copy-start(f32[64]{0:T(128)S(1)} %broadcast_multiply_fusion.8) | copy-start | bytes 772
  148.1 36.7 %copy-start.63 = (f32[64]{0:T(128)}, f32[64]{0:T(128)S(1)}, u32[]{:S(2)}) copy-start(f32[64]{0:T(128)S(1)} %add_rsqrt_fusion.1) | copy-start | bytes 772
  149.0 40.6 %slice-start.2 = ((s8[4915200]{0:T(1024)(128)(4,1)}), s8[4194304]{0:T(1024)(128)(4,1)S(1)}, s32[]{:S(2)}) async-start(s8[4915200]{0:T(1024)(128)(4,1)} %bitcast.245), calls=%async_computation.10 | async-start | bytes 8388608
  176.2 8.6 %copy-start.29 = (bf16[16,64,768]{2,1,0:T(8,128)(2,1)}, bf16[16,64,768]{2,1,0:T(8,128)(2,1)S(1)}, u32[]{:S(2)}) copy-start(bf16[16,64,768]{2,1,0:T(8,128)(2,1)S(1)} %all_to_all.35) | copy-start | bytes 4718596
  176.2 13.4 %slice-start.3 = ((s8[4915200]{0:T(1024)(128)(4,1)}), s8[720896]{0:T(1024)(128)(4,1)S(1)}, s32[]{:S(2)}) async-start(s8[4915200]{0:T(1024)(128)(4,1)} %bitcast.245), calls=%async_computation.11 | async-start | bytes 1441792
  204.5 8.0 %copy-start.39 = (s32[2,128,16,2]{1,3,2,0:T(2,128)S(1)}, s32[2,128,16,2]{1,3,2,0:T(2,128)}, u32[]{:S(2)}) copy-start(s32[2,128,16,2]{1,3,2,0:T(2,128)} %param.29) | copy-start | bytes 98308
  207.3 29.4 %all-to-all-start.2 = ((bf16[16,72,768]{2,1,0:T(8,128)(2,1)}), bf16[16,72,768]{2,1,0:T(8,128)(2,1)}, u32[]{:S(2)}, u32[]{:S(2)}) async-start(bf16[16,72,768]{2,1,0:T(8,128)(2,1)} %pad_maximum_fusion.6), calls=%async_computation.2 | async-start | bytes 3538944 | tf_op jit(solution)/shard_map/all_to_all | solution.py:44
  240.4 14.8 %copy-start.33 = (bf16[64,768]{1,0:T(8,128)(2,1)S(1)}, bf16[64,768]{1,0:T(8,128)(2,1)}, u32[]{:S(2)}) copy-start(bf16[64,768]{1,0:T(8,128)(2,1)} %copy-done.32) | copy-start | bytes 294916
  249.0 7.5 %copy-start.66 = (pred[2]{0:T(512)(128)(4,1)S(1)}, pred[2]{0:T(512)(128)(4,1)}, u32[]{:S(2)}) copy-start(pred[2]{0:T(512)(128)(4,1)} %iota_compare_fusion.3) | copy-start | bytes 10
  270.6 11.0 %collective-permute-start.14 = (bf16[16,128,768]{2,1,0:T(8,128)(2,1)}, bf16[16,128,768]{2,1,0:T(8,128)(2,1)}, u32[]{:S(2)}, u32[]{:S(2)}) collective-permute-start(bf16[16,128,768]{2,1,0:T(8,128)(2,1)} %pad_maximum_fusion.1), channel_id=1, source_target_pairs={{0,16},{16,0},{1,17},{17,1},{2,18},{18,2},{3,19},{19,3},{4,20},{20... | collective-permute-start | bytes 9437192 | tf_op jit(solution)/shard_map/ppermute | solution.py:29
  270.8 37.7 %copy-start.52 = (f32[512]{0:T(512)}, f32[512]{0:T(512)S(1)}, u32[]{:S(2)}) copy-start(f32[512]{0:T(512)S(1)} %reduce.19) | copy-start | bytes 6148
  270.9 10.8 %copy-start.12 = (bf16[4,1,4,96,768]{4,3,2,1,0:T(8,128)(2,1)S(1)}, bf16[4,1,4,96,768]{4,3,2,1,0:T(8,128)(2,1)}, u32[]{:S(2)}) copy-start(bf16[4,1,4,96,768]{4,3,2,1,0:T(8,128)(2,1)} %get-tuple-element.127) | copy-start | bytes 7077892
  270.9 10.8 %copy-start.22 = (bf16[4,1,4,24,768]{4,3,2,1,0:T(8,128)(2,1)S(1)}, bf16[4,1,4,24,768]{4,3,2,1,0:T(8,128)(2,1)}, u32[]{:S(2)}) copy-start(bf16[4,1,4,24,768]{4,3,2,1,0:T(8,128)(2,1)} %get-tuple-element.136) | copy-start | bytes 1769476
  285.3 48.7 %all-to-all-start.3 = ((bf16[16,128,768]{2,1,0:T(8,128)(2,1)}), bf16[16,128,768]{2,1,0:T(8,128)(2,1)}, u32[]{:S(2)}, u32[]{:S(2)}) async-start(bf16[16,128,768]{2,1,0:T(8,128)(2,1)} %add_convert_fusion), calls=%async_computation.3 | async-start | bytes 6291456 | tf_op jit(solution)/shard_map/all_to_all | solution.py:44
  297.5 31.2 %collective-permute-start.15 = (bf16[16,24,3072]{2,1,0:T(8,128)(2,1)}, bf16[16,24,3072]{2,1,0:T(8,128)(2,1)}, u32[]{:S(2)}, u32[]{:S(2)}) collective-permute-start(bf16[16,24,3072]{2,1,0:T(8,128)(2,1)} %bitcast.70), channel_id=1, source_target_pairs={{0,16},{16,0},{1,17},{17,1},{2,18},{18,2},{3,19},{19,3},{4,20},{20... | collective-permute-start | bytes 7077896 | tf_op jit(solution)/shard_map/ppermute | solution.py:29
  305.1 5.6 %copy-start = (bf16[512,2304]{1,0:T(8,128)(2,1)S(1)}, bf16[512,2304]{1,0:T(8,128)(2,1)}, u32[]{:S(2)}) copy-start(bf16[512,2304]{1,0:T(8,128)(2,1)} %get-tuple-element.58.qkv_ref) | copy-start | bytes 7077892
  308.4 14.7 %copy-start.55 = (f32[512]{0:T(512)}, f32[512]{0:T(512)S(1)}, u32[]{:S(2)}) copy-start(f32[512]{0:T(512)S(1)} %broadcast_multiply_fusion.1) | copy-start | bytes 6148
  308.4 14.6 %copy-start.57 = (f32[512]{0:T(512)}, f32[512]{0:T(512)S(1)}, u32[]{:S(2)}) copy-start(f32[512]{0:T(512)S(1)} %broadcast_multiply_fusion.2) | copy-start | bytes 6148
  324.9 9.1 %copy-start.4 = (bf16[2,256,768]{2,1,0:T(8,128)(2,1)S(1)}, bf16[2,256,768]{2,1,0:T(8,128)(2,1)}, u32[]{:S(2)}) copy-start(bf16[2,256,768]{2,1,0:T(8,128)(2,1)} %param.25) | copy-start | bytes 2359300
  334.0 5.6 %copy-start.43 = (f32[1024]{0:T(1024)S(1)}, f32[1024]{0:T(1024)}, u32[]{:S(2)}) copy-start(f32[1024]{0:T(1024)} %copy-done.42) | copy-start | bytes 12292
  334.0 5.6 %copy-start.44 = (f32[1024]{0:T(1024)S(1)}, f32[1024]{0:T(1024)}, u32[]{:S(2)}) copy-start(f32[1024]{0:T(1024)} %get-tuple-element.107) | copy-start | bytes 12292
  334.0 5.6 %copy-start.49 = (f32[1024]{0:T(1024)S(1)}, f32[1024]{0:T(1024)}, u32[]{:S(2)}) copy-start(f32[1024]{0:T(1024)} %get-tuple-element.106) | copy-start | bytes 12292
  339.5 11.1 %copy-start.11 = (bf16[4,1,4,24,3072]{4,3,2,1,0:T(8,128)(2,1)S(1)}, bf16[4,1,4,24,3072]{4,3,2,1,0:T(8,128)(2,1)}, u32[]{:S(2)}) copy-start(bf16[4,1,4,24,3072]{4,3,2,1,0:T(8,128)(2,1)} %get-tuple-element.125) | copy-start | bytes 7077892
  354.6 10.6 %copy-start.18 = (bf16[2304,768]{0,1:T(8,128)(2,1)S(1)}, bf16[2304,768]{0,1:T(8,128)(2,1)}, u32[]{:S(2)}) copy-start(bf16[2304,768]{0,1:T(8,128)(2,1)} %convolution_convert_fusion.1) | copy-start | bytes 10616836
  354.6 44.1 %all-to-all-start.4 = ((bf16[16,24,3072]{2,1,0:T(8,128)(2,1)}), bf16[16,24,3072]{2,1,0:T(8,128)(2,1)}, u32[]{:S(2)}, u32[]{:S(2)}) async-start(bf16[16,24,3072]{2,1,0:T(8,128)(2,1)} %fusion.24), calls=%async_computation.4 | async-start | bytes 4718592 | tf_op jit(solution)/shard_map/all_to_all | solution.py:44
  369.5 31.2 %collective-permute-start.16 = (bf16[16,24,3200]{2,1,0:T(8,128)(2,1)}, bf16[16,24,3200]{2,1,0:T(8,128)(2,1)}, u32[]{:S(2)}, u32[]{:S(2)}) collective-permute-start(bf16[16,24,3200]{2,1,0:T(8,128)(2,1)} %pad_maximum_fusion.4), channel_id=1, source_target_pairs={{0,16},{16,0},{1,17},{17,1},{2,18},{18,2},{3,19},{19,3},{4,20},{20... | collective-permute-start | bytes 7372808 | tf_op jit(solution)/shard_map/ppermute | solution.py:29
  380.1 47.1 %collective-permute-start.18 = (bf16[4,408,768]{2,1,0:T(8,128)(2,1)}, bf16[4,408,768]{2,1,0:T(8,128)(2,1)}, u32[]{:S(2)}, u32[]{:S(2)}) collective-permute-start(bf16[4,408,768]{2,1,0:T(8,128)(2,1)} %slice_bitcast_fusion), channel_id=1, source_target_pairs={{0,16},{16,0},{1,17},{17,1},{2,18},{18,2},{3,19},{19,3},{4,20},{20... | collective-permute-start | bytes 7520264 | tf_op jit(solution)/shard_map/ppermute | solution.py:29
  404.6 36.3 %all-to-all-start.5 = ((bf16[16,24,3200]{2,1,0:T(8,128)(2,1)}), bf16[16,24,3200]{2,1,0:T(8,128)(2,1)}, u32[]{:S(2)}, u32[]{:S(2)}) async-start(bf16[16,24,3200]{2,1,0:T(8,128)(2,1)} %add_convert_fusion.1), calls=%async_computation.5 | async-start | bytes 4915200 | tf_op jit(solution)/shard_map/all_to_all | solution.py:44
  431.6 26.1 %collective-permute-start.19 = (bf16[408,768]{1,0:T(8,128)(2,1)}, bf16[408,768]{1,0:T(8,128)(2,1)}, u32[]{:S(2)}, u32[]{:S(2)}) collective-permute-start(bf16[408,768]{1,0:T(8,128)(2,1)} %get-tuple-element.131), channel_id=1, source_target_pairs={{0,1},{1,2},{2,3},{3,0},{4,5},{5,6},{6,7},{7,4},{8,9},{9,10},{10,1... | collective-permute-start | bytes 1880072 | tf_op jit(solution)/shard_map/ppermute | solution.py:29
  433.0 29.4 %collective-permute-start.21 = (bf16[408,768]{1,0:T(8,128)(2,1)}, bf16[408,768]{1,0:T(8,128)(2,1)}, u32[]{:S(2)}, u32[]{:S(2)}) collective-permute-start(bf16[408,768]{1,0:T(8,128)(2,1)} %get-tuple-element.132), channel_id=1, source_target_pairs={{0,3},{1,0},{2,1},{3,2},{4,7},{5,4},{6,5},{7,6},{8,11},{9,8},{10,9... | collective-permute-start | bytes 1880072 | tf_op jit(solution)/shard_map/ppermute | solution.py:29
  434.8 29.3 %collective-permute-start.20 = (bf16[408,768]{1,0:T(8,128)(2,1)}, bf16[408,768]{1,0:T(8,128)(2,1)}, u32[]{:S(2)}, u32[]{:S(2)}) collective-permute-start(bf16[408,768]{1,0:T(8,128)(2,1)} %get-tuple-element.133), channel_id=1, source_target_pairs={{0,2},{1,3},{2,0},{3,1},{4,6},{5,7},{6,4},{7,5},{8,10},{9,11},{10,... | collective-permute-start | bytes 1880072 | tf_op jit(solution)/shard_map/ppermute | solution.py:29
  443.6 23.9 %all-to-all-start.6 = ((bf16[4,6,10240]{2,1,0:T(8,128)(2,1)}), bf16[4,6,10240]{2,1,0:T(8,128)(2,1)S(1)}, u32[]{:S(2)}, u32[]{:S(2)}) async-start(bf16[4,6,10240]{2,1,0:T(8,128)(2,1)} %constant_dynamic-update-slice_fusion.18), calls=%async_computation.6 | async-start | bytes 1310720 | tf_op jit(solution)/shard_map/all_to_all | solution.py:44
  470.2 2.9 collective-permute-start.17
  (38 other events, 120.8 us)
Sparse Core Ops, SparseCore 0:
  27.5 72.4 all-gather.1

commit v6 on v5

--- a/solution.py
+++ b/solution.py
@@ -302,9 +302,472 @@
         ],
         compiler_params=pltpu.CompilerParams(vmem_limit_bytes=48 * 1024 * 1024),
         cost_estimate=pl.CostEstimate(
-            flops=3_000_000_000, bytes_accessed=10_000_000, transcendentals=0
+            flops=1000, bytes_accessed=1000, transcendentals=0
         ),
     )(dbranch, qkv, probs, layer)
+
+
+LIMIT = 56 * 1024 * 1024
+
+
+def whole_spec(array):
+    return pl.BlockSpec(array.shape, lambda *_: (0,) * len(array.shape))
+
+
+def call(kernel, grid, ins, in_specs, outs, out_specs, scratch, flops, size):
+    return pl.pallas_call(
+        kernel,
+        grid=grid,
+        in_specs=in_specs,
+        out_specs=out_specs,
+        out_shape=[jax.ShapeDtypeStruct(shape, kind) for shape, kind in outs],
+        scratch_shapes=scratch,
+        compiler_params=pltpu.CompilerParams(vmem_limit_bytes=LIMIT),
+        cost_estimate=pl.CostEstimate(flops=flops, bytes_accessed=size, transcendentals=0),
+    )(*ins)
+
+
+def low_three(value):
+    high = value.astype(BF).astype(F32)
+    middle = (value - high).astype(BF).astype(F32)
+    rest = (value - high - middle).astype(BF).astype(F32)
+    return [high, middle, rest]
+
+
+def logits_kernel(
+    spread_ref, w_ref, b_ref, column_ref, label_ref, expl_ref, stat_ref, part_ref, flat_ref, logits_ref
+):
+    step = pl.program_id(0)
+    count, width = spread_ref.shape
+    peers, high, _ = part_ref.shape
+    rows = high - 16
+    spread = spread_ref[...]
+    entries = w_ref.shape[0]
+    chunks = [slice(i, i + entries // 5) for i in range(0, entries, entries // 5)]
+    peak = None
+    for cut in chunks:
+        logits = dot_nt(spread, w_ref[cut, :]) + b_ref[:, cut]
+        logits_ref[:, cut] = logits
+        most = jnp.max(logits, axis=1, keepdims=True)
+        peak = most if peak is None else jnp.maximum(peak, most)
+    top = peak
+    sums = jnp.zeros((count, 1), F32)
+    label = jnp.zeros((count, 1), F32)
+    part = jnp.zeros((count, width), F32)
+    for cut in chunks:
+        expl = jnp.exp(logits_ref[:, cut] - top)
+        sums += jnp.sum(expl, axis=1, keepdims=True)
+        hit = label_ref[...] == column_ref[:, cut]
+        rest = jnp.where(hit, 0.0, expl)
+        label += jnp.sum(expl - rest, axis=1, keepdims=True)
+        other = rest.astype(BF)
+        expl_ref[:, cut] = other
+        part += dot_nn(other, w_ref[cut, :])
+    part = part.astype(BF)
+    for i in range(count // rows):
+        part_ref[step * (count // rows) + i, 0:rows, :] = part[i * rows : (i + 1) * rows]
+    lane = lax.broadcasted_iota(jnp.int32, (count, 128), 1)
+    stat = jnp.where(lane == 0, top, jnp.where(lane == 1, label, 0.0))
+    stat_ref[...] = stat
+    parts = jnp.zeros((count, 128), F32)
+    for i, value in enumerate(low_three(top) + low_three(sums)):
+        parts = jnp.where(lane == i, value, parts)
+    flat_ref[step] = parts.T[0:8]
+
+    @pl.when(step == pl.num_programs(0) - 1)
+    def _():
+        told = jnp.concatenate([flat_ref[i] for i in range(flat_ref.shape[0])], axis=1)
+        rest = told.shape[1] - width
+        last = jnp.concatenate([told[:, width:], jnp.zeros((8, width - rest), F32)], axis=1)
+        told = jnp.concatenate([told[:, :width], last], axis=0).astype(BF)
+        for i in range(peers):
+            part_ref[i, rows:, :] = told
+
+
+def logits_call(spread, vocab_w, vocab_b, column, labels, rows):
+    count, width = spread.shape
+    entries = vocab_w.shape[0]
+    block = count // 2
+    here = lambda n: pl.BlockSpec((block, n), lambda i: (i, 0))
+    ins = (spread, vocab_w, vocab_b[None, :], column[None, :], labels)
+    specs = [here(width)] + [whole_spec(a) for a in ins[1:4]] + [here(1)]
+    part = (count // rows, rows + 16, width)
+    return call(
+        logits_kernel,
+        (2,),
+        ins,
+        specs,
+        [((count, entries), BF), ((count, 128), F32), (part, BF)],
+        [here(entries), here(128), pl.BlockSpec(part, lambda i: (0, 0, 0))],
+        [pltpu.VMEM((2, 8, block), F32), pltpu.VMEM((block, entries), F32)],
+        10_000_000_000,
+        20_000_000,
+    )
+
+
+def decoder_kernel(
+    expl_ref, spread_ref, column_ref, label_ref, scale_ref, stat_ref, lse_ref, out_ref
+):
+    count, width = spread_ref.shape
+    lse = jnp.broadcast_to(lse_ref[...], (8, count)).T[:, 0:1]
+    share = jnp.exp(stat_ref[:, 0:1] - lse)
+    scale = scale_ref[...]
+    hit = label_ref[...] == column_ref[...]
+    other = (scale * share) * expl_ref[...].astype(F32)
+    dlogits = jnp.where(hit, scale * (stat_ref[:, 1:2] * share - 1.0), other).astype(BF)
+    out_ref[:, :width] = dot_tn(dlogits, spread_ref[...]).astype(BF)
+    ones = jnp.ones((count, out_ref.shape[1] - width), BF)
+    out_ref[:, width:] = dot_tn(dlogits, ones).astype(BF)
+
+
+def decoder_call(expl, spread, column, labels, scale, stat, lse):
+    count, width = spread.shape
+    entries = expl.shape[1]
+    block = entries // 5
+    ins = (expl, spread, column[None, :], labels, scale, stat, lse)
+    return call(
+        decoder_kernel,
+        (5,),
+        ins,
+        [
+            pl.BlockSpec((count, block), lambda j: (0, j)),
+            whole_spec(spread),
+            pl.BlockSpec((1, block), lambda j: (0, j)),
+        ]
+        + [whole_spec(a) for a in ins[3:]],
+        [((entries, width + 128), BF)],
+        [pl.BlockSpec((block, width + 128), lambda j: (j, 0))],
+        [],
+        1000,
+        1000,
+    )[0]
+
+
+def merge_kernel(
+    own_ref,
+    part_ref,
+    head_ref,
+    label_ref,
+    scalar_ref,
+    normed3_ref,
+    slope3_ref,
+    vec_ref,
+    picked_ref,
+    dense_ref,
+    select_ref,
+    grad_ref,
+    normed2_ref,
+    inverse2_ref,
+    lse_ref,
+    loss_ref,
+    g_dense_ref,
+    dsecond_ref,
+    dffn_ref,
+    sums_ref,
+):
+    peers, high, width = part_ref.shape
+    rows = high - 16
+    tail = peers * rows - width
+
+    def told(i):
+        first = part_ref[:, rows : rows + 8, :].astype(F32)[:, i]
+        rest = part_ref[:, rows + 8 :, :].astype(F32)[:, i, :tail]
+        return jnp.concatenate([first, rest], axis=1)
+
+    tops = told(0) + told(1) + told(2)
+    sums = told(3) + told(4) + told(5)
+    top = jnp.max(tops, axis=0, keepdims=True)
+    share = jnp.exp(tops - top)
+    total_sum = jnp.sum(sums * share, axis=0, keepdims=True)
+    lse = top + jnp.log(total_sum)
+    share = share / total_sum
+    lse_ref[...] = lse
+    mine = own_ref[0] + lax.broadcasted_iota(jnp.int32, (rows, peers * rows), 0)
+    mine = mine == lax.broadcasted_iota(jnp.int32, (rows, peers * rows), 1)
+    own_lse = jnp.sum(jnp.where(mine, lse, 0.0), axis=1, keepdims=True)
+    mixed = jnp.zeros((rows, width), F32)
+    for i in range(peers):
+        weight = jnp.sum(jnp.where(mine, share[i : i + 1], 0.0), axis=1, keepdims=True)
+        mixed += weight * part_ref[i, 0:rows, :].astype(F32)
+    label = label_ref[...]
+    label_logit = jnp.sum(head_ref[...].astype(F32) * label, axis=1, keepdims=True)
+    label_logit += scalar_ref[:, 0:1]
+    grad = scalar_ref[:, 2:3] * (mixed + (jnp.exp(label_logit - own_lse) - 1.0) * label)
+    loss_ref[...] = jnp.zeros(loss_ref.shape, F32) + jnp.sum(
+        scalar_ref[:, 1:2] * (own_lse - label_logit)
+    )
+    normed3 = normed3_ref[...]
+    ddense = norm_back(grad, normed3, scalar_ref[:, 3:4], vec_ref[9:10]) * slope3_ref[...]
+    low = ddense.astype(BF)
+    column = lambda v: jnp.sum(v, axis=0, keepdims=True)
+    g_dense_ref[...] = dot_tn(picked_ref[...], low)
+    drows = dot_nt(low, dense_ref[...]).astype(BF)
+    dout = grad_ref[...].astype(F32) + dot_tn(select_ref[...], drows)
+    normed2 = normed2_ref[...]
+    dsecond = norm_back(dout, normed2, inverse2_ref[...], vec_ref[6:7])
+    dffn = dsecond.astype(BF)
+    dsecond_ref[...] = dsecond
+    dffn_ref[...] = dffn
+    parts = [
+        column(low.astype(F32)),
+        column(grad * normed3),
+        column(grad),
+        column(dout * normed2),
+        column(dout),
+        column(dffn.astype(F32)),
+    ]
+    for i, value in enumerate(parts):
+        sums_ref[i : i + 1] = value
+
+
+def merge_call(own, *arrays, layer, dense_block):
+    part, head = arrays[0], arrays[1]
+    width = head.shape[1]
+    tokens = arrays[-1].shape[0]
+    count = part.shape[0] * (part.shape[1] - 16)
+    ins = list(arrays)
+    ins.insert(8, layer)
+    specs = [whole_spec(a) for a in arrays]
+    specs.insert(8, pl.BlockSpec((width, width), lambda *_: (0, dense_block)))
+    outs = [
+        ((1, count), F32),
+        ((8, 128), F32),
+        ((width, width), F32),
+        ((tokens, width), F32),
+        ((tokens, width), BF),
+        ((8, width), F32),
+    ]
+    return call(
+        merge_kernel,
+        (1,),
+        [own] + ins,
+        [pl.BlockSpec(memory_space=pltpu.SMEM)] + specs,
+        outs,
+        [pl.BlockSpec(shape, lambda *_: (0, 0)) for shape, _ in outs],
+        [],
+        300_000_000,
+        10_000_000,
+    )
+
+
+def keep_halves(core, block, here, away):
+    for c in range(NC):
+
+        @pl.when(core == c)
+        def _():
+            here(block(c))
+
+        @pl.when(core != c)
+        def _():
+            away(block(c))
+
+
+def shrink_kernel(core_ref, act_ref, dffn_ref, dense_ref, loss_ref, here_ref, away_ref):
+    width = dffn_ref.shape[1]
+    grad = dot_tn(act_ref[...], dffn_ref[...])
+    core = core_ref[0]
+    spot = lax.broadcasted_iota(jnp.int32, (8, width), 1)
+    first = lax.broadcasted_iota(jnp.int32, (8, width), 0) == 0
+    told = jnp.zeros((8, width), F32)
+    for i, value in enumerate(low_three(loss_ref[0:1, 0:1])):
+        told = jnp.where(first & (spot == i + 3 * core), value, told)
+
+    def put(ref, extra):
+        def store(block):
+            tall, dense = block
+            for z in range(NZ):
+                ref[z, 0:96, :] = tall[z * 96 : (z + 1) * 96].astype(BF)
+                ref[z, 96:128, :] = jnp.concatenate(
+                    [dense[z * 24 : (z + 1) * 24], extra], axis=0
+                ).astype(BF)
+
+        return store
+
+    def block(c):
+        tall = grad[c * width // 2 : (c + 1) * width // 2]
+        return tall, dense_ref[c * 96 : (c + 1) * 96, :]
+
+    keep_halves(core, block, put(here_ref, told), put(away_ref, told))
+
+
+def shrink_call(core, act, dffn, g_dense, loss):
+    tokens, width = dffn.shape
+    out = ((NY * NZ, 128, width), BF)
+    half_spec = pl.BlockSpec((NZ, 128, width), lambda y: (y, 0, 0))
+    return call(
+        shrink_kernel,
+        (NY,),
+        (core, act, dffn, g_dense, loss),
+        [
+            pl.BlockSpec(memory_space=pltpu.SMEM),
+            pl.BlockSpec((tokens, width), lambda y: (0, y)),
+            whole_spec(dffn),
+            pl.BlockSpec((width // NY, width), lambda y: (y, 0)),
+            whole_spec(loss),
+        ],
+        [out, out],
+        [half_spec, half_spec],
+        [],
+        1000,
+        1000,
+    )
+
+
+def put_wide(grad, core, here_ref, away_ref, lanes):
+    def block(c):
+        return [grad[96 * (NC * y + c) : 96 * (NC * y + c) + 96] for y in range(NY)]
+
+    def put(ref):
+        def store(parts):
+            for y, part in enumerate(parts):
+                ref[y * NZ : (y + 1) * NZ, :, lanes] = part.reshape(NZ, 24, -1).astype(BF)
+
+        return store
+
+    keep_halves(core, block, put(here_ref), put(away_ref))
+
+
+def feed_back_kernel(
+    core_ref,
+    dffn_ref,
+    shrink_ref,
+    slope_ref,
+    low_ref,
+    expand_ref,
+    dsecond_ref,
+    normed_ref,
+    inverse_ref,
+    vec_ref,
+    here_ref,
+    away_ref,
+    bias_ref,
+    dresidual_ref,
+    dbranch_ref,
+    sums_ref,
+    total_ref,
+):
+    step = pl.program_id(0)
+    dpre = (dot_nt(dffn_ref[...], shrink_ref[...]) * slope_ref[...].astype(F32)).astype(BF)
+    bias_ref[...] = jnp.sum(dpre.astype(F32), axis=0, keepdims=True)
+    more = dot_nt(dpre, expand_ref[...])
+
+    @pl.when(step == 0)
+    def _():
+        total_ref[...] = dsecond_ref[...] + more
+
+    @pl.when(step > 0)
+    def _():
+        total_ref[...] += more
+
+    put_wide(dot_tn(low_ref[...], dpre), core_ref[0], here_ref, away_ref, slice(None))
+
+    @pl.when(step == pl.num_programs(0) - 1)
+    def _():
+        dfirst = total_ref[...]
+        normed = normed_ref[...]
+        dresidual = norm_back(dfirst, normed, inverse_ref[...], vec_ref[3:4])
+        dbranch = dresidual.astype(BF)
+        dresidual_ref[...] = dresidual
+        dbranch_ref[...] = dbranch
+        sums_ref[0:1] = jnp.sum(dfirst * normed, axis=0, keepdims=True)
+        sums_ref[1:2] = jnp.sum(dfirst, axis=0, keepdims=True)
+        sums_ref[2:3] = jnp.sum(dbranch.astype(F32), axis=0, keepdims=True)
+
+
+def feed_back_call(core, dffn, shrink, slope, low, layer, expand_block, dsecond, normed, inverse, vec):
+    tokens, width = dffn.shape
+    wide = slope.shape[1]
+    half = ((NY * NZ, 24, wide), BF)
+    half_spec = pl.BlockSpec((NY * NZ, 24, width), lambda j: (0, 0, j))
+    outs = [
+        half,
+        half,
+        ((1, wide), F32),
+        ((tokens, width), F32),
+        ((tokens, width), BF),
+        ((8, width), F32),
+    ]
+    return call(
+        feed_back_kernel,
+        (wide // width,),
+        (core, dffn, shrink, slope, low, layer, dsecond, normed, inverse, vec),
+        [
+            pl.BlockSpec(memory_space=pltpu.SMEM),
+            whole_spec(dffn),
+            pl.BlockSpec((width, width), lambda j: (j, 0)),
+            pl.BlockSpec((tokens, width), lambda j: (0, j)),
+            whole_spec(low),
+            pl.BlockSpec((width, width), lambda j: (0, expand_block + j)),
+            whole_spec(dsecond),
+            whole_spec(normed),
+            whole_spec(inverse),
+            whole_spec(vec),
+        ],
+        outs,
+        [
+            half_spec,
+            half_spec,
+            pl.BlockSpec((1, width), lambda j: (0, j)),
+            pl.BlockSpec((tokens, width), lambda j: (0, 0)),
+            pl.BlockSpec((tokens, width), lambda j: (0, 0)),
+            pl.BlockSpec((8, width), lambda j: (0, 0)),
+        ],
+        [pltpu.VMEM((tokens, width), F32)],
+        1000,
+        1000,
+    )
+
+
+def last_kernel(core_ref, x_ref, dfused_ref, attended_ref, dbranch_ref, sums_ref, here_ref, away_ref):
+    width = x_ref.shape[1]
+    core = core_ref[0]
+    for i in range(4):
+        lanes = slice(i * width, (i + 1) * width)
+        if i < 3:
+            grad = dot_tn(x_ref[...], dfused_ref[:, lanes])
+        else:
+            grad = dot_tn(attended_ref[...], dbranch_ref[...])
+        put_wide(grad, core, here_ref, away_ref, lanes)
+    put_wide(sums_ref[...], core, here_ref, away_ref, slice(4 * width, 4 * width + 128))
+
+
+def last_call(core, x, dfused, attended, dbranch, sums):
+    width = x.shape[1]
+    out = ((NY * NZ, 24, 4 * width + 128), BF)
+    ins = (x, dfused, attended, dbranch, sums)
+    half_spec = pl.BlockSpec(out[0], lambda *_: (0, 0, 0))
+    return call(
+        last_kernel,
+        (1,),
+        (core,) + ins,
+        [pl.BlockSpec(memory_space=pltpu.SMEM)] + [whole_spec(a) for a in ins],
+        [out, out],
+        [half_spec, half_spec],
+        [],
+        1000,
+        1000,
+    )
+
+
+def tall_kernel(in_ref, out_ref):
+    blocks_, rows, width = out_ref.shape
+    out_ref[...] = in_ref[...].astype(F32).reshape(blocks_, rows, width).astype(BF)
+
+
+def tall_call(layer, width):
+    places = NY * NC * NZ
+    rows = layer.shape[0] // places
+    return call(
+        tall_kernel,
+        (2, NX),
+        (layer,),
+        [pl.BlockSpec((layer.shape[0] // 2, width), lambda j, k: (j, k))],
+        [((places, NX, rows, width), BF)],
+        [pl.BlockSpec((places // 2, None, rows, width), lambda j, k: (j, k, 0, 0))],
+        [],
+        1000,
+        1000,
+    )[0].reshape(-1, width)
 
 
 def body(
@@ -339,6 +802,8 @@
     heads = width // HEAD_DIM
     factor = HEAD_DIM ** (-0.5)
     at = {axis: lax.axis_index(axis) for axis in EVERY}
+    core = at["c"].astype(jnp.int32)[None]
+
     vectors = (
         b_query,
         b_value,
@@ -407,7 +872,10 @@
     ).reshape(-1)
     select = (shifted[:, None] == jnp.arange(tokens, dtype=jnp.int32)[None, :]).astype(BF)
 
-    layer, label_w, vocab_w, select = after(layer, label_w, vocab_w, select)
+    scale, labels = scale[:, None], labels[:, None]
+    layer, label_w, vocab_w, select, scale, labels = after(
+        layer, label_w, vocab_w, select, scale, labels
+    )
     label_w = swap(label_w, ("y", "z"))
     ends = [NX * width, w_expand.shape[1], 3 * width, width, width, 128]
     ends = [sum(ends[: i + 1]) for i in range(len(ends))]
@@ -416,15 +884,7 @@
     attn_block = ends[2] // width
     dense_full = layer[:, ends[3] : ends[4]]
     vec_full = layer[:, ends[4] :]
-    shrink_full = jnp.stack(
-        [
-            layer[:, k * width : (k + 1) * width].reshape(
-                NY * NC * NZ, -1, width
-            )
-            for k in range(NX)
-        ],
-        axis=1,
-    ).reshape(-1, width)
+    shrink_full = tall_call(layer, width)
     rows_of = vec_full[:, :16].T.astype(F32)
     (
         b_query,
@@ -447,6 +907,7 @@
     )
     pre = matmul(first_low, expand_full) + b_expand
     act = gelu_value(pre).astype(BF)
+    slope = gelu_slope(pre).astype(BF)
     second = first + matmul(act, shrink_full) + b_shrink
     settled, normed2, inverse2 = layer_norm(second, ffn_gain, ffn_shift)
     settled_low = settled.astype(BF)
@@ -461,127 +922,97 @@
     spread = swap(
         jnp.broadcast_to(head_out, (NY * NZ,) + head_out.shape), ("y", "z")
     ).reshape(-1, width)
-    logits = matmul_nt(spread, vocab_w) + vocab_b
-    top = jnp.max(logits, axis=1)
-    expl = jnp.exp(logits - top[:, None])
-    part_sum = jnp.sum(expl, axis=1)
-    other = jnp.where(hit, 0.0, expl).astype(BF)
-    part = matmul(other, vocab_w).astype(BF).reshape(NY * NZ, rows, width)
-    stats = jnp.stack(three(top) + three(part_sum)).astype(BF)
-    stats = jnp.concatenate([stats[:, :width], stats[:, width:].reshape(2, width)])
-    stats = jnp.broadcast_to(stats, (NY * NZ,) + stats.shape)
-    part = swap(jnp.concatenate([part, stats], axis=1), ("y", "z"))
-    stats = part[:, rows:]
-    stats = jnp.concatenate(
-        [stats[:, :6], stats[:, 6:].reshape(NY * NZ, 6, NY * NZ * rows - width)], axis=2
-    ).astype(F32)
-    tops = stats[:, 0] + stats[:, 1] + stats[:, 2]
-    sums = stats[:, 3] + stats[:, 4] + stats[:, 5]
-    top_all = jnp.max(tops, axis=0)
-    shares = jnp.exp(tops - top_all)
-    sum_all = jnp.sum(sums * shares, axis=0)
-    log_sums = top_all + jnp.log(sum_all)
-    log_sum = lax.dynamic_slice_in_dim(log_sums, own_first, rows)
-    share = lax.dynamic_slice_in_dim(shares / sum_all, own_first, rows, 1)
-    label_logit = jnp.sum(head_out.astype(F32) * label_w, axis=1) + label_b
-    mixed = jnp.sum(share[:, :, None] * part[:, :rows].astype(F32), axis=0)
-    row_grad = (loss_scale * own_weight)[:, None] * (
-        mixed + (jnp.exp(label_logit - log_sum) - 1.0)[:, None] * label_w
-    )
-    loss_own = jnp.sum(own_weight * (log_sum - label_logit))
-    g_dense_gain = column_sum(row_grad * normed3)
-    g_dense_shift = column_sum(row_grad)
-    ddense = (norm_back(row_grad, normed3, inverse3, dense_gain) * gelu_slope(dense_pre)).astype(BF)
-    g_dense = matmul_tn(picked, ddense)
-    g_dense_bias = column_sum(ddense)
-    drows = matmul_nt(ddense, dense_full).astype(BF)
-
-    dout = out_grad.reshape(tokens, width).astype(F32) + matmul_tn(select, drows)
-    g_ffn_gain = column_sum(dout * normed2)
-    g_ffn_shift = column_sum(dout)
-    dsecond = norm_back(dout, normed2, inverse2, ffn_gain)
-    dffn = dsecond.astype(BF)
-    g_shrink = matmul_tn(act, dffn)
-    loss_row = jnp.where(
-        (jnp.arange(NC) == at["c"])[None, :, None, None, None], split_three(loss_own), 0.0
-    ).astype(BF)
-    loss_row = jnp.broadcast_to(loss_row, (NY, NC, NZ, 8, width))
-    tall_pair = sum_cores([blocks(g_shrink), blocks(g_dense), loss_row], 1)
-    g_shrink_bias = column_sum(dffn)
-    dpre = (matmul_nt(dffn, shrink_full) * gelu_slope(pre)).astype(BF)
-    dpre, tall_mine = after(dpre, add_cores(tall_pair))
-    g_expand = matmul_tn(first_low, dpre)
-    wide_pair = sum_cores([blocks(g_expand)], 2)
-    g_expand_bias = column_sum(dpre)
-    dfirst = dsecond + matmul_nt(dpre, expand_full)
-    g_attn_gain = column_sum(dfirst * normed1)
-    g_attn_shift = column_sum(dfirst)
-    dresidual = norm_back(dfirst, normed1, inverse1, attn_gain)
-    dbranch = dresidual.astype(BF)
+    expl, stat, part = logits_call(spread, vocab_w, vocab_b, column, labels, rows)
+    part = swap(part, ("y", "z"))
+    scalars = jnp.stack(
+        [label_b, own_weight, loss_scale * own_weight, inverse3[:, 0]], axis=1
+    )
+    lse, loss_own, g_dense, dsecond, dffn, sums_a = merge_call(
+        own_first.astype(jnp.int32)[None],
+        part,
+        head_out,
+        label_w,
+        jnp.pad(scalars, ((0, 0), (0, 124))),
+        normed3,
+        gelu_slope(dense_pre),
+        rows_of,
+        picked,
+        select,
+        out_grad.reshape(tokens, width),
+        normed2,
+        inverse2,
+        layer=layer,
+        dense_block=attn_block + 1,
+    )
+
+    tall_pair = shrink_call(core, act, dffn, g_dense, loss_own)
+    tall_here, tall_away, dffn = after(*tall_pair, dffn)
+    tall_pair = (tall_here, give(tall_away, "c", 1))
+    wide_here, wide_away, g_expand_bias, dresidual, dbranch, sums_b = feed_back_call(
+        core, dffn, shrink_full, slope, first_low, layer, 4, dsecond, normed1, inverse1, rows_of
+    )
+    wide_pair = (wide_here, give(wide_away, "c", 1))
+    dbranch, tall_mine = after(dbranch, add_cores(tall_pair))
     tall_all = swap(tall_mine, ("y", "z"))
-    g_attn = matmul_tn(attended, dbranch)
-    g_attn_bias = column_sum(dbranch)
     dfused, fused_sum = attention_backward(dbranch, qkv, probs, layer, attn_block)
-    dfused, got, tall_all = after(dfused, wide_pair[1], tall_all)
-    wide_mine = add_cores((wide_pair[0], got))
-    g_qkv = matmul_tn(x, dfused)
-    g_query, g_value = fused_sum[0, :width], fused_sum[0, 2 * width :]
-    dinput = dresidual + matmul_nt(dfused, qkv_full)
-
-    late_sums, dfused = after(log_sums, dfused)
-    dlogits = (
-        (scale * jnp.exp(top - late_sums))[:, None] * expl
-        - jnp.where(hit, scale[:, None], 0.0)
-    ).astype(BF)
-    grad_w = matmul_tn(dlogits, spread).astype(BF).reshape(NC, NX, per, width)
-    grad_b = column_sum(dlogits).reshape(NC, NX, 1, per)
-    grad_b = jnp.pad(grad_b, ((0, 0), (0, 0), (0, 7), (0, width - per))).astype(BF)
-    grad_w = jnp.concatenate([grad_w, grad_b], axis=2)
-    grad_w = (grad_w[0].astype(F32) + give(grad_w[1], "c", 1).astype(F32)).astype(BF)
-    grad_w = total([grad_w[0]] + [give(grad_w[k], "x", k) for k in (1, 2, 3)])
-    g_vocab, g_vocab_bias = grad_w[:per].T, grad_w[per, :per]
 
     sums = jnp.stack(
         [
-            g_query,
-            g_value,
-            g_attn_bias,
-            g_attn_gain,
-            g_attn_shift,
-            g_shrink_bias,
-            g_ffn_gain,
-            g_ffn_shift,
-            g_dense_bias,
-            g_dense_gain,
-            g_dense_shift,
+            fused_sum[0, :width],
+            fused_sum[0, 2 * width :],
+            sums_b[2],
+            sums_b[0],
+            sums_b[1],
+            sums_a[5],
+            sums_a[3],
+            sums_a[4],
+            sums_a[0],
+            sums_a[1],
+            sums_a[2],
         ]
     )
     sums = jnp.concatenate([after(sums)[0].T, g_expand_bias.reshape(width, -1)], axis=1)
     sums = jnp.pad(sums, ((0, 0), (0, 128 - sums.shape[1])))
-    wide = sum_yz(wide_mine)
-    last_pair = sum_cores([blocks(g_qkv), blocks(g_attn), blocks(sums)], 2)
-    last_pair, wide, tall_all = after(last_pair, wide, tall_all)
+    last_here, last_away = last_call(core, x, dfused, attended, dbranch, sums)
+    last_away, tall_all = after(last_away, tall_all)
+    last_pair = (last_here, give(last_away, "c", 1))
+    wide_mine, tall_all = after(add_cores(wide_pair), tall_all)
+    wide_all = swap(wide_mine, ("y", "z"))
+    last_mine, wide_all = after(add_cores(last_pair), wide_all)
+    last_all = swap(last_mine, ("y", "z"))
+
+    lse, wide_mine = after(lse, wide_mine)
+    grad_w = decoder_call(expl, spread, column, labels, scale, stat, lse)
+    grad_w = grad_w.reshape(NC, NX, per, -1)
+    grad_w, grad_away, wide_all = after(grad_w[0], grad_w[1], wide_all)
+    grad_w = add_cores((grad_w, give(grad_away, "c", 1)))
+    grad_w = total([grad_w[0]] + [give(grad_w[k], "x", k) for k in (1, 2, 3)])
+
+    dinput = dresidual + matmul_nt(dfused, qkv_full)
     tall = jnp.sum(tall_all[:, :120].astype(F32), axis=0).astype(BF)
-    loss_row = split_three(jnp.sum(tall_all[:, 120, :3].astype(F32)))[:128]
+    loss_row = split_three(jnp.sum(tall_all[:, 120, :6].astype(F32)))[:128]
     tall_low = tall[:96].reshape(NX, 4, 6, width).transpose(0, 2, 1, 3).reshape(NX, 6, 4 * width)
     early = jnp.concatenate(
         [
-            wide.reshape(NX, 6, -1),
             tall_low,
             tall[96:].reshape(NX, 6, width),
             jnp.broadcast_to(loss_row, (NX, 6, 128)),
         ],
         axis=2,
     )
-    last = sum_yz(add_cores(last_pair))
-    last = sum_x(jnp.concatenate([early, last.reshape(NX, 6, -1)], axis=2))
-    ends = [w_expand.shape[1], 4 * width, width, 128, 3 * width, width, 128]
+    wide = jnp.sum(wide_all.astype(F32), axis=0).astype(BF)
+    last_all, grad_w = after(last_all, grad_w)
+    g_vocab, g_vocab_bias = grad_w[:, :width].T, grad_w[:, width]
+    last = jnp.sum(last_all.astype(F32), axis=0).astype(BF)
+    last = sum_x(
+        jnp.concatenate([early, wide.reshape(NX, 6, -1), last.reshape(NX, 6, -1)], axis=2)
+    )
+    ends = [4 * width, width, 128, w_expand.shape[1], 3 * width, width, 128]
     ends = [sum(ends[: i + 1]) for i in range(len(ends))]
-    g_expand = last[:, : ends[0]]
-    g_shrink = last[:, ends[0] : ends[1]].reshape(6, 4, width).transpose(1, 0, 2).reshape(24, width)
-    g_dense = last[:, ends[1] : ends[2]]
-    loss = jnp.full((8, 128), jnp.sum(last[0, ends[2] : ends[2] + 3]))
-    loss = (loss + give(loss, "c", 1))[0, 0]
+    g_shrink = last[:, : ends[0]].reshape(6, 4, width).transpose(1, 0, 2).reshape(24, width)
+    g_dense = last[:, ends[0] : ends[1]]
+    loss = jnp.sum(last[0, ends[1] : ends[1] + 3])
+    g_expand = last[:, ends[2] : ends[3]]
     g_qkv = last[:, ends[3] : ends[4]]
     g_attn = last[:, ends[4] : ends[5]]
     sums = last[:, ends[5] :]

time: 490 us -> 474 us (0.967)
  Pallas kernels: 23.3 us -> 114 us
  matrix products: 87.5 us -> 32 us
  other arithmetic: 83.1 us -> 43.7 us
  blocking collectives: 27.1 us -> 0 us
  waiting for transfers between devices: 109 us -> 136 us
  local copies, waits for them, and re-layouts: 62.6 us -> 53.1 us
  between operations: 27.5 us -> 21.2 us
  starting transfers between devices: 61.4 us -> 67.2 us
    pallas_call x0 -> x7, Pallas kernels: none -> 90.8 us  [call(): pl.pallas_call(kernel, grid=grid, in_specs=in_specs, out_specs=out_specs,...]
    reduce_sum x15 -> x5, other arithmetic: 39.7 us -> 6.31 us  [the longest x1 2.15 us: body(): last = jnp.sum(last_all.astype(F32), axis=0).astype(BF)]
    all_to_all x1 -> x0, blocking collectives: 27.1 us -> none  [swap(): return lax.all_to_all(array, axes, 0, 0, tiled=True)]
    dot_general x4 -> x1, matrix products: 31.6 us -> 5.64 us  [matmul_nt(): lax.dot_general(left, right, (((1,), (1,)), ((), ())), preferred_element_...]
    dot_general x7 -> x0, matrix products: 25.9 us -> none  [matmul_tn(): lax.dot_general(left, right, (((0,), (0,)), ((), ())), preferred_element_...]
    all_to_all x6 -> x7, waiting for transfers between devices: 51.6 us -> 70.4 us  [swap(): return lax.all_to_all(array, axes, 0, 0, tiled=True)]
    ppermute x8 -> x7, waiting for transfers between devices: 16.3 us -> 25.9 us  [give(): return lax.ppermute(array, axis, [(i, (i + k) % n) for i in range(n)])]
    concatenate x6 -> x0, other arithmetic: 8.39 us -> none  [the longest x3 5.32 us: half(): return cut[0] if len(cut) == 1 else jnp.concatenate(cut, axis=axis)]
  transfers between devices with their start and end apart: 29 -> 29, of which waited for: 13 -> 13; matrix products, arithmetic and copies ran while one was open for 26% -> 21% of each run, Pallas kernels for 5% -> 14%
where the time goes in v6:
time: 474 us; the launch traced here: 467 us
  waiting for transfers between devices  136 us (29%)
  Pallas kernels  114 us (24%)
  starting transfers between devices  67.2 us (14%)
  local copies, waits for them, and re-layouts  53.1 us (11%)
  other arithmetic  43.7 us (9%)
  matrix products  32 us (7%)
  between operations  21.2 us (4%)
    pallas_call x7, Pallas kernels, call(): pl.pallas_call(kernel, grid=grid, in_specs=in_specs, out_specs=out_specs,...  90.8 us
    all_to_all x7, waiting for transfers between devices, swap(): return lax.all_to_all(array, axes, 0, 0, tiled=True)  70.4 us
    all_to_all x7, starting transfers between devices, swap(): return lax.all_to_all(array, axes, 0, 0, tiled=True)  42.1 us
    dot_general x5, matrix products, matmul(): return jnp.dot(left, right, preferred_element_type=F32)  26.4 us
    ppermute x7, waiting for transfers between devices, give(): return lax.ppermute(array, axis, [(i, (i + k) % n) for i in range(n)])  25.9 us
    ppermute x14, waiting for transfers between devices, fetch(): return lax.ppermute(array, axis, [((i + k) % n, i) for i in range(n)])  21.6 us
    ppermute x14, starting transfers between devices, fetch(): return lax.ppermute(array, axis, [((i + k) % n, i) for i in range(n)])  18.7 us
    all_gather x1, waiting for transfers between devices, body(): lax.all_gather(jnp.concatenate([tall, fused], axis=1), ('y', 'c', 'z'), a...  17.7 us
  transfers between devices with their start and end apart: 29, of which 13 were waited for; matrix products, arithmetic and copies ran while one was open for 21% of the time, Pallas kernels for 14%

profile of v6, /device:TPU:0, one launch (start us, length us, event | category | flops | bytes accessed | tf_op | source)
XLA Modules:
  0.0 466.7 jit_solution(14652716847753256052)
XLA Ops:
  8.0 1.5 stack.176
  12.8 2.9 collective-permute-start.3
  17.4 2.4 collective-permute-start
  19.7 1.5 collective-permute-start.1
  22.1 1.7 collective-permute-start.2
  23.8 1.6 collective-permute-done.1
  25.4 2.5 collective-permute-done.2
  30.0 2.1 collective-permute-start.6
  33.0 2.4 collective-permute-start.10
  35.4 2.2 collective-permute-start.11
  42.1 14.0 %collective-permute-done.6 = bf16[400,768]{1,0:T(8,128)(2,1)S(1)} collective-permute-done((bf16[400,768]{1,0:T(8,128)(2,1)S(1)}, bf16[400,768]{1,0:T(8,128)(2,1)S(1)}, u32[]{:S(2)}, u32[]{:S(2)}) %collective-permute-start.6) | collective-permute-done | bytes 614432 | tf_op jit(solution)/shard_map/ppermute | solution.py:24
  56.2 3.4 collective-permute-done.8
  60.4 1.8 pad_maximum_fusion
  63.1 2.0 select_multiply_fusion.scale_ref
  67.1 1.4 select_reduce_fusion
  69.7 2.0 constant_dynamic-update-slice_fusion.15
  72.5 1.6 constant_dynamic-update-slice_fusion.13
  74.1 8.0 %fusion.12 = bf16[16,64,768]{2,1,0:T(8,128)(2,1)S(1)} fusion(bf16[3200,768,1]{1,0,2:T(8,128)(2,1)} %bitcast.151, s32[3200]{0:T(1024)S(1)} %add.330, s32[16,64]{1,0:T(8,128)S(1)} %reshape.313), kind=kOutput, calls=%fused_computation.24 | convolution fusion | flops 5037228032 | bytes 6504960 | tf_op jit(solution)/shard_map/dot_general | solution.py:128
  82.1 1.5 pad_maximum_fusion.1
  83.7 17.7 %all-gather.2.cloned.1.call-done.wq_ref.wk_ref.wv_ref.wa_ref.in_ref.dense_ref.expand_ref = bf16[768,10112]{1,0:T(8,128)(2,1)} async-done(((bf16[24,10112]{1,0:T(8,128)(2,1)}), bf16[768,10112]{1,0:T(8,128)(2,1)}) %all-gather.2.cloned.1.call-update) | async-done | bytes 15532048 | tf_op jit(solution)/shard_map/all_gather | solution.py:827
  103.4 6.9 %shard_map.409 = bf16[32,4,24,768]{3,2,1,0:T(8,128)(2,1)} custom-call(bf16[768,10112]{1,0:T(8,128)(2,1)} %all-gather.2.cloned.1.call-done.wq_ref.wk_ref.wv_ref.wa_ref.in_ref.dense_ref.expand_ref), custom_call_target="tpu_custom_call" | custom-call | flops 1000 | bytes 1000 | tf_op jit(solution)/shard_map/pallas_call | solution.py:318
  111.7 5.4 %all-to-all-start = ((bf16[16,64,896]{2,1,0:T(8,128)(2,1)}), bf16[16,64,896]{2,1,0:T(8,128)(2,1)S(1)}, u32[]{:S(2)}, u32[]{:S(2)}) async-start(bf16[16,64,896]{2,1,0:T(8,128)(2,1)} %pad_maximum_fusion.1), calls=%async_computation | async-start | bytes 3670016 | tf_op jit(solution)/shard_map/all_to_all | solution.py:44
  117.4 11.0 %shard_map.408 = (bf16[512,2304]{1,0:T(8,128)(2,1)}, bf16[2,12,256,256]{3,2,1,0:T(8,128)(2,1)}, bf16[512,768]{1,0:T(8,128)(2,1)S(1)}, f32[512,768]{1,0:T(8,128)S...) custom-call(bf16[512,768]{1,0:T(8,128)(2,1)S(1)} %bitcast.129, ...), custom_call_target="tpu_custom_call" | custom-call | flops 4000000000 | bytes 16000000 | tf_op jit(solution)/shard_map/pallas_call | solution.py:209
  128.4 9.0 %fusion.7 = (bf16[512,3072]{1,0:T(8,128)(2,1)}, bf16[512,3072]{1,0:T(8,128)(2,1)S(1)}) fusion(f32[3072]{0:T(1024)S(1)} %reshape.309, bf16[512,768]{1,0:T(8,128)(2,1)S(1)} %get-tuple-element.77.low_ref, bf16[768,10112]{1,0:T(8,128)(2,1)} %all-gather.2.cloned.1.call-done.wq_ref.wk_ref.wv_ref.wa_ref.in_ref.dense_ref.expand_ref), kind=kOutput, calls=%fused_computation.9 | convolution fusion | flops 2436366336 | bytes 11808768 | tf_op jit(solution)/shard_map/dot_general | solution.py:128
  137.4 6.2 %fusion.41 = (f32[512]{0:T(512)S(1)}, f32[512,768]{1,0:T(8,128)S(1)}) fusion(f32[768]{0:T(1024)S(1)} %get-tuple-element.133, f32[512,768]{1,0:T(8,128)S(1)} %get-tuple-element.76, bf16[512,3072]{1,0:T(8,128)(2,1)S(1)} %get-tuple-element.152.act_ref, bf16[3072,768]{1,0:T(8,128)(2,1)} %bitcast.130), kind=kOutput, calls=%fused_computation.145 | convolution fusion | flops 2417098240 | bytes 11015168 | tf_op jit(solution)/shard_map/dot_general | solution.py:128
  143.9 1.5 add_convert_fusion.4
  145.6 3.0 fusion.27
  151.1 7.8 %all-to-all-start.1 = ((bf16[16,64,768]{2,1,0:T(8,128)(2,1)}), bf16[16,64,768]{2,1,0:T(8,128)(2,1)}, u32[]{:S(2)}, u32[]{:S(2)}) async-start(bf16[16,64,768]{2,1,0:T(8,128)(2,1)} %broadcast_in_dim.59), calls=%async_computation.1 | async-start | bytes 3145728 | tf_op jit(solution)/shard_map/all_to_all | solution.py:44
  161.3 21.3 %all-to-all-done.1 = bf16[16,64,768]{2,1,0:T(8,128)(2,1)} async-done(((bf16[16,64,768]{2,1,0:T(8,128)(2,1)}), bf16[16,64,768]{2,1,0:T(8,128)(2,1)}, u32[]{:S(2)}, u32[]{:S(2)}) %all-to-all-start.1) | async-done | bytes 1572896 | tf_op jit(solution)/shard_map/all_to_all | solution.py:44
  182.6 25.3 %shard_map.410 = (bf16[1024,3200]{1,0:T(8,128)(2,1)}, f32[1024,128]{1,0:T(8,128)}, bf16[16,80,768]{2,1,0:T(8,128)(2,1)}) custom-call(bf16[1024,768]{1,0:T(8,128)(2,1)} %bitcast.48.spread_ref, bf16[3200,768]{1,0:T(8,128)(2,1)} %bitcast.152, f32[1,3200]{1,0:T(1,128)} %reshape.310.b_ref, s32[1,3200]{1,0:T(1,128)} %add.358.column_ref, s32[1024,1]{1,0:T(8,128)} %copy.128.label_ref), custom_call_target="tpu_custom_call" | custom-call | flops 10000000000 | bytes 20000000 | tf_op jit(solution)/shard_map/pallas_call | solution.py:318
  207.9 3.9 all-to-all-start.2
  213.1 1.8 convert_reduce_fusion
  216.4 22.0 %all-to-all-done.2.part_ref = bf16[16,80,768]{2,1,0:T(8,128)(2,1)S(1)} async-done(((bf16[16,80,768]{2,1,0:T(8,128)(2,1)}), bf16[16,80,768]{2,1,0:T(8,128)(2,1)S(1)}, u32[]{:S(2)}, u32[]{:S(2)}) %all-to-all-start.2) | async-done | bytes 1966112 | tf_op jit(solution)/shard_map/all_to_all | solution.py:44
  239.7 7.1 %shard_map.411 = (f32[1,1024]{1,0:T(1,128)}, f32[8,128]{1,0:T(8,128)}, f32[768,768]{1,0:T(8,128)}, f32[512,768]{1,0:T(8,128)}, bf16[512,768]{1,0:T(8,128)(2,1)}, /*index=5*/f32[8,768]{1,0:T(8,128)}) custom-call(s32[1]{0:T(128)} %bitcast.47.own_ref, bf16[16,80,768]{2,1,0:T(8,128)(2,1)} %copy-done.10, bf16[64,768]{1,0:T(8,128)(2,1)} %copy-done.25, ...), custom_call_target="tpu_custom_call" | custom-call | flops 300000000 | bytes 10000000 | tf_op jit(solution)/shard_map/pallas_call | solution.py:318
  246.8 7.7 %shard_map.412 = (bf16[16,128,768]{2,1,0:T(8,128)(2,1)}, bf16[16,128,768]{2,1,0:T(8,128)(2,1)}) custom-call(s32[1]{0:T(128)} %bitcast.46.core_ref, bf16[512,3072]{1,0:T(8,128)(2,1)} %copy-done.13, bf16[512,768]{1,0:T(8,128)(2,1)} %get-tuple-element.90.dffn_ref, f32[768,768]{1,0:T(8,128)} %get-tuple-element.86.dense_ref, f32[8,128]{1,0:T(8,128)} %get-tuple-element.87.loss_ref), custom_call_target="tpu_custom_call" | custom-call | flops 1000 | bytes 1000 | tf_op jit(solution)/shard_map/pallas_call | solution.py:318
  254.5 17.1 %shard_map.413 = (bf16[16,24,3072]{2,1,0:T(8,128)(2,1)}, bf16[16,24,3072]{2,1,0:T(8,128)(2,1)}, f32[1,3072]{1,0:T(1,128)}, f32[512,768]{1,0:T(8,128)}, bf16[512,768]{1,0:T(8,128)(2,1)}, /*index=5*/f32[8,768]{1,0:T(8,128)}) custom-call(s32[1]{0:T(128)} %bitcast.46.core_ref, bf16[512,768]{1,0:T(8,128)(2,1)} %get-tuple-element.90.dffn_ref, ...), custom_call_target="tpu_custom_call" | custom-call | flops 1000 | bytes 1000 | tf_op jit(solution)/shard_map/pallas_call | solution.py:318
  271.6 2.6 add_convert_fusion
  274.2 4.8 %all-to-all-start.3 = ((bf16[16,128,768]{2,1,0:T(8,128)(2,1)}), bf16[16,128,768]{2,1,0:T(8,128)(2,1)}, u32[]{:S(2)}, u32[]{:S(2)}) async-start(bf16[16,128,768]{2,1,0:T(8,128)(2,1)} %add_convert_fusion), calls=%async_computation.3 | async-start | bytes 6291456 | tf_op jit(solution)/shard_map/all_to_all | solution.py:44
  285.2 12.1 %shard_map.414 = (bf16[512,2304]{1,0:T(8,128)(2,1)S(1)}, f32[1,2304]{1,0:T(1,128)S(1)}) custom-call(bf16[512,768]{1,0:T(8,128)(2,1)S(1)} %copy-done.1, bf16[512,2304]{1,0:T(8,128)(2,1)S(1)} %copy-done.4, bf16[2,12,256,256]{3,2,1,0:T(8,128)(2,1)} %get-tuple-element.101.probs_ref, ...), custom_call_target="tpu_custom_call" | custom-call | flops 1000 | bytes 1000 | tf_op jit(solution)/shard_map/pallas_call | solution.py:289
  297.3 1.5 copy-done.2
  300.7 9.1 %shard_map.415 = (bf16[16,24,3200]{2,1,0:T(8,128)(2,1)}, bf16[16,24,3200]{2,1,0:T(8,128)(2,1)}) custom-call(s32[1]{0:T(128)} %bitcast.46.core_ref, bf16[512,768]{1,0:T(8,128)(2,1)} %bitcast.128, bf16[512,2304]{1,0:T(8,128)(2,1)} %copy-done.2, bf16[512,768]{1,0:T(8,128)(2,1)} %copy-done.7, bf16[512,768]{1,0:T(8,128)(2,1)} %get-tuple-element.99.dbranch_ref, ...), custom_call_target="tpu_custom_call" | custom-call | flops 1000 | bytes 1000 | tf_op jit(solution)/shard_map/pallas_call | solution.py:318
  309.8 13.2 %all-to-all-done.3 = bf16[16,128,768]{2,1,0:T(8,128)(2,1)} async-done(((bf16[16,128,768]{2,1,0:T(8,128)(2,1)}), bf16[16,128,768]{2,1,0:T(8,128)(2,1)}, u32[]{:S(2)}, u32[]{:S(2)}) %all-to-all-start.3) | async-done | bytes 3145760 | tf_op jit(solution)/shard_map/all_to_all | solution.py:44
  323.0 4.7 %add_convert_fusion.3 = bf16[16,24,3072]{2,1,0:T(8,128)(2,1)} fusion(bf16[16,24,3072]{2,1,0:T(8,128)(2,1)} %collective-permute-done.14, bf16[16,24,3072]{2,1,0:T(8,128)(2,1)} %get-tuple-element.94), kind=kLoop, calls=%fused_computation.15 | loop fusion | flops 4718592 | bytes 7077888 | tf_op jit(solution)/shard_map/convert_element_type | solution.py:63
  327.7 10.3 %all-to-all-start.4 = ((bf16[16,24,3072]{2,1,0:T(8,128)(2,1)}), bf16[16,24,3072]{2,1,0:T(8,128)(2,1)}, u32[]{:S(2)}, u32[]{:S(2)}) async-start(bf16[16,24,3072]{2,1,0:T(8,128)(2,1)} %add_convert_fusion.3), calls=%async_computation.4 | async-start | bytes 4718592 | tf_op jit(solution)/shard_map/all_to_all | solution.py:44
  338.0 17.5 %shard_map.416 = bf16[3200,896]{1,0:T(8,128)(2,1)} custom-call(bf16[1024,3200]{1,0:T(8,128)(2,1)} %get-tuple-element.112.expl_ref, bf16[1024,768]{1,0:T(8,128)(2,1)} %bitcast.48.spread_ref, s32[1,3200]{1,0:T(1,128)} %add.358.column_ref, s32[1024,1]{1,0:T(8,128)} %copy.128.label_ref, f32[1024,1]{1,0:T(8,128)} %select_multiply_fusion.scale_ref, ...), custom_call_target="tpu_custom_call" | custom-call | flops 1000 | bytes 1000 | tf_op jit(solution)/shard_map/pallas_call | solution.py:318
  355.5 5.8 %fusion.37 = (bf16[1600,896]{1,0:T(8,128)(2,1)}, bf16[1600,896]{1,0:T(8,128)(2,1)}) fusion(bf16[3200,896]{1,0:T(8,128)(2,1)} %shard_map.416), kind=kLoop, calls=%fused_computation.141 | loop fusion | bytes 11468800 | tf_op jit(solution)/shard_map/slice | solution.py:987
  361.3 1.4 copy-done.17
  362.7 3.8 add_convert_fusion.2
  366.5 5.0 %all-to-all-done.4 = bf16[16,24,3072]{2,1,0:T(8,128)(2,1)} async-done(((bf16[16,24,3072]{2,1,0:T(8,128)(2,1)}), bf16[16,24,3072]{2,1,0:T(8,128)(2,1)}, u32[]{:S(2)}, u32[]{:S(2)}) %all-to-all-start.4) | async-done | bytes 2359328 | tf_op jit(solution)/shard_map/all_to_all | solution.py:44
  371.6 5.6 %fusion.17 = f32[512,768]{1,0:T(8,128)} fusion(f32[512,768]{1,0:T(8,128)} %get-tuple-element.126, bf16[512,2304]{1,0:T(8,128)(2,1)S(1)} %copy-done.3, bf16[768,10112]{1,0:T(8,128)(2,1)} %all-gather.2.cloned.1.call-done.wq_ref.wk_ref.wv_ref.wa_ref.in_ref.dense_ref.expand_ref), kind=kOutput, calls=%fused_computation.32 | convolution fusion | flops 1812332544 | bytes 9043968 | tf_op jit(solution)/shard_map/dot_general | solution.py:136
  377.2 2.2 slice_reduce_fusion
  379.4 6.2 %all-to-all-start.5 = ((bf16[16,24,3200]{2,1,0:T(8,128)(2,1)}), bf16[16,24,3200]{2,1,0:T(8,128)(2,1)}, u32[]{:S(2)}, u32[]{:S(2)}) async-start(bf16[16,24,3200]{2,1,0:T(8,128)(2,1)} %add_convert_fusion.2), calls=%async_computation.5 | async-start | bytes 4915200 | tf_op jit(solution)/shard_map/all_to_all | solution.py:44
  385.7 1.4 convert_reduce_fusion.2
  393.3 3.4 add_convert_fusion.1
  396.7 1.4 slice_bitcast_fusion.3
  398.0 1.5 collective-permute-start.18
  399.5 3.0 collective-permute-start.19
  405.6 2.1 reduce_sum.135
  408.5 9.3 %collective-permute-done.18 = bf16[400,896]{1,0:T(8,128)(2,1)} collective-permute-done((bf16[400,896]{1,0:T(8,128)(2,1)}, bf16[400,896]{1,0:T(8,128)(2,1)}, u32[]{:S(2)}, u32[]{:S(2)}) %collective-permute-start.18) | collective-permute-done | bytes 716832 | tf_op jit(solution)/shard_map/ppermute | solution.py:29
  417.8 16.5 %collective-permute-done.19 = bf16[400,896]{1,0:T(8,128)(2,1)} collective-permute-done((bf16[400,896]{1,0:T(8,128)(2,1)}, bf16[400,896]{1,0:T(8,128)(2,1)}, u32[]{:S(2)}, u32[]{:S(2)}) %collective-permute-start.19) | collective-permute-done | bytes 716832 | tf_op jit(solution)/shard_map/ppermute | solution.py:29
  434.3 3.0 fusion.16
  437.3 2.1 reduce_sum.136
  440.2 3.7 all-to-all-start.6
  445.7 8.9 %all-to-all-done.6 = bf16[4,6,10240]{2,1,0:T(8,128)(2,1)S(1)} async-done(((bf16[4,6,10240]{2,1,0:T(8,128)(2,1)}), bf16[4,6,10240]{2,1,0:T(8,128)(2,1)S(1)}, u32[]{:S(2)}, u32[]{:S(2)}) %all-to-all-start.6) | async-done | bytes 491552 | tf_op jit(solution)/shard_map/all_to_all | solution.py:44
  (228 shorter events, 52.3 us)
Async XLA Ops:
  7.2 94.2 %all-gather.2.cloned.1.call-start = ((), (), s32[]{:S(2)}) async-start(), calls=%async_computation.7 | async-start | bytes 16017408 | tf_op jit(solution)/shard_map/all_gather | solution.py:827
  10.5 19.5 %copy-start.18 = (bf16[768,400]{0,1:T(8,128)(2,1)S(1)}, bf16[768,400]{0,1:T(8,128)(2,1)}, u32[]{:S(2)}) copy-start(bf16[768,400]{0,1:T(8,128)(2,1)} %param.48) | copy-start | bytes 1843204
  10.5 22.5 %copy-start.34 = (bf16[400]{0:T(512)(128)(2,1)S(1)}, bf16[400]{0:T(512)(128)(2,1)}, u32[]{:S(2)}) copy-start(bf16[400]{0:T(512)(128)(2,1)} %param.49) | copy-start | bytes 2404
  12.8 24.9 %copy-start.28 = (s32[2,128,16,2]{1,3,2,0:T(2,128)S(1)}, s32[2,128,16,2]{1,3,2,0:T(2,128)}, u32[]{:S(2)}) copy-start(s32[2,128,16,2]{1,3,2,0:T(2,128)} %param.29) | copy-start | bytes 98308
  12.8 16.0 %collective-permute-start.3 = (bf16[6,7040]{1,0:T(8,128)(2,1)S(1)}, bf16[6,7040]{1,0:T(8,128)(2,1)S(1)}, u32[]{:S(2)}, u32[]{:S(2)}) collective-permute-start(bf16[6,7040]{1,0:T(8,128)(2,1)S(1)} %constant_dynamic-update-slice_fusion.8), channel_id=1, source_target_pairs={{1,0},{2,1},{3,2},{0,3},{5,4},{6,5},{7,6},{4,7},{9,8},{10,9},{11,1... | collective-permute-start | bytes 253448 | tf_op jit(solution)/shard_map/ppermute | solution.py:24
  15.7 13.1 %collective-permute-start.4 = (bf16[6,7040]{1,0:T(8,128)(2,1)S(1)}, bf16[6,7040]{1,0:T(8,128)(2,1)S(1)}, u32[]{:S(2)}, u32[]{:S(2)}) collective-permute-start(bf16[6,7040]{1,0:T(8,128)(2,1)S(1)} %constant_dynamic-update-slice_fusion.8), channel_id=1, source_target_pairs={{2,0},{3,1},{0,2},{1,3},{6,4},{7,5},{4,6},{5,7},{10,8},{11,9},{8,1... | collective-permute-start | bytes 253448 | tf_op jit(solution)/shard_map/ppermute | solution.py:24
  16.5 12.3 %collective-permute-start.5 = (bf16[6,7040]{1,0:T(8,128)(2,1)S(1)}, bf16[6,7040]{1,0:T(8,128)(2,1)S(1)}, u32[]{:S(2)}, u32[]{:S(2)}) collective-permute-start(bf16[6,7040]{1,0:T(8,128)(2,1)S(1)} %constant_dynamic-update-slice_fusion.8), channel_id=1, source_target_pairs={{3,0},{0,1},{1,2},{2,3},{7,4},{4,5},{5,6},{6,7},{11,8},{8,9},{9,10... | collective-permute-start | bytes 253448 | tf_op jit(solution)/shard_map/ppermute | solution.py:24
  17.4 4.7 %collective-permute-start = (bf16[24,768]{1,0:T(8,128)(2,1)}, bf16[24,768]{1,0:T(8,128)(2,1)S(1)}, u32[]{:S(2)}, u32[]{:S(2)}) collective-permute-start(bf16[24,768]{1,0:T(8,128)(2,1)} %param.40), channel_id=1, source_target_pairs={{1,0},{2,1},{3,2},{0,3},{5,4},{6,5},{7,6},{4,7},{9,8},{10,9},{11,1... | collective-permute-start | bytes 110600 | tf_op jit(solution)/shard_map/ppermute | solution.py:24
  19.7 5.7 %collective-permute-start.1 = (bf16[24,768]{1,0:T(8,128)(2,1)}, bf16[24,768]{1,0:T(8,128)(2,1)S(1)}, u32[]{:S(2)}, u32[]{:S(2)}) collective-permute-start(bf16[24,768]{1,0:T(8,128)(2,1)} %param.40), channel_id=1, source_target_pairs={{2,0},{3,1},{0,2},{1,3},{6,4},{7,5},{4,6},{5,7},{10,8},{11,9},{8,1... | collective-permute-start | bytes 110600 | tf_op jit(solution)/shard_map/ppermute | solution.py:24
  22.1 5.8 %collective-permute-start.2 = (bf16[24,768]{1,0:T(8,128)(2,1)}, bf16[24,768]{1,0:T(8,128)(2,1)S(1)}, u32[]{:S(2)}, u32[]{:S(2)}) collective-permute-start(bf16[24,768]{1,0:T(8,128)(2,1)} %param.40), channel_id=1, source_target_pairs={{3,0},{0,1},{1,2},{2,3},{7,4},{4,5},{5,6},{6,7},{11,8},{8,9},{9,10... | collective-permute-start | bytes 110600 | tf_op jit(solution)/shard_map/ppermute | solution.py:24
  28.8 13.0 %copy-start.33 = (s32[2,1,16,2]{2,3,1,0:T(2,128)S(1)}, s32[2,1,16,2]{2,3,1,0:T(2,128)}, u32[]{:S(2)}) copy-start(s32[2,1,16,2]{2,3,1,0:T(2,128)} %param.28) | copy-start | bytes 772
  30.0 26.2 %collective-permute-start.6 = (bf16[400,768]{1,0:T(8,128)(2,1)S(1)}, bf16[400,768]{1,0:T(8,128)(2,1)S(1)}, u32[]{:S(2)}, u32[]{:S(2)}) collective-permute-start(bf16[400,768]{1,0:T(8,128)(2,1)S(1)} %bitcast.138), channel_id=1, source_target_pairs={{1,0},{2,1},{3,2},{0,3},{5,4},{6,5},{7,6},{4,7},{9,8},{10,9},{11,1... | collective-permute-start | bytes 1843208 | tf_op jit(solution)/shard_map/ppermute | solution.py:24
  32.1 24.1 %collective-permute-start.7 = (bf16[400,768]{1,0:T(8,128)(2,1)S(1)}, bf16[400,768]{1,0:T(8,128)(2,1)S(1)}, u32[]{:S(2)}, u32[]{:S(2)}) collective-permute-start(bf16[400,768]{1,0:T(8,128)(2,1)S(1)} %bitcast.139), channel_id=1, source_target_pairs={{2,0},{3,1},{0,2},{1,3},{6,4},{7,5},{4,6},{5,7},{10,8},{11,9},{8,1... | collective-permute-start | bytes 1843208 | tf_op jit(solution)/shard_map/ppermute | solution.py:24
  32.2 27.4 %collective-permute-start.8 = (bf16[400,768]{1,0:T(8,128)(2,1)S(1)}, bf16[400,768]{1,0:T(8,128)(2,1)S(1)}, u32[]{:S(2)}, u32[]{:S(2)}) collective-permute-start(bf16[400,768]{1,0:T(8,128)(2,1)S(1)} %bitcast.140), channel_id=1, source_target_pairs={{3,0},{0,1},{1,2},{2,3},{7,4},{4,5},{5,6},{6,7},{11,8},{8,9},{9,10... | collective-permute-start | bytes 1843208 | tf_op jit(solution)/shard_map/ppermute | solution.py:24
  33.0 32.2 %collective-permute-start.10 = (bf16[400]{0:T(512)(128)(2,1)S(1)}, bf16[400]{0:T(512)(128)(2,1)S(1)}, u32[]{:S(2)}, u32[]{:S(2)}) collective-permute-start(bf16[400]{0:T(512)(128)(2,1)S(1)} %copy-done.34), channel_id=1, source_target_pairs={{1,0},{2,1},{3,2},{0,3},{5,4},{6,5},{7,6},{4,7},{9,8},{10,9},{11,1... | collective-permute-start | bytes 2408 | tf_op jit(solution)/shard_map/ppermute | solution.py:24
  35.4 29.8 %collective-permute-start.11 = (bf16[400]{0:T(512)(128)(2,1)S(1)}, bf16[400]{0:T(512)(128)(2,1)S(1)}, u32[]{:S(2)}, u32[]{:S(2)}) collective-permute-start(bf16[400]{0:T(512)(128)(2,1)S(1)} %copy-done.34), channel_id=1, source_target_pairs={{2,0},{3,1},{0,2},{1,3},{6,4},{7,5},{4,6},{5,7},{10,8},{11,9},{8,1... | collective-permute-start | bytes 2408 | tf_op jit(solution)/shard_map/ppermute | solution.py:24
  42.1 21.0 %copy-start.24 = (f32[1024,1]{1,0:T(8,128)S(1)}, f32[1024,1]{1,0:T(8,128)}, u32[]{:S(2)}) copy-start(f32[1024,1]{1,0:T(8,128)} %reshape.314) | copy-start | bytes 12292
  56.2 3.4 copy-start.19
  56.2 9.1 %collective-permute-start.12 = (bf16[400]{0:T(512)(128)(2,1)S(1)}, bf16[400]{0:T(512)(128)(2,1)S(1)}, u32[]{:S(2)}, u32[]{:S(2)}) collective-permute-start(bf16[400]{0:T(512)(128)(2,1)S(1)} %copy-done.34), channel_id=1, source_target_pairs={{3,0},{0,1},{1,2},{2,3},{7,4},{4,5},{5,6},{6,7},{11,8},{8,9},{9,10... | collective-permute-start | bytes 2408 | tf_op jit(solution)/shard_map/ppermute | solution.py:24
  56.2 3.4 copy-start.21
  59.5 0.8 copy-start.22
  60.4 6.2 %copy-start.32 = (s32[2,256]{1,0:T(2,128)S(1)}, s32[2,256]{1,0:T(2,128)}, u32[]{:S(2)}) copy-start(s32[2,256]{1,0:T(2,128)} %param.27) | copy-start | bytes 6148
  62.1 10.4 %collective-permute-start.9 = (bf16[4,400,768]{2,1,0:T(8,128)(2,1)}, bf16[4,400,768]{2,1,0:T(8,128)(2,1)S(1)}, u32[]{:S(2)}, u32[]{:S(2)}) collective-permute-start(bf16[4,400,768]{2,1,0:T(8,128)(2,1)} %pad_maximum_fusion), channel_id=1, source_target_pairs={{16,0},{0,16},{17,1},{1,17},{18,2},{2,18},{19,3},{3,19},{20,4},{4,... | collective-permute-start | bytes 7372808 | tf_op jit(solution)/shard_map/ppermute | solution.py:24
  62.2 83.1 %copy-start.26 = (bf16[64,512]{1,0:T(8,128)(2,1)}, bf16[64,512]{1,0:T(8,128)(2,1)S(1)}, u32[]{:S(2)}) copy-start(bf16[64,512]{1,0:T(8,128)(2,1)S(1)} %fusion.28.select_ref) | copy-start | bytes 196612
  63.1 5.7 %copy-start.20 = (bf16[400,768]{1,0:T(8,128)(2,1)S(1)}, bf16[400,768]{1,0:T(8,128)(2,1)}, u32[]{:S(2)}) copy-start(bf16[400,768]{1,0:T(8,128)(2,1)} %copy-done.19) | copy-start | bytes 1843204
  65.3 1.6 collective-permute-start.13
  67.1 4.6 copy-start.23
  110.4 6.9 %copy-start.8 = (f32[16,768]{1,0:T(8,128)}, f32[16,768]{1,0:T(8,128)S(1)}, u32[]{:S(2)}) copy-start(f32[16,768]{1,0:T(8,128)S(1)} %copy.127.vec_ref) | copy-start | bytes 147460
  110.4 7.0 %copy-start = (bf16[2,256,768]{2,1,0:T(8,128)(2,1)S(1)}, bf16[2,256,768]{2,1,0:T(8,128)(2,1)}, u32[]{:S(2)}) copy-start(bf16[2,256,768]{2,1,0:T(8,128)(2,1)} %param.25) | copy-start | bytes 2359300
  111.7 33.6 %all-to-all-start = ((bf16[16,64,896]{2,1,0:T(8,128)(2,1)}), bf16[16,64,896]{2,1,0:T(8,128)(2,1)S(1)}, u32[]{:S(2)}, u32[]{:S(2)}) async-start(bf16[16,64,896]{2,1,0:T(8,128)(2,1)} %pad_maximum_fusion.1), calls=%async_computation | async-start | bytes 3670016 | tf_op jit(solution)/shard_map/all_to_all | solution.py:44
  128.4 9.0 %copy-start.5 = (f32[512,768]{1,0:T(8,128)}, f32[512,768]{1,0:T(8,128)S(1)}, u32[]{:S(2)}) copy-start(f32[512,768]{1,0:T(8,128)S(1)} %get-tuple-element.92.normed_ref) | copy-start | bytes 4718596
  128.4 9.0 %copy-start.6 = (bf16[512,768]{1,0:T(8,128)(2,1)}, bf16[512,768]{1,0:T(8,128)(2,1)S(1)}, u32[]{:S(2)}) copy-start(bf16[512,768]{1,0:T(8,128)(2,1)S(1)} %get-tuple-element.77.low_ref) | copy-start | bytes 2359300
  128.4 9.0 %copy-start.7 = (bf16[512,768]{1,0:T(8,128)(2,1)}, bf16[512,768]{1,0:T(8,128)(2,1)S(1)}, u32[]{:S(2)}) copy-start(bf16[512,768]{1,0:T(8,128)(2,1)S(1)} %get-tuple-element.103.attended_ref) | copy-start | bytes 2359300
  128.4 9.0 %copy-start.9 = (f32[512,1]{1,0:T(8,128)}, f32[512,1]{1,0:T(8,128)S(1)}, u32[]{:S(2)}) copy-start(f32[512,1]{1,0:T(8,128)S(1)} %get-tuple-element.93.inverse_ref) | copy-start | bytes 6148
  137.4 6.2 %copy-start.13 = (bf16[512,3072]{1,0:T(8,128)(2,1)}, bf16[512,3072]{1,0:T(8,128)(2,1)S(1)}, u32[]{:S(2)}) copy-start(bf16[512,3072]{1,0:T(8,128)(2,1)S(1)} %get-tuple-element.152.act_ref) | copy-start | bytes 9437188
  145.3 5.7 %copy-start.15 = (bf16[512,768]{1,0:T(8,128)(2,1)}, bf16[512,768]{1,0:T(8,128)(2,1)S(1)}, u32[]{:S(2)}) copy-start(bf16[512,768]{1,0:T(8,128)(2,1)S(1)} %get-tuple-element.149) | copy-start | bytes 2359300
  145.4 5.7 %copy-start.11 = (bf16[16,64,896]{2,1,0:T(8,128)(2,1)}, bf16[16,64,896]{2,1,0:T(8,128)(2,1)S(1)}, u32[]{:S(2)}) copy-start(bf16[16,64,896]{2,1,0:T(8,128)(2,1)S(1)} %all-to-all-done) | copy-start | bytes 5505028
  145.6 5.5 %copy-start.27 = (bf16[64,768]{1,0:T(8,128)(2,1)}, bf16[64,768]{1,0:T(8,128)(2,1)S(1)}, u32[]{:S(2)}) copy-start(bf16[64,768]{1,0:T(8,128)(2,1)S(1)} %convolution_convert_fusion.picked_ref) | copy-start | bytes 294916
  149.8 58.2 %copy-start.25 = (bf16[64,768]{1,0:T(8,128)(2,1)}, bf16[64,768]{1,0:T(8,128)(2,1)S(1)}, u32[]{:S(2)}) copy-start(bf16[64,768]{1,0:T(8,128)(2,1)S(1)} %get-tuple-element.147.head_ref) | copy-start | bytes 294916
  151.1 31.5 %all-to-all-start.1 = ((bf16[16,64,768]{2,1,0:T(8,128)(2,1)}), bf16[16,64,768]{2,1,0:T(8,128)(2,1)}, u32[]{:S(2)}, u32[]{:S(2)}) async-start(bf16[16,64,768]{2,1,0:T(8,128)(2,1)} %broadcast_in_dim.59), calls=%async_computation.1 | async-start | bytes 3145728 | tf_op jit(solution)/shard_map/all_to_all | solution.py:44
  207.9 30.5 %all-to-all-start.2 = ((bf16[16,80,768]{2,1,0:T(8,128)(2,1)}), bf16[16,80,768]{2,1,0:T(8,128)(2,1)S(1)}, u32[]{:S(2)}, u32[]{:S(2)}) async-start(bf16[16,80,768]{2,1,0:T(8,128)(2,1)} %get-tuple-element.83), calls=%async_computation.2 | async-start | bytes 3932160 | tf_op jit(solution)/shard_map/all_to_all | solution.py:44
  238.4 1.3 copy-start.10
  254.5 17.1 %collective-permute-start.15 = (bf16[16,128,768]{2,1,0:T(8,128)(2,1)}, bf16[16,128,768]{2,1,0:T(8,128)(2,1)S(1)}, u32[]{:S(2)}, u32[]{:S(2)}) collective-permute-start(bf16[16,128,768]{2,1,0:T(8,128)(2,1)} %get-tuple-element.98), channel_id=1, source_target_pairs={{0,16},{16,0},{1,17},{17,1},{2,18},{18,2},{3,19},{19,3},{4,20},{20... | collective-permute-start | bytes 9437192 | tf_op jit(solution)/shard_map/ppermute | solution.py:29
  254.5 17.1 %copy-start.14 = (bf16[16,128,768]{2,1,0:T(8,128)(2,1)S(1)}, bf16[16,128,768]{2,1,0:T(8,128)(2,1)}, u32[]{:S(2)}) copy-start(bf16[16,128,768]{2,1,0:T(8,128)(2,1)} %get-tuple-element.97) | copy-start | bytes 9437188
  274.2 7.6 %copy-start.30 = (f32[8,768]{1,0:T(8,128)S(1)}, f32[8,768]{1,0:T(8,128)}, u32[]{:S(2)}) copy-start(f32[8,768]{1,0:T(8,128)} %get-tuple-element.106) | copy-start | bytes 73732
  274.2 9.9 %copy-start.31 = (f32[1,3072]{1,0:T(1,128)S(1)}, f32[1,3072]{1,0:T(1,128)}, u32[]{:S(2)}) copy-start(f32[1,3072]{1,0:T(1,128)} %get-tuple-element.107) | copy-start | bytes 36868
  274.2 11.0 %copy-start.1 = (bf16[512,768]{1,0:T(8,128)(2,1)S(1)}, bf16[512,768]{1,0:T(8,128)(2,1)}, u32[]{:S(2)}) copy-start(bf16[512,768]{1,0:T(8,128)(2,1)} %get-tuple-element.99.dbranch_ref) | copy-start | bytes 2359300
  274.2 11.0 %copy-start.4 = (bf16[512,2304]{1,0:T(8,128)(2,1)S(1)}, bf16[512,2304]{1,0:T(8,128)(2,1)}, u32[]{:S(2)}) copy-start(bf16[512,2304]{1,0:T(8,128)(2,1)} %get-tuple-element.100.qkv_ref) | copy-start | bytes 7077892
  274.2 48.8 %all-to-all-start.3 = ((bf16[16,128,768]{2,1,0:T(8,128)(2,1)}), bf16[16,128,768]{2,1,0:T(8,128)(2,1)}, u32[]{:S(2)}, u32[]{:S(2)}) async-start(bf16[16,128,768]{2,1,0:T(8,128)(2,1)} %add_convert_fusion), calls=%async_computation.3 | async-start | bytes 6291456 | tf_op jit(solution)/shard_map/all_to_all | solution.py:44
  279.0 44.0 %collective-permute-start.14 = (bf16[16,24,3072]{2,1,0:T(8,128)(2,1)}, bf16[16,24,3072]{2,1,0:T(8,128)(2,1)}, u32[]{:S(2)}, u32[]{:S(2)}) collective-permute-start(bf16[16,24,3072]{2,1,0:T(8,128)(2,1)} %get-tuple-element.95), channel_id=1, source_target_pairs={{0,16},{16,0},{1,17},{17,1},{2,18},{18,2},{3,19},{19,3},{4,20},{20... | collective-permute-start | bytes 7077896 | tf_op jit(solution)/shard_map/ppermute | solution.py:29
  285.2 13.6 %copy-start.29 = (f32[3,768]{1,0:T(4,128)S(1)}, f32[3,768]{1,0:T(4,128)}, u32[]{:S(2)}) copy-start(f32[3,768]{1,0:T(4,128)} %slice.196) | copy-start | bytes 27652
  297.3 1.5 copy-start.2
  323.0 38.3 %collective-permute-start.16 = (bf16[16,24,3200]{2,1,0:T(8,128)(2,1)}, bf16[16,24,3200]{2,1,0:T(8,128)(2,1)S(1)}, u32[]{:S(2)}, u32[]{:S(2)}) collective-permute-start(bf16[16,24,3200]{2,1,0:T(8,128)(2,1)} %get-tuple-element.119), channel_id=1, source_target_pairs={{0,16},{16,0},{1,17},{17,1},{2,18},{18,2},{3,19},{19,3},{4,20},{20... | collective-permute-start | bytes 7372808 | tf_op jit(solution)/shard_map/ppermute | solution.py:29
  327.7 43.9 %all-to-all-start.4 = ((bf16[16,24,3072]{2,1,0:T(8,128)(2,1)}), bf16[16,24,3072]{2,1,0:T(8,128)(2,1)}, u32[]{:S(2)}, u32[]{:S(2)}) async-start(bf16[16,24,3072]{2,1,0:T(8,128)(2,1)} %add_convert_fusion.3), calls=%async_computation.4 | async-start | bytes 4718592 | tf_op jit(solution)/shard_map/all_to_all | solution.py:44
  355.5 7.2 %copy-start.16 = (bf16[16,24,3200]{2,1,0:T(8,128)(2,1)S(1)}, bf16[16,24,3200]{2,1,0:T(8,128)(2,1)}, u32[]{:S(2)}) copy-start(bf16[16,24,3200]{2,1,0:T(8,128)(2,1)} %get-tuple-element.118) | copy-start | bytes 7372804
  361.3 1.4 copy-start.17
  362.7 8.9 %copy-start.3 = (bf16[512,2304]{1,0:T(8,128)(2,1)S(1)}, bf16[512,2304]{1,0:T(8,128)(2,1)}, u32[]{:S(2)}) copy-start(bf16[512,2304]{1,0:T(8,128)(2,1)} %copy-done.2) | copy-start | bytes 7077892
  371.6 21.7 %collective-permute-start.17 = (bf16[4,400,896]{2,1,0:T(8,128)(2,1)}, bf16[4,400,896]{2,1,0:T(8,128)(2,1)}, u32[]{:S(2)}, u32[]{:S(2)}) collective-permute-start(bf16[4,400,896]{2,1,0:T(8,128)(2,1)} %bitcast.137), channel_id=1, source_target_pairs={{0,16},{16,0},{1,17},{17,1},{2,18},{18,2},{3,19},{19,3},{4,20},{20... | collective-permute-start | bytes 8601608 | tf_op jit(solution)/shard_map/ppermute | solution.py:29
  379.4 57.9 %all-to-all-start.5 = ((bf16[16,24,3200]{2,1,0:T(8,128)(2,1)}), bf16[16,24,3200]{2,1,0:T(8,128)(2,1)}, u32[]{:S(2)}, u32[]{:S(2)}) async-start(bf16[16,24,3200]{2,1,0:T(8,128)(2,1)} %add_convert_fusion.2), calls=%async_computation.5 | async-start | bytes 4915200 | tf_op jit(solution)/shard_map/all_to_all | solution.py:44
  398.0 19.7 %collective-permute-start.18 = (bf16[400,896]{1,0:T(8,128)(2,1)}, bf16[400,896]{1,0:T(8,128)(2,1)}, u32[]{:S(2)}, u32[]{:S(2)}) collective-permute-start(bf16[400,896]{1,0:T(8,128)(2,1)} %get-tuple-element.155), channel_id=1, source_target_pairs={{0,1},{1,2},{2,3},{3,0},{4,5},{5,6},{6,7},{7,4},{8,9},{9,10},{10,1... | collective-permute-start | bytes 2150408 | tf_op jit(solution)/shard_map/ppermute | solution.py:29
  399.5 34.8 %collective-permute-start.19 = (bf16[400,896]{1,0:T(8,128)(2,1)}, bf16[400,896]{1,0:T(8,128)(2,1)}, u32[]{:S(2)}, u32[]{:S(2)}) collective-permute-start(bf16[400,896]{1,0:T(8,128)(2,1)} %get-tuple-element.157), channel_id=1, source_target_pairs={{0,2},{1,3},{2,0},{3,1},{4,6},{5,7},{6,4},{7,5},{8,10},{9,11},{10,... | collective-permute-start | bytes 2150408 | tf_op jit(solution)/shard_map/ppermute | solution.py:29
  402.5 31.8 %collective-permute-start.20 = (bf16[400,896]{1,0:T(8,128)(2,1)}, bf16[400,896]{1,0:T(8,128)(2,1)}, u32[]{:S(2)}, u32[]{:S(2)}) collective-permute-start(bf16[400,896]{1,0:T(8,128)(2,1)} %get-tuple-element.156), channel_id=1, source_target_pairs={{0,3},{1,0},{2,1},{3,2},{4,7},{5,4},{6,5},{7,6},{8,11},{9,8},{10,9... | collective-permute-start | bytes 2150408 | tf_op jit(solution)/shard_map/ppermute | solution.py:29
  437.3 6.6 %copy-start.12 = (f32[400,896]{1,0:T(8,128)S(1)}, f32[400,896]{1,0:T(8,128)}, u32[]{:S(2)}) copy-start(f32[400,896]{1,0:T(8,128)} %fusion.16) | copy-start | bytes 4300804
  440.2 14.4 %all-to-all-start.6 = ((bf16[4,6,10240]{2,1,0:T(8,128)(2,1)}), bf16[4,6,10240]{2,1,0:T(8,128)(2,1)S(1)}, u32[]{:S(2)}, u32[]{:S(2)}) async-start(bf16[4,6,10240]{2,1,0:T(8,128)(2,1)} %constant_dynamic-update-slice_fusion.18), calls=%async_computation.6 | async-start | bytes 1310720 | tf_op jit(solution)/shard_map/all_to_all | solution.py:44
Sparse Core Ops, SparseCore 0:
  30.1 71.2 all-gather.1

commit v7 on v6

--- a/solution.py
+++ b/solution.py
@@ -1,3 +1,5 @@
+import functools
+
 import jax
 import jax.numpy as jnp
 from jax import lax
@@ -406,18 +408,17 @@
 
 
 def decoder_kernel(
-    expl_ref, spread_ref, column_ref, label_ref, scale_ref, stat_ref, lse_ref, out_ref
+    expl_ref, spread_ref, column_ref, label_ref, scale_ref, stat_ref, lse_ref, out_ref, sum_ref
 ):
-    count, width = spread_ref.shape
+    count = spread_ref.shape[0]
     lse = jnp.broadcast_to(lse_ref[...], (8, count)).T[:, 0:1]
     share = jnp.exp(stat_ref[:, 0:1] - lse)
     scale = scale_ref[...]
     hit = label_ref[...] == column_ref[...]
     other = (scale * share) * expl_ref[...].astype(F32)
     dlogits = jnp.where(hit, scale * (stat_ref[:, 1:2] * share - 1.0), other).astype(BF)
-    out_ref[:, :width] = dot_tn(dlogits, spread_ref[...]).astype(BF)
-    ones = jnp.ones((count, out_ref.shape[1] - width), BF)
-    out_ref[:, width:] = dot_tn(dlogits, ones).astype(BF)
+    out_ref[...] = dot_tn(dlogits, spread_ref[...]).astype(BF)
+    sum_ref[...] = jnp.sum(dlogits.astype(F32), axis=0, keepdims=True)
 
 
 def decoder_call(expl, spread, column, labels, scale, stat, lse):
@@ -435,12 +436,15 @@
             pl.BlockSpec((1, block), lambda j: (0, j)),
         ]
         + [whole_spec(a) for a in ins[3:]],
-        [((entries, width + 128), BF)],
-        [pl.BlockSpec((block, width + 128), lambda j: (j, 0))],
+        [((entries, width), BF), ((1, entries), F32)],
+        [
+            pl.BlockSpec((block, width), lambda j: (j, 0)),
+            pl.BlockSpec((1, block), lambda j: (0, j)),
+        ],
         [],
         1000,
         1000,
-    )[0]
+    )
 
 
 def merge_kernel(
@@ -627,25 +631,13 @@
     keep_halves(core, block, put(here_ref), put(away_ref))
 
 
-def feed_back_kernel(
-    core_ref,
-    dffn_ref,
-    shrink_ref,
-    slope_ref,
-    low_ref,
-    expand_ref,
-    dsecond_ref,
-    normed_ref,
-    inverse_ref,
-    vec_ref,
-    here_ref,
-    away_ref,
-    bias_ref,
-    dresidual_ref,
-    dbranch_ref,
-    sums_ref,
-    total_ref,
-):
+def feed_back_kernel(closing, core_ref, *refs):
+    dffn_ref, shrink_ref, slope_ref, low_ref, expand_ref, before_ref = refs[:6]
+    if closing:
+        normed_ref, inverse_ref, vec_ref = refs[6:9]
+        here_ref, away_ref, bias_ref, dresidual_ref, dbranch_ref, sums_ref, total_ref = refs[11:]
+    else:
+        here_ref, away_ref, bias_ref, total_ref = refs[6:]
     step = pl.program_id(0)
     dpre = (dot_nt(dffn_ref[...], shrink_ref[...]) * slope_ref[...].astype(F32)).astype(BF)
     bias_ref[...] = jnp.sum(dpre.astype(F32), axis=0, keepdims=True)
@@ -653,13 +645,15 @@
 
     @pl.when(step == 0)
     def _():
-        total_ref[...] = dsecond_ref[...] + more
+        total_ref[...] = before_ref[...] + more
 
     @pl.when(step > 0)
     def _():
         total_ref[...] += more
 
     put_wide(dot_tn(low_ref[...], dpre), core_ref[0], here_ref, away_ref, slice(None))
+    if not closing:
+        return
 
     @pl.when(step == pl.num_programs(0) - 1)
     def _():
@@ -674,48 +668,43 @@
         sums_ref[2:3] = jnp.sum(dbranch.astype(F32), axis=0, keepdims=True)
 
 
-def feed_back_call(core, dffn, shrink, slope, low, layer, expand_block, dsecond, normed, inverse, vec):
+def feed_back_call(core, dffn, shrink, slope, low, layer, expand_block, before, rest=None):
     tokens, width = dffn.shape
     wide = slope.shape[1]
+    steps = wide // width // 2
+    closing = rest is not None
+    at = steps if closing else 0
     half = ((NY * NZ, 24, wide), BF)
-    half_spec = pl.BlockSpec((NY * NZ, 24, width), lambda j: (0, 0, j))
-    outs = [
-        half,
-        half,
-        ((1, wide), F32),
-        ((tokens, width), F32),
-        ((tokens, width), BF),
-        ((8, width), F32),
+    half_spec = pl.BlockSpec((NY * NZ, 24, width), lambda j: (0, 0, at + j))
+    flat = pl.BlockSpec((tokens, width), lambda j: (0, 0))
+    outs = [half, half, ((1, wide // 2), F32), ((tokens, width), F32)]
+    out_specs = [half_spec, half_spec, pl.BlockSpec((1, width), lambda j: (0, j)), flat]
+    ins = [core, dffn, shrink, slope, low, layer, before]
+    in_specs = [
+        pl.BlockSpec(memory_space=pltpu.SMEM),
+        whole_spec(dffn),
+        pl.BlockSpec((width, width), lambda j: (at + j, 0)),
+        pl.BlockSpec((tokens, width), lambda j: (0, at + j)),
+        whole_spec(low),
+        pl.BlockSpec((width, width), lambda j: (0, expand_block + at + j)),
+        whole_spec(before),
     ]
-    return call(
-        feed_back_kernel,
-        (wide // width,),
-        (core, dffn, shrink, slope, low, layer, dsecond, normed, inverse, vec),
-        [
-            pl.BlockSpec(memory_space=pltpu.SMEM),
-            whole_spec(dffn),
-            pl.BlockSpec((width, width), lambda j: (j, 0)),
-            pl.BlockSpec((tokens, width), lambda j: (0, j)),
-            whole_spec(low),
-            pl.BlockSpec((width, width), lambda j: (0, expand_block + j)),
-            whole_spec(dsecond),
-            whole_spec(normed),
-            whole_spec(inverse),
-            whole_spec(vec),
-        ],
-        outs,
-        [
-            half_spec,
-            half_spec,
-            pl.BlockSpec((1, width), lambda j: (0, j)),
-            pl.BlockSpec((tokens, width), lambda j: (0, 0)),
-            pl.BlockSpec((tokens, width), lambda j: (0, 0)),
-            pl.BlockSpec((8, width), lambda j: (0, 0)),
-        ],
-        [pltpu.VMEM((tokens, width), F32)],
-        1000,
-        1000,
-    )
+    if closing:
+        outs += [((tokens, width), BF), ((8, width), F32)]
+        out_specs += [flat, pl.BlockSpec((8, width), lambda j: (0, 0))]
+        ins += rest
+        in_specs += [whole_spec(a) for a in rest[:3]] + [pl.BlockSpec(memory_space=pl.ANY)] * 2
+    return pl.pallas_call(
+        functools.partial(feed_back_kernel, closing),
+        grid=(steps,),
+        in_specs=in_specs,
+        out_specs=out_specs,
+        out_shape=[jax.ShapeDtypeStruct(shape, kind) for shape, kind in outs],
+        scratch_shapes=[pltpu.VMEM((tokens, width), F32)] if closing else [],
+        input_output_aliases={10: 0, 11: 1} if closing else {},
+        compiler_params=pltpu.CompilerParams(vmem_limit_bytes=LIMIT),
+        cost_estimate=pl.CostEstimate(flops=1000, bytes_accessed=1000, transcendentals=0),
+    )(*ins)
 
 
 def last_kernel(core_ref, x_ref, dfused_ref, attended_ref, dbranch_ref, sums_ref, here_ref, away_ref):
@@ -948,11 +937,23 @@
     tall_pair = shrink_call(core, act, dffn, g_dense, loss_own)
     tall_here, tall_away, dffn = after(*tall_pair, dffn)
     tall_pair = (tall_here, give(tall_away, "c", 1))
-    wide_here, wide_away, g_expand_bias, dresidual, dbranch, sums_b = feed_back_call(
-        core, dffn, shrink_full, slope, first_low, layer, 4, dsecond, normed1, inverse1, rows_of
-    )
+    wide_here, wide_away, bias_low, half_first = feed_back_call(
+        core, dffn, shrink_full, slope, first_low, layer, 4, dsecond
+    )
+    half_first, tall_mine = after(half_first, add_cores(tall_pair))
+    wide_here, wide_away, bias_high, dresidual, dbranch, sums_b = feed_back_call(
+        core,
+        dffn,
+        shrink_full,
+        slope,
+        first_low,
+        layer,
+        4,
+        half_first,
+        [normed1, inverse1, rows_of, wide_here, wide_away],
+    )
+    g_expand_bias = jnp.concatenate([bias_low, bias_high], axis=1)
     wide_pair = (wide_here, give(wide_away, "c", 1))
-    dbranch, tall_mine = after(dbranch, add_cores(tall_pair))
     tall_all = swap(tall_mine, ("y", "z"))
     dfused, fused_sum = attention_backward(dbranch, qkv, probs, layer, attn_block)
 
@@ -982,13 +983,15 @@
     last_all = swap(last_mine, ("y", "z"))
 
     lse, wide_mine = after(lse, wide_mine)
-    grad_w = decoder_call(expl, spread, column, labels, scale, stat, lse)
-    grad_w = grad_w.reshape(NC, NX, per, -1)
-    grad_w, grad_away, wide_all = after(grad_w[0], grad_w[1], wide_all)
+    grad_w, grad_b = decoder_call(expl, spread, column, labels, scale, stat, lse)
+    grad_b = grad_b.reshape(NC, NX, 1, per)
+    grad_b = jnp.pad(grad_b, ((0, 0), (0, 0), (0, 7), (0, width - per))).astype(BF)
+    grad_w = grad_w.reshape(NC, NX, per, width)
+    grad_w, grad_away = (jnp.concatenate([grad_w[i], grad_b[i]], axis=1) for i in range(NC))
+    grad_w, grad_away, wide_all = after(grad_w, grad_away, wide_all)
     grad_w = add_cores((grad_w, give(grad_away, "c", 1)))
     grad_w = total([grad_w[0]] + [give(grad_w[k], "x", k) for k in (1, 2, 3)])
 
-    dinput = dresidual + matmul_nt(dfused, qkv_full)
     tall = jnp.sum(tall_all[:, :120].astype(F32), axis=0).astype(BF)
     loss_row = split_three(jnp.sum(tall_all[:, 120, :6].astype(F32)))[:128]
     tall_low = tall[:96].reshape(NX, 4, 6, width).transpose(0, 2, 1, 3).reshape(NX, 6, 4 * width)
@@ -1001,8 +1004,9 @@
         axis=2,
     )
     wide = jnp.sum(wide_all.astype(F32), axis=0).astype(BF)
-    last_all, grad_w = after(last_all, grad_w)
-    g_vocab, g_vocab_bias = grad_w[:, :width].T, grad_w[:, width]
+    last_all, grad_w, dfused = after(last_all, grad_w, dfused)
+    dinput = dresidual + matmul_nt(dfused, qkv_full)
+    g_vocab, g_vocab_bias = grad_w[:per].T, grad_w[per, :per]
     last = jnp.sum(last_all.astype(F32), axis=0).astype(BF)
     last = sum_x(
         jnp.concatenate([early, wide.reshape(NX, 6, -1), last.reshape(NX, 6, -1)], axis=2)

time: 474 us -> 450 us (0.949)
  waiting for transfers between devices: 136 us -> 117 us
    pallas_call x0 -> x2, Pallas kernels: none -> 21.5 us  [feed_back_call(): pl.pallas_call(functools.partial(feed_back_kernel, closing), grid=(steps,...]
    pallas_call x7 -> x6, Pallas kernels: 90.8 us -> 71.3 us  [call(): pl.pallas_call(kernel, grid=grid, in_specs=in_specs, out_specs=out_specs,...]
    all_to_all x7, waiting for transfers between devices: 70.4 us -> 57.9 us  [swap(): return lax.all_to_all(array, axes, 0, 0, tiled=True)]
  transfers between devices with their start and end apart: 29 -> 29, of which waited for: 13 -> 14; matrix products, arithmetic and copies ran while one was open for 21% -> 22% of each run, Pallas kernels for 14% -> 16%
where the time goes in v7:
time: 450 us; the launch traced here: 442 us
  waiting for transfers between devices  117 us (26%)
  Pallas kernels  116 us (26%)
  starting transfers between devices  64.9 us (14%)
  local copies, waits for them, and re-layouts  50.6 us (11%)
  other arithmetic  43.6 us (10%)
  matrix products  28.6 us (6%)
  between operations  21.3 us (5%)
    pallas_call x6, Pallas kernels, call(): pl.pallas_call(kernel, grid=grid, in_specs=in_specs, out_specs=out_specs,...  71.3 us
    all_to_all x7, waiting for transfers between devices, swap(): return lax.all_to_all(array, axes, 0, 0, tiled=True)  57.9 us
    all_to_all x7, starting transfers between devices, swap(): return lax.all_to_all(array, axes, 0, 0, tiled=True)  38 us
    ppermute x7, waiting for transfers between devices, give(): return lax.ppermute(array, axis, [(i, (i + k) % n) for i in range(n)])  23.1 us
    dot_general x5, matrix products, matmul(): return jnp.dot(left, right, preferred_element_type=F32)  22.8 us
    pallas_call x2, Pallas kernels, feed_back_call(): pl.pallas_call(functools.partial(feed_back_kernel, closing), grid=(steps,...  21.5 us
    ppermute x14, starting transfers between devices, fetch(): return lax.ppermute(array, axis, [((i + k) % n, i) for i in range(n)])  21 us
    unnamed x99, local copies, waits for them, and re-layouts  18.7 us
  transfers between devices with their start and end apart: 29, of which 14 were waited for; matrix products, arithmetic and copies ran while one was open for 22% of the time, Pallas kernels for 16%

profile of v7, /device:TPU:0, one launch (start us, length us, event | category | flops | bytes accessed | tf_op | source)
XLA Modules:
  0.0 442.2 jit_solution(7056196122170113385)
XLA Ops:
  7.2 2.9 collective-permute-start
  10.2 2.3 collective-permute-start.1
  13.3 1.5 stack.176
  17.9 1.8 collective-permute-start.5
  21.3 2.0 collective-permute-start.3
  24.2 2.0 collective-permute-done.3
  27.3 2.7 collective-permute-start.7
  30.1 1.9 collective-permute-start.6
  32.1 3.1 collective-permute-start.10
  39.7 6.1 %collective-permute-done.7 = bf16[400,768]{1,0:T(8,128)(2,1)S(1)} collective-permute-done((bf16[400,768]{1,0:T(8,128)(2,1)S(1)}, bf16[400,768]{1,0:T(8,128)(2,1)S(1)}, u32[]{:S(2)}, u32[]{:S(2)}) %collective-permute-start.7) | collective-permute-done | bytes 614432 | tf_op jit(solution)/shard_map/ppermute | solution.py:26
  45.8 2.6 collective-permute-start.11
  48.4 9.1 %collective-permute-done.6 = bf16[400,768]{1,0:T(8,128)(2,1)S(1)} collective-permute-done((bf16[400,768]{1,0:T(8,128)(2,1)S(1)}, bf16[400,768]{1,0:T(8,128)(2,1)S(1)}, u32[]{:S(2)}, u32[]{:S(2)}) %collective-permute-start.6) | collective-permute-done | bytes 614432 | tf_op jit(solution)/shard_map/ppermute | solution.py:26
  58.5 1.7 pad_maximum_fusion.2
  65.1 1.4 select_reduce_fusion
  66.8 2.0 constant_dynamic-update-slice_fusion.16
  70.5 1.7 constant_dynamic-update-slice_fusion.13
  72.1 8.2 %fusion.12 = bf16[16,64,768]{2,1,0:T(8,128)(2,1)S(1)} fusion(bf16[3200,768,1]{1,0,2:T(8,128)(2,1)} %bitcast.159, s32[3200]{0:T(1024)S(1)} %add.332, s32[16,64]{1,0:T(8,128)S(1)} %reshape.318), kind=kOutput, calls=%fused_computation.26 | convolution fusion | flops 5037228032 | bytes 6504960 | tf_op jit(solution)/shard_map/dot_general | solution.py:130
  80.3 1.5 pad_maximum_fusion.3
  81.9 18.1 %all-gather.2.cloned.1.call-done.wq_ref.wk_ref.wv_ref.wa_ref.in_ref.dense_ref.refs_4_ = bf16[768,10112]{1,0:T(8,128)(2,1)} async-done(((bf16[24,10112]{1,0:T(8,128)(2,1)}), bf16[768,10112]{1,0:T(8,128)(2,1)}) %all-gather.2.cloned.1.call-update) | async-done | bytes 15532048 | tf_op jit(solution)/shard_map/all_gather | solution.py:816
  103.4 6.9 %shard_map.409 = bf16[32,4,24,768]{3,2,1,0:T(8,128)(2,1)} custom-call(bf16[768,10112]{1,0:T(8,128)(2,1)} %all-gather.2.cloned.1.call-done.wq_ref.wk_ref.wv_ref.wa_ref.in_ref.dense_ref.refs_4_), custom_call_target="tpu_custom_call" | custom-call | flops 1000 | bytes 1000 | tf_op jit(solution)/shard_map/pallas_call | solution.py:320
  110.3 5.5 %all-to-all-start = ((bf16[16,64,896]{2,1,0:T(8,128)(2,1)}), bf16[16,64,896]{2,1,0:T(8,128)(2,1)S(1)}, u32[]{:S(2)}, u32[]{:S(2)}) async-start(bf16[16,64,896]{2,1,0:T(8,128)(2,1)} %pad_maximum_fusion.3), calls=%async_computation | async-start | bytes 3670016 | tf_op jit(solution)/shard_map/all_to_all | solution.py:46
  116.1 11.0 %shard_map.408 = (bf16[512,2304]{1,0:T(8,128)(2,1)}, bf16[2,12,256,256]{3,2,1,0:T(8,128)(2,1)}, bf16[512,768]{1,0:T(8,128)(2,1)S(1)}, f32[512,768]{1,0:T(8,128)S...) custom-call(bf16[512,768]{1,0:T(8,128)(2,1)S(1)} %bitcast.134, ...), custom_call_target="tpu_custom_call" | custom-call | flops 4000000000 | bytes 16000000 | tf_op jit(solution)/shard_map/pallas_call | solution.py:211
  127.1 9.0 %fusion.7 = (bf16[512,3072]{1,0:T(8,128)(2,1)}, bf16[512,3072]{1,0:T(8,128)(2,1)S(1)}) fusion(f32[3072]{0:T(1024)S(1)} %reshape.314, bf16[512,768]{1,0:T(8,128)(2,1)S(1)} %get-tuple-element.84.refs_3_, bf16[768,10112]{1,0:T(8,128)(2,1)} %all-gather.2.cloned.1.call-done.wq_ref.wk_ref.wv_ref.wa_ref.in_ref.dense_ref.refs_4_), kind=kOutput, calls=%fused_computation.9 | convolution fusion | flops 2436366336 | bytes 11808768 | tf_op jit(solution)/shard_map/dot_general | solution.py:130
  136.1 2.7 fusion.43
  139.2 1.5 add_convert_fusion.4
  140.6 3.2 all-to-all-done
  144.1 2.8 fusion.27
  148.0 1.4 broadcast_in_dim.59
  149.3 4.9 %all-to-all-start.1 = ((bf16[16,64,768]{2,1,0:T(8,128)(2,1)}), bf16[16,64,768]{2,1,0:T(8,128)(2,1)S(1)}, u32[]{:S(2)}, u32[]{:S(2)}) async-start(bf16[16,64,768]{2,1,0:T(8,128)(2,1)} %broadcast_in_dim.59), calls=%async_computation.1 | async-start | bytes 3145728 | tf_op jit(solution)/shard_map/all_to_all | solution.py:46
  156.7 21.2 %all-to-all-done.1 = bf16[16,64,768]{2,1,0:T(8,128)(2,1)S(1)} async-done(((bf16[16,64,768]{2,1,0:T(8,128)(2,1)}), bf16[16,64,768]{2,1,0:T(8,128)(2,1)S(1)}, u32[]{:S(2)}, u32[]{:S(2)}) %all-to-all-start.1) | async-done | bytes 1572896 | tf_op jit(solution)/shard_map/all_to_all | solution.py:46
  179.0 25.3 %shard_map.410 = (bf16[1024,3200]{1,0:T(8,128)(2,1)}, f32[1024,128]{1,0:T(8,128)}, bf16[16,80,768]{2,1,0:T(8,128)(2,1)}) custom-call(bf16[1024,768]{1,0:T(8,128)(2,1)} %bitcast.140, bf16[3200,768]{1,0:T(8,128)(2,1)} %bitcast.160, f32[1,3200]{1,0:T(1,128)} %reshape.315.b_ref, s32[1,3200]{1,0:T(1,128)} %add.360.column_ref, s32[1024,1]{1,0:T(8,128)} %copy.133.label_ref), custom_call_target="tpu_custom_call" | custom-call | flops 10000000000 | bytes 20000000 | tf_op jit(solution)/shard_map/pallas_call | solution.py:320
  204.3 3.9 all-to-all-start.2
  209.5 1.8 convert_reduce_fusion
  212.7 22.0 %all-to-all-done.2.part_ref = bf16[16,80,768]{2,1,0:T(8,128)(2,1)S(1)} async-done(((bf16[16,80,768]{2,1,0:T(8,128)(2,1)}), bf16[16,80,768]{2,1,0:T(8,128)(2,1)S(1)}, u32[]{:S(2)}, u32[]{:S(2)}) %all-to-all-start.2) | async-done | bytes 1966112 | tf_op jit(solution)/shard_map/all_to_all | solution.py:46
  236.1 7.1 %shard_map.411 = (f32[1,1024]{1,0:T(1,128)}, f32[8,128]{1,0:T(8,128)}, f32[768,768]{1,0:T(8,128)}, f32[512,768]{1,0:T(8,128)}, bf16[512,768]{1,0:T(8,128)(2,1)}, /*index=5*/f32[8,768]{1,0:T(8,128)}) custom-call(s32[1]{0:T(128)} %bitcast.47.own_ref, bf16[16,80,768]{2,1,0:T(8,128)(2,1)} %copy-done.11, bf16[64,768]{1,0:T(8,128)(2,1)} %copy-done.27, ...), custom_call_target="tpu_custom_call" | custom-call | flops 300000000 | bytes 10000000 | tf_op jit(solution)/shard_map/pallas_call | solution.py:320
  243.2 7.7 %shard_map.412 = (bf16[16,128,768]{2,1,0:T(8,128)(2,1)}, bf16[16,128,768]{2,1,0:T(8,128)(2,1)}) custom-call(s32[1]{0:T(128)} %bitcast.46.core_ref, bf16[512,3072]{1,0:T(8,128)(2,1)} %copy-done.15, bf16[512,768]{1,0:T(8,128)(2,1)} %get-tuple-element.97.dffn_ref.refs_0_, f32[768,768]{1,0:T(8,128)} %get-tuple-element.93.dense_ref, ...), custom_call_target="tpu_custom_call" | custom-call | flops 1000 | bytes 1000 | tf_op jit(solution)/shard_map/pallas_call | solution.py:320
  250.9 9.9 %shard_map.413 = (bf16[16,24,3072]{2,1,0:T(8,128)(2,1)}, bf16[16,24,3072]{2,1,0:T(8,128)(2,1)}, f32[1,1536]{1,0:T(1,128)}, f32[512,768]{1,0:T(8,128)}) custom-call(s32[1]{0:T(128)} %bitcast.46.core_ref, bf16[512,768]{1,0:T(8,128)(2,1)} %get-tuple-element.97.dffn_ref.refs_0_, bf16[3072,768]{1,0:T(8,128)(2,1)} %bitcast.135, ...), custom_call_target="tpu_custom_call" | custom-call | flops 1000 | bytes 1000 | tf_op jit(solution)/shard_map/pallas_call | solution.py:697
  260.8 2.6 add_convert_fusion
  263.4 3.8 all-to-all-start.3
  267.2 11.7 %shard_map.414 = (bf16[16,24,3072]{2,1,0:T(8,128)(2,1)}, bf16[16,24,3072]{2,1,0:T(8,128)(2,1)}, f32[1,1536]{1,0:T(1,128)}, f32[512,768]{1,0:T(8,128)}, bf16[512,768]{1,0:T(8,128)(2,1)}, /*index=5*/f32[8,768]{1,0:T(8,128)}) custom-call(s32[1]{0:T(128)} %bitcast.46.core_ref, ...), custom_call_target="tpu_custom_call", output_to_operand_aliasing={{0}: (10, {}), {1}: (11, {})} | custom-call | flops 1000 | bytes 1000 | tf_op jit(solution)/shard_map/pallas_call | solution.py:697
  280.8 12.1 %shard_map.415 = (bf16[512,2304]{1,0:T(8,128)(2,1)S(1)}, f32[1,2304]{1,0:T(1,128)S(1)}) custom-call(bf16[512,768]{1,0:T(8,128)(2,1)S(1)} %copy-done.2, bf16[512,2304]{1,0:T(8,128)(2,1)S(1)} %copy-done.5, bf16[2,12,256,256]{3,2,1,0:T(8,128)(2,1)} %get-tuple-element.111.probs_ref, ...), custom_call_target="tpu_custom_call" | custom-call | flops 1000 | bytes 1000 | tf_op jit(solution)/shard_map/pallas_call | solution.py:291
  292.9 1.4 copy-done.3
  299.9 1.9 select_maximum_fusion.sums_ref
  301.8 9.2 %shard_map.416 = (bf16[16,24,3200]{2,1,0:T(8,128)(2,1)}, bf16[16,24,3200]{2,1,0:T(8,128)(2,1)}) custom-call(s32[1]{0:T(128)} %bitcast.46.core_ref, bf16[512,768]{1,0:T(8,128)(2,1)} %bitcast.133, bf16[512,2304]{1,0:T(8,128)(2,1)} %copy-done.3, bf16[512,768]{1,0:T(8,128)(2,1)} %copy-done.7, bf16[512,768]{1,0:T(8,128)(2,1)} %get-tuple-element.109.dbranch_ref, ...), custom_call_target="tpu_custom_call" | custom-call | flops 1000 | bytes 1000 | tf_op jit(solution)/shard_map/pallas_call | solution.py:320
  311.1 4.6 %add_convert_fusion.3 = bf16[16,24,3072]{2,1,0:T(8,128)(2,1)} fusion(bf16[16,24,3072]{2,1,0:T(8,128)(2,1)} %collective-permute-done.15, bf16[16,24,3072]{2,1,0:T(8,128)(2,1)} %get-tuple-element.107), kind=kLoop, calls=%fused_computation.15 | loop fusion | flops 4718592 | bytes 7077888 | tf_op jit(solution)/shard_map/convert_element_type | solution.py:65
  315.8 10.2 %all-to-all-start.4 = ((bf16[16,24,3072]{2,1,0:T(8,128)(2,1)}), bf16[16,24,3072]{2,1,0:T(8,128)(2,1)}, u32[]{:S(2)}, u32[]{:S(2)}) async-start(bf16[16,24,3072]{2,1,0:T(8,128)(2,1)} %add_convert_fusion.3), calls=%async_computation.4 | async-start | bytes 4718592 | tf_op jit(solution)/shard_map/all_to_all | solution.py:46
  326.0 15.1 %shard_map.417 = (bf16[3200,768]{1,0:T(8,128)(2,1)}, f32[1,3200]{1,0:T(1,128)}) custom-call(bf16[1024,3200]{1,0:T(8,128)(2,1)} %get-tuple-element.123.expl_ref, bf16[1024,768]{1,0:T(8,128)(2,1)} %bitcast.141, s32[1,3200]{1,0:T(1,128)} %add.360.column_ref, s32[1024,1]{1,0:T(8,128)} %copy.133.label_ref, f32[1024,1]{1,0:T(8,128)} %select_multiply_fusion.scale_ref, ...), custom_call_target="tpu_custom_call" | custom-call | flops 1000 | bytes 1000 | tf_op jit(solution)/shard_map/pallas_call | solution.py:320
  341.9 2.8 fusion.39
  344.7 2.5 pad_maximum_fusion
  347.7 3.8 add_convert_fusion.2
  351.5 8.1 %all-to-all-done.4 = bf16[16,24,3072]{2,1,0:T(8,128)(2,1)} async-done(((bf16[16,24,3072]{2,1,0:T(8,128)(2,1)}), bf16[16,24,3072]{2,1,0:T(8,128)(2,1)}, u32[]{:S(2)}, u32[]{:S(2)}) %all-to-all-start.4) | async-done | bytes 2359328 | tf_op jit(solution)/shard_map/all_to_all | solution.py:46
  365.1 6.2 %all-to-all-start.5 = ((bf16[16,24,3200]{2,1,0:T(8,128)(2,1)}), bf16[16,24,3200]{2,1,0:T(8,128)(2,1)}, u32[]{:S(2)}, u32[]{:S(2)}) async-start(bf16[16,24,3200]{2,1,0:T(8,128)(2,1)} %add_convert_fusion.2), calls=%async_computation.5 | async-start | bytes 4915200 | tf_op jit(solution)/shard_map/all_to_all | solution.py:46
  373.8 3.1 add_convert_fusion.1
  378.2 1.5 collective-permute-start.18
  379.7 1.7 collective-permute-start.20
  381.4 1.8 collective-permute-start.19
  384.5 2.1 reduce_sum.135
  387.3 8.5 %collective-permute-done.18 = bf16[408,768]{1,0:T(8,128)(2,1)S(1)} collective-permute-done((bf16[408,768]{1,0:T(8,128)(2,1)}, bf16[408,768]{1,0:T(8,128)(2,1)S(1)}, u32[]{:S(2)}, u32[]{:S(2)}) %collective-permute-start.18) | collective-permute-done | bytes 626720 | tf_op jit(solution)/shard_map/ppermute | solution.py:31
  397.0 13.3 %collective-permute-done.19 = bf16[408,768]{1,0:T(8,128)(2,1)} collective-permute-done((bf16[408,768]{1,0:T(8,128)(2,1)}, bf16[408,768]{1,0:T(8,128)(2,1)}, u32[]{:S(2)}, u32[]{:S(2)}) %collective-permute-start.19) | collective-permute-done | bytes 626720 | tf_op jit(solution)/shard_map/ppermute | solution.py:31
  410.4 2.6 fusion.19
  413.0 2.2 reduce_sum.136
  415.9 3.5 all-to-all-start.6
  419.5 5.7 %fusion.15 = f32[512,768]{1,0:T(8,128)} fusion(f32[512,768]{1,0:T(8,128)} %get-tuple-element.139, bf16[512,2304]{1,0:T(8,128)(2,1)S(1)} %copy-done.4, bf16[768,10112]{1,0:T(8,128)(2,1)} %all-gather.2.cloned.1.call-done.wq_ref.wk_ref.wv_ref.wa_ref.in_ref.dense_ref.refs_4_), kind=kOutput, calls=%fused_computation.31 | convolution fusion | flops 1812332544 | bytes 9043968 | tf_op jit(solution)/shard_map/dot_general | solution.py:138
  426.9 3.2 all-to-all-done.6
  (232 shorter events, 55.6 us)
Async XLA Ops:
  7.2 92.8 %all-gather.2.cloned.1.call-start = ((), (), s32[]{:S(2)}) async-start(), calls=%async_computation.7 | async-start | bytes 16017408 | tf_op jit(solution)/shard_map/all_gather | solution.py:816
  7.2 14.1 %collective-permute-start = (bf16[24,768]{1,0:T(8,128)(2,1)}, bf16[24,768]{1,0:T(8,128)(2,1)S(1)}, u32[]{:S(2)}, u32[]{:S(2)}) collective-permute-start(bf16[24,768]{1,0:T(8,128)(2,1)} %param.40), channel_id=1, source_target_pairs={{1,0},{2,1},{3,2},{0,3},{5,4},{6,5},{7,6},{4,7},{9,8},{10,9},{11,1... | collective-permute-start | bytes 110600 | tf_op jit(solution)/shard_map/ppermute | solution.py:26
  10.1 13.1 %collective-permute-start.2 = (bf16[24,768]{1,0:T(8,128)(2,1)}, bf16[24,768]{1,0:T(8,128)(2,1)S(1)}, u32[]{:S(2)}, u32[]{:S(2)}) collective-permute-start(bf16[24,768]{1,0:T(8,128)(2,1)} %param.40), channel_id=1, source_target_pairs={{3,0},{0,1},{1,2},{2,3},{7,4},{4,5},{5,6},{6,7},{11,8},{8,9},{9,10... | collective-permute-start | bytes 110600 | tf_op jit(solution)/shard_map/ppermute | solution.py:26
  10.2 13.1 %collective-permute-start.1 = (bf16[24,768]{1,0:T(8,128)(2,1)}, bf16[24,768]{1,0:T(8,128)(2,1)S(1)}, u32[]{:S(2)}, u32[]{:S(2)}) collective-permute-start(bf16[24,768]{1,0:T(8,128)(2,1)} %param.40), channel_id=1, source_target_pairs={{2,0},{3,1},{0,2},{1,3},{6,4},{7,5},{4,6},{5,7},{10,8},{11,9},{8,1... | collective-permute-start | bytes 110600 | tf_op jit(solution)/shard_map/ppermute | solution.py:26
  17.9 8.3 %collective-permute-start.5 = (bf16[6,7040]{1,0:T(8,128)(2,1)S(1)}, bf16[6,7040]{1,0:T(8,128)(2,1)S(1)}, u32[]{:S(2)}, u32[]{:S(2)}) collective-permute-start(bf16[6,7040]{1,0:T(8,128)(2,1)S(1)} %constant_dynamic-update-slice_fusion.8), channel_id=1, source_target_pairs={{3,0},{0,1},{1,2},{2,3},{7,4},{4,5},{5,6},{6,7},{11,8},{8,9},{9,10... | collective-permute-start | bytes 253448 | tf_op jit(solution)/shard_map/ppermute | solution.py:26
  19.7 6.5 %collective-permute-start.4 = (bf16[6,7040]{1,0:T(8,128)(2,1)S(1)}, bf16[6,7040]{1,0:T(8,128)(2,1)S(1)}, u32[]{:S(2)}, u32[]{:S(2)}) collective-permute-start(bf16[6,7040]{1,0:T(8,128)(2,1)S(1)} %constant_dynamic-update-slice_fusion.8), channel_id=1, source_target_pairs={{2,0},{3,1},{0,2},{1,3},{6,4},{7,5},{4,6},{5,7},{10,8},{11,9},{8,1... | collective-permute-start | bytes 253448 | tf_op jit(solution)/shard_map/ppermute | solution.py:26
  21.3 4.9 %collective-permute-start.3 = (bf16[6,7040]{1,0:T(8,128)(2,1)S(1)}, bf16[6,7040]{1,0:T(8,128)(2,1)S(1)}, u32[]{:S(2)}, u32[]{:S(2)}) collective-permute-start(bf16[6,7040]{1,0:T(8,128)(2,1)S(1)} %constant_dynamic-update-slice_fusion.8), channel_id=1, source_target_pairs={{1,0},{2,1},{3,2},{0,3},{5,4},{6,5},{7,6},{4,7},{9,8},{10,9},{11,1... | collective-permute-start | bytes 253448 | tf_op jit(solution)/shard_map/ppermute | solution.py:26
  24.1 3.2 copy-start.19
  24.1 8.0 %copy-start.34 = (bf16[400]{0:T(512)(128)(2,1)S(1)}, bf16[400]{0:T(512)(128)(2,1)}, u32[]{:S(2)}) copy-start(bf16[400]{0:T(512)(128)(2,1)} %param.49) | copy-start | bytes 2404
  24.2 11.8 %copy-start.33 = (s32[2,1,16,2]{2,3,1,0:T(2,128)S(1)}, s32[2,1,16,2]{2,3,1,0:T(2,128)}, u32[]{:S(2)}) copy-start(s32[2,1,16,2]{2,3,1,0:T(2,128)} %param.28) | copy-start | bytes 772
  24.2 12.0 %copy-start.30 = (s32[2,128,16,2]{1,3,2,0:T(2,128)S(1)}, s32[2,128,16,2]{1,3,2,0:T(2,128)}, u32[]{:S(2)}) copy-start(s32[2,128,16,2]{1,3,2,0:T(2,128)} %param.29) | copy-start | bytes 98308
  27.3 18.4 %collective-permute-start.7 = (bf16[400,768]{1,0:T(8,128)(2,1)S(1)}, bf16[400,768]{1,0:T(8,128)(2,1)S(1)}, u32[]{:S(2)}, u32[]{:S(2)}) collective-permute-start(bf16[400,768]{1,0:T(8,128)(2,1)S(1)} %bitcast.146), channel_id=1, source_target_pairs={{2,0},{3,1},{0,2},{1,3},{6,4},{7,5},{4,6},{5,7},{10,8},{11,9},{8,1... | collective-permute-start | bytes 1843208 | tf_op jit(solution)/shard_map/ppermute | solution.py:26
  30.1 27.4 %collective-permute-start.6 = (bf16[400,768]{1,0:T(8,128)(2,1)S(1)}, bf16[400,768]{1,0:T(8,128)(2,1)S(1)}, u32[]{:S(2)}, u32[]{:S(2)}) collective-permute-start(bf16[400,768]{1,0:T(8,128)(2,1)S(1)} %bitcast.147), channel_id=1, source_target_pairs={{1,0},{2,1},{3,2},{0,3},{5,4},{6,5},{7,6},{4,7},{9,8},{10,9},{11,1... | collective-permute-start | bytes 1843208 | tf_op jit(solution)/shard_map/ppermute | solution.py:26
  31.9 25.6 %collective-permute-start.8 = (bf16[400,768]{1,0:T(8,128)(2,1)S(1)}, bf16[400,768]{1,0:T(8,128)(2,1)S(1)}, u32[]{:S(2)}, u32[]{:S(2)}) collective-permute-start(bf16[400,768]{1,0:T(8,128)(2,1)S(1)} %bitcast.148), channel_id=1, source_target_pairs={{3,0},{0,1},{1,2},{2,3},{7,4},{4,5},{5,6},{6,7},{11,8},{8,9},{9,10... | collective-permute-start | bytes 1843208 | tf_op jit(solution)/shard_map/ppermute | solution.py:26
  32.1 30.1 %collective-permute-start.10 = (bf16[400]{0:T(512)(128)(2,1)S(1)}, bf16[400]{0:T(512)(128)(2,1)S(1)}, u32[]{:S(2)}, u32[]{:S(2)}) collective-permute-start(bf16[400]{0:T(512)(128)(2,1)S(1)} %copy-done.34), channel_id=1, source_target_pairs={{1,0},{2,1},{3,2},{0,3},{5,4},{6,5},{7,6},{4,7},{9,8},{10,9},{11,1... | collective-permute-start | bytes 2408 | tf_op jit(solution)/shard_map/ppermute | solution.py:26
  35.2 27.1 %collective-permute-start.12 = (bf16[400]{0:T(512)(128)(2,1)S(1)}, bf16[400]{0:T(512)(128)(2,1)S(1)}, u32[]{:S(2)}, u32[]{:S(2)}) collective-permute-start(bf16[400]{0:T(512)(128)(2,1)S(1)} %copy-done.34), channel_id=1, source_target_pairs={{3,0},{0,1},{1,2},{2,3},{7,4},{4,5},{5,6},{6,7},{11,8},{8,9},{9,10... | collective-permute-start | bytes 2408 | tf_op jit(solution)/shard_map/ppermute | solution.py:26
  45.8 11.7 %copy-start.20 = (bf16[400,768]{1,0:T(8,128)(2,1)}, bf16[400,768]{1,0:T(8,128)(2,1)S(1)}, u32[]{:S(2)}) copy-start(bf16[400,768]{1,0:T(8,128)(2,1)S(1)} %collective-permute-done.7) | copy-start | bytes 1843204
  45.8 16.5 %collective-permute-start.11 = (bf16[400]{0:T(512)(128)(2,1)S(1)}, bf16[400]{0:T(512)(128)(2,1)S(1)}, u32[]{:S(2)}, u32[]{:S(2)}) collective-permute-start(bf16[400]{0:T(512)(128)(2,1)S(1)} %copy-done.34), channel_id=1, source_target_pairs={{2,0},{3,1},{0,2},{1,3},{6,4},{7,5},{4,6},{5,7},{10,8},{11,9},{8,1... | collective-permute-start | bytes 2408 | tf_op jit(solution)/shard_map/ppermute | solution.py:26
  57.5 0.8 copy-start.24
  57.5 1.0 copy-start.22
  58.5 2.7 copy-start.25
  58.5 2.7 copy-start.26
  60.2 3.3 copy-start.32
  60.2 10.2 %collective-permute-start.9 = (bf16[4,400,768]{2,1,0:T(8,128)(2,1)}, bf16[4,400,768]{2,1,0:T(8,128)(2,1)S(1)}, u32[]{:S(2)}, u32[]{:S(2)}) collective-permute-start(bf16[4,400,768]{2,1,0:T(8,128)(2,1)} %pad_maximum_fusion.2), channel_id=1, source_target_pairs={{16,0},{0,16},{17,1},{1,17},{18,2},{2,18},{19,3},{3,19},{20,4},{4,... | collective-permute-start | bytes 7372808 | tf_op jit(solution)/shard_map/ppermute | solution.py:26
  60.3 83.5 %copy-start.28 = (bf16[64,512]{1,0:T(8,128)(2,1)}, bf16[64,512]{1,0:T(8,128)(2,1)S(1)}, u32[]{:S(2)}) copy-start(bf16[64,512]{1,0:T(8,128)(2,1)S(1)} %fusion.28.select_ref) | copy-start | bytes 196612
  61.2 7.5 %copy-start.21 = (bf16[400,768]{1,0:T(8,128)(2,1)S(1)}, bf16[400,768]{1,0:T(8,128)(2,1)}, u32[]{:S(2)}) copy-start(bf16[400,768]{1,0:T(8,128)(2,1)} %copy-done.20) | copy-start | bytes 1843204
  62.3 2.6 collective-permute-start.13
  65.0 4.6 %copy-start.23 = (bf16[400,768]{1,0:T(8,128)(2,1)S(1)}, bf16[400,768]{1,0:T(8,128)(2,1)}, u32[]{:S(2)}) copy-start(bf16[400,768]{1,0:T(8,128)(2,1)} %copy-done.22) | copy-start | bytes 1843204
  102.3 13.7 %copy-start.8 = (f32[16,768]{1,0:T(8,128)}, f32[16,768]{1,0:T(8,128)S(1)}, u32[]{:S(2)}) copy-start(f32[16,768]{1,0:T(8,128)S(1)} %copy.132.vec_ref.refs_8_) | copy-start | bytes 147460
  110.3 5.8 %copy-start = (bf16[2,256,768]{2,1,0:T(8,128)(2,1)S(1)}, bf16[2,256,768]{2,1,0:T(8,128)(2,1)}, u32[]{:S(2)}) copy-start(bf16[2,256,768]{2,1,0:T(8,128)(2,1)} %param.25) | copy-start | bytes 2359300
  110.3 33.5 %all-to-all-start = ((bf16[16,64,896]{2,1,0:T(8,128)(2,1)}), bf16[16,64,896]{2,1,0:T(8,128)(2,1)S(1)}, u32[]{:S(2)}, u32[]{:S(2)}) async-start(bf16[16,64,896]{2,1,0:T(8,128)(2,1)} %pad_maximum_fusion.3), calls=%async_computation | async-start | bytes 3670016 | tf_op jit(solution)/shard_map/all_to_all | solution.py:46
  127.1 9.0 %copy-start.1 = (bf16[512,768]{1,0:T(8,128)(2,1)}, bf16[512,768]{1,0:T(8,128)(2,1)S(1)}, u32[]{:S(2)}) copy-start(bf16[512,768]{1,0:T(8,128)(2,1)S(1)} %get-tuple-element.84.refs_3_) | copy-start | bytes 2359300
  127.1 9.0 %copy-start.6 = (f32[512,768]{1,0:T(8,128)}, f32[512,768]{1,0:T(8,128)S(1)}, u32[]{:S(2)}) copy-start(f32[512,768]{1,0:T(8,128)S(1)} %get-tuple-element.103.refs_6_) | copy-start | bytes 4718596
  127.1 9.0 %copy-start.7 = (bf16[512,768]{1,0:T(8,128)(2,1)}, bf16[512,768]{1,0:T(8,128)(2,1)S(1)}, u32[]{:S(2)}) copy-start(bf16[512,768]{1,0:T(8,128)(2,1)S(1)} %get-tuple-element.113.attended_ref) | copy-start | bytes 2359300
  127.1 9.0 %copy-start.9 = (f32[512,1]{1,0:T(8,128)}, f32[512,1]{1,0:T(8,128)S(1)}, u32[]{:S(2)}) copy-start(f32[512,1]{1,0:T(8,128)S(1)} %get-tuple-element.104.refs_7_) | copy-start | bytes 6148
  127.1 9.0 %copy-start.10 = (bf16[32,4,24,768]{3,2,1,0:T(8,128)(2,1)S(1)}, bf16[32,4,24,768]{3,2,1,0:T(8,128)(2,1)}, u32[]{:S(2)}) copy-start(bf16[32,4,24,768]{3,2,1,0:T(8,128)(2,1)} %shard_map.409) | copy-start | bytes 14155780
  136.1 2.7 copy-start.15
  140.6 8.7 %copy-start.17 = (bf16[512,768]{1,0:T(8,128)(2,1)}, bf16[512,768]{1,0:T(8,128)(2,1)S(1)}, u32[]{:S(2)}) copy-start(bf16[512,768]{1,0:T(8,128)(2,1)S(1)} %get-tuple-element.163) | copy-start | bytes 2359300
  143.8 5.5 %copy-start.12 = (bf16[16,64,896]{2,1,0:T(8,128)(2,1)}, bf16[16,64,896]{2,1,0:T(8,128)(2,1)S(1)}, u32[]{:S(2)}) copy-start(bf16[16,64,896]{2,1,0:T(8,128)(2,1)S(1)} %all-to-all-done) | copy-start | bytes 5505028
  144.1 5.3 %copy-start.29 = (bf16[64,768]{1,0:T(8,128)(2,1)}, bf16[64,768]{1,0:T(8,128)(2,1)S(1)}, u32[]{:S(2)}) copy-start(bf16[64,768]{1,0:T(8,128)(2,1)S(1)} %convolution_convert_fusion.picked_ref) | copy-start | bytes 294916
  148.0 8.7 %copy-start.27 = (bf16[64,768]{1,0:T(8,128)(2,1)}, bf16[64,768]{1,0:T(8,128)(2,1)S(1)}, u32[]{:S(2)}) copy-start(bf16[64,768]{1,0:T(8,128)(2,1)S(1)} %get-tuple-element.161.head_ref) | copy-start | bytes 294916
  149.3 28.5 %all-to-all-start.1 = ((bf16[16,64,768]{2,1,0:T(8,128)(2,1)}), bf16[16,64,768]{2,1,0:T(8,128)(2,1)S(1)}, u32[]{:S(2)}, u32[]{:S(2)}) async-start(bf16[16,64,768]{2,1,0:T(8,128)(2,1)} %broadcast_in_dim.59), calls=%async_computation.1 | async-start | bytes 3145728 | tf_op jit(solution)/shard_map/all_to_all | solution.py:46
  177.9 1.1 copy-start.13
  204.3 30.4 %all-to-all-start.2 = ((bf16[16,80,768]{2,1,0:T(8,128)(2,1)}), bf16[16,80,768]{2,1,0:T(8,128)(2,1)S(1)}, u32[]{:S(2)}, u32[]{:S(2)}) async-start(bf16[16,80,768]{2,1,0:T(8,128)(2,1)} %get-tuple-element.90), calls=%async_computation.2 | async-start | bytes 3932160 | tf_op jit(solution)/shard_map/all_to_all | solution.py:46
  234.7 1.3 copy-start.11
  250.9 9.9 %collective-permute-start.14 = (bf16[16,128,768]{2,1,0:T(8,128)(2,1)}, bf16[16,128,768]{2,1,0:T(8,128)(2,1)S(1)}, u32[]{:S(2)}, u32[]{:S(2)}) collective-permute-start(bf16[16,128,768]{2,1,0:T(8,128)(2,1)} %get-tuple-element.101), channel_id=1, source_target_pairs={{0,16},{16,0},{1,17},{17,1},{2,18},{18,2},{3,19},{19,3},{4,20},{20... | collective-permute-start | bytes 9437192 | tf_op jit(solution)/shard_map/ppermute | solution.py:31
  250.9 9.9 %copy-start.16 = (bf16[16,128,768]{2,1,0:T(8,128)(2,1)S(1)}, bf16[16,128,768]{2,1,0:T(8,128)(2,1)}, u32[]{:S(2)}) copy-start(bf16[16,128,768]{2,1,0:T(8,128)(2,1)} %get-tuple-element.100) | copy-start | bytes 9437188
  263.4 47.7 %all-to-all-start.3 = ((bf16[16,128,768]{2,1,0:T(8,128)(2,1)}), bf16[16,128,768]{2,1,0:T(8,128)(2,1)S(1)}, u32[]{:S(2)}, u32[]{:S(2)}) async-start(bf16[16,128,768]{2,1,0:T(8,128)(2,1)} %add_convert_fusion), calls=%async_computation.3 | async-start | bytes 6291456 | tf_op jit(solution)/shard_map/all_to_all | solution.py:46
  267.2 12.4 %copy-start.31 = (f32[8,768]{1,0:T(8,128)S(1)}, f32[8,768]{1,0:T(8,128)}, u32[]{:S(2)}) copy-start(f32[8,768]{1,0:T(8,128)} %get-tuple-element.116) | copy-start | bytes 73732
  267.2 12.4 %copy-start.5 = (bf16[512,2304]{1,0:T(8,128)(2,1)S(1)}, bf16[512,2304]{1,0:T(8,128)(2,1)}, u32[]{:S(2)}) copy-start(bf16[512,2304]{1,0:T(8,128)(2,1)} %get-tuple-element.110.qkv_ref) | copy-start | bytes 7077892
  278.9 32.2 %collective-permute-start.15 = (bf16[16,24,3072]{2,1,0:T(8,128)(2,1)}, bf16[16,24,3072]{2,1,0:T(8,128)(2,1)}, u32[]{:S(2)}, u32[]{:S(2)}) collective-permute-start(bf16[16,24,3072]{2,1,0:T(8,128)(2,1)} %get-tuple-element.108), channel_id=1, source_target_pairs={{0,16},{16,0},{1,17},{17,1},{2,18},{18,2},{3,19},{19,3},{4,20},{20... | collective-permute-start | bytes 7077896 | tf_op jit(solution)/shard_map/ppermute | solution.py:31
  279.6 1.1 copy-start.2
  292.8 1.4 copy-start.3
  311.1 36.1 %collective-permute-start.16 = (bf16[16,24,3200]{2,1,0:T(8,128)(2,1)}, bf16[16,24,3200]{2,1,0:T(8,128)(2,1)}, u32[]{:S(2)}, u32[]{:S(2)}) collective-permute-start(bf16[16,24,3200]{2,1,0:T(8,128)(2,1)} %get-tuple-element.132), channel_id=1, source_target_pairs={{0,16},{16,0},{1,17},{17,1},{2,18},{18,2},{3,19},{19,3},{4,20},{20... | collective-permute-start | bytes 7372808 | tf_op jit(solution)/shard_map/ppermute | solution.py:31
  315.8 43.8 %all-to-all-start.4 = ((bf16[16,24,3072]{2,1,0:T(8,128)(2,1)}), bf16[16,24,3072]{2,1,0:T(8,128)(2,1)}, u32[]{:S(2)}, u32[]{:S(2)}) async-start(bf16[16,24,3072]{2,1,0:T(8,128)(2,1)} %add_convert_fusion.3), calls=%async_computation.4 | async-start | bytes 4718592 | tf_op jit(solution)/shard_map/all_to_all | solution.py:46
  344.7 3.0 copy-start.18
  359.6 14.2 %collective-permute-start.17 = (bf16[4,408,768]{2,1,0:T(8,128)(2,1)}, bf16[4,408,768]{2,1,0:T(8,128)(2,1)}, u32[]{:S(2)}, u32[]{:S(2)}) collective-permute-start(bf16[4,408,768]{2,1,0:T(8,128)(2,1)} %get-tuple-element.137), channel_id=1, source_target_pairs={{0,16},{16,0},{1,17},{17,1},{2,18},{18,2},{3,19},{19,3},{4,20},{20... | collective-permute-start | bytes 7520264 | tf_op jit(solution)/shard_map/ppermute | solution.py:31
  365.1 47.8 %all-to-all-start.5 = ((bf16[16,24,3200]{2,1,0:T(8,128)(2,1)}), bf16[16,24,3200]{2,1,0:T(8,128)(2,1)}, u32[]{:S(2)}, u32[]{:S(2)}) async-start(bf16[16,24,3200]{2,1,0:T(8,128)(2,1)} %add_convert_fusion.2), calls=%async_computation.5 | async-start | bytes 4915200 | tf_op jit(solution)/shard_map/all_to_all | solution.py:46
  378.2 17.7 %collective-permute-start.18 = (bf16[408,768]{1,0:T(8,128)(2,1)}, bf16[408,768]{1,0:T(8,128)(2,1)S(1)}, u32[]{:S(2)}, u32[]{:S(2)}) collective-permute-start(bf16[408,768]{1,0:T(8,128)(2,1)} %get-tuple-element.169), channel_id=1, source_target_pairs={{0,1},{1,2},{2,3},{3,0},{4,5},{5,6},{6,7},{7,4},{8,9},{9,10},{10,1... | collective-permute-start | bytes 1880072 | tf_op jit(solution)/shard_map/ppermute | solution.py:31
  379.7 17.3 %collective-permute-start.20 = (bf16[408,768]{1,0:T(8,128)(2,1)}, bf16[408,768]{1,0:T(8,128)(2,1)}, u32[]{:S(2)}, u32[]{:S(2)}) collective-permute-start(bf16[408,768]{1,0:T(8,128)(2,1)} %get-tuple-element.170), channel_id=1, source_target_pairs={{0,3},{1,0},{2,1},{3,2},{4,7},{5,4},{6,5},{7,6},{8,11},{9,8},{10,9... | collective-permute-start | bytes 1880072 | tf_op jit(solution)/shard_map/ppermute | solution.py:31
  381.4 28.9 %collective-permute-start.19 = (bf16[408,768]{1,0:T(8,128)(2,1)}, bf16[408,768]{1,0:T(8,128)(2,1)}, u32[]{:S(2)}, u32[]{:S(2)}) collective-permute-start(bf16[408,768]{1,0:T(8,128)(2,1)} %get-tuple-element.171), channel_id=1, source_target_pairs={{0,2},{1,3},{2,0},{3,1},{4,6},{5,7},{6,4},{7,5},{8,10},{9,11},{10,... | collective-permute-start | bytes 1880072 | tf_op jit(solution)/shard_map/ppermute | solution.py:31
  413.0 6.5 %copy-start.4 = (bf16[512,2304]{1,0:T(8,128)(2,1)S(1)}, bf16[512,2304]{1,0:T(8,128)(2,1)}, u32[]{:S(2)}) copy-start(bf16[512,2304]{1,0:T(8,128)(2,1)} %copy-done.3) | copy-start | bytes 7077892
  415.9 14.2 %all-to-all-start.6 = ((bf16[4,6,10240]{2,1,0:T(8,128)(2,1)}), bf16[4,6,10240]{2,1,0:T(8,128)(2,1)S(1)}, u32[]{:S(2)}, u32[]{:S(2)}) async-start(bf16[4,6,10240]{2,1,0:T(8,128)(2,1)} %constant_dynamic-update-slice_fusion.18), calls=%async_computation.6 | async-start | bytes 1310720 | tf_op jit(solution)/shard_map/all_to_all | solution.py:46
  419.4 5.8 %copy-start.14 = (f32[408,768]{1,0:T(8,128)S(1)}, f32[408,768]{1,0:T(8,128)}, u32[]{:S(2)}) copy-start(f32[408,768]{1,0:T(8,128)} %fusion.19) | copy-start | bytes 3760132
Sparse Core Ops, SparseCore 0:
  27.5 72.4 all-gather.1

commit v8 on v7

--- a/solution.py
+++ b/solution.py
@@ -554,44 +554,23 @@
     )
 
 
-def keep_halves(core, block, here, away):
-    for c in range(NC):
-
-        @pl.when(core == c)
-        def _():
-            here(block(c))
-
-        @pl.when(core != c)
-        def _():
-            away(block(c))
-
-
-def shrink_kernel(core_ref, act_ref, dffn_ref, dense_ref, loss_ref, here_ref, away_ref):
+def shrink_kernel(
+    core_ref, act_ref, dffn_ref, dense_ref, loss_ref, here_ref, away_ref, grad_ref
+):
     width = dffn_ref.shape[1]
-    grad = dot_tn(act_ref[...], dffn_ref[...])
+    grad_ref[...] = dot_tn(act_ref[...], dffn_ref[...])
     core = core_ref[0]
     spot = lax.broadcasted_iota(jnp.int32, (8, width), 1)
     first = lax.broadcasted_iota(jnp.int32, (8, width), 0) == 0
     told = jnp.zeros((8, width), F32)
     for i, value in enumerate(low_three(loss_ref[0:1, 0:1])):
         told = jnp.where(first & (spot == i + 3 * core), value, told)
-
-    def put(ref, extra):
-        def store(block):
-            tall, dense = block
-            for z in range(NZ):
-                ref[z, 0:96, :] = tall[z * 96 : (z + 1) * 96].astype(BF)
-                ref[z, 96:128, :] = jnp.concatenate(
-                    [dense[z * 24 : (z + 1) * 24], extra], axis=0
-                ).astype(BF)
-
-        return store
-
-    def block(c):
-        tall = grad[c * width // 2 : (c + 1) * width // 2]
-        return tall, dense_ref[c * 96 : (c + 1) * 96, :]
-
-    keep_halves(core, block, put(here_ref, told), put(away_ref, told))
+    for ref, c in ((here_ref, core), (away_ref, 1 - core)):
+        for z in range(NZ):
+            tall = pl.ds(pl.multiple_of(c * (width // 2) + z * 96, 8), 96)
+            flat = pl.ds(pl.multiple_of(c * 96 + z * 24, 8), 24)
+            ref[z, 0:96, :] = grad_ref[tall, :].astype(BF)
+            ref[z, 96:128, :] = jnp.concatenate([dense_ref[flat, :], told], axis=0).astype(BF)
 
 
 def shrink_call(core, act, dffn, g_dense, loss):
@@ -611,33 +590,29 @@
         ],
         [out, out],
         [half_spec, half_spec],
-        [],
+        [pltpu.VMEM((width, width), F32)],
         1000,
         1000,
     )
 
 
-def put_wide(grad, core, here_ref, away_ref, lanes):
-    def block(c):
-        return [grad[96 * (NC * y + c) : 96 * (NC * y + c) + 96] for y in range(NY)]
-
-    def put(ref):
-        def store(parts):
-            for y, part in enumerate(parts):
-                ref[y * NZ : (y + 1) * NZ, :, lanes] = part.reshape(NZ, 24, -1).astype(BF)
-
-        return store
-
-    keep_halves(core, block, put(here_ref), put(away_ref))
+def put_wide(grad_ref, core, here_ref, away_ref, lanes):
+    for ref, c in ((here_ref, core), (away_ref, 1 - core)):
+        for y in range(NY):
+            rows = pl.ds(pl.multiple_of((NC * y + c) * 96, 8), 96)
+            ref[y * NZ : (y + 1) * NZ, :, lanes] = (
+                grad_ref[rows, :].reshape(NZ, 24, -1).astype(BF)
+            )
 
 
 def feed_back_kernel(closing, core_ref, *refs):
     dffn_ref, shrink_ref, slope_ref, low_ref, expand_ref, before_ref = refs[:6]
     if closing:
         normed_ref, inverse_ref, vec_ref = refs[6:9]
-        here_ref, away_ref, bias_ref, dresidual_ref, dbranch_ref, sums_ref, total_ref = refs[11:]
+        here_ref, away_ref, bias_ref, dresidual_ref, dbranch_ref, sums_ref = refs[11:17]
+        grad_ref, total_ref = refs[17:]
     else:
-        here_ref, away_ref, bias_ref, total_ref = refs[6:]
+        here_ref, away_ref, bias_ref, total_ref, grad_ref = refs[6:]
     step = pl.program_id(0)
     dpre = (dot_nt(dffn_ref[...], shrink_ref[...]) * slope_ref[...].astype(F32)).astype(BF)
     bias_ref[...] = jnp.sum(dpre.astype(F32), axis=0, keepdims=True)
@@ -651,7 +626,8 @@
     def _():
         total_ref[...] += more
 
-    put_wide(dot_tn(low_ref[...], dpre), core_ref[0], here_ref, away_ref, slice(None))
+    grad_ref[...] = dot_tn(low_ref[...], dpre)
+    put_wide(grad_ref, core_ref[0], here_ref, away_ref, slice(None))
     if not closing:
         return
 
@@ -700,24 +676,27 @@
         in_specs=in_specs,
         out_specs=out_specs,
         out_shape=[jax.ShapeDtypeStruct(shape, kind) for shape, kind in outs],
-        scratch_shapes=[pltpu.VMEM((tokens, width), F32)] if closing else [],
+        scratch_shapes=[pltpu.VMEM((width, width), F32)]
+        + ([pltpu.VMEM((tokens, width), F32)] if closing else []),
         input_output_aliases={10: 0, 11: 1} if closing else {},
         compiler_params=pltpu.CompilerParams(vmem_limit_bytes=LIMIT),
         cost_estimate=pl.CostEstimate(flops=1000, bytes_accessed=1000, transcendentals=0),
     )(*ins)
 
 
-def last_kernel(core_ref, x_ref, dfused_ref, attended_ref, dbranch_ref, sums_ref, here_ref, away_ref):
+def last_kernel(
+    core_ref, x_ref, dfused_ref, attended_ref, dbranch_ref, sums_ref, here_ref, away_ref, grad_ref
+):
     width = x_ref.shape[1]
     core = core_ref[0]
     for i in range(4):
         lanes = slice(i * width, (i + 1) * width)
         if i < 3:
-            grad = dot_tn(x_ref[...], dfused_ref[:, lanes])
+            grad_ref[i % 2] = dot_tn(x_ref[...], dfused_ref[:, lanes])
         else:
-            grad = dot_tn(attended_ref[...], dbranch_ref[...])
-        put_wide(grad, core, here_ref, away_ref, lanes)
-    put_wide(sums_ref[...], core, here_ref, away_ref, slice(4 * width, 4 * width + 128))
+            grad_ref[i % 2] = dot_tn(attended_ref[...], dbranch_ref[...])
+        put_wide(grad_ref.at[i % 2], core, here_ref, away_ref, lanes)
+    put_wide(sums_ref, core, here_ref, away_ref, slice(4 * width, 4 * width + 128))
 
 
 def last_call(core, x, dfused, attended, dbranch, sums):
@@ -732,7 +711,7 @@
         [pl.BlockSpec(memory_space=pltpu.SMEM)] + [whole_spec(a) for a in ins],
         [out, out],
         [half_spec, half_spec],
-        [],
+        [pltpu.VMEM((2, width, width), F32)],
         1000,
         1000,
     )
@@ -989,7 +968,8 @@
     grad_w = grad_w.reshape(NC, NX, per, width)
     grad_w, grad_away = (jnp.concatenate([grad_w[i], grad_b[i]], axis=1) for i in range(NC))
     grad_w, grad_away, wide_all = after(grad_w, grad_away, wide_all)
-    grad_w = add_cores((grad_w, give(grad_away, "c", 1)))
+    grad_away, tall_all = after(give(grad_away, "c", 1), tall_all)
+    grad_w = add_cores((grad_w, grad_away))
     grad_w = total([grad_w[0]] + [give(grad_w[k], "x", k) for k in (1, 2, 3)])
 
     tall = jnp.sum(tall_all[:, :120].astype(F32), axis=0).astype(BF)

time: 450 us -> 448 us (level)
  transfers between devices with their start and end apart: 29 -> 29, of which waited for: 14 -> 14; matrix products, arithmetic and copies ran while one was open for 22% -> 21% of each run, Pallas kernels for 16% -> 15%
where the time goes in v8:
time: 448 us; the launch traced here: 441 us
  waiting for transfers between devices  120 us (27%)
  Pallas kernels  114 us (25%)
  starting transfers between devices  65 us (15%)
  local copies, waits for them, and re-layouts  49.5 us (11%)
  other arithmetic  42.3 us (9%)
  matrix products  28.6 us (6%)
  between operations  21.3 us (5%)
    pallas_call x6, Pallas kernels, call(): pl.pallas_call(kernel, grid=grid, in_specs=in_specs, out_specs=out_specs,...  69.6 us
    all_to_all x7, waiting for transfers between devices, swap(): return lax.all_to_all(array, axes, 0, 0, tiled=True)  59.4 us
    all_to_all x7, starting transfers between devices, swap(): return lax.all_to_all(array, axes, 0, 0, tiled=True)  37.7 us
    ppermute x7, waiting for transfers between devices, give(): return lax.ppermute(array, axis, [(i, (i + k) % n) for i in range(n)])  24 us
    dot_general x5, matrix products, matmul(): return jnp.dot(left, right, preferred_element_type=F32)  22.8 us
    pallas_call x2, Pallas kernels, feed_back_call(): pl.pallas_call(functools.partial(feed_back_kernel, closing), grid=(steps,...  21.5 us
    ppermute x14, starting transfers between devices, fetch(): return lax.ppermute(array, axis, [((i + k) % n, i) for i in range(n)])  21 us
    unnamed x99, local copies, waits for them, and re-layouts  18.7 us
  transfers between devices with their start and end apart: 29, of which 14 were waited for; matrix products, arithmetic and copies ran while one was open for 21% of the time, Pallas kernels for 15%

profile of v8, /device:TPU:0, one launch (start us, length us, event | category | flops | bytes accessed | tf_op | source)
XLA Modules:
  0.0 440.8 jit_solution(5936175353855280031)
XLA Ops:
  7.2 2.9 collective-permute-start
  10.2 2.3 collective-permute-start.1
  13.3 1.5 stack.176
  17.9 1.8 collective-permute-start.5
  21.3 2.0 collective-permute-start.3
  24.2 2.0 collective-permute-done.3
  27.3 2.7 collective-permute-start.7
  30.1 1.9 collective-permute-start.6
  32.1 3.1 collective-permute-start.10
  39.7 6.1 %collective-permute-done.7 = bf16[400,768]{1,0:T(8,128)(2,1)S(1)} collective-permute-done((bf16[400,768]{1,0:T(8,128)(2,1)S(1)}, bf16[400,768]{1,0:T(8,128)(2,1)S(1)}, u32[]{:S(2)}, u32[]{:S(2)}) %collective-permute-start.7) | collective-permute-done | bytes 614432 | tf_op jit(solution)/shard_map/ppermute | solution.py:26
  45.8 2.6 collective-permute-start.11
  48.4 9.1 %collective-permute-done.6 = bf16[400,768]{1,0:T(8,128)(2,1)S(1)} collective-permute-done((bf16[400,768]{1,0:T(8,128)(2,1)S(1)}, bf16[400,768]{1,0:T(8,128)(2,1)S(1)}, u32[]{:S(2)}, u32[]{:S(2)}) %collective-permute-start.6) | collective-permute-done | bytes 614432 | tf_op jit(solution)/shard_map/ppermute | solution.py:26
  58.5 1.7 pad_maximum_fusion.2
  65.1 1.4 select_reduce_fusion
  66.8 2.0 constant_dynamic-update-slice_fusion.16
  70.5 1.7 constant_dynamic-update-slice_fusion.13
  72.1 8.2 %fusion.12 = bf16[16,64,768]{2,1,0:T(8,128)(2,1)S(1)} fusion(bf16[3200,768,1]{1,0,2:T(8,128)(2,1)} %bitcast.159, s32[3200]{0:T(1024)S(1)} %add.332, s32[16,64]{1,0:T(8,128)S(1)} %reshape.318), kind=kOutput, calls=%fused_computation.26 | convolution fusion | flops 5037228032 | bytes 6504960 | tf_op jit(solution)/shard_map/dot_general | solution.py:130
  80.3 1.5 pad_maximum_fusion.3
  81.9 18.1 %all-gather.2.cloned.1.call-done.wq_ref.wk_ref.wv_ref.wa_ref.in_ref.dense_ref.refs_4_ = bf16[768,10112]{1,0:T(8,128)(2,1)} async-done(((bf16[24,10112]{1,0:T(8,128)(2,1)}), bf16[768,10112]{1,0:T(8,128)(2,1)}) %all-gather.2.cloned.1.call-update) | async-done | bytes 15532048 | tf_op jit(solution)/shard_map/all_gather | solution.py:795
  103.4 6.9 %shard_map.409 = bf16[32,4,24,768]{3,2,1,0:T(8,128)(2,1)} custom-call(bf16[768,10112]{1,0:T(8,128)(2,1)} %all-gather.2.cloned.1.call-done.wq_ref.wk_ref.wv_ref.wa_ref.in_ref.dense_ref.refs_4_), custom_call_target="tpu_custom_call" | custom-call | flops 1000 | bytes 1000 | tf_op jit(solution)/shard_map/pallas_call | solution.py:320
  110.3 5.5 %all-to-all-start = ((bf16[16,64,896]{2,1,0:T(8,128)(2,1)}), bf16[16,64,896]{2,1,0:T(8,128)(2,1)S(1)}, u32[]{:S(2)}, u32[]{:S(2)}) async-start(bf16[16,64,896]{2,1,0:T(8,128)(2,1)} %pad_maximum_fusion.3), calls=%async_computation | async-start | bytes 3670016 | tf_op jit(solution)/shard_map/all_to_all | solution.py:46
  116.1 11.0 %shard_map.408 = (bf16[512,2304]{1,0:T(8,128)(2,1)}, bf16[2,12,256,256]{3,2,1,0:T(8,128)(2,1)}, bf16[512,768]{1,0:T(8,128)(2,1)S(1)}, f32[512,768]{1,0:T(8,128)S...) custom-call(bf16[512,768]{1,0:T(8,128)(2,1)S(1)} %bitcast.134, ...), custom_call_target="tpu_custom_call" | custom-call | flops 4000000000 | bytes 16000000 | tf_op jit(solution)/shard_map/pallas_call | solution.py:211
  127.1 9.0 %fusion.7 = (bf16[512,3072]{1,0:T(8,128)(2,1)}, bf16[512,3072]{1,0:T(8,128)(2,1)S(1)}) fusion(f32[3072]{0:T(1024)S(1)} %reshape.314, bf16[512,768]{1,0:T(8,128)(2,1)S(1)} %get-tuple-element.86.refs_3_, bf16[768,10112]{1,0:T(8,128)(2,1)} %all-gather.2.cloned.1.call-done.wq_ref.wk_ref.wv_ref.wa_ref.in_ref.dense_ref.refs_4_), kind=kOutput, calls=%fused_computation.9 | convolution fusion | flops 2436366336 | bytes 11808768 | tf_op jit(solution)/shard_map/dot_general | solution.py:130
  136.1 2.7 fusion.43
  139.2 1.5 add_convert_fusion.4
  140.6 3.2 all-to-all-done
  144.1 2.8 fusion.27
  149.3 4.9 %all-to-all-start.1 = ((bf16[16,64,768]{2,1,0:T(8,128)(2,1)}), bf16[16,64,768]{2,1,0:T(8,128)(2,1)S(1)}, u32[]{:S(2)}, u32[]{:S(2)}) async-start(bf16[16,64,768]{2,1,0:T(8,128)(2,1)} %broadcast_in_dim.57), calls=%async_computation.1 | async-start | bytes 3145728 | tf_op jit(solution)/shard_map/all_to_all | solution.py:46
  156.7 21.2 %all-to-all-done.1 = bf16[16,64,768]{2,1,0:T(8,128)(2,1)S(1)} async-done(((bf16[16,64,768]{2,1,0:T(8,128)(2,1)}), bf16[16,64,768]{2,1,0:T(8,128)(2,1)S(1)}, u32[]{:S(2)}, u32[]{:S(2)}) %all-to-all-start.1) | async-done | bytes 1572896 | tf_op jit(solution)/shard_map/all_to_all | solution.py:46
  179.0 25.3 %shard_map.410 = (bf16[1024,3200]{1,0:T(8,128)(2,1)}, f32[1024,128]{1,0:T(8,128)}, bf16[16,80,768]{2,1,0:T(8,128)(2,1)}) custom-call(bf16[1024,768]{1,0:T(8,128)(2,1)} %bitcast.140, bf16[3200,768]{1,0:T(8,128)(2,1)} %bitcast.160, f32[1,3200]{1,0:T(1,128)} %reshape.315.b_ref, s32[1,3200]{1,0:T(1,128)} %add.359.column_ref, s32[1024,1]{1,0:T(8,128)} %copy.133.label_ref), custom_call_target="tpu_custom_call" | custom-call | flops 10000000000 | bytes 20000000 | tf_op jit(solution)/shard_map/pallas_call | solution.py:320
  204.3 3.9 all-to-all-start.2
  209.5 1.8 convert_reduce_fusion
  212.8 22.0 %all-to-all-done.2.part_ref = bf16[16,80,768]{2,1,0:T(8,128)(2,1)S(1)} async-done(((bf16[16,80,768]{2,1,0:T(8,128)(2,1)}), bf16[16,80,768]{2,1,0:T(8,128)(2,1)S(1)}, u32[]{:S(2)}, u32[]{:S(2)}) %all-to-all-start.2) | async-done | bytes 1966112 | tf_op jit(solution)/shard_map/all_to_all | solution.py:46
  236.1 7.1 %shard_map.411 = (f32[1,1024]{1,0:T(1,128)}, f32[8,128]{1,0:T(8,128)}, f32[768,768]{1,0:T(8,128)}, f32[512,768]{1,0:T(8,128)}, bf16[512,768]{1,0:T(8,128)(2,1)}, /*index=5*/f32[8,768]{1,0:T(8,128)}) custom-call(s32[1]{0:T(128)} %bitcast.47.own_ref, bf16[16,80,768]{2,1,0:T(8,128)(2,1)} %copy-done.11, bf16[64,768]{1,0:T(8,128)(2,1)} %copy-done.27, ...), custom_call_target="tpu_custom_call" | custom-call | flops 300000000 | bytes 10000000 | tf_op jit(solution)/shard_map/pallas_call | solution.py:320
  243.2 7.5 %shard_map.412 = (bf16[16,128,768]{2,1,0:T(8,128)(2,1)}, bf16[16,128,768]{2,1,0:T(8,128)(2,1)}) custom-call(s32[1]{0:T(128)} %bitcast.53.core_ref, bf16[512,3072]{1,0:T(8,128)(2,1)} %copy-done.15, bf16[512,768]{1,0:T(8,128)(2,1)} %get-tuple-element.103.dffn_ref.refs_0_, f32[768,768]{1,0:T(8,128)} %get-tuple-element.99.dense_ref, ...), custom_call_target="tpu_custom_call" | custom-call | flops 1000 | bytes 1000 | tf_op jit(solution)/shard_map/pallas_call | solution.py:320
  250.7 9.9 %shard_map.413 = (bf16[16,24,3072]{2,1,0:T(8,128)(2,1)}, bf16[16,24,3072]{2,1,0:T(8,128)(2,1)}, f32[1,1536]{1,0:T(1,128)}, f32[512,768]{1,0:T(8,128)}) custom-call(s32[1]{0:T(128)} %bitcast.53.core_ref, bf16[512,768]{1,0:T(8,128)(2,1)} %get-tuple-element.103.dffn_ref.refs_0_, bf16[3072,768]{1,0:T(8,128)(2,1)} %bitcast.135, ...), custom_call_target="tpu_custom_call" | custom-call | flops 1000 | bytes 1000 | tf_op jit(solution)/shard_map/pallas_call | solution.py:673
  260.6 2.6 add_convert_fusion
  263.2 3.8 all-to-all-start.3
  267.1 11.6 %shard_map.414 = (bf16[16,24,3072]{2,1,0:T(8,128)(2,1)}, bf16[16,24,3072]{2,1,0:T(8,128)(2,1)}, f32[1,1536]{1,0:T(1,128)}, f32[512,768]{1,0:T(8,128)}, bf16[512,768]{1,0:T(8,128)(2,1)}, /*index=5*/f32[8,768]{1,0:T(8,128)}) custom-call(s32[1]{0:T(128)} %bitcast.53.core_ref, ...), custom_call_target="tpu_custom_call", output_to_operand_aliasing={{0}: (10, {}), {1}: (11, {})} | custom-call | flops 1000 | bytes 1000 | tf_op jit(solution)/shard_map/pallas_call | solution.py:673
  280.6 12.1 %shard_map.415 = (bf16[512,2304]{1,0:T(8,128)(2,1)S(1)}, f32[1,2304]{1,0:T(1,128)S(1)}) custom-call(bf16[512,768]{1,0:T(8,128)(2,1)S(1)} %copy-done.2, bf16[512,2304]{1,0:T(8,128)(2,1)S(1)} %copy-done.5, bf16[2,12,256,256]{3,2,1,0:T(8,128)(2,1)} %get-tuple-element.117.probs_ref, ...), custom_call_target="tpu_custom_call" | custom-call | flops 1000 | bytes 1000 | tf_op jit(solution)/shard_map/pallas_call | solution.py:291
  292.7 1.4 copy-done.3
  299.7 1.9 select_maximum_fusion.sums_ref
  301.6 7.7 %shard_map.416 = (bf16[16,24,3200]{2,1,0:T(8,128)(2,1)}, bf16[16,24,3200]{2,1,0:T(8,128)(2,1)}) custom-call(s32[1]{0:T(128)} %bitcast.53.core_ref, bf16[512,768]{1,0:T(8,128)(2,1)} %bitcast.133, bf16[512,2304]{1,0:T(8,128)(2,1)} %copy-done.3, bf16[512,768]{1,0:T(8,128)(2,1)} %copy-done.7, bf16[512,768]{1,0:T(8,128)(2,1)} %get-tuple-element.115.dbranch_ref, ...), custom_call_target="tpu_custom_call" | custom-call | flops 1000 | bytes 1000 | tf_op jit(solution)/shard_map/pallas_call | solution.py:320
  309.3 1.8 all-to-all-done.3
  311.0 4.6 %add_convert_fusion.3 = bf16[16,24,3072]{2,1,0:T(8,128)(2,1)} fusion(bf16[16,24,3072]{2,1,0:T(8,128)(2,1)} %collective-permute-done.15, bf16[16,24,3072]{2,1,0:T(8,128)(2,1)} %get-tuple-element.113), kind=kLoop, calls=%fused_computation.15 | loop fusion | flops 4718592 | bytes 7077888 | tf_op jit(solution)/shard_map/convert_element_type | solution.py:65
  315.7 9.9 %all-to-all-start.4 = ((bf16[16,24,3072]{2,1,0:T(8,128)(2,1)}), bf16[16,24,3072]{2,1,0:T(8,128)(2,1)}, u32[]{:S(2)}, u32[]{:S(2)}) async-start(bf16[16,24,3072]{2,1,0:T(8,128)(2,1)} %add_convert_fusion.3), calls=%async_computation.4 | async-start | bytes 4718592 | tf_op jit(solution)/shard_map/all_to_all | solution.py:46
  325.6 15.2 %shard_map.417 = (bf16[3200,768]{1,0:T(8,128)(2,1)}, f32[1,3200]{1,0:T(1,128)}) custom-call(bf16[1024,3200]{1,0:T(8,128)(2,1)} %get-tuple-element.92.expl_ref, bf16[1024,768]{1,0:T(8,128)(2,1)} %bitcast.141, s32[1,3200]{1,0:T(1,128)} %add.359.column_ref, s32[1024,1]{1,0:T(8,128)} %copy.133.label_ref, f32[1024,1]{1,0:T(8,128)} %select_multiply_fusion.scale_ref, ...), custom_call_target="tpu_custom_call" | custom-call | flops 1000 | bytes 1000 | tf_op jit(solution)/shard_map/pallas_call | solution.py:320
  341.6 2.8 fusion.39
  344.4 2.5 pad_maximum_fusion
  347.4 3.8 add_convert_fusion.2
  351.2 8.1 %all-to-all-done.4 = bf16[16,24,3072]{2,1,0:T(8,128)(2,1)} async-done(((bf16[16,24,3072]{2,1,0:T(8,128)(2,1)}), bf16[16,24,3072]{2,1,0:T(8,128)(2,1)}, u32[]{:S(2)}, u32[]{:S(2)}) %all-to-all-start.4) | async-done | bytes 2359328 | tf_op jit(solution)/shard_map/all_to_all | solution.py:46
  359.5 6.2 %all-to-all-start.5 = ((bf16[16,24,3200]{2,1,0:T(8,128)(2,1)}), bf16[16,24,3200]{2,1,0:T(8,128)(2,1)}, u32[]{:S(2)}, u32[]{:S(2)}) async-start(bf16[16,24,3200]{2,1,0:T(8,128)(2,1)} %add_convert_fusion.2), calls=%async_computation.5 | async-start | bytes 4915200 | tf_op jit(solution)/shard_map/all_to_all | solution.py:46
  365.8 2.1 reduce_sum.135
  375.2 3.1 add_convert_fusion.1
  378.4 1.5 collective-permute-start.18
  379.9 1.8 collective-permute-start.20
  381.7 1.9 collective-permute-start.19
  386.3 9.6 %collective-permute-done.18 = bf16[408,768]{1,0:T(8,128)(2,1)S(1)} collective-permute-done((bf16[408,768]{1,0:T(8,128)(2,1)S(1)}, bf16[408,768]{1,0:T(8,128)(2,1)S(1)}, u32[]{:S(2)}, u32[]{:S(2)}) %collective-permute-start.18) | collective-permute-done | bytes 626720 | tf_op jit(solution)/shard_map/ppermute | solution.py:31
  395.9 12.7 %collective-permute-done.20 = bf16[408,768]{1,0:T(8,128)(2,1)S(1)} collective-permute-done((bf16[408,768]{1,0:T(8,128)(2,1)S(1)}, bf16[408,768]{1,0:T(8,128)(2,1)S(1)}, u32[]{:S(2)}, u32[]{:S(2)}) %collective-permute-start.20) | collective-permute-done | bytes 626720 | tf_op jit(solution)/shard_map/ppermute | solution.py:31
  408.6 1.6 collective-permute-done.19
  411.6 2.2 reduce_sum.136
  414.6 3.5 all-to-all-start.6
  418.1 5.7 %fusion.15 = f32[512,768]{1,0:T(8,128)} fusion(f32[512,768]{1,0:T(8,128)} %get-tuple-element.143, bf16[512,2304]{1,0:T(8,128)(2,1)S(1)} %copy-done.4, bf16[768,10112]{1,0:T(8,128)(2,1)} %all-gather.2.cloned.1.call-done.wq_ref.wk_ref.wv_ref.wa_ref.in_ref.dense_ref.refs_4_), kind=kOutput, calls=%fused_computation.31 | convolution fusion | flops 1812332544 | bytes 9043968 | tf_op jit(solution)/shard_map/dot_general | solution.py:138
  425.5 3.2 all-to-all-done.6
  (232 shorter events, 56.1 us)
Async XLA Ops:
  7.2 92.8 %all-gather.2.cloned.1.call-start = ((), (), s32[]{:S(2)}) async-start(), calls=%async_computation.7 | async-start | bytes 16017408 | tf_op jit(solution)/shard_map/all_gather | solution.py:795
  7.2 14.1 %collective-permute-start = (bf16[24,768]{1,0:T(8,128)(2,1)}, bf16[24,768]{1,0:T(8,128)(2,1)S(1)}, u32[]{:S(2)}, u32[]{:S(2)}) collective-permute-start(bf16[24,768]{1,0:T(8,128)(2,1)} %param.40), channel_id=1, source_target_pairs={{1,0},{2,1},{3,2},{0,3},{5,4},{6,5},{7,6},{4,7},{9,8},{10,9},{11,1... | collective-permute-start | bytes 110600 | tf_op jit(solution)/shard_map/ppermute | solution.py:26
  10.1 13.1 %collective-permute-start.2 = (bf16[24,768]{1,0:T(8,128)(2,1)}, bf16[24,768]{1,0:T(8,128)(2,1)S(1)}, u32[]{:S(2)}, u32[]{:S(2)}) collective-permute-start(bf16[24,768]{1,0:T(8,128)(2,1)} %param.40), channel_id=1, source_target_pairs={{3,0},{0,1},{1,2},{2,3},{7,4},{4,5},{5,6},{6,7},{11,8},{8,9},{9,10... | collective-permute-start | bytes 110600 | tf_op jit(solution)/shard_map/ppermute | solution.py:26
  10.2 13.1 %collective-permute-start.1 = (bf16[24,768]{1,0:T(8,128)(2,1)}, bf16[24,768]{1,0:T(8,128)(2,1)S(1)}, u32[]{:S(2)}, u32[]{:S(2)}) collective-permute-start(bf16[24,768]{1,0:T(8,128)(2,1)} %param.40), channel_id=1, source_target_pairs={{2,0},{3,1},{0,2},{1,3},{6,4},{7,5},{4,6},{5,7},{10,8},{11,9},{8,1... | collective-permute-start | bytes 110600 | tf_op jit(solution)/shard_map/ppermute | solution.py:26
  17.9 8.3 %collective-permute-start.5 = (bf16[6,7040]{1,0:T(8,128)(2,1)S(1)}, bf16[6,7040]{1,0:T(8,128)(2,1)S(1)}, u32[]{:S(2)}, u32[]{:S(2)}) collective-permute-start(bf16[6,7040]{1,0:T(8,128)(2,1)S(1)} %constant_dynamic-update-slice_fusion.8), channel_id=1, source_target_pairs={{3,0},{0,1},{1,2},{2,3},{7,4},{4,5},{5,6},{6,7},{11,8},{8,9},{9,10... | collective-permute-start | bytes 253448 | tf_op jit(solution)/shard_map/ppermute | solution.py:26
  19.7 6.5 %collective-permute-start.4 = (bf16[6,7040]{1,0:T(8,128)(2,1)S(1)}, bf16[6,7040]{1,0:T(8,128)(2,1)S(1)}, u32[]{:S(2)}, u32[]{:S(2)}) collective-permute-start(bf16[6,7040]{1,0:T(8,128)(2,1)S(1)} %constant_dynamic-update-slice_fusion.8), channel_id=1, source_target_pairs={{2,0},{3,1},{0,2},{1,3},{6,4},{7,5},{4,6},{5,7},{10,8},{11,9},{8,1... | collective-permute-start | bytes 253448 | tf_op jit(solution)/shard_map/ppermute | solution.py:26
  21.3 4.9 %collective-permute-start.3 = (bf16[6,7040]{1,0:T(8,128)(2,1)S(1)}, bf16[6,7040]{1,0:T(8,128)(2,1)S(1)}, u32[]{:S(2)}, u32[]{:S(2)}) collective-permute-start(bf16[6,7040]{1,0:T(8,128)(2,1)S(1)} %constant_dynamic-update-slice_fusion.8), channel_id=1, source_target_pairs={{1,0},{2,1},{3,2},{0,3},{5,4},{6,5},{7,6},{4,7},{9,8},{10,9},{11,1... | collective-permute-start | bytes 253448 | tf_op jit(solution)/shard_map/ppermute | solution.py:26
  24.1 3.2 copy-start.19
  24.1 8.0 %copy-start.34 = (bf16[400]{0:T(512)(128)(2,1)S(1)}, bf16[400]{0:T(512)(128)(2,1)}, u32[]{:S(2)}) copy-start(bf16[400]{0:T(512)(128)(2,1)} %param.49) | copy-start | bytes 2404
  24.2 11.8 %copy-start.33 = (s32[2,1,16,2]{2,3,1,0:T(2,128)S(1)}, s32[2,1,16,2]{2,3,1,0:T(2,128)}, u32[]{:S(2)}) copy-start(s32[2,1,16,2]{2,3,1,0:T(2,128)} %param.28) | copy-start | bytes 772
  24.2 12.0 %copy-start.30 = (s32[2,128,16,2]{1,3,2,0:T(2,128)S(1)}, s32[2,128,16,2]{1,3,2,0:T(2,128)}, u32[]{:S(2)}) copy-start(s32[2,128,16,2]{1,3,2,0:T(2,128)} %param.29) | copy-start | bytes 98308
  27.3 18.4 %collective-permute-start.7 = (bf16[400,768]{1,0:T(8,128)(2,1)S(1)}, bf16[400,768]{1,0:T(8,128)(2,1)S(1)}, u32[]{:S(2)}, u32[]{:S(2)}) collective-permute-start(bf16[400,768]{1,0:T(8,128)(2,1)S(1)} %bitcast.146), channel_id=1, source_target_pairs={{2,0},{3,1},{0,2},{1,3},{6,4},{7,5},{4,6},{5,7},{10,8},{11,9},{8,1... | collective-permute-start | bytes 1843208 | tf_op jit(solution)/shard_map/ppermute | solution.py:26
  30.1 27.4 %collective-permute-start.6 = (bf16[400,768]{1,0:T(8,128)(2,1)S(1)}, bf16[400,768]{1,0:T(8,128)(2,1)S(1)}, u32[]{:S(2)}, u32[]{:S(2)}) collective-permute-start(bf16[400,768]{1,0:T(8,128)(2,1)S(1)} %bitcast.147), channel_id=1, source_target_pairs={{1,0},{2,1},{3,2},{0,3},{5,4},{6,5},{7,6},{4,7},{9,8},{10,9},{11,1... | collective-permute-start | bytes 1843208 | tf_op jit(solution)/shard_map/ppermute | solution.py:26
  31.9 25.6 %collective-permute-start.8 = (bf16[400,768]{1,0:T(8,128)(2,1)S(1)}, bf16[400,768]{1,0:T(8,128)(2,1)S(1)}, u32[]{:S(2)}, u32[]{:S(2)}) collective-permute-start(bf16[400,768]{1,0:T(8,128)(2,1)S(1)} %bitcast.148), channel_id=1, source_target_pairs={{3,0},{0,1},{1,2},{2,3},{7,4},{4,5},{5,6},{6,7},{11,8},{8,9},{9,10... | collective-permute-start | bytes 1843208 | tf_op jit(solution)/shard_map/ppermute | solution.py:26
  32.1 30.1 %collective-permute-start.10 = (bf16[400]{0:T(512)(128)(2,1)S(1)}, bf16[400]{0:T(512)(128)(2,1)S(1)}, u32[]{:S(2)}, u32[]{:S(2)}) collective-permute-start(bf16[400]{0:T(512)(128)(2,1)S(1)} %copy-done.34), channel_id=1, source_target_pairs={{1,0},{2,1},{3,2},{0,3},{5,4},{6,5},{7,6},{4,7},{9,8},{10,9},{11,1... | collective-permute-start | bytes 2408 | tf_op jit(solution)/shard_map/ppermute | solution.py:26
  35.2 27.1 %collective-permute-start.12 = (bf16[400]{0:T(512)(128)(2,1)S(1)}, bf16[400]{0:T(512)(128)(2,1)S(1)}, u32[]{:S(2)}, u32[]{:S(2)}) collective-permute-start(bf16[400]{0:T(512)(128)(2,1)S(1)} %copy-done.34), channel_id=1, source_target_pairs={{3,0},{0,1},{1,2},{2,3},{7,4},{4,5},{5,6},{6,7},{11,8},{8,9},{9,10... | collective-permute-start | bytes 2408 | tf_op jit(solution)/shard_map/ppermute | solution.py:26
  45.8 11.7 %copy-start.20 = (bf16[400,768]{1,0:T(8,128)(2,1)}, bf16[400,768]{1,0:T(8,128)(2,1)S(1)}, u32[]{:S(2)}) copy-start(bf16[400,768]{1,0:T(8,128)(2,1)S(1)} %collective-permute-done.7) | copy-start | bytes 1843204
  45.8 16.5 %collective-permute-start.11 = (bf16[400]{0:T(512)(128)(2,1)S(1)}, bf16[400]{0:T(512)(128)(2,1)S(1)}, u32[]{:S(2)}, u32[]{:S(2)}) collective-permute-start(bf16[400]{0:T(512)(128)(2,1)S(1)} %copy-done.34), channel_id=1, source_target_pairs={{2,0},{3,1},{0,2},{1,3},{6,4},{7,5},{4,6},{5,7},{10,8},{11,9},{8,1... | collective-permute-start | bytes 2408 | tf_op jit(solution)/shard_map/ppermute | solution.py:26
  57.5 0.8 copy-start.24
  57.5 1.0 copy-start.22
  58.5 2.7 copy-start.25
  58.5 2.7 copy-start.26
  60.2 3.3 copy-start.32
  60.2 10.2 %collective-permute-start.9 = (bf16[4,400,768]{2,1,0:T(8,128)(2,1)}, bf16[4,400,768]{2,1,0:T(8,128)(2,1)S(1)}, u32[]{:S(2)}, u32[]{:S(2)}) collective-permute-start(bf16[4,400,768]{2,1,0:T(8,128)(2,1)} %pad_maximum_fusion.2), channel_id=1, source_target_pairs={{16,0},{0,16},{17,1},{1,17},{18,2},{2,18},{19,3},{3,19},{20,4},{4,... | collective-permute-start | bytes 7372808 | tf_op jit(solution)/shard_map/ppermute | solution.py:26
  60.3 83.5 %copy-start.28 = (bf16[64,512]{1,0:T(8,128)(2,1)}, bf16[64,512]{1,0:T(8,128)(2,1)S(1)}, u32[]{:S(2)}) copy-start(bf16[64,512]{1,0:T(8,128)(2,1)S(1)} %fusion.28.select_ref) | copy-start | bytes 196612
  61.2 7.5 %copy-start.21 = (bf16[400,768]{1,0:T(8,128)(2,1)S(1)}, bf16[400,768]{1,0:T(8,128)(2,1)}, u32[]{:S(2)}) copy-start(bf16[400,768]{1,0:T(8,128)(2,1)} %copy-done.20) | copy-start | bytes 1843204
  62.3 2.6 collective-permute-start.13
  65.0 4.6 %copy-start.23 = (bf16[400,768]{1,0:T(8,128)(2,1)S(1)}, bf16[400,768]{1,0:T(8,128)(2,1)}, u32[]{:S(2)}) copy-start(bf16[400,768]{1,0:T(8,128)(2,1)} %copy-done.22) | copy-start | bytes 1843204
  102.3 13.7 %copy-start.8 = (f32[16,768]{1,0:T(8,128)}, f32[16,768]{1,0:T(8,128)S(1)}, u32[]{:S(2)}) copy-start(f32[16,768]{1,0:T(8,128)S(1)} %copy.132.vec_ref.refs_8_) | copy-start | bytes 147460
  110.3 5.8 %copy-start = (bf16[2,256,768]{2,1,0:T(8,128)(2,1)S(1)}, bf16[2,256,768]{2,1,0:T(8,128)(2,1)}, u32[]{:S(2)}) copy-start(bf16[2,256,768]{2,1,0:T(8,128)(2,1)} %param.25) | copy-start | bytes 2359300
  110.3 33.5 %all-to-all-start = ((bf16[16,64,896]{2,1,0:T(8,128)(2,1)}), bf16[16,64,896]{2,1,0:T(8,128)(2,1)S(1)}, u32[]{:S(2)}, u32[]{:S(2)}) async-start(bf16[16,64,896]{2,1,0:T(8,128)(2,1)} %pad_maximum_fusion.3), calls=%async_computation | async-start | bytes 3670016 | tf_op jit(solution)/shard_map/all_to_all | solution.py:46
  127.1 9.0 %copy-start.1 = (bf16[512,768]{1,0:T(8,128)(2,1)}, bf16[512,768]{1,0:T(8,128)(2,1)S(1)}, u32[]{:S(2)}) copy-start(bf16[512,768]{1,0:T(8,128)(2,1)S(1)} %get-tuple-element.86.refs_3_) | copy-start | bytes 2359300
  127.1 9.0 %copy-start.6 = (f32[512,768]{1,0:T(8,128)}, f32[512,768]{1,0:T(8,128)S(1)}, u32[]{:S(2)}) copy-start(f32[512,768]{1,0:T(8,128)S(1)} %get-tuple-element.109.refs_6_) | copy-start | bytes 4718596
  127.1 9.0 %copy-start.7 = (bf16[512,768]{1,0:T(8,128)(2,1)}, bf16[512,768]{1,0:T(8,128)(2,1)S(1)}, u32[]{:S(2)}) copy-start(bf16[512,768]{1,0:T(8,128)(2,1)S(1)} %get-tuple-element.119.attended_ref) | copy-start | bytes 2359300
  127.1 9.0 %copy-start.9 = (f32[512,1]{1,0:T(8,128)}, f32[512,1]{1,0:T(8,128)S(1)}, u32[]{:S(2)}) copy-start(f32[512,1]{1,0:T(8,128)S(1)} %get-tuple-element.110.refs_7_) | copy-start | bytes 6148
  127.1 9.0 %copy-start.10 = (bf16[32,4,24,768]{3,2,1,0:T(8,128)(2,1)S(1)}, bf16[32,4,24,768]{3,2,1,0:T(8,128)(2,1)}, u32[]{:S(2)}) copy-start(bf16[32,4,24,768]{3,2,1,0:T(8,128)(2,1)} %shard_map.409) | copy-start | bytes 14155780
  136.1 2.7 copy-start.15
  140.6 8.7 %copy-start.17 = (bf16[512,768]{1,0:T(8,128)(2,1)}, bf16[512,768]{1,0:T(8,128)(2,1)S(1)}, u32[]{:S(2)}) copy-start(bf16[512,768]{1,0:T(8,128)(2,1)S(1)} %get-tuple-element.167) | copy-start | bytes 2359300
  143.8 5.5 %copy-start.12 = (bf16[16,64,896]{2,1,0:T(8,128)(2,1)}, bf16[16,64,896]{2,1,0:T(8,128)(2,1)S(1)}, u32[]{:S(2)}) copy-start(bf16[16,64,896]{2,1,0:T(8,128)(2,1)S(1)} %all-to-all-done) | copy-start | bytes 5505028
  144.1 5.3 %copy-start.29 = (bf16[64,768]{1,0:T(8,128)(2,1)}, bf16[64,768]{1,0:T(8,128)(2,1)S(1)}, u32[]{:S(2)}) copy-start(bf16[64,768]{1,0:T(8,128)(2,1)S(1)} %convolution_convert_fusion.picked_ref) | copy-start | bytes 294916
  148.0 8.7 %copy-start.27 = (bf16[64,768]{1,0:T(8,128)(2,1)}, bf16[64,768]{1,0:T(8,128)(2,1)S(1)}, u32[]{:S(2)}) copy-start(bf16[64,768]{1,0:T(8,128)(2,1)S(1)} %get-tuple-element.165.head_ref) | copy-start | bytes 294916
  149.3 28.5 %all-to-all-start.1 = ((bf16[16,64,768]{2,1,0:T(8,128)(2,1)}), bf16[16,64,768]{2,1,0:T(8,128)(2,1)S(1)}, u32[]{:S(2)}, u32[]{:S(2)}) async-start(bf16[16,64,768]{2,1,0:T(8,128)(2,1)} %broadcast_in_dim.57), calls=%async_computation.1 | async-start | bytes 3145728 | tf_op jit(solution)/shard_map/all_to_all | solution.py:46
  177.9 1.2 copy-start.13
  204.3 30.4 %all-to-all-start.2 = ((bf16[16,80,768]{2,1,0:T(8,128)(2,1)}), bf16[16,80,768]{2,1,0:T(8,128)(2,1)S(1)}, u32[]{:S(2)}, u32[]{:S(2)}) async-start(bf16[16,80,768]{2,1,0:T(8,128)(2,1)} %get-tuple-element.95), calls=%async_computation.2 | async-start | bytes 3932160 | tf_op jit(solution)/shard_map/all_to_all | solution.py:46
  234.8 1.3 copy-start.11
  250.7 9.9 %collective-permute-start.14 = (bf16[16,128,768]{2,1,0:T(8,128)(2,1)}, bf16[16,128,768]{2,1,0:T(8,128)(2,1)S(1)}, u32[]{:S(2)}, u32[]{:S(2)}) collective-permute-start(bf16[16,128,768]{2,1,0:T(8,128)(2,1)} %get-tuple-element.107), channel_id=1, source_target_pairs={{0,16},{16,0},{1,17},{17,1},{2,18},{18,2},{3,19},{19,3},{4,20},{20... | collective-permute-start | bytes 9437192 | tf_op jit(solution)/shard_map/ppermute | solution.py:31
  250.7 9.9 %copy-start.16 = (bf16[16,128,768]{2,1,0:T(8,128)(2,1)S(1)}, bf16[16,128,768]{2,1,0:T(8,128)(2,1)}, u32[]{:S(2)}) copy-start(bf16[16,128,768]{2,1,0:T(8,128)(2,1)} %get-tuple-element.106) | copy-start | bytes 9437188
  263.2 47.8 %all-to-all-start.3 = ((bf16[16,128,768]{2,1,0:T(8,128)(2,1)}), bf16[16,128,768]{2,1,0:T(8,128)(2,1)S(1)}, u32[]{:S(2)}, u32[]{:S(2)}) async-start(bf16[16,128,768]{2,1,0:T(8,128)(2,1)} %add_convert_fusion), calls=%async_computation.3 | async-start | bytes 6291456 | tf_op jit(solution)/shard_map/all_to_all | solution.py:46
  267.0 12.4 %copy-start.31 = (f32[8,768]{1,0:T(8,128)S(1)}, f32[8,768]{1,0:T(8,128)}, u32[]{:S(2)}) copy-start(f32[8,768]{1,0:T(8,128)} %get-tuple-element.122) | copy-start | bytes 73732
  267.1 12.4 %copy-start.5 = (bf16[512,2304]{1,0:T(8,128)(2,1)S(1)}, bf16[512,2304]{1,0:T(8,128)(2,1)}, u32[]{:S(2)}) copy-start(bf16[512,2304]{1,0:T(8,128)(2,1)} %get-tuple-element.116.qkv_ref) | copy-start | bytes 7077892
  278.7 32.4 %collective-permute-start.15 = (bf16[16,24,3072]{2,1,0:T(8,128)(2,1)}, bf16[16,24,3072]{2,1,0:T(8,128)(2,1)}, u32[]{:S(2)}, u32[]{:S(2)}) collective-permute-start(bf16[16,24,3072]{2,1,0:T(8,128)(2,1)} %get-tuple-element.114), channel_id=1, source_target_pairs={{0,16},{16,0},{1,17},{17,1},{2,18},{18,2},{3,19},{19,3},{4,20},{20... | collective-permute-start | bytes 7077896 | tf_op jit(solution)/shard_map/ppermute | solution.py:31
  279.4 1.1 copy-start.2
  292.7 1.4 copy-start.3
  311.0 35.9 %collective-permute-start.16 = (bf16[16,24,3200]{2,1,0:T(8,128)(2,1)}, bf16[16,24,3200]{2,1,0:T(8,128)(2,1)}, u32[]{:S(2)}, u32[]{:S(2)}) collective-permute-start(bf16[16,24,3200]{2,1,0:T(8,128)(2,1)} %get-tuple-element.133), channel_id=1, source_target_pairs={{0,16},{16,0},{1,17},{17,1},{2,18},{18,2},{3,19},{19,3},{4,20},{20... | collective-permute-start | bytes 7372808 | tf_op jit(solution)/shard_map/ppermute | solution.py:31
  315.7 43.6 %all-to-all-start.4 = ((bf16[16,24,3072]{2,1,0:T(8,128)(2,1)}), bf16[16,24,3072]{2,1,0:T(8,128)(2,1)}, u32[]{:S(2)}, u32[]{:S(2)}) async-start(bf16[16,24,3072]{2,1,0:T(8,128)(2,1)} %add_convert_fusion.3), calls=%async_computation.4 | async-start | bytes 4718592 | tf_op jit(solution)/shard_map/all_to_all | solution.py:46
  344.4 3.0 copy-start.18
  359.3 8.6 %collective-permute-start.17 = (bf16[4,408,768]{2,1,0:T(8,128)(2,1)}, bf16[4,408,768]{2,1,0:T(8,128)(2,1)}, u32[]{:S(2)}, u32[]{:S(2)}) collective-permute-start(bf16[4,408,768]{2,1,0:T(8,128)(2,1)} %get-tuple-element.135), channel_id=1, source_target_pairs={{0,16},{16,0},{1,17},{17,1},{2,18},{18,2},{3,19},{19,3},{4,20},{20... | collective-permute-start | bytes 7520264 | tf_op jit(solution)/shard_map/ppermute | solution.py:31
  359.5 52.1 %all-to-all-start.5 = ((bf16[16,24,3200]{2,1,0:T(8,128)(2,1)}), bf16[16,24,3200]{2,1,0:T(8,128)(2,1)}, u32[]{:S(2)}, u32[]{:S(2)}) async-start(bf16[16,24,3200]{2,1,0:T(8,128)(2,1)} %add_convert_fusion.2), calls=%async_computation.5 | async-start | bytes 4915200 | tf_op jit(solution)/shard_map/all_to_all | solution.py:46
  378.4 17.5 %collective-permute-start.18 = (bf16[408,768]{1,0:T(8,128)(2,1)S(1)}, bf16[408,768]{1,0:T(8,128)(2,1)S(1)}, u32[]{:S(2)}, u32[]{:S(2)}) collective-permute-start(bf16[408,768]{1,0:T(8,128)(2,1)S(1)} %get-tuple-element.173), channel_id=1, source_target_pairs={{0,1},{1,2},{2,3},{3,0},{4,5},{5,6},{6,7},{7,4},{8,9},{9,10},{10,1... | collective-permute-start | bytes 1880072 | tf_op jit(solution)/shard_map/ppermute | solution.py:31
  379.9 28.7 %collective-permute-start.20 = (bf16[408,768]{1,0:T(8,128)(2,1)S(1)}, bf16[408,768]{1,0:T(8,128)(2,1)S(1)}, u32[]{:S(2)}, u32[]{:S(2)}) collective-permute-start(bf16[408,768]{1,0:T(8,128)(2,1)S(1)} %get-tuple-element.174), channel_id=1, source_target_pairs={{0,3},{1,0},{2,1},{3,2},{4,7},{5,4},{6,5},{7,6},{8,11},{9,8},{10,9... | collective-permute-start | bytes 1880072 | tf_op jit(solution)/shard_map/ppermute | solution.py:31
  381.7 28.5 %collective-permute-start.19 = (bf16[408,768]{1,0:T(8,128)(2,1)S(1)}, bf16[408,768]{1,0:T(8,128)(2,1)S(1)}, u32[]{:S(2)}, u32[]{:S(2)}) collective-permute-start(bf16[408,768]{1,0:T(8,128)(2,1)S(1)} %get-tuple-element.175), channel_id=1, source_target_pairs={{0,2},{1,3},{2,0},{3,1},{4,6},{5,7},{6,4},{7,5},{8,10},{9,11},{10,... | collective-permute-start | bytes 1880072 | tf_op jit(solution)/shard_map/ppermute | solution.py:31
  411.6 6.5 %copy-start.4 = (bf16[512,2304]{1,0:T(8,128)(2,1)S(1)}, bf16[512,2304]{1,0:T(8,128)(2,1)}, u32[]{:S(2)}) copy-start(bf16[512,2304]{1,0:T(8,128)(2,1)} %copy-done.3) | copy-start | bytes 7077892
  414.6 14.2 %all-to-all-start.6 = ((bf16[4,6,10240]{2,1,0:T(8,128)(2,1)}), bf16[4,6,10240]{2,1,0:T(8,128)(2,1)S(1)}, u32[]{:S(2)}, u32[]{:S(2)}) async-start(bf16[4,6,10240]{2,1,0:T(8,128)(2,1)} %constant_dynamic-update-slice_fusion.18), calls=%async_computation.6 | async-start | bytes 1310720 | tf_op jit(solution)/shard_map/all_to_all | solution.py:46
  418.1 5.8 %copy-start.14 = (f32[408,768]{1,0:T(8,128)S(1)}, f32[408,768]{1,0:T(8,128)}, u32[]{:S(2)}) copy-start(f32[408,768]{1,0:T(8,128)} %fusion.19) | copy-start | bytes 3760132
Sparse Core Ops, SparseCore 0:
  27.5 72.4 all-gather.1

commit v9 on v8

--- a/solution.py
+++ b/solution.py
@@ -241,7 +241,7 @@
         ],
         compiler_params=pltpu.CompilerParams(vmem_limit_bytes=48 * 1024 * 1024),
         cost_estimate=pl.CostEstimate(
-            flops=4_000_000_000, bytes_accessed=16_000_000, transcendentals=2_000_000
+            flops=1000, bytes_accessed=1000, transcendentals=0
         ),
     )(x, segments[:, None, :], segments[:, :, None], layer, layer, layer, layer, vec)
 
@@ -717,25 +717,122 @@
     )
 
 
-def tall_kernel(in_ref, out_ref):
-    blocks_, rows, width = out_ref.shape
-    out_ref[...] = in_ref[...].astype(F32).reshape(blocks_, rows, width).astype(BF)
-
-
-def tall_call(layer, width):
-    places = NY * NC * NZ
-    rows = layer.shape[0] // places
+def feed_kernel(
+    low_ref,
+    expand_ref,
+    bias_ref,
+    tall_ref,
+    first_ref,
+    vec_ref,
+    select_ref,
+    dense_ref,
+    act_ref,
+    slope_ref,
+    shrink_ref,
+    settled_ref,
+    normed2_ref,
+    inverse2_ref,
+    picked_ref,
+    head_ref,
+    spread_ref,
+    normed3_ref,
+    inverse3_ref,
+    slope3_ref,
+    total_ref,
+    rows_ref,
+):
+    step = pl.program_id(0)
+    width = low_ref.shape[1]
+    groups, places, rows, _ = rows_ref.shape
+    for k in range(places):
+        part = tall_ref[:, k * width : (k + 1) * width].astype(F32)
+        rows_ref[:, k] = part.reshape(groups, rows, width)
+    shrink = rows_ref[...].reshape(width, width).astype(BF)
+    shrink_ref[...] = shrink
+    pre = dot_nn(low_ref[...], expand_ref[...]) + bias_ref[...]
+    half = 0.5 * (1.0 + lax.erf(pre * HALF_ROOT))
+    act = (pre * half).astype(BF)
+    act_ref[...] = act
+    slope_ref[...] = (half + pre * NORMAL_PEAK * jnp.exp(-0.5 * pre * pre)).astype(BF)
+    more = dot_nn(act, shrink)
+
+    @pl.when(step == 0)
+    def _():
+        total_ref[...] = first_ref[...] + more
+
+    @pl.when(step > 0)
+    def _():
+        total_ref[...] += more
+
+    @pl.when(step == pl.num_programs(0) - 1)
+    def _():
+        second = total_ref[...] + vec_ref[5:6]
+        settled, normed2, inverse2 = layer_norm(second, vec_ref[6:7], vec_ref[7:8])
+        low = settled.astype(BF)
+        settled_ref[...] = low
+        normed2_ref[...] = normed2
+        inverse2_ref[...] = inverse2
+        picked = dot_nn(select_ref[...], low).astype(BF)
+        picked_ref[...] = picked
+        dense = dot_nn(picked, dense_ref[...]) + vec_ref[8:9]
+        value, normed3, inverse3 = layer_norm(gelu_value(dense), vec_ref[9:10], vec_ref[10:11])
+        head = value.astype(BF)
+        head_ref[...] = head
+        for i in range(spread_ref.shape[0]):
+            spread_ref[i] = head
+        normed3_ref[...] = normed3
+        inverse3_ref[...] = inverse3
+        slope3_ref[...] = gelu_slope(dense)
+
+
+def feed_call(low, layer, expand_block, dense_block, b_expand, first, vec, select):
+    tokens, width = low.shape
+    wide = b_expand.shape[0]
+    steps = wide // width
+    count = select.shape[0]
+    places = NY * NC * NZ // steps
+    rows = layer.shape[0] // (NY * NC * NZ)
+    bias = b_expand[None, :]
+    chunk = pl.BlockSpec((tokens, width), lambda j: (0, j))
+    outs = [
+        ((tokens, wide), BF),
+        ((tokens, wide), BF),
+        ((wide, width), BF),
+        ((tokens, width), BF),
+        ((tokens, width), F32),
+        ((tokens, 1), F32),
+        ((count, width), BF),
+        ((count, width), BF),
+        ((NY * NZ, count, width), BF),
+        ((count, width), F32),
+        ((count, 1), F32),
+        ((count, width), F32),
+    ]
+    out_specs = [chunk, chunk, pl.BlockSpec((width, width), lambda j: (j, 0))]
+    for shape, _ in outs[3:]:
+        out_specs.append(
+            pl.BlockSpec(shape, (lambda j: (0, 0)) if len(shape) == 2 else (lambda j: (0, 0, 0)))
+        )
     return call(
-        tall_kernel,
-        (2, NX),
-        (layer,),
-        [pl.BlockSpec((layer.shape[0] // 2, width), lambda j, k: (j, k))],
-        [((places, NX, rows, width), BF)],
-        [pl.BlockSpec((places // 2, None, rows, width), lambda j, k: (j, k, 0, 0))],
-        [],
+        feed_kernel,
+        (steps,),
+        (low, layer, bias, layer, first, vec, select, layer),
+        [
+            whole_spec(low),
+            pl.BlockSpec((width, width), lambda j: (0, expand_block + j)),
+            pl.BlockSpec((1, width), lambda j: (0, j)),
+            pl.BlockSpec((places * rows, NX * width), lambda j: (j, 0)),
+            whole_spec(first),
+            whole_spec(vec),
+            whole_spec(select),
+            pl.BlockSpec((width, width), lambda j: (0, dense_block)),
+        ],
+        outs,
+        out_specs,
+        [pltpu.VMEM((tokens, width), F32), pltpu.VMEM((places, NX, rows, width), F32)],
         1000,
         1000,
-    )[0].reshape(-1, width)
+    )
 
 
 def body(
@@ -852,7 +949,6 @@
     attn_block = ends[2] // width
     dense_full = layer[:, ends[3] : ends[4]]
     vec_full = layer[:, ends[4] :]
-    shrink_full = tall_call(layer, width)
     rows_of = vec_full[:, :16].T.astype(F32)
     (
         b_query,
@@ -873,23 +969,25 @@
     qkv, probs, attended, first, first_low, normed1, inverse1 = attention_forward(
         x, segments, layer, attn_block - 3, rows_of
     )
-    pre = matmul(first_low, expand_full) + b_expand
-    act = gelu_value(pre).astype(BF)
-    slope = gelu_slope(pre).astype(BF)
-    second = first + matmul(act, shrink_full) + b_shrink
-    settled, normed2, inverse2 = layer_norm(second, ffn_gain, ffn_shift)
-    settled_low = settled.astype(BF)
-
-    select, label_w = after(select, label_w)
+    (
+        act,
+        slope,
+        shrink_full,
+        settled_low,
+        normed2,
+        inverse2,
+        picked,
+        head_out,
+        head_sent,
+        normed3,
+        inverse3,
+        slope3,
+    ) = feed_call(first_low, layer, 4, attn_block + 1, b_expand, first, rows_of, select)
+
+    head_sent, label_w = after(head_sent, label_w)
     label_w = jnp.sum(label_w.astype(F32), axis=0)
     label_w, label_b = label_w[:, :width], label_w[:, width]
-    picked = matmul(select, settled_low).astype(BF)
-    dense_pre = matmul(picked, dense_full) + b_dense
-    head_val, normed3, inverse3 = layer_norm(gelu_value(dense_pre), dense_gain, dense_shift)
-    head_out = head_val.astype(BF)
-    spread = swap(
-        jnp.broadcast_to(head_out, (NY * NZ,) + head_out.shape), ("y", "z")
-    ).reshape(-1, width)
+    spread = swap(head_sent, ("y", "z")).reshape(-1, width)
     expl, stat, part = logits_call(spread, vocab_w, vocab_b, column, labels, rows)
     part = swap(part, ("y", "z"))
     scalars = jnp.stack(
@@ -902,7 +1000,7 @@
         label_w,
         jnp.pad(scalars, ((0, 0), (0, 124))),
         normed3,
-        gelu_slope(dense_pre),
+        slope3,
         rows_of,
         picked,
         select,

time: 448 us -> 441 us (0.984)
  matrix products: 28.6 us -> 13.9 us
  Pallas kernels: 114 us -> 123 us
    dot_general x5 -> x1, matrix products: 22.8 us -> 8.18 us  [matmul(): return jnp.dot(left, right, preferred_element_type=F32)]
    pallas_call x6, Pallas kernels: 69.6 us -> 78.5 us  [call(): pl.pallas_call(kernel, grid=grid, in_specs=in_specs, out_specs=out_specs,...]
    unnamed x99 -> x89, local copies, waits for them, and re-layouts: 18.7 us -> 22.3 us
  transfers between devices with their start and end apart: 29 -> 29, of which waited for: 14 -> 13; matrix products, arithmetic and copies ran while one was open for 21% -> 19% of each run, Pallas kernels for 15% -> 19%
where the time goes in v9:
time: 441 us; the launch traced here: 434 us
  Pallas kernels  123 us (28%)
  waiting for transfers between devices  118 us (27%)
  starting transfers between devices  67.7 us (15%)
  local copies, waits for them, and re-layouts  50.1 us (11%)
  other arithmetic  40 us (9%)
  between operations  21.3 us (5%)
  matrix products  13.9 us (3%)
    pallas_call x6, Pallas kernels, call(): pl.pallas_call(kernel, grid=grid, in_specs=in_specs, out_specs=out_specs,...  78.5 us
    all_to_all x7, waiting for transfers between devices, swap(): return lax.all_to_all(array, axes, 0, 0, tiled=True)  57.3 us
    all_to_all x7, starting transfers between devices, swap(): return lax.all_to_all(array, axes, 0, 0, tiled=True)  40.5 us
    ppermute x7, waiting for transfers between devices, give(): return lax.ppermute(array, axis, [(i, (i + k) % n) for i in range(n)])  24.2 us
    unnamed x89, local copies, waits for them, and re-layouts  22.3 us
    pallas_call x2, Pallas kernels, feed_back_call(): pl.pallas_call(functools.partial(feed_back_kernel, closing), grid=(steps,...  21.4 us
    ppermute x14, starting transfers between devices, fetch(): return lax.ppermute(array, axis, [((i + k) % n, i) for i in range(n)])  21 us
    all_gather x1, waiting for transfers between devices, body(): lax.all_gather(jnp.concatenate([tall, fused], axis=1), ('y', 'c', 'z'), a...  18.1 us
  transfers between devices with their start and end apart: 29, of which 13 were waited for; matrix products, arithmetic and copies ran while one was open for 19% of the time, Pallas kernels for 19%

profile of v9, /device:TPU:0, one launch (start us, length us, event | category | flops | bytes accessed | tf_op | source)
XLA Modules:
  0.0 433.6 jit_solution(17689648131109348204)
XLA Ops:
  7.2 2.9 collective-permute-start
  10.2 2.3 collective-permute-start.1
  13.3 1.5 stack.176
  17.9 1.8 collective-permute-start.5
  21.3 2.0 collective-permute-start.3
  24.2 2.0 collective-permute-done.3
  27.4 2.7 collective-permute-start.7
  30.1 1.9 collective-permute-start.6
  32.1 3.1 collective-permute-start.10
  37.3 1.4 reshape.264
  39.7 6.1 %collective-permute-done.7 = bf16[400,768]{1,0:T(8,128)(2,1)S(1)} collective-permute-done((bf16[400,768]{1,0:T(8,128)(2,1)S(1)}, bf16[400,768]{1,0:T(8,128)(2,1)S(1)}, u32[]{:S(2)}, u32[]{:S(2)}) %collective-permute-start.7) | collective-permute-done | bytes 614432 | tf_op jit(solution)/shard_map/ppermute | solution.py:26
  45.8 2.6 collective-permute-start.11
  48.4 9.1 %collective-permute-done.6 = bf16[400,768]{1,0:T(8,128)(2,1)S(1)} collective-permute-done((bf16[400,768]{1,0:T(8,128)(2,1)S(1)}, bf16[400,768]{1,0:T(8,128)(2,1)S(1)}, u32[]{:S(2)}, u32[]{:S(2)}) %collective-permute-start.6) | collective-permute-done | bytes 614432 | tf_op jit(solution)/shard_map/ppermute | solution.py:26
  58.5 1.7 pad_maximum_fusion.2
  65.1 1.4 select_reduce_fusion
  66.8 1.9 constant_dynamic-update-slice_fusion.16
  70.5 1.7 constant_dynamic-update-slice_fusion.13
  72.2 8.2 %fusion.6 = bf16[16,64,768]{2,1,0:T(8,128)(2,1)S(1)} fusion(bf16[3200,768,1]{1,0,2:T(8,128)(2,1)} %bitcast.143, s32[3200]{0:T(1024)S(1)} %add.230, s32[16,64]{1,0:T(8,128)S(1)} %reshape.263), kind=kOutput, calls=%fused_computation.17 | convolution fusion | flops 5037228032 | bytes 6504960 | tf_op jit(solution)/shard_map/dot_general | solution.py:130
  80.3 1.5 pad_maximum_fusion.3
  81.8 18.1 %all-gather.2.cloned.1.call-done.wq_ref.wk_ref.wv_ref.wa_ref.expand_ref.tall_ref.dense_ref.refs_4_ = bf16[768,10112]{1,0:T(8,128)(2,1)} async-done(((bf16[24,10112]{1,0:T(8,128)(2,1)}), bf16[768,10112]{1,0:T(8,128)(2,1)}) %all-gather.2.cloned.1.call-update) | async-done | bytes 15532048 | tf_op jit(solution)/shard_map/all_gather | solution.py:892
  100.0 5.4 %all-to-all-start = ((bf16[16,64,896]{2,1,0:T(8,128)(2,1)}), bf16[16,64,896]{2,1,0:T(8,128)(2,1)S(1)}, u32[]{:S(2)}, u32[]{:S(2)}) async-start(bf16[16,64,896]{2,1,0:T(8,128)(2,1)} %pad_maximum_fusion.3), calls=%async_computation | async-start | bytes 3670016 | tf_op jit(solution)/shard_map/all_to_all | solution.py:46
  106.6 11.0 %shard_map.408 = (bf16[512,2304]{1,0:T(8,128)(2,1)}, bf16[2,12,256,256]{3,2,1,0:T(8,128)(2,1)}, bf16[512,768]{1,0:T(8,128)(2,1)S(1)}, f32[512,768]{1,0:T(8,128)S...) custom-call(bf16[512,768]{1,0:T(8,128)(2,1)S(1)} %bitcast.124, ...), custom_call_target="tpu_custom_call" | custom-call | flops 1000 | bytes 1000 | tf_op jit(solution)/shard_map/pallas_call | solution.py:211
  118.5 1.2 copy-done.6
  124.4 15.8 %shard_map.409 = (bf16[512,3072]{1,0:T(8,128)(2,1)}, bf16[512,3072]{1,0:T(8,128)(2,1)}, bf16[3072,768]{1,0:T(8,128)(2,1)}, bf16[512,768]{1,0:T(8,128)(2,1)}, f32...) custom-call(bf16[512,768]{1,0:T(8,128)(2,1)} %copy-done, ...), custom_call_target="tpu_custom_call" | custom-call | flops 1000 | bytes 1000 | tf_op jit(solution)/shard_map/pallas_call | solution.py:320
  140.2 7.8 %all-to-all-start.1 = ((bf16[16,64,768]{2,1,0:T(8,128)(2,1)}), bf16[16,64,768]{2,1,0:T(8,128)(2,1)}, u32[]{:S(2)}, u32[]{:S(2)}) async-start(bf16[16,64,768]{2,1,0:T(8,128)(2,1)} %get-tuple-element.103), calls=%async_computation.1 | async-start | bytes 3145728 | tf_op jit(solution)/shard_map/all_to_all | solution.py:46
  150.5 21.2 %all-to-all-done.1 = bf16[16,64,768]{2,1,0:T(8,128)(2,1)} async-done(((bf16[16,64,768]{2,1,0:T(8,128)(2,1)}), bf16[16,64,768]{2,1,0:T(8,128)(2,1)}, u32[]{:S(2)}, u32[]{:S(2)}) %all-to-all-start.1) | async-done | bytes 1572896 | tf_op jit(solution)/shard_map/all_to_all | solution.py:46
  171.8 25.3 %shard_map.410 = (bf16[1024,3200]{1,0:T(8,128)(2,1)}, f32[1024,128]{1,0:T(8,128)}, bf16[16,80,768]{2,1,0:T(8,128)(2,1)}) custom-call(bf16[1024,768]{1,0:T(8,128)(2,1)} %bitcast.45.spread_ref, bf16[3200,768]{1,0:T(8,128)(2,1)} %bitcast.144, f32[1,3200]{1,0:T(1,128)} %reshape.260.b_ref, s32[1,3200]{1,0:T(1,128)} %add.234.column_ref, s32[1024,1]{1,0:T(8,128)} %copy.134.label_ref), custom_call_target="tpu_custom_call" | custom-call | flops 10000000000 | bytes 20000000 | tf_op jit(solution)/shard_map/pallas_call | solution.py:320
  197.0 3.9 all-to-all-start.2
  201.3 1.8 convert_reduce_fusion
  204.5 23.0 %all-to-all-done.2.part_ref = bf16[16,80,768]{2,1,0:T(8,128)(2,1)S(1)} async-done(((bf16[16,80,768]{2,1,0:T(8,128)(2,1)}), bf16[16,80,768]{2,1,0:T(8,128)(2,1)S(1)}, u32[]{:S(2)}, u32[]{:S(2)}) %all-to-all-start.2) | async-done | bytes 1966112 | tf_op jit(solution)/shard_map/all_to_all | solution.py:46
  227.5 1.3 copy-done.11
  228.8 7.1 %shard_map.411 = (f32[1,1024]{1,0:T(1,128)}, f32[8,128]{1,0:T(8,128)}, f32[768,768]{1,0:T(8,128)}, f32[512,768]{1,0:T(8,128)}, bf16[512,768]{1,0:T(8,128)(2,1)}, /*index=5*/f32[8,768]{1,0:T(8,128)}) custom-call(s32[1]{0:T(128)} %bitcast.46.own_ref, bf16[16,80,768]{2,1,0:T(8,128)(2,1)} %copy-done.11, bf16[64,768]{1,0:T(8,128)(2,1)} %get-tuple-element.110.head_ref, ...), custom_call_target="tpu_custom_call" | custom-call | flops 300000000 | bytes 10000000 | tf_op jit(solution)/shard_map/pallas_call | solution.py:320
  235.9 7.5 %shard_map.412 = (bf16[16,128,768]{2,1,0:T(8,128)(2,1)}, bf16[16,128,768]{2,1,0:T(8,128)(2,1)}) custom-call(s32[1]{0:T(128)} %bitcast.50.core_ref, bf16[512,3072]{1,0:T(8,128)(2,1)} %get-tuple-element.119.act_ref, bf16[512,768]{1,0:T(8,128)(2,1)} %get-tuple-element.125.dffn_ref.refs_0_, f32[768,768]{1,0:T(8,128)} %get-tuple-element.121.dense_ref, ...), custom_call_target="tpu_custom_call" | custom-call | flops 1000 | bytes 1000 | tf_op jit(solution)/shard_map/pallas_call | solution.py:320
  243.5 9.8 %shard_map.413 = (bf16[16,24,3072]{2,1,0:T(8,128)(2,1)}, bf16[16,24,3072]{2,1,0:T(8,128)(2,1)}, f32[1,1536]{1,0:T(1,128)}, f32[512,768]{1,0:T(8,128)}) custom-call(s32[1]{0:T(128)} %bitcast.50.core_ref, bf16[512,768]{1,0:T(8,128)(2,1)} %get-tuple-element.125.dffn_ref.refs_0_, bf16[3072,768]{1,0:T(8,128)(2,1)} %get-tuple-element.126.refs_1_, ...), custom_call_target="tpu_custom_call" | custom-call | flops 1000 | bytes 1000 | tf_op jit(solution)/shard_map/pallas_call | solution.py:673
  253.3 2.7 add_convert_fusion
  256.0 3.8 all-to-all-start.3
  259.8 11.6 %shard_map.414 = (bf16[16,24,3072]{2,1,0:T(8,128)(2,1)}, bf16[16,24,3072]{2,1,0:T(8,128)(2,1)}, f32[1,1536]{1,0:T(1,128)}, f32[512,768]{1,0:T(8,128)}, bf16[512,768]{1,0:T(8,128)(2,1)}, /*index=5*/f32[8,768]{1,0:T(8,128)}) custom-call(s32[1]{0:T(128)} %bitcast.50.core_ref, ...), custom_call_target="tpu_custom_call", output_to_operand_aliasing={{0}: (10, {}), {1}: (11, {})} | custom-call | flops 1000 | bytes 1000 | tf_op jit(solution)/shard_map/pallas_call | solution.py:673
  273.3 12.1 %shard_map.415 = (bf16[512,2304]{1,0:T(8,128)(2,1)S(1)}, f32[1,2304]{1,0:T(1,128)S(1)}) custom-call(bf16[512,768]{1,0:T(8,128)(2,1)S(1)} %copy-done.2, bf16[512,2304]{1,0:T(8,128)(2,1)S(1)} %copy-done.5, bf16[2,12,256,256]{3,2,1,0:T(8,128)(2,1)} %get-tuple-element.141.probs_ref, ...), custom_call_target="tpu_custom_call" | custom-call | flops 1000 | bytes 1000 | tf_op jit(solution)/shard_map/pallas_call | solution.py:291
  285.3 1.4 copy-done.3
  288.2 1.3 stack.204
  292.4 1.9 select_maximum_fusion.sums_ref
  294.3 7.7 %shard_map.416 = (bf16[16,24,3200]{2,1,0:T(8,128)(2,1)}, bf16[16,24,3200]{2,1,0:T(8,128)(2,1)}) custom-call(s32[1]{0:T(128)} %bitcast.50.core_ref, bf16[512,768]{1,0:T(8,128)(2,1)} %bitcast.123, bf16[512,2304]{1,0:T(8,128)(2,1)} %copy-done.3, bf16[512,768]{1,0:T(8,128)(2,1)} %copy-done.9, bf16[512,768]{1,0:T(8,128)(2,1)} %get-tuple-element.139.dbranch_ref, ...), custom_call_target="tpu_custom_call" | custom-call | flops 1000 | bytes 1000 | tf_op jit(solution)/shard_map/pallas_call | solution.py:320
  302.0 1.8 all-to-all-done.3
  303.7 4.6 %add_convert_fusion.3 = bf16[16,24,3072]{2,1,0:T(8,128)(2,1)} fusion(bf16[16,24,3072]{2,1,0:T(8,128)(2,1)} %collective-permute-done.15, bf16[16,24,3072]{2,1,0:T(8,128)(2,1)} %get-tuple-element.137), kind=kLoop, calls=%fused_computation.8 | loop fusion | flops 4718592 | bytes 7077888 | tf_op jit(solution)/shard_map/convert_element_type | solution.py:65
  308.4 9.9 %all-to-all-start.4 = ((bf16[16,24,3072]{2,1,0:T(8,128)(2,1)}), bf16[16,24,3072]{2,1,0:T(8,128)(2,1)}, u32[]{:S(2)}, u32[]{:S(2)}) async-start(bf16[16,24,3072]{2,1,0:T(8,128)(2,1)} %add_convert_fusion.3), calls=%async_computation.4 | async-start | bytes 4718592 | tf_op jit(solution)/shard_map/all_to_all | solution.py:46
  318.3 15.1 %shard_map.417 = (bf16[3200,768]{1,0:T(8,128)(2,1)}, f32[1,3200]{1,0:T(1,128)}) custom-call(bf16[1024,3200]{1,0:T(8,128)(2,1)} %get-tuple-element.106.expl_ref, bf16[1024,768]{1,0:T(8,128)(2,1)} %bitcast.45.spread_ref, s32[1,3200]{1,0:T(1,128)} %add.234.column_ref, s32[1024,1]{1,0:T(8,128)} %copy.134.label_ref, f32[1024,1]{1,0:T(8,128)} %select_multiply_fusion.scale_ref, ...), custom_call_target="tpu_custom_call" | custom-call | flops 1000 | bytes 1000 | tf_op jit(solution)/shard_map/pallas_call | solution.py:320
  334.2 2.8 fusion.23
  337.0 2.5 pad_maximum_fusion
  340.0 3.9 add_convert_fusion.2
  343.9 8.1 %all-to-all-done.4 = bf16[16,24,3072]{2,1,0:T(8,128)(2,1)} async-done(((bf16[16,24,3072]{2,1,0:T(8,128)(2,1)}), bf16[16,24,3072]{2,1,0:T(8,128)(2,1)}, u32[]{:S(2)}, u32[]{:S(2)}) %all-to-all-start.4) | async-done | bytes 2359328 | tf_op jit(solution)/shard_map/all_to_all | solution.py:46
  352.2 6.2 %all-to-all-start.5 = ((bf16[16,24,3200]{2,1,0:T(8,128)(2,1)}), bf16[16,24,3200]{2,1,0:T(8,128)(2,1)}, u32[]{:S(2)}, u32[]{:S(2)}) async-start(bf16[16,24,3200]{2,1,0:T(8,128)(2,1)} %add_convert_fusion.2), calls=%async_computation.5 | async-start | bytes 4915200 | tf_op jit(solution)/shard_map/all_to_all | solution.py:46
  358.4 2.1 reduce_sum.95
  367.9 3.1 add_convert_fusion.1
  371.1 1.6 collective-permute-start.18
  372.6 1.8 collective-permute-start.20
  374.4 1.8 collective-permute-start.19
  378.8 9.8 %collective-permute-done.18 = bf16[408,768]{1,0:T(8,128)(2,1)S(1)} collective-permute-done((bf16[408,768]{1,0:T(8,128)(2,1)S(1)}, bf16[408,768]{1,0:T(8,128)(2,1)S(1)}, u32[]{:S(2)}, u32[]{:S(2)}) %collective-permute-start.18) | collective-permute-done | bytes 626720 | tf_op jit(solution)/shard_map/ppermute | solution.py:31
  388.6 12.7 %collective-permute-done.20 = bf16[408,768]{1,0:T(8,128)(2,1)S(1)} collective-permute-done((bf16[408,768]{1,0:T(8,128)(2,1)S(1)}, bf16[408,768]{1,0:T(8,128)(2,1)S(1)}, u32[]{:S(2)}, u32[]{:S(2)}) %collective-permute-start.20) | collective-permute-done | bytes 626720 | tf_op jit(solution)/shard_map/ppermute | solution.py:31
  401.3 1.6 collective-permute-done.19
  402.9 1.4 fusion.13
  404.3 2.2 reduce_sum.96
  407.3 3.5 all-to-all-start.6
  410.8 5.7 %fusion.9 = f32[512,768]{1,0:T(8,128)} fusion(f32[512,768]{1,0:T(8,128)} %get-tuple-element.167, bf16[512,2304]{1,0:T(8,128)(2,1)S(1)} %copy-done.4, bf16[768,10112]{1,0:T(8,128)(2,1)} %all-gather.2.cloned.1.call-done.wq_ref.wk_ref.wv_ref.wa_ref.expand_ref.tall_ref.dense_ref.refs_4_), kind=kOutput, calls=%fused_computation.18 | convolution fusion | flops 1812332544 | bytes 9043968 | tf_op jit(solution)/shard_map/dot_general | solution.py:138
  418.2 3.2 all-to-all-done.6
  (205 shorter events, 48.7 us)
Async XLA Ops:
  7.2 92.8 %all-gather.2.cloned.1.call-start = ((), (), s32[]{:S(2)}) async-start(), calls=%async_computation.7 | async-start | bytes 16017408 | tf_op jit(solution)/shard_map/all_gather | solution.py:892
  7.2 14.1 %collective-permute-start = (bf16[24,768]{1,0:T(8,128)(2,1)}, bf16[24,768]{1,0:T(8,128)(2,1)S(1)}, u32[]{:S(2)}, u32[]{:S(2)}) collective-permute-start(bf16[24,768]{1,0:T(8,128)(2,1)} %param.40), channel_id=1, source_target_pairs={{1,0},{2,1},{3,2},{0,3},{5,4},{6,5},{7,6},{4,7},{9,8},{10,9},{11,1... | collective-permute-start | bytes 110600 | tf_op jit(solution)/shard_map/ppermute | solution.py:26
  10.1 13.1 %collective-permute-start.2 = (bf16[24,768]{1,0:T(8,128)(2,1)}, bf16[24,768]{1,0:T(8,128)(2,1)S(1)}, u32[]{:S(2)}, u32[]{:S(2)}) collective-permute-start(bf16[24,768]{1,0:T(8,128)(2,1)} %param.40), channel_id=1, source_target_pairs={{3,0},{0,1},{1,2},{2,3},{7,4},{4,5},{5,6},{6,7},{11,8},{8,9},{9,10... | collective-permute-start | bytes 110600 | tf_op jit(solution)/shard_map/ppermute | solution.py:26
  10.2 13.1 %collective-permute-start.1 = (bf16[24,768]{1,0:T(8,128)(2,1)}, bf16[24,768]{1,0:T(8,128)(2,1)S(1)}, u32[]{:S(2)}, u32[]{:S(2)}) collective-permute-start(bf16[24,768]{1,0:T(8,128)(2,1)} %param.40), channel_id=1, source_target_pairs={{2,0},{3,1},{0,2},{1,3},{6,4},{7,5},{4,6},{5,7},{10,8},{11,9},{8,1... | collective-permute-start | bytes 110600 | tf_op jit(solution)/shard_map/ppermute | solution.py:26
  17.9 8.3 %collective-permute-start.5 = (bf16[6,7040]{1,0:T(8,128)(2,1)S(1)}, bf16[6,7040]{1,0:T(8,128)(2,1)S(1)}, u32[]{:S(2)}, u32[]{:S(2)}) collective-permute-start(bf16[6,7040]{1,0:T(8,128)(2,1)S(1)} %constant_dynamic-update-slice_fusion.8), channel_id=1, source_target_pairs={{3,0},{0,1},{1,2},{2,3},{7,4},{4,5},{5,6},{6,7},{11,8},{8,9},{9,10... | collective-permute-start | bytes 253448 | tf_op jit(solution)/shard_map/ppermute | solution.py:26
  19.7 6.5 %collective-permute-start.4 = (bf16[6,7040]{1,0:T(8,128)(2,1)S(1)}, bf16[6,7040]{1,0:T(8,128)(2,1)S(1)}, u32[]{:S(2)}, u32[]{:S(2)}) collective-permute-start(bf16[6,7040]{1,0:T(8,128)(2,1)S(1)} %constant_dynamic-update-slice_fusion.8), channel_id=1, source_target_pairs={{2,0},{3,1},{0,2},{1,3},{6,4},{7,5},{4,6},{5,7},{10,8},{11,9},{8,1... | collective-permute-start | bytes 253448 | tf_op jit(solution)/shard_map/ppermute | solution.py:26
  21.3 4.9 %collective-permute-start.3 = (bf16[6,7040]{1,0:T(8,128)(2,1)S(1)}, bf16[6,7040]{1,0:T(8,128)(2,1)S(1)}, u32[]{:S(2)}, u32[]{:S(2)}) collective-permute-start(bf16[6,7040]{1,0:T(8,128)(2,1)S(1)} %constant_dynamic-update-slice_fusion.8), channel_id=1, source_target_pairs={{1,0},{2,1},{3,2},{0,3},{5,4},{6,5},{7,6},{4,7},{9,8},{10,9},{11,1... | collective-permute-start | bytes 253448 | tf_op jit(solution)/shard_map/ppermute | solution.py:26
  24.1 3.2 copy-start.16
  24.1 8.0 %copy-start.29 = (bf16[400]{0:T(512)(128)(2,1)S(1)}, bf16[400]{0:T(512)(128)(2,1)}, u32[]{:S(2)}) copy-start(bf16[400]{0:T(512)(128)(2,1)} %param.49) | copy-start | bytes 2404
  24.2 11.8 %copy-start.28 = (s32[2,1,16,2]{2,3,1,0:T(2,128)S(1)}, s32[2,1,16,2]{2,3,1,0:T(2,128)}, u32[]{:S(2)}) copy-start(s32[2,1,16,2]{2,3,1,0:T(2,128)} %param.28) | copy-start | bytes 772
  24.2 12.0 %copy-start.24 = (s32[2,128,16,2]{1,3,2,0:T(2,128)S(1)}, s32[2,128,16,2]{1,3,2,0:T(2,128)}, u32[]{:S(2)}) copy-start(s32[2,128,16,2]{1,3,2,0:T(2,128)} %param.29) | copy-start | bytes 98308
  27.4 18.4 %collective-permute-start.7 = (bf16[400,768]{1,0:T(8,128)(2,1)S(1)}, bf16[400,768]{1,0:T(8,128)(2,1)S(1)}, u32[]{:S(2)}, u32[]{:S(2)}) collective-permute-start(bf16[400,768]{1,0:T(8,128)(2,1)S(1)} %bitcast.130), channel_id=1, source_target_pairs={{2,0},{3,1},{0,2},{1,3},{6,4},{7,5},{4,6},{5,7},{10,8},{11,9},{8,1... | collective-permute-start | bytes 1843208 | tf_op jit(solution)/shard_map/ppermute | solution.py:26
  30.1 27.4 %collective-permute-start.6 = (bf16[400,768]{1,0:T(8,128)(2,1)S(1)}, bf16[400,768]{1,0:T(8,128)(2,1)S(1)}, u32[]{:S(2)}, u32[]{:S(2)}) collective-permute-start(bf16[400,768]{1,0:T(8,128)(2,1)S(1)} %bitcast.131), channel_id=1, source_target_pairs={{1,0},{2,1},{3,2},{0,3},{5,4},{6,5},{7,6},{4,7},{9,8},{10,9},{11,1... | collective-permute-start | bytes 1843208 | tf_op jit(solution)/shard_map/ppermute | solution.py:26
  31.9 25.6 %collective-permute-start.8 = (bf16[400,768]{1,0:T(8,128)(2,1)S(1)}, bf16[400,768]{1,0:T(8,128)(2,1)S(1)}, u32[]{:S(2)}, u32[]{:S(2)}) collective-permute-start(bf16[400,768]{1,0:T(8,128)(2,1)S(1)} %bitcast.132), channel_id=1, source_target_pairs={{3,0},{0,1},{1,2},{2,3},{7,4},{4,5},{5,6},{6,7},{11,8},{8,9},{9,10... | collective-permute-start | bytes 1843208 | tf_op jit(solution)/shard_map/ppermute | solution.py:26
  32.1 30.7 %collective-permute-start.10 = (bf16[400]{0:T(512)(128)(2,1)S(1)}, bf16[400]{0:T(512)(128)(2,1)S(1)}, u32[]{:S(2)}, u32[]{:S(2)}) collective-permute-start(bf16[400]{0:T(512)(128)(2,1)S(1)} %copy-done.29), channel_id=1, source_target_pairs={{1,0},{2,1},{3,2},{0,3},{5,4},{6,5},{7,6},{4,7},{9,8},{10,9},{11,1... | collective-permute-start | bytes 2408 | tf_op jit(solution)/shard_map/ppermute | solution.py:26
  35.2 27.7 %collective-permute-start.12 = (bf16[400]{0:T(512)(128)(2,1)S(1)}, bf16[400]{0:T(512)(128)(2,1)S(1)}, u32[]{:S(2)}, u32[]{:S(2)}) collective-permute-start(bf16[400]{0:T(512)(128)(2,1)S(1)} %copy-done.29), channel_id=1, source_target_pairs={{3,0},{0,1},{1,2},{2,3},{7,4},{4,5},{5,6},{6,7},{11,8},{8,9},{9,10... | collective-permute-start | bytes 2408 | tf_op jit(solution)/shard_map/ppermute | solution.py:26
  45.8 11.7 %copy-start.17 = (bf16[400,768]{1,0:T(8,128)(2,1)}, bf16[400,768]{1,0:T(8,128)(2,1)S(1)}, u32[]{:S(2)}) copy-start(bf16[400,768]{1,0:T(8,128)(2,1)S(1)} %collective-permute-done.7) | copy-start | bytes 1843204
  45.8 17.1 %collective-permute-start.11 = (bf16[400]{0:T(512)(128)(2,1)S(1)}, bf16[400]{0:T(512)(128)(2,1)S(1)}, u32[]{:S(2)}, u32[]{:S(2)}) collective-permute-start(bf16[400]{0:T(512)(128)(2,1)S(1)} %copy-done.29), channel_id=1, source_target_pairs={{2,0},{3,1},{0,2},{1,3},{6,4},{7,5},{4,6},{5,7},{10,8},{11,9},{8,1... | collective-permute-start | bytes 2408 | tf_op jit(solution)/shard_map/ppermute | solution.py:26
  57.5 0.8 copy-start.21
  57.5 1.0 copy-start.19
  58.5 3.3 copy-start.22
  58.5 3.3 copy-start.23
  60.3 10.2 %collective-permute-start.9 = (bf16[4,400,768]{2,1,0:T(8,128)(2,1)}, bf16[4,400,768]{2,1,0:T(8,128)(2,1)S(1)}, u32[]{:S(2)}, u32[]{:S(2)}) collective-permute-start(bf16[4,400,768]{2,1,0:T(8,128)(2,1)} %pad_maximum_fusion.2), channel_id=1, source_target_pairs={{16,0},{0,16},{17,1},{1,17},{18,2},{2,18},{19,3},{3,19},{20,4},{4,... | collective-permute-start | bytes 7372808 | tf_op jit(solution)/shard_map/ppermute | solution.py:26
  61.9 6.9 %copy-start.18 = (bf16[400,768]{1,0:T(8,128)(2,1)S(1)}, bf16[400,768]{1,0:T(8,128)(2,1)}, u32[]{:S(2)}) copy-start(bf16[400,768]{1,0:T(8,128)(2,1)} %copy-done.17) | copy-start | bytes 1843204
  62.9 2.1 collective-permute-start.13
  65.1 4.5 %copy-start.20 = (bf16[400,768]{1,0:T(8,128)(2,1)S(1)}, bf16[400,768]{1,0:T(8,128)(2,1)}, u32[]{:S(2)}) copy-start(bf16[400,768]{1,0:T(8,128)(2,1)} %copy-done.19) | copy-start | bytes 1843204
  81.8 23.5 %copy-start.27 = (s32[2,256]{1,0:T(2,128)S(1)}, s32[2,256]{1,0:T(2,128)}, u32[]{:S(2)}) copy-start(s32[2,256]{1,0:T(2,128)} %param.27) | copy-start | bytes 6148
  81.8 24.8 %copy-start.1 = (bf16[2,256,768]{2,1,0:T(8,128)(2,1)S(1)}, bf16[2,256,768]{2,1,0:T(8,128)(2,1)}, u32[]{:S(2)}) copy-start(bf16[2,256,768]{2,1,0:T(8,128)(2,1)} %param.25) | copy-start | bytes 2359300
  100.0 40.2 %all-to-all-start = ((bf16[16,64,896]{2,1,0:T(8,128)(2,1)}), bf16[16,64,896]{2,1,0:T(8,128)(2,1)S(1)}, u32[]{:S(2)}, u32[]{:S(2)}) async-start(bf16[16,64,896]{2,1,0:T(8,128)(2,1)} %pad_maximum_fusion.3), calls=%async_computation | async-start | bytes 3670016 | tf_op jit(solution)/shard_map/all_to_all | solution.py:46
  106.6 11.0 %copy-start.8 = (f32[16,768]{1,0:T(8,128)}, f32[16,768]{1,0:T(8,128)S(1)}, u32[]{:S(2)}) copy-start(f32[16,768]{1,0:T(8,128)S(1)} %copy.132.vec_ref.refs_8_) | copy-start | bytes 147460
  117.7 0.9 copy-start
  118.5 1.2 copy-start.6
  119.7 1.1 copy-start.7
  120.9 0.9 copy-start.9
  121.8 0.7 copy-start.10
  140.2 56.8 %copy-start.12 = (bf16[16,64,896]{2,1,0:T(8,128)(2,1)}, bf16[16,64,896]{2,1,0:T(8,128)(2,1)S(1)}, u32[]{:S(2)}) copy-start(bf16[16,64,896]{2,1,0:T(8,128)(2,1)S(1)} %all-to-all-done) | copy-start | bytes 5505028
  140.2 31.5 %all-to-all-start.1 = ((bf16[16,64,768]{2,1,0:T(8,128)(2,1)}), bf16[16,64,768]{2,1,0:T(8,128)(2,1)}, u32[]{:S(2)}, u32[]{:S(2)}) async-start(bf16[16,64,768]{2,1,0:T(8,128)(2,1)} %get-tuple-element.103), calls=%async_computation.1 | async-start | bytes 3145728 | tf_op jit(solution)/shard_map/all_to_all | solution.py:46
  197.0 6.8 %copy-start.25 = (f32[64,1]{1,0:T(8,128)S(1)}, f32[64,1]{1,0:T(8,128)}, u32[]{:S(2)}) copy-start(f32[64,1]{1,0:T(8,128)} %get-tuple-element.112) | copy-start | bytes 772
  197.0 30.5 %all-to-all-start.2 = ((bf16[16,80,768]{2,1,0:T(8,128)(2,1)}), bf16[16,80,768]{2,1,0:T(8,128)(2,1)S(1)}, u32[]{:S(2)}, u32[]{:S(2)}) async-start(bf16[16,80,768]{2,1,0:T(8,128)(2,1)} %get-tuple-element.109), calls=%async_computation.2 | async-start | bytes 3932160 | tf_op jit(solution)/shard_map/all_to_all | solution.py:46
  227.5 1.3 copy-start.11
  243.5 9.8 %collective-permute-start.14 = (bf16[16,128,768]{2,1,0:T(8,128)(2,1)}, bf16[16,128,768]{2,1,0:T(8,128)(2,1)S(1)}, u32[]{:S(2)}, u32[]{:S(2)}) collective-permute-start(bf16[16,128,768]{2,1,0:T(8,128)(2,1)} %get-tuple-element.131), channel_id=1, source_target_pairs={{0,16},{16,0},{1,17},{17,1},{2,18},{18,2},{3,19},{19,3},{4,20},{20... | collective-permute-start | bytes 9437192 | tf_op jit(solution)/shard_map/ppermute | solution.py:31
  243.5 9.8 %copy-start.14 = (bf16[16,128,768]{2,1,0:T(8,128)(2,1)S(1)}, bf16[16,128,768]{2,1,0:T(8,128)(2,1)}, u32[]{:S(2)}) copy-start(bf16[16,128,768]{2,1,0:T(8,128)(2,1)} %get-tuple-element.130) | copy-start | bytes 9437188
  256.0 47.8 %all-to-all-start.3 = ((bf16[16,128,768]{2,1,0:T(8,128)(2,1)}), bf16[16,128,768]{2,1,0:T(8,128)(2,1)S(1)}, u32[]{:S(2)}, u32[]{:S(2)}) async-start(bf16[16,128,768]{2,1,0:T(8,128)(2,1)} %add_convert_fusion), calls=%async_computation.3 | async-start | bytes 6291456 | tf_op jit(solution)/shard_map/all_to_all | solution.py:46
  259.7 12.4 %copy-start.26 = (f32[8,768]{1,0:T(8,128)S(1)}, f32[8,768]{1,0:T(8,128)}, u32[]{:S(2)}) copy-start(f32[8,768]{1,0:T(8,128)} %get-tuple-element.146) | copy-start | bytes 73732
  259.8 12.4 %copy-start.5 = (bf16[512,2304]{1,0:T(8,128)(2,1)S(1)}, bf16[512,2304]{1,0:T(8,128)(2,1)}, u32[]{:S(2)}) copy-start(bf16[512,2304]{1,0:T(8,128)(2,1)} %get-tuple-element.140.qkv_ref) | copy-start | bytes 7077892
  271.3 32.4 %collective-permute-start.15 = (bf16[16,24,3072]{2,1,0:T(8,128)(2,1)}, bf16[16,24,3072]{2,1,0:T(8,128)(2,1)}, u32[]{:S(2)}, u32[]{:S(2)}) collective-permute-start(bf16[16,24,3072]{2,1,0:T(8,128)(2,1)} %get-tuple-element.138), channel_id=1, source_target_pairs={{0,16},{16,0},{1,17},{17,1},{2,18},{18,2},{3,19},{19,3},{4,20},{20... | collective-permute-start | bytes 7077896 | tf_op jit(solution)/shard_map/ppermute | solution.py:31
  272.1 1.1 copy-start.2
  285.3 1.4 copy-start.3
  303.7 35.8 %collective-permute-start.16 = (bf16[16,24,3200]{2,1,0:T(8,128)(2,1)}, bf16[16,24,3200]{2,1,0:T(8,128)(2,1)}, u32[]{:S(2)}, u32[]{:S(2)}) collective-permute-start(bf16[16,24,3200]{2,1,0:T(8,128)(2,1)} %get-tuple-element.157), channel_id=1, source_target_pairs={{0,16},{16,0},{1,17},{17,1},{2,18},{18,2},{3,19},{19,3},{4,20},{20... | collective-permute-start | bytes 7372808 | tf_op jit(solution)/shard_map/ppermute | solution.py:31
  308.4 43.6 %all-to-all-start.4 = ((bf16[16,24,3072]{2,1,0:T(8,128)(2,1)}), bf16[16,24,3072]{2,1,0:T(8,128)(2,1)}, u32[]{:S(2)}, u32[]{:S(2)}) async-start(bf16[16,24,3072]{2,1,0:T(8,128)(2,1)} %add_convert_fusion.3), calls=%async_computation.4 | async-start | bytes 4718592 | tf_op jit(solution)/shard_map/all_to_all | solution.py:46
  337.0 3.0 copy-start.15
  352.0 8.6 %collective-permute-start.17 = (bf16[4,408,768]{2,1,0:T(8,128)(2,1)}, bf16[4,408,768]{2,1,0:T(8,128)(2,1)}, u32[]{:S(2)}, u32[]{:S(2)}) collective-permute-start(bf16[4,408,768]{2,1,0:T(8,128)(2,1)} %get-tuple-element.159), channel_id=1, source_target_pairs={{0,16},{16,0},{1,17},{17,1},{2,18},{18,2},{3,19},{19,3},{4,20},{20... | collective-permute-start | bytes 7520264 | tf_op jit(solution)/shard_map/ppermute | solution.py:31
  352.2 52.1 %all-to-all-start.5 = ((bf16[16,24,3200]{2,1,0:T(8,128)(2,1)}), bf16[16,24,3200]{2,1,0:T(8,128)(2,1)}, u32[]{:S(2)}, u32[]{:S(2)}) async-start(bf16[16,24,3200]{2,1,0:T(8,128)(2,1)} %add_convert_fusion.2), calls=%async_computation.5 | async-start | bytes 4915200 | tf_op jit(solution)/shard_map/all_to_all | solution.py:46
  371.1 17.5 %collective-permute-start.18 = (bf16[408,768]{1,0:T(8,128)(2,1)S(1)}, bf16[408,768]{1,0:T(8,128)(2,1)S(1)}, u32[]{:S(2)}, u32[]{:S(2)}) collective-permute-start(bf16[408,768]{1,0:T(8,128)(2,1)S(1)} %get-tuple-element.183), channel_id=1, source_target_pairs={{0,1},{1,2},{2,3},{3,0},{4,5},{5,6},{6,7},{7,4},{8,9},{9,10},{10,1... | collective-permute-start | bytes 1880072 | tf_op jit(solution)/shard_map/ppermute | solution.py:31
  372.6 28.7 %collective-permute-start.20 = (bf16[408,768]{1,0:T(8,128)(2,1)S(1)}, bf16[408,768]{1,0:T(8,128)(2,1)S(1)}, u32[]{:S(2)}, u32[]{:S(2)}) collective-permute-start(bf16[408,768]{1,0:T(8,128)(2,1)S(1)} %get-tuple-element.184), channel_id=1, source_target_pairs={{0,3},{1,0},{2,1},{3,2},{4,7},{5,4},{6,5},{7,6},{8,11},{9,8},{10,9... | collective-permute-start | bytes 1880072 | tf_op jit(solution)/shard_map/ppermute | solution.py:31
  374.4 28.6 %collective-permute-start.19 = (bf16[408,768]{1,0:T(8,128)(2,1)S(1)}, bf16[408,768]{1,0:T(8,128)(2,1)S(1)}, u32[]{:S(2)}, u32[]{:S(2)}) collective-permute-start(bf16[408,768]{1,0:T(8,128)(2,1)S(1)} %get-tuple-element.185), channel_id=1, source_target_pairs={{0,2},{1,3},{2,0},{3,1},{4,6},{5,7},{6,4},{7,5},{8,10},{9,11},{10,... | collective-permute-start | bytes 1880072 | tf_op jit(solution)/shard_map/ppermute | solution.py:31
  404.3 6.5 %copy-start.4 = (bf16[512,2304]{1,0:T(8,128)(2,1)S(1)}, bf16[512,2304]{1,0:T(8,128)(2,1)}, u32[]{:S(2)}) copy-start(bf16[512,2304]{1,0:T(8,128)(2,1)} %copy-done.3) | copy-start | bytes 7077892
  407.3 14.2 %all-to-all-start.6 = ((bf16[4,6,10240]{2,1,0:T(8,128)(2,1)}), bf16[4,6,10240]{2,1,0:T(8,128)(2,1)S(1)}, u32[]{:S(2)}, u32[]{:S(2)}) async-start(bf16[4,6,10240]{2,1,0:T(8,128)(2,1)} %constant_dynamic-update-slice_fusion.18), calls=%async_computation.6 | async-start | bytes 1310720 | tf_op jit(solution)/shard_map/all_to_all | solution.py:46
  410.8 5.8 %copy-start.13 = (f32[408,768]{1,0:T(8,128)S(1)}, f32[408,768]{1,0:T(8,128)}, u32[]{:S(2)}) copy-start(f32[408,768]{1,0:T(8,128)} %fusion.13) | copy-start | bytes 3760132
Sparse Core Ops, SparseCore 0:
  27.5 72.4 all-gather.1

commit v10 on v9

--- a/solution.py
+++ b/solution.py
@@ -239,7 +239,7 @@
             jax.ShapeDtypeStruct((tokens, width), F32),
             jax.ShapeDtypeStruct((tokens, 1), F32),
         ],
-        compiler_params=pltpu.CompilerParams(vmem_limit_bytes=48 * 1024 * 1024),
+        compiler_params=pltpu.CompilerParams(vmem_limit_bytes=36 * 1024 * 1024),
         cost_estimate=pl.CostEstimate(
             flops=1000, bytes_accessed=1000, transcendentals=0
         ),
@@ -302,21 +302,21 @@
             jax.ShapeDtypeStruct((tokens, 3 * width), BF),
             jax.ShapeDtypeStruct((1, 3 * width), F32),
         ],
-        compiler_params=pltpu.CompilerParams(vmem_limit_bytes=48 * 1024 * 1024),
+        compiler_params=pltpu.CompilerParams(vmem_limit_bytes=36 * 1024 * 1024),
         cost_estimate=pl.CostEstimate(
             flops=1000, bytes_accessed=1000, transcendentals=0
         ),
     )(dbranch, qkv, probs, layer)
 
 
-LIMIT = 56 * 1024 * 1024
+LIMIT = 40 * 1024 * 1024
 
 
 def whole_spec(array):
     return pl.BlockSpec(array.shape, lambda *_: (0,) * len(array.shape))
 
 
-def call(kernel, grid, ins, in_specs, outs, out_specs, scratch, flops, size):
+def call(kernel, grid, ins, in_specs, outs, out_specs, scratch, flops, size, limit=LIMIT):
     return pl.pallas_call(
         kernel,
         grid=grid,
@@ -324,7 +324,7 @@
         out_specs=out_specs,
         out_shape=[jax.ShapeDtypeStruct(shape, kind) for shape, kind in outs],
         scratch_shapes=scratch,
-        compiler_params=pltpu.CompilerParams(vmem_limit_bytes=LIMIT),
+        compiler_params=pltpu.CompilerParams(vmem_limit_bytes=limit),
         cost_estimate=pl.CostEstimate(flops=flops, bytes_accessed=size, transcendentals=0),
     )(*ins)
 
@@ -404,6 +404,7 @@
         [pltpu.VMEM((2, 8, block), F32), pltpu.VMEM((block, entries), F32)],
         10_000_000_000,
         20_000_000,
+        56 * 1024 * 1024,
     )
 
 
@@ -685,10 +686,44 @@
 
 
 def last_kernel(
-    core_ref, x_ref, dfused_ref, attended_ref, dbranch_ref, sums_ref, here_ref, away_ref, grad_ref
+    core_ref,
+    x_ref,
+    dfused_ref,
+    attended_ref,
+    dbranch_ref,
+    fused_ref,
+    low_ref,
+    high_ref,
+    bias_ref,
+    here_ref,
+    away_ref,
+    grad_ref,
+    sums_ref,
+    flat_ref,
 ):
     width = x_ref.shape[1]
     core = core_ref[0]
+    flat_ref[...] = jnp.zeros(flat_ref.shape, F32)
+    rows = [
+        fused_ref[:, :width],
+        fused_ref[:, 2 * width :],
+        high_ref[2:3],
+        high_ref[0:1],
+        high_ref[1:2],
+        low_ref[5:6],
+        low_ref[3:4],
+        low_ref[4:5],
+        low_ref[0:1],
+        low_ref[1:2],
+        low_ref[2:3],
+    ]
+    for i, row in enumerate(rows):
+        flat_ref[i : i + 1] = row
+    sums = flat_ref[...].T
+    lane = lax.broadcasted_iota(jnp.int32, sums.shape, 1)
+    for i in range(4):
+        sums = jnp.where(lane == len(rows) + i, bias_ref[:, i : i + 1], sums)
+    sums_ref[...] = sums
     for i in range(4):
         lanes = slice(i * width, (i + 1) * width)
         if i < 3:
@@ -699,10 +734,9 @@
     put_wide(sums_ref, core, here_ref, away_ref, slice(4 * width, 4 * width + 128))
 
 
-def last_call(core, x, dfused, attended, dbranch, sums):
-    width = x.shape[1]
+def last_call(core, *ins):
+    width = ins[0].shape[1]
     out = ((NY * NZ, 24, 4 * width + 128), BF)
-    ins = (x, dfused, attended, dbranch, sums)
     half_spec = pl.BlockSpec(out[0], lambda *_: (0, 0, 0))
     return call(
         last_kernel,
@@ -711,7 +745,11 @@
         [pl.BlockSpec(memory_space=pltpu.SMEM)] + [whole_spec(a) for a in ins],
         [out, out],
         [half_spec, half_spec],
-        [pltpu.VMEM((2, width, width), F32)],
+        [
+            pltpu.VMEM((2, width, width), F32),
+            pltpu.VMEM((width, 128), F32),
+            pltpu.VMEM((128, width), F32),
+        ],
         1000,
         1000,
     )
@@ -1034,24 +1072,17 @@
     tall_all = swap(tall_mine, ("y", "z"))
     dfused, fused_sum = attention_backward(dbranch, qkv, probs, layer, attn_block)
 
-    sums = jnp.stack(
-        [
-            fused_sum[0, :width],
-            fused_sum[0, 2 * width :],
-            sums_b[2],
-            sums_b[0],
-            sums_b[1],
-            sums_a[5],
-            sums_a[3],
-            sums_a[4],
-            sums_a[0],
-            sums_a[1],
-            sums_a[2],
-        ]
-    )
-    sums = jnp.concatenate([after(sums)[0].T, g_expand_bias.reshape(width, -1)], axis=1)
-    sums = jnp.pad(sums, ((0, 0), (0, 128 - sums.shape[1])))
-    last_here, last_away = last_call(core, x, dfused, attended, dbranch, sums)
+    last_here, last_away = last_call(
+        core,
+        x,
+        dfused,
+        attended,
+        dbranch,
+        fused_sum,
+        sums_a,
+        sums_b,
+        g_expand_bias.reshape(width, -1),
+    )
     last_away, tall_all = after(last_away, tall_all)
     last_pair = (last_here, give(last_away, "c", 1))
     wide_mine, tall_all = after(add_cores(wide_pair), tall_all)

time: 441 us -> 450 us (1.020)
  local copies, waits for them, and re-layouts: 50.1 us -> 78.1 us
  Pallas kernels: 123 us -> 102 us
    unnamed x89 -> x175, local copies, waits for them, and re-layouts: 22.3 us -> 54.8 us
    pallas_call x6, Pallas kernels: 78.5 us -> 63.8 us  [call(): pl.pallas_call(kernel, grid=grid, in_specs=in_specs, out_specs=out_specs,...]
  transfers between devices with their start and end apart: 29 -> 29, of which waited for: 13 -> 13; matrix products, arithmetic and copies ran while one was open for 19% -> 17% of each run, Pallas kernels for 19% -> 15%
where the time goes in v10:
time: 450 us; the launch traced here: 442 us
  waiting for transfers between devices  120 us (27%)
  Pallas kernels  102 us (23%)
  local copies, waits for them, and re-layouts  78.1 us (17%)
  starting transfers between devices  70 us (16%)
  other arithmetic  36.7 us (8%)
  between operations  21.4 us (5%)
  matrix products  13.9 us (3%)
    pallas_call x6, Pallas kernels, call(): pl.pallas_call(kernel, grid=grid, in_specs=in_specs, out_specs=out_specs,...  63.8 us
    all_to_all x7, waiting for transfers between devices, swap(): return lax.all_to_all(array, axes, 0, 0, tiled=True)  59.1 us
    unnamed x175, local copies, waits for them, and re-layouts  54.8 us
    all_to_all x7, starting transfers between devices, swap(): return lax.all_to_all(array, axes, 0, 0, tiled=True)  43.1 us
    ppermute x7, waiting for transfers between devices, give(): return lax.ppermute(array, axis, [(i, (i + k) % n) for i in range(n)])  24.2 us
    ppermute x14, starting transfers between devices, fetch(): return lax.ppermute(array, axis, [((i + k) % n, i) for i in range(n)])  21 us
    ppermute x14, waiting for transfers between devices, fetch(): return lax.ppermute(array, axis, [((i + k) % n, i) for i in range(n)])  18.5 us
    all_gather x1, waiting for transfers between devices, body(): lax.all_gather(jnp.concatenate([tall, fused], axis=1), ('y', 'c', 'z'), a...  18.1 us
  transfers between devices with their start and end apart: 29, of which 13 were waited for; matrix products, arithmetic and copies ran while one was open for 17% of the time, Pallas kernels for 15%

profile of v10, /device:TPU:0, one launch (start us, length us, event | category | flops | bytes accessed | tf_op | source)
XLA Modules:
  0.0 442.4 jit_solution(13119318935086164818)
XLA Ops:
  7.2 2.9 collective-permute-start
  10.2 2.3 collective-permute-start.1
  13.3 1.5 stack.172
  17.9 1.8 collective-permute-start.5
  21.3 2.0 collective-permute-start.3
  24.2 2.0 collective-permute-done.3
  27.3 2.7 collective-permute-start.7
  30.1 1.9 collective-permute-start.6
  32.1 3.1 collective-permute-start.10
  39.7 6.1 %collective-permute-done.7 = bf16[400,768]{1,0:T(8,128)(2,1)S(1)} collective-permute-done((bf16[400,768]{1,0:T(8,128)(2,1)S(1)}, bf16[400,768]{1,0:T(8,128)(2,1)S(1)}, u32[]{:S(2)}, u32[]{:S(2)}) %collective-permute-start.7) | collective-permute-done | bytes 614432 | tf_op jit(solution)/shard_map/ppermute | solution.py:26
  45.8 2.6 collective-permute-start.11
  48.4 9.1 %collective-permute-done.6 = bf16[400,768]{1,0:T(8,128)(2,1)S(1)} collective-permute-done((bf16[400,768]{1,0:T(8,128)(2,1)S(1)}, bf16[400,768]{1,0:T(8,128)(2,1)S(1)}, u32[]{:S(2)}, u32[]{:S(2)}) %collective-permute-start.6) | collective-permute-done | bytes 614432 | tf_op jit(solution)/shard_map/ppermute | solution.py:26
  58.5 1.7 pad_maximum_fusion.2
  66.8 1.9 constant_dynamic-update-slice_fusion.16
  70.5 1.6 constant_dynamic-update-slice_fusion.13
  72.1 8.2 %fusion.6 = bf16[16,64,768]{2,1,0:T(8,128)(2,1)S(1)} fusion(bf16[3200,768,1]{1,0,2:T(8,128)(2,1)} %bitcast.141, s32[3200]{0:T(1024)S(1)} %add.228, s32[16,64]{1,0:T(8,128)S(1)} %reshape.263), kind=kOutput, calls=%fused_computation.17 | convolution fusion | flops 5037228032 | bytes 6504960 | tf_op jit(solution)/shard_map/dot_general | solution.py:130
  80.3 1.6 pad_maximum_fusion.3
  81.9 18.1 %all-gather.2.cloned.1.call-done.wq_ref.wk_ref.wv_ref.wa_ref.expand_ref.tall_ref.dense_ref.refs_4_ = bf16[768,10112]{1,0:T(8,128)(2,1)} async-done(((bf16[24,10112]{1,0:T(8,128)(2,1)}), bf16[768,10112]{1,0:T(8,128)(2,1)}) %all-gather.2.cloned.1.call-update) | async-done | bytes 15532048 | tf_op jit(solution)/shard_map/all_gather | solution.py:930
  99.9 5.4 %all-to-all-start = ((bf16[16,64,896]{2,1,0:T(8,128)(2,1)}), bf16[16,64,896]{2,1,0:T(8,128)(2,1)}, u32[]{:S(2)}, u32[]{:S(2)}) async-start(bf16[16,64,896]{2,1,0:T(8,128)(2,1)} %pad_maximum_fusion.3), calls=%async_computation | async-start | bytes 3670016 | tf_op jit(solution)/shard_map/all_to_all | solution.py:46
  106.7 9.7 %shard_map.408 = (bf16[512,2304]{1,0:T(8,128)(2,1)S(1)}, bf16[2,12,256,256]{3,2,1,0:T(8,128)(2,1)S(1)}, bf16[512,768]{1,0:T(8,128)(2,1)S(1)}, f32[512,768]{1,0:T...) custom-call(bf16[512,768]{1,0:T(8,128)(2,1)S(1)} %bitcast.122, ...), custom_call_target="tpu_custom_call" | custom-call | flops 1000 | bytes 1000 | tf_op jit(solution)/shard_map/pallas_call | solution.py:211
  117.2 1.6 copy-done.14
  118.9 1.4 copy-done.23
  128.1 12.9 %shard_map.409 = (bf16[512,3072]{1,0:T(8,128)(2,1)S(1)}, bf16[512,3072]{1,0:T(8,128)(2,1)S(1)}, bf16[3072,768]{1,0:T(8,128)(2,1)}, bf16[512,768]{1,0:T(8,128)(2,...) custom-call(bf16[512,768]{1,0:T(8,128)(2,1)S(1)} %copy-done.6, ...), custom_call_target="tpu_custom_call" | custom-call | flops 1000 | bytes 1000 | tf_op jit(solution)/shard_map/pallas_call | solution.py:320
  141.0 1.7 copy-done.12
  147.6 7.8 %all-to-all-start.1 = ((bf16[16,64,768]{2,1,0:T(8,128)(2,1)}), bf16[16,64,768]{2,1,0:T(8,128)(2,1)}, u32[]{:S(2)}, u32[]{:S(2)}) async-start(bf16[16,64,768]{2,1,0:T(8,128)(2,1)} %copy-done.33), calls=%async_computation.1 | async-start | bytes 3145728 | tf_op jit(solution)/shard_map/all_to_all | solution.py:46
  157.9 21.2 %all-to-all-done.1 = bf16[16,64,768]{2,1,0:T(8,128)(2,1)} async-done(((bf16[16,64,768]{2,1,0:T(8,128)(2,1)}), bf16[16,64,768]{2,1,0:T(8,128)(2,1)}, u32[]{:S(2)}, u32[]{:S(2)}) %all-to-all-start.1) | async-done | bytes 1572896 | tf_op jit(solution)/shard_map/all_to_all | solution.py:46
  179.1 25.3 %shard_map.410 = (bf16[1024,3200]{1,0:T(8,128)(2,1)}, f32[1024,128]{1,0:T(8,128)}, bf16[16,80,768]{2,1,0:T(8,128)(2,1)}) custom-call(bf16[1024,768]{1,0:T(8,128)(2,1)} %bitcast.45.spread_ref, bf16[3200,768]{1,0:T(8,128)(2,1)} %bitcast.142, f32[1,3200]{1,0:T(1,128)} %reshape.260.b_ref, s32[1,3200]{1,0:T(1,128)} %add.232.column_ref, s32[1024,1]{1,0:T(8,128)} %copy.118.label_ref), custom_call_target="tpu_custom_call" | custom-call | flops 10000000000 | bytes 20000000 | tf_op jit(solution)/shard_map/pallas_call | solution.py:320
  204.4 4.6 %all-to-all-start.2 = ((bf16[16,80,768]{2,1,0:T(8,128)(2,1)}), bf16[16,80,768]{2,1,0:T(8,128)(2,1)}, u32[]{:S(2)}, u32[]{:S(2)}) async-start(bf16[16,80,768]{2,1,0:T(8,128)(2,1)} %get-tuple-element.109), calls=%async_computation.2 | async-start | bytes 3932160 | tf_op jit(solution)/shard_map/all_to_all | solution.py:46
  210.0 1.8 convert_reduce_fusion
  211.9 22.9 %all-to-all-done.2.part_ref = bf16[16,80,768]{2,1,0:T(8,128)(2,1)} async-done(((bf16[16,80,768]{2,1,0:T(8,128)(2,1)}), bf16[16,80,768]{2,1,0:T(8,128)(2,1)}, u32[]{:S(2)}, u32[]{:S(2)}) %all-to-all-start.2) | async-done | bytes 1966112 | tf_op jit(solution)/shard_map/all_to_all | solution.py:46
  242.0 4.9 %shard_map.411 = (f32[1,1024]{1,0:T(1,128)S(1)}, f32[8,128]{1,0:T(8,128)S(1)}, f32[768,768]{1,0:T(8,128)S(1)}, f32[512,768]{1,0:T(8,128)S(1)}, bf16[512,768]{1,0:T(8,128)(2,1)S(1)}, /*index=5*/f32[8,768]{1,0:T(8,128)S(1)}) custom-call(s32[1]{0:T(128)} %bitcast.46.own_ref, bf16[16,80,768]{2,1,0:T(8,128)(2,1)} %all-to-all-done.2.part_ref, ...), custom_call_target="tpu_custom_call" | custom-call | flops 300000000 | bytes 10000000 | tf_op jit(solution)/shard_map/pallas_call | solution.py:320
  247.4 4.0 shard_map.412
  251.6 7.9 %shard_map.413 = (bf16[16,24,3072]{2,1,0:T(8,128)(2,1)S(1)}, bf16[16,24,3072]{2,1,0:T(8,128)(2,1)}, f32[1,1536]{1,0:T(1,128)S(1)}, f32[512,768]{1,0:T(8,128)S(1)}) custom-call(s32[1]{0:T(128)} %bitcast.50.core_ref, bf16[512,768]{1,0:T(8,128)(2,1)S(1)} %get-tuple-element.125.dffn_ref.refs_0_, bf16[3072,768]{1,0:T(8,128)(2,1)} %get-tuple-element.126.refs_1_, ...), custom_call_target="tpu_custom_call" | custom-call | flops 1000 | bytes 1000 | tf_op jit(solution)/shard_map/pallas_call | solution.py:674
  259.5 2.9 add_convert_fusion
  262.4 4.9 %all-to-all-start.3 = ((bf16[16,128,768]{2,1,0:T(8,128)(2,1)}), bf16[16,128,768]{2,1,0:T(8,128)(2,1)}, u32[]{:S(2)}, u32[]{:S(2)}) async-start(bf16[16,128,768]{2,1,0:T(8,128)(2,1)} %add_convert_fusion), calls=%async_computation.3 | async-start | bytes 6291456 | tf_op jit(solution)/shard_map/all_to_all | solution.py:46
  271.3 9.2 %shard_map.414 = (bf16[16,24,3072]{2,1,0:T(8,128)(2,1)S(1)}, bf16[16,24,3072]{2,1,0:T(8,128)(2,1)}, f32[1,1536]{1,0:T(1,128)S(1)}, f32[512,768]{1,0:T(8,128)S(1)...) custom-call(s32[1]{0:T(128)} %bitcast.50.core_ref, ...), custom_call_target="tpu_custom_call", output_to_operand_aliasing={{0}: (10, {}), {1}: (11, {})} | custom-call | flops 1000 | bytes 1000 | tf_op jit(solution)/shard_map/pallas_call | solution.py:674
  281.1 11.7 %shard_map.415 = (bf16[512,2304]{1,0:T(8,128)(2,1)S(1)}, f32[1,2304]{1,0:T(1,128)S(1)}) custom-call(bf16[512,768]{1,0:T(8,128)(2,1)S(1)} %get-tuple-element.139.dbranch_ref, bf16[512,2304]{1,0:T(8,128)(2,1)S(1)} %copy-done.24, bf16[2,12,256,256]{3,2,1,0:T(8,128)(2,1)S(1)} %copy-done.15, ...), custom_call_target="tpu_custom_call" | custom-call | flops 1000 | bytes 1000 | tf_op jit(solution)/shard_map/pallas_call | solution.py:291
  297.2 1.7 copy-done.21
  301.4 3.1 shard_map.416
  304.6 1.4 copy-done.18
  306.0 1.5 copy-done.57
  307.5 3.4 all-to-all-done.3
  310.9 4.0 add_convert_fusion.3
  314.9 10.7 %all-to-all-start.4 = ((bf16[16,24,3072]{2,1,0:T(8,128)(2,1)}), bf16[16,24,3072]{2,1,0:T(8,128)(2,1)}, u32[]{:S(2)}, u32[]{:S(2)}) async-start(bf16[16,24,3072]{2,1,0:T(8,128)(2,1)} %add_convert_fusion.3), calls=%async_computation.4 | async-start | bytes 4718592 | tf_op jit(solution)/shard_map/all_to_all | solution.py:46
  325.6 13.6 %shard_map.417 = (bf16[3200,768]{1,0:T(8,128)(2,1)S(1)}, f32[1,3200]{1,0:T(1,128)S(1)}) custom-call(bf16[1024,3200]{1,0:T(8,128)(2,1)} %get-tuple-element.106.expl_ref, bf16[1024,768]{1,0:T(8,128)(2,1)} %bitcast.45.spread_ref, s32[1,3200]{1,0:T(1,128)S(1)} %copy-done.52, s32[1024,1]{1,0:T(8,128)S(1)} %copy-done.26, f32[1024,1]{1,0:T(8,128)S(1)} %copy-done.25, ...), custom_call_target="tpu_custom_call" | custom-call | flops 1000 | bytes 1000 | tf_op jit(solution)/shard_map/pallas_call | solution.py:320
  339.3 2.3 copy-done.9
  341.7 2.8 fusion.23
  344.5 1.7 pad_maximum_fusion
  347.1 3.8 add_convert_fusion.2
  350.9 8.3 %all-to-all-done.4 = bf16[16,24,3072]{2,1,0:T(8,128)(2,1)} async-done(((bf16[16,24,3072]{2,1,0:T(8,128)(2,1)}), bf16[16,24,3072]{2,1,0:T(8,128)(2,1)}, u32[]{:S(2)}, u32[]{:S(2)}) %all-to-all-start.4) | async-done | bytes 2359328 | tf_op jit(solution)/shard_map/all_to_all | solution.py:46
  359.2 6.2 %all-to-all-start.5 = ((bf16[16,24,3200]{2,1,0:T(8,128)(2,1)}), bf16[16,24,3200]{2,1,0:T(8,128)(2,1)}, u32[]{:S(2)}, u32[]{:S(2)}) async-start(bf16[16,24,3200]{2,1,0:T(8,128)(2,1)} %add_convert_fusion.2), calls=%async_computation.5 | async-start | bytes 4915200 | tf_op jit(solution)/shard_map/all_to_all | solution.py:46
  365.4 2.1 reduce_sum.95
  373.9 2.2 slice_reduce_fusion
  377.5 2.3 add_convert_fusion.1
  379.9 1.5 collective-permute-start.18
  381.5 1.8 collective-permute-start.20
  383.2 1.8 collective-permute-start.19
  387.6 9.8 %collective-permute-done.18 = bf16[408,768]{1,0:T(8,128)(2,1)S(1)} collective-permute-done((bf16[408,768]{1,0:T(8,128)(2,1)S(1)}, bf16[408,768]{1,0:T(8,128)(2,1)S(1)}, u32[]{:S(2)}, u32[]{:S(2)}) %collective-permute-start.18) | collective-permute-done | bytes 626720 | tf_op jit(solution)/shard_map/ppermute | solution.py:31
  397.5 12.7 %collective-permute-done.20 = bf16[408,768]{1,0:T(8,128)(2,1)S(1)} collective-permute-done((bf16[408,768]{1,0:T(8,128)(2,1)S(1)}, bf16[408,768]{1,0:T(8,128)(2,1)S(1)}, u32[]{:S(2)}, u32[]{:S(2)}) %collective-permute-start.20) | collective-permute-done | bytes 626720 | tf_op jit(solution)/shard_map/ppermute | solution.py:31
  410.2 1.6 collective-permute-done.19
  413.2 2.2 reduce_sum.96
  416.1 3.5 all-to-all-start.6
  419.7 5.7 %fusion.9 = f32[512,768]{1,0:T(8,128)} fusion(f32[512,768]{1,0:T(8,128)} %copy-done.58, bf16[512,2304]{1,0:T(8,128)(2,1)S(1)} %copy-done.22, bf16[768,10112]{1,0:T(8,128)(2,1)} %all-gather.2.cloned.1.call-done.wq_ref.wk_ref.wv_ref.wa_ref.expand_ref.tall_ref.dense_ref.refs_4_), kind=kOutput, calls=%fused_computation.18 | convolution fusion | flops 1812332544 | bytes 9043968 | tf_op jit(solution)/shard_map/dot_general | solution.py:138
  427.1 3.2 all-to-all-done.6
  (282 shorter events, 73.2 us)
Async XLA Ops:
  7.2 92.8 %all-gather.2.cloned.1.call-start = ((), (), s32[]{:S(2)}) async-start(), calls=%async_computation.7 | async-start | bytes 16017408 | tf_op jit(solution)/shard_map/all_gather | solution.py:930
  7.2 14.1 %collective-permute-start = (bf16[24,768]{1,0:T(8,128)(2,1)}, bf16[24,768]{1,0:T(8,128)(2,1)S(1)}, u32[]{:S(2)}, u32[]{:S(2)}) collective-permute-start(bf16[24,768]{1,0:T(8,128)(2,1)} %param.40), channel_id=1, source_target_pairs={{1,0},{2,1},{3,2},{0,3},{5,4},{6,5},{7,6},{4,7},{9,8},{10,9},{11,1... | collective-permute-start | bytes 110600 | tf_op jit(solution)/shard_map/ppermute | solution.py:26
  10.1 13.1 %collective-permute-start.2 = (bf16[24,768]{1,0:T(8,128)(2,1)}, bf16[24,768]{1,0:T(8,128)(2,1)S(1)}, u32[]{:S(2)}, u32[]{:S(2)}) collective-permute-start(bf16[24,768]{1,0:T(8,128)(2,1)} %param.40), channel_id=1, source_target_pairs={{3,0},{0,1},{1,2},{2,3},{7,4},{4,5},{5,6},{6,7},{11,8},{8,9},{9,10... | collective-permute-start | bytes 110600 | tf_op jit(solution)/shard_map/ppermute | solution.py:26
  10.2 13.1 %collective-permute-start.1 = (bf16[24,768]{1,0:T(8,128)(2,1)}, bf16[24,768]{1,0:T(8,128)(2,1)S(1)}, u32[]{:S(2)}, u32[]{:S(2)}) collective-permute-start(bf16[24,768]{1,0:T(8,128)(2,1)} %param.40), channel_id=1, source_target_pairs={{2,0},{3,1},{0,2},{1,3},{6,4},{7,5},{4,6},{5,7},{10,8},{11,9},{8,1... | collective-permute-start | bytes 110600 | tf_op jit(solution)/shard_map/ppermute | solution.py:26
  17.9 8.3 %collective-permute-start.5 = (bf16[6,7040]{1,0:T(8,128)(2,1)S(1)}, bf16[6,7040]{1,0:T(8,128)(2,1)S(1)}, u32[]{:S(2)}, u32[]{:S(2)}) collective-permute-start(bf16[6,7040]{1,0:T(8,128)(2,1)S(1)} %constant_dynamic-update-slice_fusion.8), channel_id=1, source_target_pairs={{3,0},{0,1},{1,2},{2,3},{7,4},{4,5},{5,6},{6,7},{11,8},{8,9},{9,10... | collective-permute-start | bytes 253448 | tf_op jit(solution)/shard_map/ppermute | solution.py:26
  19.7 6.5 %collective-permute-start.4 = (bf16[6,7040]{1,0:T(8,128)(2,1)S(1)}, bf16[6,7040]{1,0:T(8,128)(2,1)S(1)}, u32[]{:S(2)}, u32[]{:S(2)}) collective-permute-start(bf16[6,7040]{1,0:T(8,128)(2,1)S(1)} %constant_dynamic-update-slice_fusion.8), channel_id=1, source_target_pairs={{2,0},{3,1},{0,2},{1,3},{6,4},{7,5},{4,6},{5,7},{10,8},{11,9},{8,1... | collective-permute-start | bytes 253448 | tf_op jit(solution)/shard_map/ppermute | solution.py:26
  21.3 4.9 %collective-permute-start.3 = (bf16[6,7040]{1,0:T(8,128)(2,1)S(1)}, bf16[6,7040]{1,0:T(8,128)(2,1)S(1)}, u32[]{:S(2)}, u32[]{:S(2)}) collective-permute-start(bf16[6,7040]{1,0:T(8,128)(2,1)S(1)} %constant_dynamic-update-slice_fusion.8), channel_id=1, source_target_pairs={{1,0},{2,1},{3,2},{0,3},{5,4},{6,5},{7,6},{4,7},{9,8},{10,9},{11,1... | collective-permute-start | bytes 253448 | tf_op jit(solution)/shard_map/ppermute | solution.py:26
  24.1 3.2 copy-start.60
  24.1 8.0 %copy-start.72 = (bf16[400]{0:T(512)(128)(2,1)S(1)}, bf16[400]{0:T(512)(128)(2,1)}, u32[]{:S(2)}) copy-start(bf16[400]{0:T(512)(128)(2,1)} %param.49) | copy-start | bytes 2404
  24.2 11.8 %copy-start.71 = (s32[2,1,16,2]{2,3,1,0:T(2,128)S(1)}, s32[2,1,16,2]{2,3,1,0:T(2,128)}, u32[]{:S(2)}) copy-start(s32[2,1,16,2]{2,3,1,0:T(2,128)} %param.28) | copy-start | bytes 772
  24.2 12.0 %copy-start.68 = (s32[2,128,16,2]{1,3,2,0:T(2,128)S(1)}, s32[2,128,16,2]{1,3,2,0:T(2,128)}, u32[]{:S(2)}) copy-start(s32[2,128,16,2]{1,3,2,0:T(2,128)} %param.29) | copy-start | bytes 98308
  27.3 18.4 %collective-permute-start.7 = (bf16[400,768]{1,0:T(8,128)(2,1)S(1)}, bf16[400,768]{1,0:T(8,128)(2,1)S(1)}, u32[]{:S(2)}, u32[]{:S(2)}) collective-permute-start(bf16[400,768]{1,0:T(8,128)(2,1)S(1)} %bitcast.130), channel_id=1, source_target_pairs={{2,0},{3,1},{0,2},{1,3},{6,4},{7,5},{4,6},{5,7},{10,8},{11,9},{8,1... | collective-permute-start | bytes 1843208 | tf_op jit(solution)/shard_map/ppermute | solution.py:26
  30.1 27.4 %collective-permute-start.6 = (bf16[400,768]{1,0:T(8,128)(2,1)S(1)}, bf16[400,768]{1,0:T(8,128)(2,1)S(1)}, u32[]{:S(2)}, u32[]{:S(2)}) collective-permute-start(bf16[400,768]{1,0:T(8,128)(2,1)S(1)} %bitcast.131), channel_id=1, source_target_pairs={{1,0},{2,1},{3,2},{0,3},{5,4},{6,5},{7,6},{4,7},{9,8},{10,9},{11,1... | collective-permute-start | bytes 1843208 | tf_op jit(solution)/shard_map/ppermute | solution.py:26
  31.9 25.6 %collective-permute-start.8 = (bf16[400,768]{1,0:T(8,128)(2,1)S(1)}, bf16[400,768]{1,0:T(8,128)(2,1)S(1)}, u32[]{:S(2)}, u32[]{:S(2)}) collective-permute-start(bf16[400,768]{1,0:T(8,128)(2,1)S(1)} %bitcast.132), channel_id=1, source_target_pairs={{3,0},{0,1},{1,2},{2,3},{7,4},{4,5},{5,6},{6,7},{11,8},{8,9},{9,10... | collective-permute-start | bytes 1843208 | tf_op jit(solution)/shard_map/ppermute | solution.py:26
  32.1 30.1 %collective-permute-start.10 = (bf16[400]{0:T(512)(128)(2,1)S(1)}, bf16[400]{0:T(512)(128)(2,1)S(1)}, u32[]{:S(2)}, u32[]{:S(2)}) collective-permute-start(bf16[400]{0:T(512)(128)(2,1)S(1)} %copy-done.72), channel_id=1, source_target_pairs={{1,0},{2,1},{3,2},{0,3},{5,4},{6,5},{7,6},{4,7},{9,8},{10,9},{11,1... | collective-permute-start | bytes 2408 | tf_op jit(solution)/shard_map/ppermute | solution.py:26
  35.2 27.1 %collective-permute-start.12 = (bf16[400]{0:T(512)(128)(2,1)S(1)}, bf16[400]{0:T(512)(128)(2,1)S(1)}, u32[]{:S(2)}, u32[]{:S(2)}) collective-permute-start(bf16[400]{0:T(512)(128)(2,1)S(1)} %copy-done.72), channel_id=1, source_target_pairs={{3,0},{0,1},{1,2},{2,3},{7,4},{4,5},{5,6},{6,7},{11,8},{8,9},{9,10... | collective-permute-start | bytes 2408 | tf_op jit(solution)/shard_map/ppermute | solution.py:26
  45.8 11.7 %copy-start.61 = (bf16[400,768]{1,0:T(8,128)(2,1)}, bf16[400,768]{1,0:T(8,128)(2,1)S(1)}, u32[]{:S(2)}) copy-start(bf16[400,768]{1,0:T(8,128)(2,1)S(1)} %collective-permute-done.7) | copy-start | bytes 1843204
  45.8 16.5 %collective-permute-start.11 = (bf16[400]{0:T(512)(128)(2,1)S(1)}, bf16[400]{0:T(512)(128)(2,1)S(1)}, u32[]{:S(2)}, u32[]{:S(2)}) collective-permute-start(bf16[400]{0:T(512)(128)(2,1)S(1)} %copy-done.72), channel_id=1, source_target_pairs={{2,0},{3,1},{0,2},{1,3},{6,4},{7,5},{4,6},{5,7},{10,8},{11,9},{8,1... | collective-permute-start | bytes 2408 | tf_op jit(solution)/shard_map/ppermute | solution.py:26
  58.5 2.7 copy-start.66
  58.5 2.7 copy-start.67
  60.3 10.2 %collective-permute-start.9 = (bf16[4,400,768]{2,1,0:T(8,128)(2,1)}, bf16[4,400,768]{2,1,0:T(8,128)(2,1)S(1)}, u32[]{:S(2)}, u32[]{:S(2)}) collective-permute-start(bf16[4,400,768]{2,1,0:T(8,128)(2,1)} %pad_maximum_fusion.2), channel_id=1, source_target_pairs={{16,0},{0,16},{17,1},{1,17},{18,2},{2,18},{19,3},{3,19},{20,4},{4,... | collective-permute-start | bytes 7372808 | tf_op jit(solution)/shard_map/ppermute | solution.py:26
  61.3 7.5 %copy-start.62 = (bf16[400,768]{1,0:T(8,128)(2,1)S(1)}, bf16[400,768]{1,0:T(8,128)(2,1)}, u32[]{:S(2)}) copy-start(bf16[400,768]{1,0:T(8,128)(2,1)} %copy-done.61) | copy-start | bytes 1843204
  62.3 2.7 collective-permute-start.13
  65.1 4.6 %copy-start.64 = (bf16[400,768]{1,0:T(8,128)(2,1)S(1)}, bf16[400,768]{1,0:T(8,128)(2,1)}, u32[]{:S(2)}) copy-start(bf16[400,768]{1,0:T(8,128)(2,1)} %copy-done.63) | copy-start | bytes 1843204
  81.9 23.5 %copy-start.70 = (s32[2,256]{1,0:T(2,128)S(1)}, s32[2,256]{1,0:T(2,128)}, u32[]{:S(2)}) copy-start(s32[2,256]{1,0:T(2,128)} %param.27) | copy-start | bytes 6148
  81.9 24.8 %copy-start.10 = (bf16[2,256,768]{2,1,0:T(8,128)(2,1)S(1)}, bf16[2,256,768]{2,1,0:T(8,128)(2,1)}, u32[]{:S(2)}) copy-start(bf16[2,256,768]{2,1,0:T(8,128)(2,1)} %param.25) | copy-start | bytes 2359300
  99.9 47.7 %all-to-all-start = ((bf16[16,64,896]{2,1,0:T(8,128)(2,1)}), bf16[16,64,896]{2,1,0:T(8,128)(2,1)}, u32[]{:S(2)}, u32[]{:S(2)}) async-start(bf16[16,64,896]{2,1,0:T(8,128)(2,1)} %pad_maximum_fusion.3), calls=%async_computation | async-start | bytes 3670016 | tf_op jit(solution)/shard_map/all_to_all | solution.py:46
  147.6 56.8 %copy-start.50 = (bf16[64,768]{1,0:T(8,128)(2,1)}, bf16[64,768]{1,0:T(8,128)(2,1)S(1)}, u32[]{:S(2)}) copy-start(bf16[64,768]{1,0:T(8,128)(2,1)S(1)} %get-tuple-element.110.head_ref) | copy-start | bytes 294916
  147.6 104.0 %copy-start = (bf16[512,3072]{1,0:T(8,128)(2,1)}, bf16[512,3072]{1,0:T(8,128)(2,1)S(1)}, u32[]{:S(2)}) copy-start(bf16[512,3072]{1,0:T(8,128)(2,1)S(1)} %get-tuple-element.127.refs_2_) | copy-start | bytes 9437188
  147.6 31.5 %all-to-all-start.1 = ((bf16[16,64,768]{2,1,0:T(8,128)(2,1)}), bf16[16,64,768]{2,1,0:T(8,128)(2,1)}, u32[]{:S(2)}, u32[]{:S(2)}) async-start(bf16[16,64,768]{2,1,0:T(8,128)(2,1)} %copy-done.33), calls=%async_computation.1 | async-start | bytes 3145728 | tf_op jit(solution)/shard_map/all_to_all | solution.py:46
  204.4 30.4 %all-to-all-start.2 = ((bf16[16,80,768]{2,1,0:T(8,128)(2,1)}), bf16[16,80,768]{2,1,0:T(8,128)(2,1)}, u32[]{:S(2)}, u32[]{:S(2)}) async-start(bf16[16,80,768]{2,1,0:T(8,128)(2,1)} %get-tuple-element.109), calls=%async_computation.2 | async-start | bytes 3932160 | tf_op jit(solution)/shard_map/all_to_all | solution.py:46
  242.0 5.5 %copy-start.13 = (bf16[512,3072]{1,0:T(8,128)(2,1)S(1)}, bf16[512,3072]{1,0:T(8,128)(2,1)}, u32[]{:S(2)}) copy-start(bf16[512,3072]{1,0:T(8,128)(2,1)} %copy-done.12) | copy-start | bytes 9437188
  247.4 4.2 copy-start.3
  247.4 4.2 copy-start.7
  251.5 8.0 %collective-permute-start.14 = (bf16[16,128,768]{2,1,0:T(8,128)(2,1)S(1)}, bf16[16,128,768]{2,1,0:T(8,128)(2,1)S(1)}, u32[]{:S(2)}, u32[]{:S(2)}) collective-permute-start(bf16[16,128,768]{2,1,0:T(8,128)(2,1)S(1)} %get-tuple-element.131), channel_id=1, source_target_pairs={{0,16},{16,0},{1,17},{17,1},{2,18},{18,2},{3,19},{19,3},{4,20},{20... | collective-permute-start | bytes 9437192 | tf_op jit(solution)/shard_map/ppermute | solution.py:31
  259.5 2.9 copy-start.1
  259.5 2.9 copy-start.29
  262.4 4.9 %copy-start.2 = (bf16[16,24,3072]{2,1,0:T(8,128)(2,1)S(1)}, bf16[16,24,3072]{2,1,0:T(8,128)(2,1)}, u32[]{:S(2)}) copy-start(bf16[16,24,3072]{2,1,0:T(8,128)(2,1)} %copy-done.1) | copy-start | bytes 7077892
  262.4 4.9 %copy-start.4 = (bf16[512,768]{1,0:T(8,128)(2,1)S(1)}, bf16[512,768]{1,0:T(8,128)(2,1)}, u32[]{:S(2)}) copy-start(bf16[512,768]{1,0:T(8,128)(2,1)} %copy-done.3) | copy-start | bytes 2359300
  262.4 4.9 %copy-start.41 = (f32[512,1]{1,0:T(8,128)S(1)}, f32[512,1]{1,0:T(8,128)}, u32[]{:S(2)}) copy-start(f32[512,1]{1,0:T(8,128)} %copy-done.40) | copy-start | bytes 6148
  262.4 48.5 %all-to-all-start.3 = ((bf16[16,128,768]{2,1,0:T(8,128)(2,1)}), bf16[16,128,768]{2,1,0:T(8,128)(2,1)}, u32[]{:S(2)}, u32[]{:S(2)}) async-start(bf16[16,128,768]{2,1,0:T(8,128)(2,1)} %add_convert_fusion), calls=%async_computation.3 | async-start | bytes 6291456 | tf_op jit(solution)/shard_map/all_to_all | solution.py:46
  271.3 9.8 %copy-start.15 = (bf16[2,12,256,256]{3,2,1,0:T(8,128)(2,1)S(1)}, bf16[2,12,256,256]{3,2,1,0:T(8,128)(2,1)}, u32[]{:S(2)}) copy-start(bf16[2,12,256,256]{3,2,1,0:T(8,128)(2,1)} %copy-done.14) | copy-start | bytes 9437188
  271.3 9.8 %copy-start.24 = (bf16[512,2304]{1,0:T(8,128)(2,1)S(1)}, bf16[512,2304]{1,0:T(8,128)(2,1)}, u32[]{:S(2)}) copy-start(bf16[512,2304]{1,0:T(8,128)(2,1)} %copy-done.23) | copy-start | bytes 7077892
  280.5 12.4 %copy-start.16 = (bf16[512,768]{1,0:T(8,128)(2,1)}, bf16[512,768]{1,0:T(8,128)(2,1)S(1)}, u32[]{:S(2)}) copy-start(bf16[512,768]{1,0:T(8,128)(2,1)S(1)} %get-tuple-element.139.dbranch_ref) | copy-start | bytes 2359300
  280.5 12.4 %copy-start.55 = (f32[8,768]{1,0:T(8,128)}, f32[8,768]{1,0:T(8,128)S(1)}, u32[]{:S(2)}) copy-start(f32[8,768]{1,0:T(8,128)S(1)} %get-tuple-element.146.high_ref) | copy-start | bytes 73732
  280.5 12.4 %copy-start.58 = (f32[512,768]{1,0:T(8,128)}, f32[512,768]{1,0:T(8,128)S(1)}, u32[]{:S(2)}) copy-start(f32[512,768]{1,0:T(8,128)S(1)} %get-tuple-element.167) | copy-start | bytes 4718596
  280.5 30.4 %collective-permute-start.15 = (bf16[16,24,3072]{2,1,0:T(8,128)(2,1)}, bf16[16,24,3072]{2,1,0:T(8,128)(2,1)}, u32[]{:S(2)}, u32[]{:S(2)}) collective-permute-start(bf16[16,24,3072]{2,1,0:T(8,128)(2,1)} %get-tuple-element.138), channel_id=1, source_target_pairs={{0,16},{16,0},{1,17},{17,1},{2,18},{18,2},{3,19},{19,3},{4,20},{20... | collective-permute-start | bytes 7077896 | tf_op jit(solution)/shard_map/ppermute | solution.py:31
  281.1 14.9 %copy-start.11 = (bf16[2,256,768]{2,1,0:T(8,128)(2,1)S(1)}, bf16[2,256,768]{2,1,0:T(8,128)(2,1)}, u32[]{:S(2)}) copy-start(bf16[2,256,768]{2,1,0:T(8,128)(2,1)} %param.25) | copy-start | bytes 2359300
  310.9 35.2 %collective-permute-start.16 = (bf16[16,24,3200]{2,1,0:T(8,128)(2,1)}, bf16[16,24,3200]{2,1,0:T(8,128)(2,1)}, u32[]{:S(2)}, u32[]{:S(2)}) collective-permute-start(bf16[16,24,3200]{2,1,0:T(8,128)(2,1)} %copy-done.57), channel_id=1, source_target_pairs={{0,16},{16,0},{1,17},{17,1},{2,18},{18,2},{3,19},{19,3},{4,20},{20... | collective-permute-start | bytes 7372808 | tf_op jit(solution)/shard_map/ppermute | solution.py:31
  314.9 10.7 %copy-start.25 = (f32[1024,1]{1,0:T(8,128)S(1)}, f32[1024,1]{1,0:T(8,128)}, u32[]{:S(2)}) copy-start(f32[1024,1]{1,0:T(8,128)} %select_multiply_fusion.scale_ref) | copy-start | bytes 12292
  314.9 10.7 %copy-start.26 = (s32[1024,1]{1,0:T(8,128)S(1)}, s32[1024,1]{1,0:T(8,128)}, u32[]{:S(2)}) copy-start(s32[1024,1]{1,0:T(8,128)} %copy.118.label_ref) | copy-start | bytes 12292
  314.9 10.7 %copy-start.39 = (f32[1024,128]{1,0:T(8,128)S(1)}, f32[1024,128]{1,0:T(8,128)}, u32[]{:S(2)}) copy-start(f32[1024,128]{1,0:T(8,128)} %get-tuple-element.108.stat_ref) | copy-start | bytes 1572868
  314.9 10.7 %copy-start.52 = (s32[1,3200]{1,0:T(1,128)S(1)}, s32[1,3200]{1,0:T(1,128)}, u32[]{:S(2)}) copy-start(s32[1,3200]{1,0:T(1,128)} %add.232.column_ref) | copy-start | bytes 38404
  314.9 44.3 %all-to-all-start.4 = ((bf16[16,24,3072]{2,1,0:T(8,128)(2,1)}), bf16[16,24,3072]{2,1,0:T(8,128)(2,1)}, u32[]{:S(2)}, u32[]{:S(2)}) async-start(bf16[16,24,3072]{2,1,0:T(8,128)(2,1)} %add_convert_fusion.3), calls=%async_computation.4 | async-start | bytes 4718592 | tf_op jit(solution)/shard_map/all_to_all | solution.py:46
  339.3 2.3 copy-start.9
  344.5 2.6 copy-start.19
  359.2 8.4 %collective-permute-start.17 = (bf16[4,408,768]{2,1,0:T(8,128)(2,1)}, bf16[4,408,768]{2,1,0:T(8,128)(2,1)}, u32[]{:S(2)}, u32[]{:S(2)}) collective-permute-start(bf16[4,408,768]{2,1,0:T(8,128)(2,1)} %get-tuple-element.159), channel_id=1, source_target_pairs={{0,16},{16,0},{1,17},{17,1},{2,18},{18,2},{3,19},{19,3},{4,20},{20... | collective-permute-start | bytes 7520264 | tf_op jit(solution)/shard_map/ppermute | solution.py:31
  359.2 54.0 %all-to-all-start.5 = ((bf16[16,24,3200]{2,1,0:T(8,128)(2,1)}), bf16[16,24,3200]{2,1,0:T(8,128)(2,1)}, u32[]{:S(2)}, u32[]{:S(2)}) async-start(bf16[16,24,3200]{2,1,0:T(8,128)(2,1)} %add_convert_fusion.2), calls=%async_computation.5 | async-start | bytes 4915200 | tf_op jit(solution)/shard_map/all_to_all | solution.py:46
  379.9 17.5 %collective-permute-start.18 = (bf16[408,768]{1,0:T(8,128)(2,1)S(1)}, bf16[408,768]{1,0:T(8,128)(2,1)S(1)}, u32[]{:S(2)}, u32[]{:S(2)}) collective-permute-start(bf16[408,768]{1,0:T(8,128)(2,1)S(1)} %get-tuple-element.183), channel_id=1, source_target_pairs={{0,1},{1,2},{2,3},{3,0},{4,5},{5,6},{6,7},{7,4},{8,9},{9,10},{10,1... | collective-permute-start | bytes 1880072 | tf_op jit(solution)/shard_map/ppermute | solution.py:31
  381.5 28.7 %collective-permute-start.20 = (bf16[408,768]{1,0:T(8,128)(2,1)S(1)}, bf16[408,768]{1,0:T(8,128)(2,1)S(1)}, u32[]{:S(2)}, u32[]{:S(2)}) collective-permute-start(bf16[408,768]{1,0:T(8,128)(2,1)S(1)} %get-tuple-element.184), channel_id=1, source_target_pairs={{0,3},{1,0},{2,1},{3,2},{4,7},{5,4},{6,5},{7,6},{8,11},{9,8},{10,9... | collective-permute-start | bytes 1880072 | tf_op jit(solution)/shard_map/ppermute | solution.py:31
  383.2 28.6 %collective-permute-start.19 = (bf16[408,768]{1,0:T(8,128)(2,1)S(1)}, bf16[408,768]{1,0:T(8,128)(2,1)S(1)}, u32[]{:S(2)}, u32[]{:S(2)}) collective-permute-start(bf16[408,768]{1,0:T(8,128)(2,1)S(1)} %get-tuple-element.185), channel_id=1, source_target_pairs={{0,2},{1,3},{2,0},{3,1},{4,6},{5,7},{6,4},{7,5},{8,10},{9,11},{10,... | collective-permute-start | bytes 1880072 | tf_op jit(solution)/shard_map/ppermute | solution.py:31
  413.2 6.5 %copy-start.22 = (bf16[512,2304]{1,0:T(8,128)(2,1)S(1)}, bf16[512,2304]{1,0:T(8,128)(2,1)}, u32[]{:S(2)}) copy-start(bf16[512,2304]{1,0:T(8,128)(2,1)} %copy-done.20) | copy-start | bytes 7077892
  416.1 14.2 %all-to-all-start.6 = ((bf16[4,6,10240]{2,1,0:T(8,128)(2,1)}), bf16[4,6,10240]{2,1,0:T(8,128)(2,1)S(1)}, u32[]{:S(2)}, u32[]{:S(2)}) async-start(bf16[4,6,10240]{2,1,0:T(8,128)(2,1)} %constant_dynamic-update-slice_fusion.18), calls=%async_computation.6 | async-start | bytes 1310720 | tf_op jit(solution)/shard_map/all_to_all | solution.py:46
  419.6 5.8 %copy-start.59 = (f32[408,768]{1,0:T(8,128)S(1)}, f32[408,768]{1,0:T(8,128)}, u32[]{:S(2)}) copy-start(f32[408,768]{1,0:T(8,128)} %fusion.13) | copy-start | bytes 3760132
  (38 other events, 42.1 us)
Sparse Core Ops, SparseCore 0:
  27.5 72.4 all-gather.1

commit v11 on v10

--- a/solution.py
+++ b/solution.py
@@ -239,7 +239,7 @@
             jax.ShapeDtypeStruct((tokens, width), F32),
             jax.ShapeDtypeStruct((tokens, 1), F32),
         ],
-        compiler_params=pltpu.CompilerParams(vmem_limit_bytes=36 * 1024 * 1024),
+        compiler_params=pltpu.CompilerParams(vmem_limit_bytes=60 * 1024 * 1024),
         cost_estimate=pl.CostEstimate(
             flops=1000, bytes_accessed=1000, transcendentals=0
         ),
@@ -302,14 +302,15 @@
             jax.ShapeDtypeStruct((tokens, 3 * width), BF),
             jax.ShapeDtypeStruct((1, 3 * width), F32),
         ],
-        compiler_params=pltpu.CompilerParams(vmem_limit_bytes=36 * 1024 * 1024),
+        compiler_params=pltpu.CompilerParams(vmem_limit_bytes=60 * 1024 * 1024),
         cost_estimate=pl.CostEstimate(
             flops=1000, bytes_accessed=1000, transcendentals=0
         ),
     )(dbranch, qkv, probs, layer)
 
 
-LIMIT = 40 * 1024 * 1024
+LIMIT = 56 * 1024 * 1024
+SMALL = 56 * 1024 * 1024
 
 
 def whole_spec(array):
@@ -594,6 +595,7 @@
         [pltpu.VMEM((width, width), F32)],
         1000,
         1000,
+        SMALL,
     )
 
 

time: 450 us -> 438 us (0.973)
  local copies, waits for them, and re-layouts: 78.1 us -> 42.1 us
  Pallas kernels: 102 us -> 126 us
    unnamed x175 -> x71, local copies, waits for them, and re-layouts: 54.8 us -> 16.1 us
    pallas_call x6, Pallas kernels: 63.8 us -> 78.6 us  [call(): pl.pallas_call(kernel, grid=grid, in_specs=in_specs, out_specs=out_specs,...]
    all_to_all x7, waiting for transfers between devices: 59.1 us -> 64.1 us  [swap(): return lax.all_to_all(array, axes, 0, 0, tiled=True)]
  transfers between devices with their start and end apart: 29 -> 29, of which waited for: 13 -> 13; matrix products, arithmetic and copies ran while one was open for 17% -> 18% of each run, Pallas kernels for 15% -> 20%
where the time goes in v11:
time: 438 us; the launch traced here: 431 us
  Pallas kernels  126 us (29%)
  waiting for transfers between devices  124 us (28%)
  starting transfers between devices  67.6 us (15%)
  local copies, waits for them, and re-layouts  42.1 us (10%)
  other arithmetic  36.3 us (8%)
  between operations  21.2 us (5%)
  matrix products  14.1 us (3%)
    pallas_call x6, Pallas kernels, call(): pl.pallas_call(kernel, grid=grid, in_specs=in_specs, out_specs=out_specs,...  78.6 us
    all_to_all x7, waiting for transfers between devices, swap(): return lax.all_to_all(array, axes, 0, 0, tiled=True)  64.1 us
    all_to_all x7, starting transfers between devices, swap(): return lax.all_to_all(array, axes, 0, 0, tiled=True)  40.5 us
    ppermute x7, waiting for transfers between devices, give(): return lax.ppermute(array, axis, [(i, (i + k) % n) for i in range(n)])  24.1 us
    pallas_call x2, Pallas kernels, feed_back_call(): pl.pallas_call(functools.partial(feed_back_kernel, closing), grid=(steps,...  21.5 us
    ppermute x14, starting transfers between devices, fetch(): return lax.ppermute(array, axis, [((i + k) % n, i) for i in range(n)])  21 us
    all_gather x1, waiting for transfers between devices, body(): lax.all_gather(jnp.concatenate([tall, fused], axis=1), ('y', 'c', 'z'), a...  18.1 us
    ppermute x14, waiting for transfers between devices, fetch(): return lax.ppermute(array, axis, [((i + k) % n, i) for i in range(n)])  17.9 us
  transfers between devices with their start and end apart: 29, of which 13 were waited for; matrix products, arithmetic and copies ran while one was open for 18% of the time, Pallas kernels for 20%

profile of v11, /device:TPU:0, one launch (start us, length us, event | category | flops | bytes accessed | tf_op | source)
XLA Modules:
  0.0 431.3 jit_solution(5081408530480568036)
XLA Ops:
  7.2 2.9 collective-permute-start
  10.2 2.3 collective-permute-start.1
  13.3 1.5 stack.172
  17.9 1.8 collective-permute-start.5
  21.3 2.0 collective-permute-start.3
  24.2 2.0 collective-permute-done.3
  27.3 2.7 collective-permute-start.7
  30.1 1.9 collective-permute-start.6
  32.1 3.1 collective-permute-start.10
  37.3 1.3 reshape.264
  39.7 6.1 %collective-permute-done.7 = bf16[400,768]{1,0:T(8,128)(2,1)S(1)} collective-permute-done((bf16[400,768]{1,0:T(8,128)(2,1)S(1)}, bf16[400,768]{1,0:T(8,128)(2,1)S(1)}, u32[]{:S(2)}, u32[]{:S(2)}) %collective-permute-start.7) | collective-permute-done | bytes 614432 | tf_op jit(solution)/shard_map/ppermute | solution.py:26
  45.8 2.6 collective-permute-start.11
  48.4 9.1 %collective-permute-done.6 = bf16[400,768]{1,0:T(8,128)(2,1)S(1)} collective-permute-done((bf16[400,768]{1,0:T(8,128)(2,1)S(1)}, bf16[400,768]{1,0:T(8,128)(2,1)S(1)}, u32[]{:S(2)}, u32[]{:S(2)}) %collective-permute-start.6) | collective-permute-done | bytes 614432 | tf_op jit(solution)/shard_map/ppermute | solution.py:26
  58.5 1.7 pad_maximum_fusion.2
  65.1 1.4 select_reduce_fusion
  66.8 2.0 constant_dynamic-update-slice_fusion.16
  70.5 1.7 constant_dynamic-update-slice_fusion.13
  72.1 8.2 %fusion.6 = bf16[16,64,768]{2,1,0:T(8,128)(2,1)S(1)} fusion(bf16[3200,768,1]{1,0,2:T(8,128)(2,1)} %bitcast.143, s32[3200]{0:T(1024)S(1)} %add.228, s32[16,64]{1,0:T(8,128)S(1)} %reshape.263), kind=kOutput, calls=%fused_computation.17 | convolution fusion | flops 5037228032 | bytes 6504960 | tf_op jit(solution)/shard_map/dot_general | solution.py:130
  80.3 1.5 pad_maximum_fusion.3
  81.8 18.1 %all-gather.2.cloned.1.call-done.wq_ref.wk_ref.wv_ref.wa_ref.expand_ref.tall_ref.dense_ref.refs_4_ = bf16[768,10112]{1,0:T(8,128)(2,1)} async-done(((bf16[24,10112]{1,0:T(8,128)(2,1)}), bf16[768,10112]{1,0:T(8,128)(2,1)}) %all-gather.2.cloned.1.call-update) | async-done | bytes 15532048 | tf_op jit(solution)/shard_map/all_gather | solution.py:932
  99.9 5.4 %all-to-all-start = ((bf16[16,64,896]{2,1,0:T(8,128)(2,1)}), bf16[16,64,896]{2,1,0:T(8,128)(2,1)S(1)}, u32[]{:S(2)}, u32[]{:S(2)}) async-start(bf16[16,64,896]{2,1,0:T(8,128)(2,1)} %pad_maximum_fusion.3), calls=%async_computation | async-start | bytes 3670016 | tf_op jit(solution)/shard_map/all_to_all | solution.py:46
  108.5 11.7 %shard_map.408 = (bf16[512,2304]{1,0:T(8,128)(2,1)}, bf16[2,12,256,256]{3,2,1,0:T(8,128)(2,1)}, bf16[512,768]{1,0:T(8,128)(2,1)}, f32[512,768]{1,0:T(8,128)}, bf...) custom-call(bf16[512,768]{1,0:T(8,128)(2,1)} %bitcast.129, s32[2,1,256]{2,1,0:T(1,128)} %broadcast_in_dim.43.row_ref, ...), custom_call_target="tpu_custom_call" | custom-call | flops 1000 | bytes 1000 | tf_op jit(solution)/shard_map/pallas_call | solution.py:211
  120.2 1.0 slice_convert_fusion
  122.1 15.8 %shard_map.409 = (bf16[512,3072]{1,0:T(8,128)(2,1)}, bf16[512,3072]{1,0:T(8,128)(2,1)}, bf16[3072,768]{1,0:T(8,128)(2,1)}, bf16[512,768]{1,0:T(8,128)(2,1)}, f32...) custom-call(bf16[512,768]{1,0:T(8,128)(2,1)} %get-tuple-element.97.l, ...), custom_call_target="tpu_custom_call" | custom-call | flops 1000 | bytes 1000 | tf_op jit(solution)/shard_map/pallas_call | solution.py:321
  137.9 7.8 %all-to-all-start.1 = ((bf16[16,64,768]{2,1,0:T(8,128)(2,1)}), bf16[16,64,768]{2,1,0:T(8,128)(2,1)S(1)}, u32[]{:S(2)}, u32[]{:S(2)}) async-start(bf16[16,64,768]{2,1,0:T(8,128)(2,1)} %get-tuple-element.103), calls=%async_computation.1 | async-start | bytes 3145728 | tf_op jit(solution)/shard_map/all_to_all | solution.py:46
  147.1 1.0 copy.118.label_ref
  148.2 21.2 %all-to-all-done.1 = bf16[16,64,768]{2,1,0:T(8,128)(2,1)S(1)} async-done(((bf16[16,64,768]{2,1,0:T(8,128)(2,1)}), bf16[16,64,768]{2,1,0:T(8,128)(2,1)S(1)}, u32[]{:S(2)}, u32[]{:S(2)}) %all-to-all-start.1) | async-done | bytes 1572896 | tf_op jit(solution)/shard_map/all_to_all | solution.py:46
  169.3 1.1 copy-done.2
  170.5 25.3 %shard_map.410 = (bf16[1024,3200]{1,0:T(8,128)(2,1)}, f32[1024,128]{1,0:T(8,128)}, bf16[16,80,768]{2,1,0:T(8,128)(2,1)}) custom-call(bf16[1024,768]{1,0:T(8,128)(2,1)} %bitcast.124, bf16[3200,768]{1,0:T(8,128)(2,1)} %bitcast.144, f32[1,3200]{1,0:T(1,128)} %reshape.260.b_ref, s32[1,3200]{1,0:T(1,128)} %add.232.column_ref, s32[1024,1]{1,0:T(8,128)} %copy.118.label_ref), custom_call_target="tpu_custom_call" | custom-call | flops 10000000000 | bytes 20000000 | tf_op jit(solution)/shard_map/pallas_call | solution.py:321
  195.8 3.9 all-to-all-start.2
  200.1 1.8 convert_reduce_fusion
  203.3 23.0 %all-to-all-done.2.part_ref = bf16[16,80,768]{2,1,0:T(8,128)(2,1)S(1)} async-done(((bf16[16,80,768]{2,1,0:T(8,128)(2,1)}), bf16[16,80,768]{2,1,0:T(8,128)(2,1)S(1)}, u32[]{:S(2)}, u32[]{:S(2)}) %all-to-all-start.2) | async-done | bytes 1966112 | tf_op jit(solution)/shard_map/all_to_all | solution.py:46
  226.3 1.3 copy-done
  227.6 7.1 %shard_map.411 = (f32[1,1024]{1,0:T(1,128)}, f32[8,128]{1,0:T(8,128)}, f32[768,768]{1,0:T(8,128)}, f32[512,768]{1,0:T(8,128)}, bf16[512,768]{1,0:T(8,128)(2,1)}, /*index=5*/f32[8,768]{1,0:T(8,128)}) custom-call(s32[1]{0:T(128)} %bitcast.46.own_ref, bf16[16,80,768]{2,1,0:T(8,128)(2,1)} %copy-done, bf16[64,768]{1,0:T(8,128)(2,1)} %get-tuple-element.110.head_ref, ...), custom_call_target="tpu_custom_call" | custom-call | flops 300000000 | bytes 10000000 | tf_op jit(solution)/shard_map/pallas_call | solution.py:321
  234.7 7.5 %shard_map.412 = (bf16[16,128,768]{2,1,0:T(8,128)(2,1)}, bf16[16,128,768]{2,1,0:T(8,128)(2,1)}) custom-call(s32[1]{0:T(128)} %bitcast.50.core_ref, bf16[512,3072]{1,0:T(8,128)(2,1)} %get-tuple-element.119.act_ref, bf16[512,768]{1,0:T(8,128)(2,1)} %get-tuple-element.125.dffn_ref.refs_0_, f32[768,768]{1,0:T(8,128)} %get-tuple-element.121.dense_ref, ...), custom_call_target="tpu_custom_call" | custom-call | flops 1000 | bytes 1000 | tf_op jit(solution)/shard_map/pallas_call | solution.py:321
  242.2 9.9 %shard_map.413 = (bf16[16,24,3072]{2,1,0:T(8,128)(2,1)}, bf16[16,24,3072]{2,1,0:T(8,128)(2,1)}, f32[1,1536]{1,0:T(1,128)}, f32[512,768]{1,0:T(8,128)}) custom-call(s32[1]{0:T(128)} %bitcast.50.core_ref, bf16[512,768]{1,0:T(8,128)(2,1)} %get-tuple-element.125.dffn_ref.refs_0_, bf16[3072,768]{1,0:T(8,128)(2,1)} %get-tuple-element.126.refs_1_, ...), custom_call_target="tpu_custom_call" | custom-call | flops 1000 | bytes 1000 | tf_op jit(solution)/shard_map/pallas_call | solution.py:676
  252.1 2.6 add_convert_fusion
  254.7 3.8 all-to-all-start.3
  258.5 11.6 %shard_map.414 = (bf16[16,24,3072]{2,1,0:T(8,128)(2,1)}, bf16[16,24,3072]{2,1,0:T(8,128)(2,1)}, f32[1,1536]{1,0:T(1,128)}, f32[512,768]{1,0:T(8,128)}, bf16[512,768]{1,0:T(8,128)(2,1)}, /*index=5*/f32[8,768]{1,0:T(8,128)}) custom-call(s32[1]{0:T(128)} %bitcast.50.core_ref, ...), custom_call_target="tpu_custom_call", output_to_operand_aliasing={{0}: (10, {}), {1}: (11, {})} | custom-call | flops 1000 | bytes 1000 | tf_op jit(solution)/shard_map/pallas_call | solution.py:676
  270.8 13.9 %shard_map.415 = (bf16[512,2304]{1,0:T(8,128)(2,1)}, f32[1,2304]{1,0:T(1,128)}) custom-call(bf16[512,768]{1,0:T(8,128)(2,1)} %get-tuple-element.139.dbranch_ref, bf16[512,2304]{1,0:T(8,128)(2,1)} %get-tuple-element.140.qkv_ref, bf16[2,12,256,256]{3,2,1,0:T(8,128)(2,1)} %get-tuple-element.141.probs_ref, ...), custom_call_target="tpu_custom_call" | custom-call | flops 1000 | bytes 1000 | tf_op jit(solution)/shard_map/pallas_call | solution.py:291
  284.8 1.1 reshape.247.bias_ref
  285.9 7.8 %shard_map.416 = (bf16[16,24,3200]{2,1,0:T(8,128)(2,1)}, bf16[16,24,3200]{2,1,0:T(8,128)(2,1)}) custom-call(s32[1]{0:T(128)} %bitcast.50.core_ref, bf16[512,768]{1,0:T(8,128)(2,1)} %bitcast.130, bf16[512,2304]{1,0:T(8,128)(2,1)} %get-tuple-element.168.dfused_ref, bf16[512,768]{1,0:T(8,128)(2,1)} %get-tuple-element.143.attended_ref, ...), custom_call_target="tpu_custom_call" | custom-call | flops 1000 | bytes 1000 | tf_op jit(solution)/shard_map/pallas_call | solution.py:321
  293.8 8.7 %all-to-all-done.3 = bf16[16,128,768]{2,1,0:T(8,128)(2,1)S(1)} async-done(((bf16[16,128,768]{2,1,0:T(8,128)(2,1)}), bf16[16,128,768]{2,1,0:T(8,128)(2,1)S(1)}, u32[]{:S(2)}, u32[]{:S(2)}) %all-to-all-start.3) | async-done | bytes 3145760 | tf_op jit(solution)/shard_map/all_to_all | solution.py:46
  302.5 4.7 %add_convert_fusion.3 = bf16[16,24,3072]{2,1,0:T(8,128)(2,1)} fusion(bf16[16,24,3072]{2,1,0:T(8,128)(2,1)} %collective-permute-done.15, bf16[16,24,3072]{2,1,0:T(8,128)(2,1)} %get-tuple-element.137), kind=kLoop, calls=%fused_computation.8 | loop fusion | flops 4718592 | bytes 7077888 | tf_op jit(solution)/shard_map/convert_element_type | solution.py:65
  307.2 10.0 %all-to-all-start.4 = ((bf16[16,24,3072]{2,1,0:T(8,128)(2,1)}), bf16[16,24,3072]{2,1,0:T(8,128)(2,1)}, u32[]{:S(2)}, u32[]{:S(2)}) async-start(bf16[16,24,3072]{2,1,0:T(8,128)(2,1)} %add_convert_fusion.3), calls=%async_computation.4 | async-start | bytes 4718592 | tf_op jit(solution)/shard_map/all_to_all | solution.py:46
  317.1 15.1 %shard_map.417 = (bf16[3200,768]{1,0:T(8,128)(2,1)}, f32[1,3200]{1,0:T(1,128)}) custom-call(bf16[1024,3200]{1,0:T(8,128)(2,1)} %get-tuple-element.106.expl_ref, bf16[1024,768]{1,0:T(8,128)(2,1)} %bitcast.125, s32[1,3200]{1,0:T(1,128)} %add.232.column_ref, s32[1024,1]{1,0:T(8,128)} %copy.118.label_ref, f32[1024,1]{1,0:T(8,128)} %select_multiply_fusion.scale_ref, ...), custom_call_target="tpu_custom_call" | custom-call | flops 1000 | bytes 1000 | tf_op jit(solution)/shard_map/pallas_call | solution.py:321
  333.1 2.8 fusion.23
  335.8 2.5 pad_maximum_fusion
  338.8 3.8 add_convert_fusion.2
  342.6 8.1 %all-to-all-done.4 = bf16[16,24,3072]{2,1,0:T(8,128)(2,1)} async-done(((bf16[16,24,3072]{2,1,0:T(8,128)(2,1)}), bf16[16,24,3072]{2,1,0:T(8,128)(2,1)}, u32[]{:S(2)}, u32[]{:S(2)}) %all-to-all-start.4) | async-done | bytes 2359328 | tf_op jit(solution)/shard_map/all_to_all | solution.py:46
  351.0 6.2 %all-to-all-start.5 = ((bf16[16,24,3200]{2,1,0:T(8,128)(2,1)}), bf16[16,24,3200]{2,1,0:T(8,128)(2,1)}, u32[]{:S(2)}, u32[]{:S(2)}) async-start(bf16[16,24,3200]{2,1,0:T(8,128)(2,1)} %add_convert_fusion.2), calls=%async_computation.5 | async-start | bytes 4915200 | tf_op jit(solution)/shard_map/all_to_all | solution.py:46
  357.3 2.1 reduce_sum.95
  366.7 3.1 add_convert_fusion.1
  369.9 1.5 collective-permute-start.18
  371.4 1.8 collective-permute-start.20
  373.2 1.8 collective-permute-start.19
  377.6 9.8 %collective-permute-done.18 = bf16[408,768]{1,0:T(8,128)(2,1)S(1)} collective-permute-done((bf16[408,768]{1,0:T(8,128)(2,1)S(1)}, bf16[408,768]{1,0:T(8,128)(2,1)S(1)}, u32[]{:S(2)}, u32[]{:S(2)}) %collective-permute-start.18) | collective-permute-done | bytes 626720 | tf_op jit(solution)/shard_map/ppermute | solution.py:31
  387.4 12.7 %collective-permute-done.20 = bf16[408,768]{1,0:T(8,128)(2,1)S(1)} collective-permute-done((bf16[408,768]{1,0:T(8,128)(2,1)S(1)}, bf16[408,768]{1,0:T(8,128)(2,1)S(1)}, u32[]{:S(2)}, u32[]{:S(2)}) %collective-permute-start.20) | collective-permute-done | bytes 626720 | tf_op jit(solution)/shard_map/ppermute | solution.py:31
  400.1 1.6 collective-permute-done.19
  402.1 2.2 reduce_sum.96
  405.0 3.5 all-to-all-start.6
  408.5 5.9 %fusion.9 = f32[512,768]{1,0:T(8,128)} fusion(f32[512,768]{1,0:T(8,128)S(1)} %copy-done.20, bf16[512,2304]{1,0:T(8,128)(2,1)} %get-tuple-element.168.dfused_ref, bf16[768,10112]{1,0:T(8,128)(2,1)} %all-gather.2.cloned.1.call-done.wq_ref.wk_ref.wv_ref.wa_ref.expand_ref.tall_ref.dense_ref.refs_4_), kind=kOutput, calls=%fused_computation.18 | convolution fusion | flops 1812332544 | bytes 9043968 | tf_op jit(solution)/shard_map/dot_general | solution.py:138
  415.0 1.1 slice_bitcast_fusion
  416.1 3.1 all-to-all-done.6
  (178 shorter events, 38.7 us)
Async XLA Ops:
  7.2 92.7 %all-gather.2.cloned.1.call-start = ((), (), s32[]{:S(2)}) async-start(), calls=%async_computation.7 | async-start | bytes 16017408 | tf_op jit(solution)/shard_map/all_gather | solution.py:932
  7.2 14.1 %collective-permute-start = (bf16[24,768]{1,0:T(8,128)(2,1)}, bf16[24,768]{1,0:T(8,128)(2,1)S(1)}, u32[]{:S(2)}, u32[]{:S(2)}) collective-permute-start(bf16[24,768]{1,0:T(8,128)(2,1)} %param.40), channel_id=1, source_target_pairs={{1,0},{2,1},{3,2},{0,3},{5,4},{6,5},{7,6},{4,7},{9,8},{10,9},{11,1... | collective-permute-start | bytes 110600 | tf_op jit(solution)/shard_map/ppermute | solution.py:26
  10.1 13.1 %collective-permute-start.2 = (bf16[24,768]{1,0:T(8,128)(2,1)}, bf16[24,768]{1,0:T(8,128)(2,1)S(1)}, u32[]{:S(2)}, u32[]{:S(2)}) collective-permute-start(bf16[24,768]{1,0:T(8,128)(2,1)} %param.40), channel_id=1, source_target_pairs={{3,0},{0,1},{1,2},{2,3},{7,4},{4,5},{5,6},{6,7},{11,8},{8,9},{9,10... | collective-permute-start | bytes 110600 | tf_op jit(solution)/shard_map/ppermute | solution.py:26
  10.2 13.1 %collective-permute-start.1 = (bf16[24,768]{1,0:T(8,128)(2,1)}, bf16[24,768]{1,0:T(8,128)(2,1)S(1)}, u32[]{:S(2)}, u32[]{:S(2)}) collective-permute-start(bf16[24,768]{1,0:T(8,128)(2,1)} %param.40), channel_id=1, source_target_pairs={{2,0},{3,1},{0,2},{1,3},{6,4},{7,5},{4,6},{5,7},{10,8},{11,9},{8,1... | collective-permute-start | bytes 110600 | tf_op jit(solution)/shard_map/ppermute | solution.py:26
  17.9 8.3 %collective-permute-start.5 = (bf16[6,7040]{1,0:T(8,128)(2,1)S(1)}, bf16[6,7040]{1,0:T(8,128)(2,1)S(1)}, u32[]{:S(2)}, u32[]{:S(2)}) collective-permute-start(bf16[6,7040]{1,0:T(8,128)(2,1)S(1)} %constant_dynamic-update-slice_fusion.8), channel_id=1, source_target_pairs={{3,0},{0,1},{1,2},{2,3},{7,4},{4,5},{5,6},{6,7},{11,8},{8,9},{9,10... | collective-permute-start | bytes 253448 | tf_op jit(solution)/shard_map/ppermute | solution.py:26
  19.7 6.5 %collective-permute-start.4 = (bf16[6,7040]{1,0:T(8,128)(2,1)S(1)}, bf16[6,7040]{1,0:T(8,128)(2,1)S(1)}, u32[]{:S(2)}, u32[]{:S(2)}) collective-permute-start(bf16[6,7040]{1,0:T(8,128)(2,1)S(1)} %constant_dynamic-update-slice_fusion.8), channel_id=1, source_target_pairs={{2,0},{3,1},{0,2},{1,3},{6,4},{7,5},{4,6},{5,7},{10,8},{11,9},{8,1... | collective-permute-start | bytes 253448 | tf_op jit(solution)/shard_map/ppermute | solution.py:26
  21.3 4.9 %collective-permute-start.3 = (bf16[6,7040]{1,0:T(8,128)(2,1)S(1)}, bf16[6,7040]{1,0:T(8,128)(2,1)S(1)}, u32[]{:S(2)}, u32[]{:S(2)}) collective-permute-start(bf16[6,7040]{1,0:T(8,128)(2,1)S(1)} %constant_dynamic-update-slice_fusion.8), channel_id=1, source_target_pairs={{1,0},{2,1},{3,2},{0,3},{5,4},{6,5},{7,6},{4,7},{9,8},{10,9},{11,1... | collective-permute-start | bytes 253448 | tf_op jit(solution)/shard_map/ppermute | solution.py:26
  24.1 3.2 copy-start.5
  24.1 8.0 %copy-start.19 = (bf16[400]{0:T(512)(128)(2,1)S(1)}, bf16[400]{0:T(512)(128)(2,1)}, u32[]{:S(2)}) copy-start(bf16[400]{0:T(512)(128)(2,1)} %param.49) | copy-start | bytes 2404
  24.2 11.8 %copy-start.18 = (s32[2,1,16,2]{2,3,1,0:T(2,128)S(1)}, s32[2,1,16,2]{2,3,1,0:T(2,128)}, u32[]{:S(2)}) copy-start(s32[2,1,16,2]{2,3,1,0:T(2,128)} %param.28) | copy-start | bytes 772
  24.2 12.0 %copy-start.13 = (s32[2,128,16,2]{1,3,2,0:T(2,128)S(1)}, s32[2,128,16,2]{1,3,2,0:T(2,128)}, u32[]{:S(2)}) copy-start(s32[2,128,16,2]{1,3,2,0:T(2,128)} %param.29) | copy-start | bytes 98308
  27.3 18.4 %collective-permute-start.7 = (bf16[400,768]{1,0:T(8,128)(2,1)S(1)}, bf16[400,768]{1,0:T(8,128)(2,1)S(1)}, u32[]{:S(2)}, u32[]{:S(2)}) collective-permute-start(bf16[400,768]{1,0:T(8,128)(2,1)S(1)} %bitcast.131), channel_id=1, source_target_pairs={{2,0},{3,1},{0,2},{1,3},{6,4},{7,5},{4,6},{5,7},{10,8},{11,9},{8,1... | collective-permute-start | bytes 1843208 | tf_op jit(solution)/shard_map/ppermute | solution.py:26
  30.1 27.4 %collective-permute-start.6 = (bf16[400,768]{1,0:T(8,128)(2,1)S(1)}, bf16[400,768]{1,0:T(8,128)(2,1)S(1)}, u32[]{:S(2)}, u32[]{:S(2)}) collective-permute-start(bf16[400,768]{1,0:T(8,128)(2,1)S(1)} %bitcast.132), channel_id=1, source_target_pairs={{1,0},{2,1},{3,2},{0,3},{5,4},{6,5},{7,6},{4,7},{9,8},{10,9},{11,1... | collective-permute-start | bytes 1843208 | tf_op jit(solution)/shard_map/ppermute | solution.py:26
  31.9 25.6 %collective-permute-start.8 = (bf16[400,768]{1,0:T(8,128)(2,1)S(1)}, bf16[400,768]{1,0:T(8,128)(2,1)S(1)}, u32[]{:S(2)}, u32[]{:S(2)}) collective-permute-start(bf16[400,768]{1,0:T(8,128)(2,1)S(1)} %bitcast.133), channel_id=1, source_target_pairs={{3,0},{0,1},{1,2},{2,3},{7,4},{4,5},{5,6},{6,7},{11,8},{8,9},{9,10... | collective-permute-start | bytes 1843208 | tf_op jit(solution)/shard_map/ppermute | solution.py:26
  32.1 30.8 %collective-permute-start.10 = (bf16[400]{0:T(512)(128)(2,1)S(1)}, bf16[400]{0:T(512)(128)(2,1)S(1)}, u32[]{:S(2)}, u32[]{:S(2)}) collective-permute-start(bf16[400]{0:T(512)(128)(2,1)S(1)} %copy-done.19), channel_id=1, source_target_pairs={{1,0},{2,1},{3,2},{0,3},{5,4},{6,5},{7,6},{4,7},{9,8},{10,9},{11,1... | collective-permute-start | bytes 2408 | tf_op jit(solution)/shard_map/ppermute | solution.py:26
  35.2 27.7 %collective-permute-start.12 = (bf16[400]{0:T(512)(128)(2,1)S(1)}, bf16[400]{0:T(512)(128)(2,1)S(1)}, u32[]{:S(2)}, u32[]{:S(2)}) collective-permute-start(bf16[400]{0:T(512)(128)(2,1)S(1)} %copy-done.19), channel_id=1, source_target_pairs={{3,0},{0,1},{1,2},{2,3},{7,4},{4,5},{5,6},{6,7},{11,8},{8,9},{9,10... | collective-permute-start | bytes 2408 | tf_op jit(solution)/shard_map/ppermute | solution.py:26
  45.8 11.7 %copy-start.6 = (bf16[400,768]{1,0:T(8,128)(2,1)}, bf16[400,768]{1,0:T(8,128)(2,1)S(1)}, u32[]{:S(2)}) copy-start(bf16[400,768]{1,0:T(8,128)(2,1)S(1)} %collective-permute-done.7) | copy-start | bytes 1843204
  45.8 17.1 %collective-permute-start.11 = (bf16[400]{0:T(512)(128)(2,1)S(1)}, bf16[400]{0:T(512)(128)(2,1)S(1)}, u32[]{:S(2)}, u32[]{:S(2)}) collective-permute-start(bf16[400]{0:T(512)(128)(2,1)S(1)} %copy-done.19), channel_id=1, source_target_pairs={{2,0},{3,1},{0,2},{1,3},{6,4},{7,5},{4,6},{5,7},{10,8},{11,9},{8,1... | collective-permute-start | bytes 2408 | tf_op jit(solution)/shard_map/ppermute | solution.py:26
  57.5 0.8 copy-start.10
  57.5 1.0 copy-start.8
  58.5 3.4 copy-start.11
  58.5 3.4 copy-start.12
  60.2 10.2 %collective-permute-start.9 = (bf16[4,400,768]{2,1,0:T(8,128)(2,1)}, bf16[4,400,768]{2,1,0:T(8,128)(2,1)S(1)}, u32[]{:S(2)}, u32[]{:S(2)}) collective-permute-start(bf16[4,400,768]{2,1,0:T(8,128)(2,1)} %pad_maximum_fusion.2), channel_id=1, source_target_pairs={{16,0},{0,16},{17,1},{1,17},{18,2},{2,18},{19,3},{3,19},{20,4},{4,... | collective-permute-start | bytes 7372808 | tf_op jit(solution)/shard_map/ppermute | solution.py:26
  61.9 6.9 %copy-start.7 = (bf16[400,768]{1,0:T(8,128)(2,1)S(1)}, bf16[400,768]{1,0:T(8,128)(2,1)}, u32[]{:S(2)}) copy-start(bf16[400,768]{1,0:T(8,128)(2,1)} %copy-done.6) | copy-start | bytes 1843204
  62.9 2.0 collective-permute-start.13
  65.1 4.6 %copy-start.9 = (bf16[400,768]{1,0:T(8,128)(2,1)S(1)}, bf16[400,768]{1,0:T(8,128)(2,1)}, u32[]{:S(2)}) copy-start(bf16[400,768]{1,0:T(8,128)(2,1)} %copy-done.8) | copy-start | bytes 1843204
  81.8 23.5 %copy-start.15 = (s32[2,256]{1,0:T(2,128)S(1)}, s32[2,256]{1,0:T(2,128)}, u32[]{:S(2)}) copy-start(s32[2,256]{1,0:T(2,128)} %param.27) | copy-start | bytes 6148
  99.9 38.0 %all-to-all-start = ((bf16[16,64,896]{2,1,0:T(8,128)(2,1)}), bf16[16,64,896]{2,1,0:T(8,128)(2,1)S(1)}, u32[]{:S(2)}, u32[]{:S(2)}) async-start(bf16[16,64,896]{2,1,0:T(8,128)(2,1)} %pad_maximum_fusion.3), calls=%async_computation | async-start | bytes 3670016 | tf_op jit(solution)/shard_map/all_to_all | solution.py:46
  137.9 57.9 %copy-start.1 = (bf16[16,64,896]{2,1,0:T(8,128)(2,1)}, bf16[16,64,896]{2,1,0:T(8,128)(2,1)S(1)}, u32[]{:S(2)}) copy-start(bf16[16,64,896]{2,1,0:T(8,128)(2,1)S(1)} %all-to-all-done) | copy-start | bytes 5505028
  137.9 31.4 %all-to-all-start.1 = ((bf16[16,64,768]{2,1,0:T(8,128)(2,1)}), bf16[16,64,768]{2,1,0:T(8,128)(2,1)S(1)}, u32[]{:S(2)}, u32[]{:S(2)}) async-start(bf16[16,64,768]{2,1,0:T(8,128)(2,1)} %get-tuple-element.103), calls=%async_computation.1 | async-start | bytes 3145728 | tf_op jit(solution)/shard_map/all_to_all | solution.py:46
  169.3 1.1 copy-start.2
  195.8 6.8 %copy-start.14 = (f32[64,1]{1,0:T(8,128)S(1)}, f32[64,1]{1,0:T(8,128)}, u32[]{:S(2)}) copy-start(f32[64,1]{1,0:T(8,128)} %get-tuple-element.112) | copy-start | bytes 772
  195.8 30.4 %all-to-all-start.2 = ((bf16[16,80,768]{2,1,0:T(8,128)(2,1)}), bf16[16,80,768]{2,1,0:T(8,128)(2,1)S(1)}, u32[]{:S(2)}, u32[]{:S(2)}) async-start(bf16[16,80,768]{2,1,0:T(8,128)(2,1)} %get-tuple-element.109), calls=%async_computation.2 | async-start | bytes 3932160 | tf_op jit(solution)/shard_map/all_to_all | solution.py:46
  226.3 1.3 copy-start
  242.2 9.9 %collective-permute-start.14 = (bf16[16,128,768]{2,1,0:T(8,128)(2,1)}, bf16[16,128,768]{2,1,0:T(8,128)(2,1)S(1)}, u32[]{:S(2)}, u32[]{:S(2)}) collective-permute-start(bf16[16,128,768]{2,1,0:T(8,128)(2,1)} %get-tuple-element.131), channel_id=1, source_target_pairs={{0,16},{16,0},{1,17},{17,1},{2,18},{18,2},{3,19},{19,3},{4,20},{20... | collective-permute-start | bytes 9437192 | tf_op jit(solution)/shard_map/ppermute | solution.py:31
  242.2 9.9 %copy-start.3 = (bf16[16,128,768]{2,1,0:T(8,128)(2,1)S(1)}, bf16[16,128,768]{2,1,0:T(8,128)(2,1)}, u32[]{:S(2)}) copy-start(bf16[16,128,768]{2,1,0:T(8,128)(2,1)} %get-tuple-element.130) | copy-start | bytes 9437188
  254.7 47.8 %all-to-all-start.3 = ((bf16[16,128,768]{2,1,0:T(8,128)(2,1)}), bf16[16,128,768]{2,1,0:T(8,128)(2,1)S(1)}, u32[]{:S(2)}, u32[]{:S(2)}) async-start(bf16[16,128,768]{2,1,0:T(8,128)(2,1)} %add_convert_fusion), calls=%async_computation.3 | async-start | bytes 6291456 | tf_op jit(solution)/shard_map/all_to_all | solution.py:46
  270.1 32.4 %collective-permute-start.15 = (bf16[16,24,3072]{2,1,0:T(8,128)(2,1)}, bf16[16,24,3072]{2,1,0:T(8,128)(2,1)}, u32[]{:S(2)}, u32[]{:S(2)}) collective-permute-start(bf16[16,24,3072]{2,1,0:T(8,128)(2,1)} %get-tuple-element.138), channel_id=1, source_target_pairs={{0,16},{16,0},{1,17},{17,1},{2,18},{18,2},{3,19},{19,3},{4,20},{20... | collective-permute-start | bytes 7077896 | tf_op jit(solution)/shard_map/ppermute | solution.py:31
  270.8 13.9 %copy-start.16 = (f32[1,1536]{1,0:T(1,128)S(1)}, f32[1,1536]{1,0:T(1,128)}, u32[]{:S(2)}) copy-start(f32[1,1536]{1,0:T(1,128)} %get-tuple-element.147) | copy-start | bytes 18436
  270.8 13.9 %copy-start.17 = (f32[1,1536]{1,0:T(1,128)S(1)}, f32[1,1536]{1,0:T(1,128)}, u32[]{:S(2)}) copy-start(f32[1,1536]{1,0:T(1,128)} %get-tuple-element.148) | copy-start | bytes 18436
  302.5 35.9 %collective-permute-start.16 = (bf16[16,24,3200]{2,1,0:T(8,128)(2,1)}, bf16[16,24,3200]{2,1,0:T(8,128)(2,1)}, u32[]{:S(2)}, u32[]{:S(2)}) collective-permute-start(bf16[16,24,3200]{2,1,0:T(8,128)(2,1)} %get-tuple-element.157), channel_id=1, source_target_pairs={{0,16},{16,0},{1,17},{17,1},{2,18},{18,2},{3,19},{19,3},{4,20},{20... | collective-permute-start | bytes 7372808 | tf_op jit(solution)/shard_map/ppermute | solution.py:31
  307.2 43.6 %all-to-all-start.4 = ((bf16[16,24,3072]{2,1,0:T(8,128)(2,1)}), bf16[16,24,3072]{2,1,0:T(8,128)(2,1)}, u32[]{:S(2)}, u32[]{:S(2)}) async-start(bf16[16,24,3072]{2,1,0:T(8,128)(2,1)} %add_convert_fusion.3), calls=%async_computation.4 | async-start | bytes 4718592 | tf_op jit(solution)/shard_map/all_to_all | solution.py:46
  335.8 3.0 copy-start.4
  350.8 8.6 %collective-permute-start.17 = (bf16[4,408,768]{2,1,0:T(8,128)(2,1)}, bf16[4,408,768]{2,1,0:T(8,128)(2,1)}, u32[]{:S(2)}, u32[]{:S(2)}) collective-permute-start(bf16[4,408,768]{2,1,0:T(8,128)(2,1)} %get-tuple-element.159), channel_id=1, source_target_pairs={{0,16},{16,0},{1,17},{17,1},{2,18},{18,2},{3,19},{19,3},{4,20},{20... | collective-permute-start | bytes 7520264 | tf_op jit(solution)/shard_map/ppermute | solution.py:31
  351.0 51.0 %all-to-all-start.5 = ((bf16[16,24,3200]{2,1,0:T(8,128)(2,1)}), bf16[16,24,3200]{2,1,0:T(8,128)(2,1)}, u32[]{:S(2)}, u32[]{:S(2)}) async-start(bf16[16,24,3200]{2,1,0:T(8,128)(2,1)} %add_convert_fusion.2), calls=%async_computation.5 | async-start | bytes 4915200 | tf_op jit(solution)/shard_map/all_to_all | solution.py:46
  369.9 17.5 %collective-permute-start.18 = (bf16[408,768]{1,0:T(8,128)(2,1)S(1)}, bf16[408,768]{1,0:T(8,128)(2,1)S(1)}, u32[]{:S(2)}, u32[]{:S(2)}) collective-permute-start(bf16[408,768]{1,0:T(8,128)(2,1)S(1)} %get-tuple-element.183), channel_id=1, source_target_pairs={{0,1},{1,2},{2,3},{3,0},{4,5},{5,6},{6,7},{7,4},{8,9},{9,10},{10,1... | collective-permute-start | bytes 1880072 | tf_op jit(solution)/shard_map/ppermute | solution.py:31
  371.4 28.7 %collective-permute-start.20 = (bf16[408,768]{1,0:T(8,128)(2,1)S(1)}, bf16[408,768]{1,0:T(8,128)(2,1)S(1)}, u32[]{:S(2)}, u32[]{:S(2)}) collective-permute-start(bf16[408,768]{1,0:T(8,128)(2,1)S(1)} %get-tuple-element.184), channel_id=1, source_target_pairs={{0,3},{1,0},{2,1},{3,2},{4,7},{5,4},{6,5},{7,6},{8,11},{9,8},{10,9... | collective-permute-start | bytes 1880072 | tf_op jit(solution)/shard_map/ppermute | solution.py:31
  373.2 28.5 %collective-permute-start.19 = (bf16[408,768]{1,0:T(8,128)(2,1)S(1)}, bf16[408,768]{1,0:T(8,128)(2,1)S(1)}, u32[]{:S(2)}, u32[]{:S(2)}) collective-permute-start(bf16[408,768]{1,0:T(8,128)(2,1)S(1)} %get-tuple-element.185), channel_id=1, source_target_pairs={{0,2},{1,3},{2,0},{3,1},{4,6},{5,7},{6,4},{7,5},{8,10},{9,11},{10,... | collective-permute-start | bytes 1880072 | tf_op jit(solution)/shard_map/ppermute | solution.py:31
  402.0 6.4 %copy-start.20 = (f32[512,768]{1,0:T(8,128)S(1)}, f32[512,768]{1,0:T(8,128)}, u32[]{:S(2)}) copy-start(f32[512,768]{1,0:T(8,128)} %get-tuple-element.167) | copy-start | bytes 4718596
  405.0 14.2 %all-to-all-start.6 = ((bf16[4,6,10240]{2,1,0:T(8,128)(2,1)}), bf16[4,6,10240]{2,1,0:T(8,128)(2,1)S(1)}, u32[]{:S(2)}, u32[]{:S(2)}) async-start(bf16[4,6,10240]{2,1,0:T(8,128)(2,1)} %constant_dynamic-update-slice_fusion.18), calls=%async_computation.6 | async-start | bytes 1310720 | tf_op jit(solution)/shard_map/all_to_all | solution.py:46
Sparse Core Ops, SparseCore 0:
  27.5 72.4 all-gather.1

commit v12 on v11

--- a/solution.py
+++ b/solution.py
@@ -757,6 +757,18 @@
     )
 
 
+def pair_kernel(own_ref, got_ref, out_ref):
+    out_ref[...] = (own_ref[...].astype(F32) + got_ref[...].astype(F32)).astype(BF)
+
+
+def pair_call(own, got):
+    places, rows, width = own.shape
+    spec = pl.BlockSpec((places // 4, rows, width), lambda i: (i, 0, 0))
+    return call(
+        pair_kernel, (4,), (own, got), [spec] * 2, [(own.shape, BF)], [spec], [], 1000, 1000
+    )[0]
+
+
 def feed_kernel(
     low_ref,
     expand_ref,
@@ -1085,9 +1097,8 @@
         sums_b,
         g_expand_bias.reshape(width, -1),
     )
-    last_away, tall_all = after(last_away, tall_all)
+    last_away, wide_mine, tall_all = after(last_away, pair_call(*wide_pair), tall_all)
     last_pair = (last_here, give(last_away, "c", 1))
-    wide_mine, tall_all = after(add_cores(wide_pair), tall_all)
     wide_all = swap(wide_mine, ("y", "z"))
     last_mine, wide_all = after(add_cores(last_pair), wide_all)
     last_all = swap(last_mine, ("y", "z"))

time: 438 us -> 434 us (level)
  other arithmetic: 36.3 us -> 31.6 us
    convert_element_type x4 -> x3, other arithmetic: 14.2 us -> 9.53 us  [add_cores(): return (pair[0].astype(F32) + pair[1].astype(F32)).astype(BF)]
    pallas_call x6 -> x7, Pallas kernels: 78.6 us -> 83.1 us  [call(): pl.pallas_call(kernel, grid=grid, in_specs=in_specs, out_specs=out_specs,...]
    all_to_all x7, waiting for transfers between devices: 64.1 us -> 59.6 us  [swap(): return lax.all_to_all(array, axes, 0, 0, tiled=True)]
  transfers between devices with their start and end apart: 29 -> 29, of which waited for: 13 -> 13; matrix products, arithmetic and copies ran while one was open for 18% -> 17% of each run, Pallas kernels for 20% -> 21%
where the time goes in v12:
time: 434 us; the launch traced here: 427 us
  Pallas kernels  130 us (30%)
  waiting for transfers between devices  120 us (28%)
  starting transfers between devices  67.6 us (16%)
  local copies, waits for them, and re-layouts  42.1 us (10%)
  other arithmetic  31.6 us (7%)
  between operations  21.2 us (5%)
  matrix products  14.1 us (3%)
    pallas_call x7, Pallas kernels, call(): pl.pallas_call(kernel, grid=grid, in_specs=in_specs, out_specs=out_specs,...  83.1 us
    all_to_all x7, waiting for transfers between devices, swap(): return lax.all_to_all(array, axes, 0, 0, tiled=True)  59.6 us
    all_to_all x7, starting transfers between devices, swap(): return lax.all_to_all(array, axes, 0, 0, tiled=True)  40.7 us
    ppermute x7, waiting for transfers between devices, give(): return lax.ppermute(array, axis, [(i, (i + k) % n) for i in range(n)])  24.2 us
    pallas_call x2, Pallas kernels, feed_back_call(): pl.pallas_call(functools.partial(feed_back_kernel, closing), grid=(steps,...  21.5 us
    ppermute x14, starting transfers between devices, fetch(): return lax.ppermute(array, axis, [((i + k) % n, i) for i in range(n)])  21 us
    all_gather x1, waiting for transfers between devices, body(): lax.all_gather(jnp.concatenate([tall, fused], axis=1), ('y', 'c', 'z'), a...  18.1 us
    ppermute x14, waiting for transfers between devices, fetch(): return lax.ppermute(array, axis, [((i + k) % n, i) for i in range(n)])  17.9 us
  transfers between devices with their start and end apart: 29, of which 13 were waited for; matrix products, arithmetic and copies ran while one was open for 17% of the time, Pallas kernels for 21%

profile of v12, /device:TPU:0, one launch (start us, length us, event | category | flops | bytes accessed | tf_op | source)
XLA Modules:
  0.0 426.6 jit_solution(12090170573697705671)
XLA Ops:
  7.2 2.9 collective-permute-start
  10.2 2.3 collective-permute-start.1
  13.3 1.5 stack.172
  17.9 1.8 collective-permute-start.5
  21.3 2.0 collective-permute-start.3
  24.2 2.0 collective-permute-done.3
  27.3 2.7 collective-permute-start.7
  30.1 1.9 collective-permute-start.6
  32.1 3.1 collective-permute-start.10
  37.3 1.3 reshape.264
  39.7 6.1 %collective-permute-done.7 = bf16[400,768]{1,0:T(8,128)(2,1)S(1)} collective-permute-done((bf16[400,768]{1,0:T(8,128)(2,1)S(1)}, bf16[400,768]{1,0:T(8,128)(2,1)S(1)}, u32[]{:S(2)}, u32[]{:S(2)}) %collective-permute-start.7) | collective-permute-done | bytes 614432 | tf_op jit(solution)/shard_map/ppermute | solution.py:26
  45.8 2.6 collective-permute-start.11
  48.4 9.1 %collective-permute-done.6 = bf16[400,768]{1,0:T(8,128)(2,1)S(1)} collective-permute-done((bf16[400,768]{1,0:T(8,128)(2,1)S(1)}, bf16[400,768]{1,0:T(8,128)(2,1)S(1)}, u32[]{:S(2)}, u32[]{:S(2)}) %collective-permute-start.6) | collective-permute-done | bytes 614432 | tf_op jit(solution)/shard_map/ppermute | solution.py:26
  58.5 1.7 pad_maximum_fusion.2
  65.1 1.4 select_reduce_fusion
  66.8 2.0 constant_dynamic-update-slice_fusion.16
  70.5 1.7 constant_dynamic-update-slice_fusion.13
  72.1 8.2 %fusion.6 = bf16[16,64,768]{2,1,0:T(8,128)(2,1)S(1)} fusion(bf16[3200,768,1]{1,0,2:T(8,128)(2,1)} %bitcast.143, s32[3200]{0:T(1024)S(1)} %add.225, s32[16,64]{1,0:T(8,128)S(1)} %reshape.263), kind=kOutput, calls=%fused_computation.16 | convolution fusion | flops 5037228032 | bytes 6504960 | tf_op jit(solution)/shard_map/dot_general | solution.py:130
  80.3 1.5 pad_maximum_fusion.3
  81.8 18.1 %all-gather.2.cloned.1.call-done.wq_ref.wk_ref.wv_ref.wa_ref.expand_ref.tall_ref.dense_ref.refs_4_ = bf16[768,10112]{1,0:T(8,128)(2,1)} async-done(((bf16[24,10112]{1,0:T(8,128)(2,1)}), bf16[768,10112]{1,0:T(8,128)(2,1)}) %all-gather.2.cloned.1.call-update) | async-done | bytes 15532048 | tf_op jit(solution)/shard_map/all_gather | solution.py:944
  99.9 5.4 %all-to-all-start = ((bf16[16,64,896]{2,1,0:T(8,128)(2,1)}), bf16[16,64,896]{2,1,0:T(8,128)(2,1)S(1)}, u32[]{:S(2)}, u32[]{:S(2)}) async-start(bf16[16,64,896]{2,1,0:T(8,128)(2,1)} %pad_maximum_fusion.3), calls=%async_computation | async-start | bytes 3670016 | tf_op jit(solution)/shard_map/all_to_all | solution.py:46
  108.5 11.7 %shard_map.408 = (bf16[512,2304]{1,0:T(8,128)(2,1)}, bf16[2,12,256,256]{3,2,1,0:T(8,128)(2,1)}, bf16[512,768]{1,0:T(8,128)(2,1)}, f32[512,768]{1,0:T(8,128)}, bf...) custom-call(bf16[512,768]{1,0:T(8,128)(2,1)} %bitcast.129, s32[2,1,256]{2,1,0:T(1,128)} %broadcast_in_dim.43.row_ref, ...), custom_call_target="tpu_custom_call" | custom-call | flops 1000 | bytes 1000 | tf_op jit(solution)/shard_map/pallas_call | solution.py:211
  120.2 1.0 slice_convert_fusion
  122.1 15.8 %shard_map.409 = (bf16[512,3072]{1,0:T(8,128)(2,1)}, bf16[512,3072]{1,0:T(8,128)(2,1)}, bf16[3072,768]{1,0:T(8,128)(2,1)}, bf16[512,768]{1,0:T(8,128)(2,1)}, f32...) custom-call(bf16[512,768]{1,0:T(8,128)(2,1)} %get-tuple-element.96.l, ...), custom_call_target="tpu_custom_call" | custom-call | flops 1000 | bytes 1000 | tf_op jit(solution)/shard_map/pallas_call | solution.py:321
  137.9 7.8 %all-to-all-start.1 = ((bf16[16,64,768]{2,1,0:T(8,128)(2,1)}), bf16[16,64,768]{2,1,0:T(8,128)(2,1)S(1)}, u32[]{:S(2)}, u32[]{:S(2)}) async-start(bf16[16,64,768]{2,1,0:T(8,128)(2,1)} %get-tuple-element.102), calls=%async_computation.1 | async-start | bytes 3145728 | tf_op jit(solution)/shard_map/all_to_all | solution.py:46
  147.1 1.0 copy.118.label_ref
  148.2 21.2 %all-to-all-done.1 = bf16[16,64,768]{2,1,0:T(8,128)(2,1)S(1)} async-done(((bf16[16,64,768]{2,1,0:T(8,128)(2,1)}), bf16[16,64,768]{2,1,0:T(8,128)(2,1)S(1)}, u32[]{:S(2)}, u32[]{:S(2)}) %all-to-all-start.1) | async-done | bytes 1572896 | tf_op jit(solution)/shard_map/all_to_all | solution.py:46
  169.3 1.1 copy-done.2
  170.5 25.3 %shard_map.410 = (bf16[1024,3200]{1,0:T(8,128)(2,1)}, f32[1024,128]{1,0:T(8,128)}, bf16[16,80,768]{2,1,0:T(8,128)(2,1)}) custom-call(bf16[1024,768]{1,0:T(8,128)(2,1)} %bitcast.124, bf16[3200,768]{1,0:T(8,128)(2,1)} %bitcast.144, f32[1,3200]{1,0:T(1,128)} %reshape.260.b_ref, s32[1,3200]{1,0:T(1,128)} %add.229.column_ref, s32[1024,1]{1,0:T(8,128)} %copy.118.label_ref), custom_call_target="tpu_custom_call" | custom-call | flops 10000000000 | bytes 20000000 | tf_op jit(solution)/shard_map/pallas_call | solution.py:321
  195.8 3.9 all-to-all-start.2
  200.1 1.8 convert_reduce_fusion
  203.3 23.0 %all-to-all-done.2.part_ref = bf16[16,80,768]{2,1,0:T(8,128)(2,1)S(1)} async-done(((bf16[16,80,768]{2,1,0:T(8,128)(2,1)}), bf16[16,80,768]{2,1,0:T(8,128)(2,1)S(1)}, u32[]{:S(2)}, u32[]{:S(2)}) %all-to-all-start.2) | async-done | bytes 1966112 | tf_op jit(solution)/shard_map/all_to_all | solution.py:46
  226.3 1.3 copy-done
  227.6 7.1 %shard_map.411 = (f32[1,1024]{1,0:T(1,128)}, f32[8,128]{1,0:T(8,128)}, f32[768,768]{1,0:T(8,128)}, f32[512,768]{1,0:T(8,128)}, bf16[512,768]{1,0:T(8,128)(2,1)}, /*index=5*/f32[8,768]{1,0:T(8,128)}) custom-call(s32[1]{0:T(128)} %bitcast.46.own_ref, bf16[16,80,768]{2,1,0:T(8,128)(2,1)} %copy-done, bf16[64,768]{1,0:T(8,128)(2,1)} %get-tuple-element.109.head_ref, ...), custom_call_target="tpu_custom_call" | custom-call | flops 300000000 | bytes 10000000 | tf_op jit(solution)/shard_map/pallas_call | solution.py:321
  234.7 7.5 %shard_map.412 = (bf16[16,128,768]{2,1,0:T(8,128)(2,1)}, bf16[16,128,768]{2,1,0:T(8,128)(2,1)}) custom-call(s32[1]{0:T(128)} %bitcast.50.core_ref, bf16[512,3072]{1,0:T(8,128)(2,1)} %get-tuple-element.118.act_ref, bf16[512,768]{1,0:T(8,128)(2,1)} %get-tuple-element.124.dffn_ref.refs_0_, f32[768,768]{1,0:T(8,128)} %get-tuple-element.120.dense_ref, ...), custom_call_target="tpu_custom_call" | custom-call | flops 1000 | bytes 1000 | tf_op jit(solution)/shard_map/pallas_call | solution.py:321
  242.2 9.9 %shard_map.413 = (bf16[16,24,3072]{2,1,0:T(8,128)(2,1)}, bf16[16,24,3072]{2,1,0:T(8,128)(2,1)}, f32[1,1536]{1,0:T(1,128)}, f32[512,768]{1,0:T(8,128)}) custom-call(s32[1]{0:T(128)} %bitcast.50.core_ref, bf16[512,768]{1,0:T(8,128)(2,1)} %get-tuple-element.124.dffn_ref.refs_0_, bf16[3072,768]{1,0:T(8,128)(2,1)} %get-tuple-element.125.refs_1_, ...), custom_call_target="tpu_custom_call" | custom-call | flops 1000 | bytes 1000 | tf_op jit(solution)/shard_map/pallas_call | solution.py:676
  252.1 2.6 add_convert_fusion
  254.7 3.8 all-to-all-start.3
  258.5 11.6 %shard_map.414 = (bf16[16,24,3072]{2,1,0:T(8,128)(2,1)}, bf16[16,24,3072]{2,1,0:T(8,128)(2,1)}, f32[1,1536]{1,0:T(1,128)}, f32[512,768]{1,0:T(8,128)}, bf16[512,768]{1,0:T(8,128)(2,1)}, /*index=5*/f32[8,768]{1,0:T(8,128)}) custom-call(s32[1]{0:T(128)} %bitcast.50.core_ref, ...), custom_call_target="tpu_custom_call", output_to_operand_aliasing={{0}: (10, {}), {1}: (11, {})} | custom-call | flops 1000 | bytes 1000 | tf_op jit(solution)/shard_map/pallas_call | solution.py:676
  270.8 13.9 %shard_map.415 = (bf16[512,2304]{1,0:T(8,128)(2,1)}, f32[1,2304]{1,0:T(1,128)}) custom-call(bf16[512,768]{1,0:T(8,128)(2,1)} %get-tuple-element.136.dbranch_ref, bf16[512,2304]{1,0:T(8,128)(2,1)} %get-tuple-element.137.qkv_ref, bf16[2,12,256,256]{3,2,1,0:T(8,128)(2,1)} %get-tuple-element.138.probs_ref, ...), custom_call_target="tpu_custom_call" | custom-call | flops 1000 | bytes 1000 | tf_op jit(solution)/shard_map/pallas_call | solution.py:291
  284.8 1.1 reshape.247.bias_ref
  286.0 7.8 %shard_map.416 = (bf16[16,24,3200]{2,1,0:T(8,128)(2,1)}, bf16[16,24,3200]{2,1,0:T(8,128)(2,1)}) custom-call(s32[1]{0:T(128)} %bitcast.50.core_ref, bf16[512,768]{1,0:T(8,128)(2,1)} %bitcast.130, bf16[512,2304]{1,0:T(8,128)(2,1)} %get-tuple-element.166.dfused_ref, bf16[512,768]{1,0:T(8,128)(2,1)} %get-tuple-element.140.attended_ref, ...), custom_call_target="tpu_custom_call" | custom-call | flops 1000 | bytes 1000 | tf_op jit(solution)/shard_map/pallas_call | solution.py:321
  293.8 4.5 %shard_map.417 = bf16[16,24,3072]{2,1,0:T(8,128)(2,1)} custom-call(bf16[16,24,3072]{2,1,0:T(8,128)(2,1)} %get-tuple-element.147.own_ref, bf16[16,24,3072]{2,1,0:T(8,128)(2,1)} %collective-permute-done.15.got_ref), custom_call_target="tpu_custom_call" | custom-call | flops 1000 | bytes 1000 | tf_op jit(solution)/shard_map/pallas_call | solution.py:321
  298.2 4.2 all-to-all-done.3
  302.5 10.0 %all-to-all-start.4 = ((bf16[16,24,3072]{2,1,0:T(8,128)(2,1)}), bf16[16,24,3072]{2,1,0:T(8,128)(2,1)}, u32[]{:S(2)}, u32[]{:S(2)}) async-start(bf16[16,24,3072]{2,1,0:T(8,128)(2,1)} %shard_map.417), calls=%async_computation.4 | async-start | bytes 4718592 | tf_op jit(solution)/shard_map/all_to_all | solution.py:46
  312.4 15.1 %shard_map.418 = (bf16[3200,768]{1,0:T(8,128)(2,1)}, f32[1,3200]{1,0:T(1,128)}) custom-call(bf16[1024,3200]{1,0:T(8,128)(2,1)} %get-tuple-element.105.expl_ref, bf16[1024,768]{1,0:T(8,128)(2,1)} %bitcast.125, s32[1,3200]{1,0:T(1,128)} %add.229.column_ref, s32[1024,1]{1,0:T(8,128)} %copy.118.label_ref, f32[1024,1]{1,0:T(8,128)} %select_multiply_fusion.scale_ref, ...), custom_call_target="tpu_custom_call" | custom-call | flops 1000 | bytes 1000 | tf_op jit(solution)/shard_map/pallas_call | solution.py:321
  328.4 2.8 fusion.23
  331.1 2.5 pad_maximum_fusion
  334.1 3.8 add_convert_fusion.2
  338.0 8.1 %all-to-all-done.4 = bf16[16,24,3072]{2,1,0:T(8,128)(2,1)} async-done(((bf16[16,24,3072]{2,1,0:T(8,128)(2,1)}), bf16[16,24,3072]{2,1,0:T(8,128)(2,1)}, u32[]{:S(2)}, u32[]{:S(2)}) %all-to-all-start.4) | async-done | bytes 2359328 | tf_op jit(solution)/shard_map/all_to_all | solution.py:46
  346.1 6.4 %all-to-all-start.5 = ((bf16[16,24,3200]{2,1,0:T(8,128)(2,1)}), bf16[16,24,3200]{2,1,0:T(8,128)(2,1)}, u32[]{:S(2)}, u32[]{:S(2)}) async-start(bf16[16,24,3200]{2,1,0:T(8,128)(2,1)} %add_convert_fusion.2), calls=%async_computation.5 | async-start | bytes 4915200 | tf_op jit(solution)/shard_map/all_to_all | solution.py:46
  352.5 2.1 reduce_sum.95
  361.9 3.1 add_convert_fusion.1
  365.2 1.5 collective-permute-start.18
  366.7 1.8 collective-permute-start.20
  368.5 1.8 collective-permute-start.19
  372.9 9.8 %collective-permute-done.18 = bf16[408,768]{1,0:T(8,128)(2,1)S(1)} collective-permute-done((bf16[408,768]{1,0:T(8,128)(2,1)S(1)}, bf16[408,768]{1,0:T(8,128)(2,1)S(1)}, u32[]{:S(2)}, u32[]{:S(2)}) %collective-permute-start.18) | collective-permute-done | bytes 626720 | tf_op jit(solution)/shard_map/ppermute | solution.py:31
  382.7 12.7 %collective-permute-done.20 = bf16[408,768]{1,0:T(8,128)(2,1)S(1)} collective-permute-done((bf16[408,768]{1,0:T(8,128)(2,1)S(1)}, bf16[408,768]{1,0:T(8,128)(2,1)S(1)}, u32[]{:S(2)}, u32[]{:S(2)}) %collective-permute-start.20) | collective-permute-done | bytes 626720 | tf_op jit(solution)/shard_map/ppermute | solution.py:31
  395.4 1.6 collective-permute-done.19
  397.3 2.2 reduce_sum.96
  400.3 3.5 all-to-all-start.6
  403.8 5.9 %fusion.9 = f32[512,768]{1,0:T(8,128)} fusion(f32[512,768]{1,0:T(8,128)S(1)} %copy-done.20, bf16[512,2304]{1,0:T(8,128)(2,1)} %get-tuple-element.166.dfused_ref, bf16[768,10112]{1,0:T(8,128)(2,1)} %all-gather.2.cloned.1.call-done.wq_ref.wk_ref.wv_ref.wa_ref.expand_ref.tall_ref.dense_ref.refs_4_), kind=kOutput, calls=%fused_computation.17 | convolution fusion | flops 1812332544 | bytes 9043968 | tf_op jit(solution)/shard_map/dot_general | solution.py:138
  410.3 1.1 slice_bitcast_fusion
  411.4 3.1 all-to-all-done.6
  (178 shorter events, 38.4 us)
Async XLA Ops:
  7.2 92.7 %all-gather.2.cloned.1.call-start = ((), (), s32[]{:S(2)}) async-start(), calls=%async_computation.7 | async-start | bytes 16017408 | tf_op jit(solution)/shard_map/all_gather | solution.py:944
  7.2 14.1 %collective-permute-start = (bf16[24,768]{1,0:T(8,128)(2,1)}, bf16[24,768]{1,0:T(8,128)(2,1)S(1)}, u32[]{:S(2)}, u32[]{:S(2)}) collective-permute-start(bf16[24,768]{1,0:T(8,128)(2,1)} %param.40), channel_id=1, source_target_pairs={{1,0},{2,1},{3,2},{0,3},{5,4},{6,5},{7,6},{4,7},{9,8},{10,9},{11,1... | collective-permute-start | bytes 110600 | tf_op jit(solution)/shard_map/ppermute | solution.py:26
  10.1 13.1 %collective-permute-start.2 = (bf16[24,768]{1,0:T(8,128)(2,1)}, bf16[24,768]{1,0:T(8,128)(2,1)S(1)}, u32[]{:S(2)}, u32[]{:S(2)}) collective-permute-start(bf16[24,768]{1,0:T(8,128)(2,1)} %param.40), channel_id=1, source_target_pairs={{3,0},{0,1},{1,2},{2,3},{7,4},{4,5},{5,6},{6,7},{11,8},{8,9},{9,10... | collective-permute-start | bytes 110600 | tf_op jit(solution)/shard_map/ppermute | solution.py:26
  10.2 13.1 %collective-permute-start.1 = (bf16[24,768]{1,0:T(8,128)(2,1)}, bf16[24,768]{1,0:T(8,128)(2,1)S(1)}, u32[]{:S(2)}, u32[]{:S(2)}) collective-permute-start(bf16[24,768]{1,0:T(8,128)(2,1)} %param.40), channel_id=1, source_target_pairs={{2,0},{3,1},{0,2},{1,3},{6,4},{7,5},{4,6},{5,7},{10,8},{11,9},{8,1... | collective-permute-start | bytes 110600 | tf_op jit(solution)/shard_map/ppermute | solution.py:26
  17.9 8.3 %collective-permute-start.5 = (bf16[6,7040]{1,0:T(8,128)(2,1)S(1)}, bf16[6,7040]{1,0:T(8,128)(2,1)S(1)}, u32[]{:S(2)}, u32[]{:S(2)}) collective-permute-start(bf16[6,7040]{1,0:T(8,128)(2,1)S(1)} %constant_dynamic-update-slice_fusion.8), channel_id=1, source_target_pairs={{3,0},{0,1},{1,2},{2,3},{7,4},{4,5},{5,6},{6,7},{11,8},{8,9},{9,10... | collective-permute-start | bytes 253448 | tf_op jit(solution)/shard_map/ppermute | solution.py:26
  19.7 6.5 %collective-permute-start.4 = (bf16[6,7040]{1,0:T(8,128)(2,1)S(1)}, bf16[6,7040]{1,0:T(8,128)(2,1)S(1)}, u32[]{:S(2)}, u32[]{:S(2)}) collective-permute-start(bf16[6,7040]{1,0:T(8,128)(2,1)S(1)} %constant_dynamic-update-slice_fusion.8), channel_id=1, source_target_pairs={{2,0},{3,1},{0,2},{1,3},{6,4},{7,5},{4,6},{5,7},{10,8},{11,9},{8,1... | collective-permute-start | bytes 253448 | tf_op jit(solution)/shard_map/ppermute | solution.py:26
  21.3 4.9 %collective-permute-start.3 = (bf16[6,7040]{1,0:T(8,128)(2,1)S(1)}, bf16[6,7040]{1,0:T(8,128)(2,1)S(1)}, u32[]{:S(2)}, u32[]{:S(2)}) collective-permute-start(bf16[6,7040]{1,0:T(8,128)(2,1)S(1)} %constant_dynamic-update-slice_fusion.8), channel_id=1, source_target_pairs={{1,0},{2,1},{3,2},{0,3},{5,4},{6,5},{7,6},{4,7},{9,8},{10,9},{11,1... | collective-permute-start | bytes 253448 | tf_op jit(solution)/shard_map/ppermute | solution.py:26
  24.1 3.2 copy-start.5
  24.1 8.0 %copy-start.19 = (bf16[400]{0:T(512)(128)(2,1)S(1)}, bf16[400]{0:T(512)(128)(2,1)}, u32[]{:S(2)}) copy-start(bf16[400]{0:T(512)(128)(2,1)} %param.49) | copy-start | bytes 2404
  24.2 11.8 %copy-start.18 = (s32[2,1,16,2]{2,3,1,0:T(2,128)S(1)}, s32[2,1,16,2]{2,3,1,0:T(2,128)}, u32[]{:S(2)}) copy-start(s32[2,1,16,2]{2,3,1,0:T(2,128)} %param.28) | copy-start | bytes 772
  24.2 12.0 %copy-start.13 = (s32[2,128,16,2]{1,3,2,0:T(2,128)S(1)}, s32[2,128,16,2]{1,3,2,0:T(2,128)}, u32[]{:S(2)}) copy-start(s32[2,128,16,2]{1,3,2,0:T(2,128)} %param.29) | copy-start | bytes 98308
  27.3 18.4 %collective-permute-start.7 = (bf16[400,768]{1,0:T(8,128)(2,1)S(1)}, bf16[400,768]{1,0:T(8,128)(2,1)S(1)}, u32[]{:S(2)}, u32[]{:S(2)}) collective-permute-start(bf16[400,768]{1,0:T(8,128)(2,1)S(1)} %bitcast.131), channel_id=1, source_target_pairs={{2,0},{3,1},{0,2},{1,3},{6,4},{7,5},{4,6},{5,7},{10,8},{11,9},{8,1... | collective-permute-start | bytes 1843208 | tf_op jit(solution)/shard_map/ppermute | solution.py:26
  30.1 27.4 %collective-permute-start.6 = (bf16[400,768]{1,0:T(8,128)(2,1)S(1)}, bf16[400,768]{1,0:T(8,128)(2,1)S(1)}, u32[]{:S(2)}, u32[]{:S(2)}) collective-permute-start(bf16[400,768]{1,0:T(8,128)(2,1)S(1)} %bitcast.132), channel_id=1, source_target_pairs={{1,0},{2,1},{3,2},{0,3},{5,4},{6,5},{7,6},{4,7},{9,8},{10,9},{11,1... | collective-permute-start | bytes 1843208 | tf_op jit(solution)/shard_map/ppermute | solution.py:26
  31.9 25.6 %collective-permute-start.8 = (bf16[400,768]{1,0:T(8,128)(2,1)S(1)}, bf16[400,768]{1,0:T(8,128)(2,1)S(1)}, u32[]{:S(2)}, u32[]{:S(2)}) collective-permute-start(bf16[400,768]{1,0:T(8,128)(2,1)S(1)} %bitcast.133), channel_id=1, source_target_pairs={{3,0},{0,1},{1,2},{2,3},{7,4},{4,5},{5,6},{6,7},{11,8},{8,9},{9,10... | collective-permute-start | bytes 1843208 | tf_op jit(solution)/shard_map/ppermute | solution.py:26
  32.1 30.8 %collective-permute-start.10 = (bf16[400]{0:T(512)(128)(2,1)S(1)}, bf16[400]{0:T(512)(128)(2,1)S(1)}, u32[]{:S(2)}, u32[]{:S(2)}) collective-permute-start(bf16[400]{0:T(512)(128)(2,1)S(1)} %copy-done.19), channel_id=1, source_target_pairs={{1,0},{2,1},{3,2},{0,3},{5,4},{6,5},{7,6},{4,7},{9,8},{10,9},{11,1... | collective-permute-start | bytes 2408 | tf_op jit(solution)/shard_map/ppermute | solution.py:26
  35.2 27.7 %collective-permute-start.12 = (bf16[400]{0:T(512)(128)(2,1)S(1)}, bf16[400]{0:T(512)(128)(2,1)S(1)}, u32[]{:S(2)}, u32[]{:S(2)}) collective-permute-start(bf16[400]{0:T(512)(128)(2,1)S(1)} %copy-done.19), channel_id=1, source_target_pairs={{3,0},{0,1},{1,2},{2,3},{7,4},{4,5},{5,6},{6,7},{11,8},{8,9},{9,10... | collective-permute-start | bytes 2408 | tf_op jit(solution)/shard_map/ppermute | solution.py:26
  45.8 11.7 %copy-start.6 = (bf16[400,768]{1,0:T(8,128)(2,1)}, bf16[400,768]{1,0:T(8,128)(2,1)S(1)}, u32[]{:S(2)}) copy-start(bf16[400,768]{1,0:T(8,128)(2,1)S(1)} %collective-permute-done.7) | copy-start | bytes 1843204
  45.8 17.1 %collective-permute-start.11 = (bf16[400]{0:T(512)(128)(2,1)S(1)}, bf16[400]{0:T(512)(128)(2,1)S(1)}, u32[]{:S(2)}, u32[]{:S(2)}) collective-permute-start(bf16[400]{0:T(512)(128)(2,1)S(1)} %copy-done.19), channel_id=1, source_target_pairs={{2,0},{3,1},{0,2},{1,3},{6,4},{7,5},{4,6},{5,7},{10,8},{11,9},{8,1... | collective-permute-start | bytes 2408 | tf_op jit(solution)/shard_map/ppermute | solution.py:26
  57.5 0.8 copy-start.10
  57.5 1.0 copy-start.8
  58.5 3.4 copy-start.11
  58.5 3.4 copy-start.12
  60.2 10.2 %collective-permute-start.9 = (bf16[4,400,768]{2,1,0:T(8,128)(2,1)}, bf16[4,400,768]{2,1,0:T(8,128)(2,1)S(1)}, u32[]{:S(2)}, u32[]{:S(2)}) collective-permute-start(bf16[4,400,768]{2,1,0:T(8,128)(2,1)} %pad_maximum_fusion.2), channel_id=1, source_target_pairs={{16,0},{0,16},{17,1},{1,17},{18,2},{2,18},{19,3},{3,19},{20,4},{4,... | collective-permute-start | bytes 7372808 | tf_op jit(solution)/shard_map/ppermute | solution.py:26
  61.9 6.9 %copy-start.7 = (bf16[400,768]{1,0:T(8,128)(2,1)S(1)}, bf16[400,768]{1,0:T(8,128)(2,1)}, u32[]{:S(2)}) copy-start(bf16[400,768]{1,0:T(8,128)(2,1)} %copy-done.6) | copy-start | bytes 1843204
  62.9 2.0 collective-permute-start.13
  65.1 4.6 %copy-start.9 = (bf16[400,768]{1,0:T(8,128)(2,1)S(1)}, bf16[400,768]{1,0:T(8,128)(2,1)}, u32[]{:S(2)}) copy-start(bf16[400,768]{1,0:T(8,128)(2,1)} %copy-done.8) | copy-start | bytes 1843204
  81.8 23.5 %copy-start.15 = (s32[2,256]{1,0:T(2,128)S(1)}, s32[2,256]{1,0:T(2,128)}, u32[]{:S(2)}) copy-start(s32[2,256]{1,0:T(2,128)} %param.27) | copy-start | bytes 6148
  99.9 38.0 %all-to-all-start = ((bf16[16,64,896]{2,1,0:T(8,128)(2,1)}), bf16[16,64,896]{2,1,0:T(8,128)(2,1)S(1)}, u32[]{:S(2)}, u32[]{:S(2)}) async-start(bf16[16,64,896]{2,1,0:T(8,128)(2,1)} %pad_maximum_fusion.3), calls=%async_computation | async-start | bytes 3670016 | tf_op jit(solution)/shard_map/all_to_all | solution.py:46
  137.9 57.9 %copy-start.1 = (bf16[16,64,896]{2,1,0:T(8,128)(2,1)}, bf16[16,64,896]{2,1,0:T(8,128)(2,1)S(1)}, u32[]{:S(2)}) copy-start(bf16[16,64,896]{2,1,0:T(8,128)(2,1)S(1)} %all-to-all-done) | copy-start | bytes 5505028
  137.9 31.4 %all-to-all-start.1 = ((bf16[16,64,768]{2,1,0:T(8,128)(2,1)}), bf16[16,64,768]{2,1,0:T(8,128)(2,1)S(1)}, u32[]{:S(2)}, u32[]{:S(2)}) async-start(bf16[16,64,768]{2,1,0:T(8,128)(2,1)} %get-tuple-element.102), calls=%async_computation.1 | async-start | bytes 3145728 | tf_op jit(solution)/shard_map/all_to_all | solution.py:46
  169.3 1.1 copy-start.2
  195.8 6.8 %copy-start.14 = (f32[64,1]{1,0:T(8,128)S(1)}, f32[64,1]{1,0:T(8,128)}, u32[]{:S(2)}) copy-start(f32[64,1]{1,0:T(8,128)} %get-tuple-element.111) | copy-start | bytes 772
  195.8 30.4 %all-to-all-start.2 = ((bf16[16,80,768]{2,1,0:T(8,128)(2,1)}), bf16[16,80,768]{2,1,0:T(8,128)(2,1)S(1)}, u32[]{:S(2)}, u32[]{:S(2)}) async-start(bf16[16,80,768]{2,1,0:T(8,128)(2,1)} %get-tuple-element.108), calls=%async_computation.2 | async-start | bytes 3932160 | tf_op jit(solution)/shard_map/all_to_all | solution.py:46
  226.3 1.3 copy-start
  242.2 9.9 %collective-permute-start.14 = (bf16[16,128,768]{2,1,0:T(8,128)(2,1)}, bf16[16,128,768]{2,1,0:T(8,128)(2,1)S(1)}, u32[]{:S(2)}, u32[]{:S(2)}) collective-permute-start(bf16[16,128,768]{2,1,0:T(8,128)(2,1)} %get-tuple-element.130), channel_id=1, source_target_pairs={{0,16},{16,0},{1,17},{17,1},{2,18},{18,2},{3,19},{19,3},{4,20},{20... | collective-permute-start | bytes 9437192 | tf_op jit(solution)/shard_map/ppermute | solution.py:31
  242.2 9.9 %copy-start.3 = (bf16[16,128,768]{2,1,0:T(8,128)(2,1)S(1)}, bf16[16,128,768]{2,1,0:T(8,128)(2,1)}, u32[]{:S(2)}) copy-start(bf16[16,128,768]{2,1,0:T(8,128)(2,1)} %get-tuple-element.129) | copy-start | bytes 9437188
  254.7 47.8 %all-to-all-start.3 = ((bf16[16,128,768]{2,1,0:T(8,128)(2,1)}), bf16[16,128,768]{2,1,0:T(8,128)(2,1)S(1)}, u32[]{:S(2)}, u32[]{:S(2)}) async-start(bf16[16,128,768]{2,1,0:T(8,128)(2,1)} %add_convert_fusion), calls=%async_computation.3 | async-start | bytes 6291456 | tf_op jit(solution)/shard_map/all_to_all | solution.py:46
  270.1 23.7 %collective-permute-start.15 = (bf16[16,24,3072]{2,1,0:T(8,128)(2,1)}, bf16[16,24,3072]{2,1,0:T(8,128)(2,1)}, u32[]{:S(2)}, u32[]{:S(2)}) collective-permute-start(bf16[16,24,3072]{2,1,0:T(8,128)(2,1)} %get-tuple-element.148), channel_id=1, source_target_pairs={{0,16},{16,0},{1,17},{17,1},{2,18},{18,2},{3,19},{19,3},{4,20},{20... | collective-permute-start | bytes 7077896 | tf_op jit(solution)/shard_map/ppermute | solution.py:31
  270.8 13.9 %copy-start.16 = (f32[1,1536]{1,0:T(1,128)S(1)}, f32[1,1536]{1,0:T(1,128)}, u32[]{:S(2)}) copy-start(f32[1,1536]{1,0:T(1,128)} %get-tuple-element.144) | copy-start | bytes 18436
  270.8 13.9 %copy-start.17 = (f32[1,1536]{1,0:T(1,128)S(1)}, f32[1,1536]{1,0:T(1,128)}, u32[]{:S(2)}) copy-start(f32[1,1536]{1,0:T(1,128)} %get-tuple-element.145) | copy-start | bytes 18436
  302.5 31.2 %collective-permute-start.16 = (bf16[16,24,3200]{2,1,0:T(8,128)(2,1)}, bf16[16,24,3200]{2,1,0:T(8,128)(2,1)}, u32[]{:S(2)}, u32[]{:S(2)}) collective-permute-start(bf16[16,24,3200]{2,1,0:T(8,128)(2,1)} %get-tuple-element.155), channel_id=1, source_target_pairs={{0,16},{16,0},{1,17},{17,1},{2,18},{18,2},{3,19},{19,3},{4,20},{20... | collective-permute-start | bytes 7372808 | tf_op jit(solution)/shard_map/ppermute | solution.py:31
  302.5 43.6 %all-to-all-start.4 = ((bf16[16,24,3072]{2,1,0:T(8,128)(2,1)}), bf16[16,24,3072]{2,1,0:T(8,128)(2,1)}, u32[]{:S(2)}, u32[]{:S(2)}) async-start(bf16[16,24,3072]{2,1,0:T(8,128)(2,1)} %shard_map.417), calls=%async_computation.4 | async-start | bytes 4718592 | tf_op jit(solution)/shard_map/all_to_all | solution.py:46
  331.1 3.0 copy-start.4
  346.1 8.5 %collective-permute-start.17 = (bf16[4,408,768]{2,1,0:T(8,128)(2,1)}, bf16[4,408,768]{2,1,0:T(8,128)(2,1)}, u32[]{:S(2)}, u32[]{:S(2)}) collective-permute-start(bf16[4,408,768]{2,1,0:T(8,128)(2,1)} %get-tuple-element.157), channel_id=1, source_target_pairs={{0,16},{16,0},{1,17},{17,1},{2,18},{18,2},{3,19},{19,3},{4,20},{20... | collective-permute-start | bytes 7520264 | tf_op jit(solution)/shard_map/ppermute | solution.py:31
  346.1 51.2 %all-to-all-start.5 = ((bf16[16,24,3200]{2,1,0:T(8,128)(2,1)}), bf16[16,24,3200]{2,1,0:T(8,128)(2,1)}, u32[]{:S(2)}, u32[]{:S(2)}) async-start(bf16[16,24,3200]{2,1,0:T(8,128)(2,1)} %add_convert_fusion.2), calls=%async_computation.5 | async-start | bytes 4915200 | tf_op jit(solution)/shard_map/all_to_all | solution.py:46
  365.2 17.5 %collective-permute-start.18 = (bf16[408,768]{1,0:T(8,128)(2,1)S(1)}, bf16[408,768]{1,0:T(8,128)(2,1)S(1)}, u32[]{:S(2)}, u32[]{:S(2)}) collective-permute-start(bf16[408,768]{1,0:T(8,128)(2,1)S(1)} %get-tuple-element.181), channel_id=1, source_target_pairs={{0,1},{1,2},{2,3},{3,0},{4,5},{5,6},{6,7},{7,4},{8,9},{9,10},{10,1... | collective-permute-start | bytes 1880072 | tf_op jit(solution)/shard_map/ppermute | solution.py:31
  366.7 28.7 %collective-permute-start.20 = (bf16[408,768]{1,0:T(8,128)(2,1)S(1)}, bf16[408,768]{1,0:T(8,128)(2,1)S(1)}, u32[]{:S(2)}, u32[]{:S(2)}) collective-permute-start(bf16[408,768]{1,0:T(8,128)(2,1)S(1)} %get-tuple-element.182), channel_id=1, source_target_pairs={{0,3},{1,0},{2,1},{3,2},{4,7},{5,4},{6,5},{7,6},{8,11},{9,8},{10,9... | collective-permute-start | bytes 1880072 | tf_op jit(solution)/shard_map/ppermute | solution.py:31
  368.5 28.6 %collective-permute-start.19 = (bf16[408,768]{1,0:T(8,128)(2,1)S(1)}, bf16[408,768]{1,0:T(8,128)(2,1)S(1)}, u32[]{:S(2)}, u32[]{:S(2)}) collective-permute-start(bf16[408,768]{1,0:T(8,128)(2,1)S(1)} %get-tuple-element.183), channel_id=1, source_target_pairs={{0,2},{1,3},{2,0},{3,1},{4,6},{5,7},{6,4},{7,5},{8,10},{9,11},{10,... | collective-permute-start | bytes 1880072 | tf_op jit(solution)/shard_map/ppermute | solution.py:31
  397.3 6.4 %copy-start.20 = (f32[512,768]{1,0:T(8,128)S(1)}, f32[512,768]{1,0:T(8,128)}, u32[]{:S(2)}) copy-start(f32[512,768]{1,0:T(8,128)} %get-tuple-element.165) | copy-start | bytes 4718596
  400.3 14.2 %all-to-all-start.6 = ((bf16[4,6,10240]{2,1,0:T(8,128)(2,1)}), bf16[4,6,10240]{2,1,0:T(8,128)(2,1)S(1)}, u32[]{:S(2)}, u32[]{:S(2)}) async-start(bf16[4,6,10240]{2,1,0:T(8,128)(2,1)} %constant_dynamic-update-slice_fusion.18), calls=%async_computation.6 | async-start | bytes 1310720 | tf_op jit(solution)/shard_map/all_to_all | solution.py:46
Sparse Core Ops, SparseCore 0:
  27.5 72.4 all-gather.1
